TPU v7x, 32 devices: a whole 2x2x4 slice. The times are simulated.
32 devices in a mesh: groups: 2 (over y), blk: 4 (over z), uly: 2 (over x), cfg: 2 (over core).
Axes of the slice: x: 2, y: 2, z: 4, core: 2. Of those that a mesh axis runs over, the one named last changes fastest.
Arguments:
- query_rows: bfloat16 [2, 1024, 1536], P('cfg', ('groups', 'blk', 'uly')), parts along dimension 1, may hold values from -6 to 6
- key_rows: bfloat16 [2, 1024, 1536], P('cfg', ('groups', 'blk', 'uly')), parts along dimension 1, may hold values from -6 to 6
- value_rows: bfloat16 [2, 1024, 1536], P('cfg', ('groups', 'blk', 'uly')), parts along dimension 1, may hold values from -6 to 6
Outputs:
- attended: bfloat16 [2, 1024, 1536], P('cfg', ('groups', 'blk', 'uly')), parts along dimension 1
There are 2 independent parts, one for each index of `groups`. A program takes and returns all parts, laid end to end along the dimension named above; each array names one. Nothing has to cross between parts.
All inputs are finite; a program needn't handle non-finite values.
Results may differ from a plain program's by a relative error of at most 0.0045.
Values may be sent and summed in bfloat16 or wider, within the bound.
No kernel may reach another device: no remote copies, remote signals or barrier semaphores. Data moves between devices by JAX's collectives and lax.ppermute only.
A program may use at most 128 MiB of HBM per device.

v0:
```python
import math

import jax
import jax.numpy as jnp
from jax import lax
from jax.sharding import PartitionSpec as P

HD = 128


def attend(queries, key_part, value_part):
    query_mat = queries[0, :, 0]
    row_count, head_count, head_size = query_mat.shape
    score_scale = 1.0 / math.sqrt(head_size)
    start_state = (
        jnp.full((head_count, row_count), -1e30, jnp.float32),
        jnp.zeros((head_count, row_count), jnp.float32),
        jnp.zeros((row_count, head_count, head_size), jnp.float32),
    )

    def absorb(state, pieces):
        key_piece = pieces[0][0, :, 0]
        value_piece = pieces[1][0, :, 0]
        scores = (
            jnp.einsum("qhd,khd->hqk", query_mat, key_piece, preferred_element_type=jnp.float32)
            * score_scale
        )
        running, totals, accumulated = state
        new_max = jnp.maximum(running, jnp.max(scores, axis=2))
        weights = jnp.exp(scores - new_max[:, :, None])
        factor = jnp.exp(running - new_max)
        totals = totals * factor + jnp.sum(weights, axis=2)
        probabilities = weights.astype(jnp.bfloat16)
        contrib = jnp.einsum(
            "hqk,khd->qhd", probabilities, value_piece, preferred_element_type=jnp.float32
        )
        accumulated = accumulated * factor.T[:, :, None] + contrib
        return (new_max, totals, accumulated)

    whole_keys, whole_values = (
        lax.all_gather(key_part, "blk", axis=1, tiled=True),
        lax.all_gather(value_part, "blk", axis=1, tiled=True),
    )
    key_count = whole_keys.shape[1]
    block_rows = math.gcd(key_count, 1024)

    def one_block(state, counter):
        offset = counter * block_rows
        key_block = lax.dynamic_slice_in_dim(whole_keys, offset, block_rows, 1)
        value_block = lax.dynamic_slice_in_dim(whole_values, offset, block_rows, 1)
        return (absorb(state, (key_block, value_block)), None)

    result, unused = lax.scan(
        one_block, start_state, jnp.arange(key_count // block_rows, dtype=jnp.int32)
    )
    output = (result[2] / result[1].T[:, :, None]).astype(jnp.bfloat16)
    return output.reshape(1, row_count, 1, head_count, head_size)


def regroup_back(attended_part):
    return lax.all_to_all(attended_part, "uly", split_axis=1, concat_axis=2, tiled=True)


def whole_pass(triple):
    return regroup_back(attend(triple[0], triple[1], triple[2]))


def local(query_rows, key_rows, value_rows):
    ulysses = lax.axis_size("uly")
    tokens = query_rows.shape[1]
    width = query_rows.shape[2]
    heads_local = width // HD // ulysses

    def split_heads(array):
        return array.reshape(1, tokens, ulysses, heads_local, HD)

    sectioned = (split_heads(query_rows), split_heads(key_rows), split_heads(value_rows))
    moved = (
        lax.all_to_all(sectioned[0], "uly", split_axis=2, concat_axis=1, tiled=True),
        lax.all_to_all(sectioned[1], "uly", split_axis=2, concat_axis=1, tiled=True),
        lax.all_to_all(sectioned[2], "uly", split_axis=2, concat_axis=1, tiled=True),
    )
    merged = whole_pass(moved)
    return merged.reshape(1, tokens, width)


def solution(mesh):
    in_specs = (
        P("cfg", ("groups", "blk", "uly"), None),
        P("cfg", ("groups", "blk", "uly"), None),
        P("cfg", ("groups", "blk", "uly"), None),
    )
    out_specs = P("cfg", ("groups", "blk", "uly"), None)
    return jax.shard_map(local, mesh=mesh, in_specs=in_specs, out_specs=out_specs, check_vma=False)
```

profile of v0, /device:TPU:0, one launch (start us, length us, event | category | flops | bytes accessed | tf_op | source)
XLA Modules:
  0.0 69.3 jit_solution(18183577460159070147)
XLA Ops:
  0.0 0.0 copy-start
  0.0 1.2 %reshape.23 = bf16[1,64,2,6,128]{4,3,2,1,0:T(8,128)(2,1)S(1)} reshape(bf16[1,64,1536]{2,1,0:T(8,128)(2,1)} %param.4) | data formatting | bytes 393216 | tf_op jit(solution)/shard_map/reshape | solution.py:75
  1.2 0.7 %copy.14 = bf16[1,64,2,6,128]{4,1,3,0,2:T(8,128)(2,1)} copy(bf16[1,64,2,6,128]{4,3,2,1,0:T(8,128)(2,1)S(1)} %reshape.23) | data formatting | bytes 393216 | tf_op jit(solution)/shard_map/reshape | solution.py:75
  1.9 4.2 %all-to-all-start.1 = ((bf16[1,64,2,6,128]{4,1,3,0,2:T(8,128)(2,1)}), bf16[1,64,2,6,128]{4,1,3,0,2:T(8,128)(2,1)S(1)}, u32[]{:S(2)}, u32[]{:S(2)}) async-start(bf16[1,64,2,6,128]{4,1,3,0,2:T(8,128)(2,1)} %copy.14), calls=%async_computation.1 | async-start | bytes 393216 | tf_op jit(solution)/shard_map/all_to_all | solution.py:80
  6.1 1.2 %reshape.22 = bf16[1,64,2,6,128]{4,3,2,1,0:T(8,128)(2,1)S(1)} reshape(bf16[1,64,1536]{2,1,0:T(8,128)(2,1)} %param.3) | data formatting | bytes 393216 | tf_op jit(solution)/shard_map/reshape | solution.py:75
  7.3 0.7 %copy.12 = bf16[1,64,2,6,128]{4,1,3,0,2:T(8,128)(2,1)} copy(bf16[1,64,2,6,128]{4,3,2,1,0:T(8,128)(2,1)S(1)} %reshape.22) | data formatting | bytes 393216 | tf_op jit(solution)/shard_map/reshape | solution.py:75
  8.0 0.0 copy-done
  8.0 0.2 reshape.24
  8.3 0.7 %copy.16 = bf16[1,64,2,6,128]{4,1,3,0,2:T(8,128)(2,1)} copy(bf16[1,64,2,6,128]{4,3,2,1,0:T(8,128)(2,1)S(1)} %reshape.24) | data formatting | bytes 393216 | tf_op jit(solution)/shard_map/reshape | solution.py:75
  9.0 2.3 %all-to-all-done.1 = bf16[1,64,2,6,128]{4,1,3,0,2:T(8,128)(2,1)S(1)} async-done(((bf16[1,64,2,6,128]{4,1,3,0,2:T(8,128)(2,1)}), bf16[1,64,2,6,128]{4,1,3,0,2:T(8,128)(2,1)S(1)}, u32[]{:S(2)}, u32[]{:S(2)}) %all-to-all-start.1) | async-done | bytes 196640 | tf_op jit(solution)/shard_map/all_to_all | solution.py:80
  11.3 3.4 %all-to-all-start = ((bf16[1,64,2,6,128]{4,1,3,0,2:T(8,128)(2,1)}), bf16[1,64,2,6,128]{4,1,3,0,2:T(8,128)(2,1)S(1)}, u32[]{:S(2)}, u32[]{:S(2)}) async-start(bf16[1,64,2,6,128]{4,1,3,0,2:T(8,128)(2,1)} %copy.12), calls=%async_computation | async-start | bytes 393216 | tf_op jit(solution)/shard_map/all_to_all | solution.py:79
  14.8 20.0 %all_gather.6 = bf16[1,512,1,6,128]{4,1,3,2,0:T(8,128)(2,1)S(1)} all-gather(bf16[1,128,1,6,128]{4,1,3,2,0:T(8,128)(2,1)S(1)} %bitcast.51), channel_id=1, replica_groups=mesh['groups'=2,'blk'=4,'uly'=2,'cfg'=2] {'blk'}, dimensions={1}, use_global_device_ids=true | all-gather | bytes 983040 | tf_op jit(solution)/shard_map/all_gather | solution.py:41
  34.8 0.0 all-to-all-done
  34.8 3.4 %all-to-all-start.2 = ((bf16[1,64,2,6,128]{4,1,3,0,2:T(8,128)(2,1)}), bf16[1,64,2,6,128]{4,1,3,0,2:T(8,128)(2,1)S(1)}, u32[]{:S(2)}, u32[]{:S(2)}) async-start(bf16[1,64,2,6,128]{4,1,3,0,2:T(8,128)(2,1)} %copy.16), calls=%async_computation.2 | async-start | bytes 393216 | tf_op jit(solution)/shard_map/all_to_all | solution.py:81
  38.2 0.4 fusion.10
  38.7 0.5 fusion
  39.2 3.8 %all-to-all-done.2 = bf16[1,64,2,6,128]{4,1,3,0,2:T(8,128)(2,1)S(1)} async-done(((bf16[1,64,2,6,128]{4,1,3,0,2:T(8,128)(2,1)}), bf16[1,64,2,6,128]{4,1,3,0,2:T(8,128)(2,1)S(1)}, u32[]{:S(2)}, u32[]{:S(2)}) %all-to-all-start.2) | async-done | bytes 196640 | tf_op jit(solution)/shard_map/all_to_all | solution.py:81
  43.0 17.1 %all_gather.7 = bf16[1,512,1,6,128]{4,1,3,2,0:T(8,128)(2,1)S(1)} all-gather(bf16[1,128,1,6,128]{4,1,3,2,0:T(8,128)(2,1)S(1)} %bitcast.52), channel_id=1, replica_groups=mesh['groups'=2,'blk'=4,'uly'=2,'cfg'=2] {'blk'}, dimensions={1}, use_global_device_ids=true | all-gather | bytes 983040 | tf_op jit(solution)/shard_map/all_gather | solution.py:42
  60.1 0.5 fusion.5
  60.7 0.1 copy.18
  60.8 7.6 %all_to_all.66 = bf16[1,128,1,6,128]{4,3,2,0,1:T(8,128)(2,1)S(1)} all-to-all(bf16[1,128,1,6,128]{4,3,2,0,1:T(8,128)(2,1)S(1)} %copy.18), channel_id=1, replica_groups=mesh['groups'=2,'blk'=4,'uly'=2,'cfg'=2] {'uly'}, dimensions={1} | all-to-all | bytes 393216 | tf_op jit(solution)/shard_map/all_to_all | solution.py:61
  68.4 0.9 %reshape.26 = bf16[1,64,1536]{2,1,0:T(8,128)(2,1)} reshape(bf16[1,64,2,1,6,128]{5,4,2,1,3,0:T(8,128)(2,1)S(1)} %bitcast.45) | data formatting | bytes 393216 | tf_op jit(solution)/shard_map/reshape | solution.py:84
  (6 shorter events, 0.1 us)
Async XLA Ops:
  0.0 8.0 %copy-start = (bf16[1,64,1536]{2,1,0:T(8,128)(2,1)S(1)}, bf16[1,64,1536]{2,1,0:T(8,128)(2,1)}, u32[]{:S(2)}) copy-start(bf16[1,64,1536]{2,1,0:T(8,128)(2,1)} %param.5) | copy-start | bytes 589828
  1.9 9.4 %all-to-all-start.1 = ((bf16[1,64,2,6,128]{4,1,3,0,2:T(8,128)(2,1)}), bf16[1,64,2,6,128]{4,1,3,0,2:T(8,128)(2,1)S(1)}, u32[]{:S(2)}, u32[]{:S(2)}) async-start(bf16[1,64,2,6,128]{4,1,3,0,2:T(8,128)(2,1)} %copy.14), calls=%async_computation.1 | async-start | bytes 393216 | tf_op jit(solution)/shard_map/all_to_all | solution.py:80
  11.3 23.5 %all-to-all-start = ((bf16[1,64,2,6,128]{4,1,3,0,2:T(8,128)(2,1)}), bf16[1,64,2,6,128]{4,1,3,0,2:T(8,128)(2,1)S(1)}, u32[]{:S(2)}, u32[]{:S(2)}) async-start(bf16[1,64,2,6,128]{4,1,3,0,2:T(8,128)(2,1)} %copy.12), calls=%async_computation | async-start | bytes 393216 | tf_op jit(solution)/shard_map/all_to_all | solution.py:79
  34.8 8.2 %all-to-all-start.2 = ((bf16[1,64,2,6,128]{4,1,3,0,2:T(8,128)(2,1)}), bf16[1,64,2,6,128]{4,1,3,0,2:T(8,128)(2,1)S(1)}, u32[]{:S(2)}, u32[]{:S(2)}) async-start(bf16[1,64,2,6,128]{4,1,3,0,2:T(8,128)(2,1)} %copy.16), calls=%async_computation.2 | async-start | bytes 393216 | tf_op jit(solution)/shard_map/all_to_all | solution.py:81
where the time goes:
time: 69.7 us; the launch traced here: 69.3 us
  blocking collectives  44.7 us (64%)
  starting transfers between devices  11.1 us (16%)
  waiting for transfers between devices  6.09 us (9%)
  local copies, waits for them, and re-layouts  5.94 us (9%)
  matrix products  0.99 us (1%)
    all_gather x1, blocking collectives, attend(): lax.all_gather(key_part, 'blk', axis=1, tiled=True)  20 us
    all_gather x1, blocking collectives, attend(): lax.all_gather(value_part, 'blk', axis=1, tiled=True)  17.1 us
    all_to_all x1, blocking collectives, regroup_back(): lax.all_to_all(attended_part, 'uly', split_axis=1, concat_axis=2, tiled=T...  7.56 us
    reshape x6, local copies, waits for them, and re-layouts, split_heads(): return array.reshape(1, tokens, ulysses, heads_local, HD)  4.8 us
    all_to_all x1, starting transfers between devices, local(): lax.all_to_all(sectioned[1], 'uly', split_axis=2, concat_axis=1, tiled=True)  4.21 us
    all_to_all x1, waiting for transfers between devices, local(): lax.all_to_all(sectioned[2], 'uly', split_axis=2, concat_axis=1, tiled=True)  3.81 us
    all_to_all x1, starting transfers between devices, local(): lax.all_to_all(sectioned[0], 'uly', split_axis=2, concat_axis=1, tiled=True)  3.43 us
    all_to_all x1, starting transfers between devices, local(): lax.all_to_all(sectioned[2], 'uly', split_axis=2, concat_axis=1, tiled=True)  3.43 us
  transfers between devices with their start and end apart: 3, of which 2 were waited for; matrix products, arithmetic and copies ran while one was open for 6% of the time, Pallas kernels for 0%

commit v1 on v0

--- a/solution.py
+++ b/solution.py
@@ -1,11 +1,16 @@
+import functools
 import math
 
 import jax
 import jax.numpy as jnp
 from jax import lax
+from jax.experimental import pallas as pl
+from jax.experimental.pallas import tpu as pltpu
 from jax.sharding import PartitionSpec as P
 
 HD = 128
+ANY = pl.BlockSpec(memory_space=pl.ANY)
+VMEM = pl.BlockSpec(memory_space=pltpu.VMEM)
 
 
 def attend(queries, key_part, value_part):
@@ -57,31 +62,147 @@
     return output.reshape(1, row_count, 1, head_count, head_size)
 
 
-def regroup_back(attended_part):
-    return lax.all_to_all(attended_part, "uly", split_axis=1, concat_axis=2, tiled=True)
-
-
-def whole_pass(triple):
-    return regroup_back(attend(triple[0], triple[1], triple[2]))
-
-
-def local(query_rows, key_rows, value_rows):
+def local_generic(query_rows, key_rows, value_rows):
     ulysses = lax.axis_size("uly")
     tokens = query_rows.shape[1]
     width = query_rows.shape[2]
     heads_local = width // HD // ulysses
 
     def split_heads(array):
-        return array.reshape(1, tokens, ulysses, heads_local, HD)
-
-    sectioned = (split_heads(query_rows), split_heads(key_rows), split_heads(value_rows))
-    moved = (
-        lax.all_to_all(sectioned[0], "uly", split_axis=2, concat_axis=1, tiled=True),
-        lax.all_to_all(sectioned[1], "uly", split_axis=2, concat_axis=1, tiled=True),
-        lax.all_to_all(sectioned[2], "uly", split_axis=2, concat_axis=1, tiled=True),
-    )
-    merged = whole_pass(moved)
+        array = array.reshape(1, tokens, ulysses, heads_local, HD)
+        return lax.all_to_all(array, "uly", split_axis=2, concat_axis=1, tiled=True)
+
+    mixed = attend(split_heads(query_rows), split_heads(key_rows), split_heads(value_rows))
+    merged = lax.all_to_all(mixed, "uly", split_axis=1, concat_axis=2, tiled=True)
     return merged.reshape(1, tokens, width)
+
+
+def pack_kernel(blocks, part, q_ref, k_ref, v_ref, *refs):
+    outs, sems = refs[:-1], refs[-1]
+    me = lax.axis_index("blk")
+    copies = []
+    for s in range(blocks):
+        columns = pl.ds(pl.multiple_of((me ^ s) * part, 128), part)
+        kv_out, q_out = outs[2 * s], outs[2 * s + 1]
+        copies.append((k_ref.at[0, :, columns], kv_out.at[0]))
+        copies.append((v_ref.at[0, :, columns], kv_out.at[1]))
+        copies.append((q_ref.at[0, :, columns], q_out))
+    started = [
+        pltpu.make_async_copy(src, dst, sems.at[at]) for at, (src, dst) in enumerate(copies)
+    ]
+    for copy in started:
+        copy.start()
+    for copy in started:
+        copy.wait()
+
+
+def attend_kernel(blocks, columns_of, *refs):
+    q_refs = refs[:blocks]
+    kv_refs = refs[blocks : blocks + blocks * columns_of]
+    out_refs = refs[blocks + blocks * columns_of :]
+    tokens, part = q_refs[0].shape
+    scale = 1.0 / math.sqrt(HD)
+    for head in range(part // HD):
+        lanes = slice(head * HD, (head + 1) * HD)
+        queries = jnp.concatenate([ref[:, lanes] for ref in q_refs], axis=0)
+        keys = jnp.concatenate([ref[0, :, lanes] for ref in kv_refs], axis=0)
+        values = jnp.concatenate([ref[1, :, lanes] for ref in kv_refs], axis=0)
+        scores = (
+            lax.dot_general(
+                queries, keys, (((1,), (1,)), ((), ())), preferred_element_type=jnp.float32
+            )
+            * scale
+        )
+        weights = jnp.exp(scores - jnp.max(scores, axis=1, keepdims=True))
+        totals = jnp.sum(weights, axis=1, keepdims=True)
+        mixed = jnp.dot(
+            weights.astype(jnp.bfloat16), values, preferred_element_type=jnp.float32
+        )
+        result = (mixed / totals).astype(jnp.bfloat16)
+        for at, ref in enumerate(out_refs):
+            ref[:, lanes] = result[at * tokens : (at + 1) * tokens]
+
+
+def unpack_kernel(blocks, part, *refs):
+    ins, out_ref, sems = refs[:blocks], refs[blocks], refs[-1]
+    me = lax.axis_index("blk")
+    started = []
+    for s in range(blocks):
+        columns = pl.ds(pl.multiple_of((me ^ s) * part, 128), part)
+        started.append(pltpu.make_async_copy(ins[s], out_ref.at[0, :, columns], sems.at[s]))
+    for copy in started:
+        copy.start()
+    for copy in started:
+        copy.wait()
+
+
+def local_blocks(query_rows, key_rows, value_rows):
+    blocks, columns_of = lax.axis_size("blk"), lax.axis_size("uly")
+    tokens, width = query_rows.shape[1:]
+    part = width // blocks
+    heads = part // HD
+    kind = query_rows.dtype
+    kv_shape = jax.ShapeDtypeStruct((2, tokens, part), kind)
+    q_shape = jax.ShapeDtypeStruct((tokens, part), kind)
+
+    packed = pl.pallas_call(
+        functools.partial(pack_kernel, blocks, part),
+        out_shape=[kv_shape, q_shape] * blocks,
+        in_specs=[ANY] * 3,
+        out_specs=[ANY] * (2 * blocks),
+        scratch_shapes=[pltpu.SemaphoreType.DMA((3 * blocks,))],
+        cost_estimate=pl.CostEstimate(flops=0, bytes_accessed=6 * tokens * width * 2, transcendentals=0),
+        name="pack",
+    )(query_rows, key_rows, value_rows)
+    own_kv, own_q = packed[0::2], packed[1::2]
+
+    def to_block(array, s):
+        return lax.ppermute(array, "blk", [(i, i ^ s) for i in range(blocks)]) if s else array
+
+    def to_column(array, t):
+        return lax.ppermute(array, "uly", [(i, (i + t) % columns_of) for i in range(columns_of)])
+
+    order = list(range(blocks))[::-1]
+    kv = {s: to_block(own_kv[s], s) for s in order}
+    queries = {s: to_block(own_q[s], s) for s in order}
+    all_kv = [kv[s] for s in range(blocks)]
+    for t in range(1, columns_of):
+        all_kv += [to_column(kv[s], t) for s in range(blocks)]
+
+    all_tokens = tokens * blocks * columns_of
+    pairs = heads * tokens * blocks * all_tokens
+    mixed = pl.pallas_call(
+        functools.partial(attend_kernel, blocks, columns_of),
+        out_shape=[q_shape] * blocks,
+        in_specs=[VMEM] * (blocks + blocks * columns_of),
+        out_specs=[VMEM] * blocks,
+        compiler_params=pltpu.CompilerParams(vmem_limit_bytes=32 * 1024 * 1024),
+        cost_estimate=pl.CostEstimate(
+            flops=4 * HD * pairs,
+            bytes_accessed=2 * part * (2 * all_tokens + 2 * tokens * blocks),
+            transcendentals=pairs,
+        ),
+        name="attend",
+    )(*[queries[s] for s in range(blocks)], *all_kv)
+
+    back = [to_block(mixed[s], s) for s in range(blocks)]
+    return pl.pallas_call(
+        functools.partial(unpack_kernel, blocks, part),
+        out_shape=jax.ShapeDtypeStruct((1, tokens, width), kind),
+        in_specs=[ANY] * blocks,
+        out_specs=ANY,
+        scratch_shapes=[pltpu.SemaphoreType.DMA((blocks,))],
+        cost_estimate=pl.CostEstimate(flops=0, bytes_accessed=2 * tokens * width * 2, transcendentals=0),
+        name="unpack",
+    )(*back)
+
+
+def local(query_rows, key_rows, value_rows):
+    blocks = lax.axis_size("blk")
+    heads = query_rows.shape[2] // HD
+    few = heads % blocks == 0 and blocks & (blocks - 1) == 0
+    plan = local_blocks if few else local_generic
+    return plan(query_rows, key_rows, value_rows)
 
 
 def solution(mesh):

time: 69.7 us -> 62.3 us (0.89)
  blocking collectives: 44.7 us -> 0 us
  Pallas kernels: 0 us -> 27.3 us
  starting transfers between devices: 11.1 us -> 21 us
  waiting for transfers between devices: 6.09 us -> 10.9 us
  local copies, waits for them, and re-layouts: 5.94 us -> 2.9 us
  matrix products: 0.99 us -> 0 us
    all_gather x2 -> x0, blocking collectives: 37.1 us -> none  [the longest x1 20 us: attend(): lax.all_gather(key_part, 'blk', axis=1, tiled=True)]
    pallas_call x0 -> x3, Pallas kernels: none -> 27.3 us  [the longest x1 19.1 us: local_blocks(): pl.pallas_call(functools.partial(pack_kernel, blocks, part), out_shape=[k...]
    ppermute x0 -> x13, starting transfers between devices: none -> 21 us  [the longest x9 16.9 us: to_block(): lax.ppermute(array, 'blk', [(i, i ^ s) for i in range(blocks)])]
    all_to_all x3 -> x0, starting transfers between devices: 11.1 us -> none  [the longest x1 4.21 us: local(): lax.all_to_all(sectioned[1], 'uly', split_axis=2, concat_axis=1, tiled=True)]
    ppermute x0 -> x13, waiting for transfers between devices: none -> 10.9 us  [the longest x9 10.9 us: to_block(): lax.ppermute(array, 'blk', [(i, i ^ s) for i in range(blocks)])]
    all_to_all x1 -> x0, blocking collectives: 7.56 us -> none  [regroup_back(): lax.all_to_all(attended_part, 'uly', split_axis=1, concat_axis=2, tiled=T...]
    all_to_all x3 -> x0, waiting for transfers between devices: 6.09 us -> none  [the longest x1 3.81 us: local(): lax.all_to_all(sectioned[2], 'uly', split_axis=2, concat_axis=1, tiled=True)]
    reshape x8 -> x0, local copies, waits for them, and re-layouts: 5.84 us -> none  [the longest x6 4.8 us: split_heads(): return array.reshape(1, tokens, ulysses, heads_local, HD)]
  transfers between devices with their start and end apart: 3 -> 13, of which waited for: 2 -> 5; matrix products, arithmetic and copies ran while one was open for 6% -> 0% of each run, Pallas kernels for 0% -> 0%
where the time goes in v1:
time: 62.3 us; the launch traced here: 62.1 us
  Pallas kernels  27.3 us (44%)
  starting transfers between devices  21 us (34%)
  waiting for transfers between devices  10.9 us (17%)
  local copies, waits for them, and re-layouts  2.9 us (5%)
    pallas_call x1, Pallas kernels, local_blocks(): pl.pallas_call(functools.partial(pack_kernel, blocks, part), out_shape=[k...  19.1 us
    ppermute x9, starting transfers between devices, to_block(): lax.ppermute(array, 'blk', [(i, i ^ s) for i in range(blocks)])  16.9 us
    ppermute x9, waiting for transfers between devices, to_block(): lax.ppermute(array, 'blk', [(i, i ^ s) for i in range(blocks)])  10.9 us
    pallas_call x1, Pallas kernels, local_blocks(): pl.pallas_call(functools.partial(unpack_kernel, blocks, part), out_shape=...  7.09 us
    ppermute x4, starting transfers between devices, to_column(): lax.ppermute(array, 'uly', [(i, (i + t) % columns_of) for i in range(colu...  4.05 us
    unnamed x12, local copies, waits for them, and re-layouts  2.9 us
  transfers between devices with their start and end apart: 13, of which 5 were waited for; matrix products, arithmetic and copies ran while one was open for 0% of the time, Pallas kernels for 0%

profile of v1, /device:TPU:0, one launch (start us, length us, event | category | flops | bytes accessed | tf_op | source)
XLA Modules:
  0.0 62.1 jit_solution(906652592652341115)
XLA Ops:
  0.0 19.1 %pack.1 = (bf16[2,64,384]{2,1,0:T(8,128)(2,1)}, bf16[64,384]{1,0:T(8,128)(2,1)}, bf16[2,64,384]{2,1,0:T(8,128)(2,1)}, bf16[64,384]{1,0:T(8,128)(2,1)}, bf16[2,64...) custom-call(bf16[1,64,1536]{2,1,0:T(8,128)(2,1)} %q_ref.1, ...), custom_call_target="tpu_custom_call" | custom-call | bytes 1179648 | tf_op jit(solution)/shard_map/pack/pallas_call | solution.py:148
  19.1 3.1 %collective-permute-start.3 = (bf16[2,64,384]{2,1,0:T(8,128)(2,1)}, bf16[2,64,384]{2,1,0:T(8,128)(2,1)S(1)}, u32[]{:S(2)}, u32[]{:S(2)}) collective-permute-start(bf16[2,64,384]{2,1,0:T(8,128)(2,1)} %get-tuple-element.22), channel_id=1, source_target_pairs={{0,4},{4,0},{8,12},{12,8},{1,5},{5,1},{9,13},{13,9},{2,6},{6,2},{1... | collective-permute-start | bytes 294920 | tf_op jit(solution)/shard_map/ppermute | solution.py:160
  22.2 2.6 %collective-permute-start.4 = (bf16[2,64,384]{2,1,0:T(8,128)(2,1)}, bf16[2,64,384]{2,1,0:T(8,128)(2,1)S(1)}, u32[]{:S(2)}, u32[]{:S(2)}) collective-permute-start(bf16[2,64,384]{2,1,0:T(8,128)(2,1)} %get-tuple-element.23), channel_id=1, source_target_pairs={{0,8},{4,12},{8,0},{12,4},{1,9},{5,13},{9,1},{13,5},{2,10},{6,14},... | collective-permute-start | bytes 294920 | tf_op jit(solution)/shard_map/ppermute | solution.py:160
  24.8 0.0 collective-permute-start.5
  24.8 0.9 %collective-permute-start = (bf16[64,384]{1,0:T(8,128)(2,1)}, bf16[64,384]{1,0:T(8,128)(2,1)S(1)}, u32[]{:S(2)}, u32[]{:S(2)}) collective-permute-start(bf16[64,384]{1,0:T(8,128)(2,1)} %get-tuple-element.18), channel_id=1, source_target_pairs={{0,4},{4,0},{8,12},{12,8},{1,5},{5,1},{9,13},{13,9},{2,6},{6,2},{1... | collective-permute-start | bytes 147464 | tf_op jit(solution)/shard_map/ppermute | solution.py:160
  25.7 3.5 %collective-permute-start.1 = (bf16[64,384]{1,0:T(8,128)(2,1)}, bf16[64,384]{1,0:T(8,128)(2,1)S(1)}, u32[]{:S(2)}, u32[]{:S(2)}) collective-permute-start(bf16[64,384]{1,0:T(8,128)(2,1)} %get-tuple-element.19), channel_id=1, source_target_pairs={{0,8},{4,12},{8,0},{12,4},{1,9},{5,13},{9,1},{13,5},{2,10},{6,14},... | collective-permute-start | bytes 147464 | tf_op jit(solution)/shard_map/ppermute | solution.py:160
  29.1 1.4 %collective-permute-done.refs_1_ = bf16[64,384]{1,0:T(8,128)(2,1)S(1)} collective-permute-done((bf16[64,384]{1,0:T(8,128)(2,1)}, bf16[64,384]{1,0:T(8,128)(2,1)S(1)}, u32[]{:S(2)}, u32[]{:S(2)}) %collective-permute-start) | collective-permute-done | bytes 49184 | tf_op jit(solution)/shard_map/ppermute | solution.py:160
  30.6 1.5 %collective-permute-start.6 = (bf16[2,64,384]{2,1,0:T(8,128)(2,1)}, bf16[2,64,384]{2,1,0:T(8,128)(2,1)S(1)}, u32[]{:S(2)}, u32[]{:S(2)}) collective-permute-start(bf16[2,64,384]{2,1,0:T(8,128)(2,1)} %get-tuple-element.21.refs_4_), channel_id=1, source_target_pairs={{0,2},{2,0},{1,3},{3,1},{4,6},{6,4},{5,7},{7,5},{8,10},{10,8},{9,1... | collective-permute-start | bytes 294920 | tf_op jit(solution)/shard_map/ppermute | solution.py:163
  32.1 0.0 collective-permute-done.3.refs_5_
  32.1 0.5 collective-permute-start.7
  32.6 1.3 %collective-permute-done.4.refs_6_ = bf16[2,64,384]{2,1,0:T(8,128)(2,1)S(1)} collective-permute-done((bf16[2,64,384]{2,1,0:T(8,128)(2,1)}, bf16[2,64,384]{2,1,0:T(8,128)(2,1)S(1)}, u32[]{:S(2)}, u32[]{:S(2)}) %collective-permute-start.4) | collective-permute-done | bytes 98336 | tf_op jit(solution)/shard_map/ppermute | solution.py:160
  34.0 1.5 %collective-permute-start.8 = (bf16[2,64,384]{2,1,0:T(8,128)(2,1)S(1)}, bf16[2,64,384]{2,1,0:T(8,128)(2,1)S(1)}, u32[]{:S(2)}, u32[]{:S(2)}) collective-permute-start(bf16[2,64,384]{2,1,0:T(8,128)(2,1)S(1)} %collective-permute-done.4.refs_6_), channel_id=1, source_target_pairs={{0,2},{2,0},{1,3},{3,1},{4,6},{6,4},{5,7},{7,5},{8,10},{10,8},{9,1... | collective-permute-start | bytes 294920 | tf_op jit(solution)/shard_map/ppermute | solution.py:163
  35.4 0.0 collective-permute-done.5.refs_7_
  35.4 0.5 collective-permute-start.9
  36.0 0.0 collective-permute-done.1.refs_2_
  36.0 2.5 %collective-permute-start.2 = (bf16[64,384]{1,0:T(8,128)(2,1)}, bf16[64,384]{1,0:T(8,128)(2,1)S(1)}, u32[]{:S(2)}, u32[]{:S(2)}) collective-permute-start(bf16[64,384]{1,0:T(8,128)(2,1)} %get-tuple-element.20), channel_id=1, source_target_pairs={{0,12},{4,8},{8,4},{12,0},{1,13},{5,9},{9,5},{13,1},{2,14},{6,10},... | collective-permute-start | bytes 147464 | tf_op jit(solution)/shard_map/ppermute | solution.py:160
  38.5 3.6 %collective-permute-done.2.refs_3_ = bf16[64,384]{1,0:T(8,128)(2,1)S(1)} collective-permute-done((bf16[64,384]{1,0:T(8,128)(2,1)}, bf16[64,384]{1,0:T(8,128)(2,1)S(1)}, u32[]{:S(2)}, u32[]{:S(2)}) %collective-permute-start.2) | collective-permute-done | bytes 49184 | tf_op jit(solution)/shard_map/ppermute | solution.py:160
  42.1 0.0 collective-permute-done.6.refs_8_
  42.1 0.0 collective-permute-done.7.refs_9_
  42.1 0.0 collective-permute-done.8.refs_10_
  42.1 0.0 collective-permute-done.9.refs_11_
  42.1 0.0 copy-start
  42.1 0.9 %copy-done = bf16[2,64,384]{2,1,0:T(8,128)(2,1)S(1)} copy-done((bf16[2,64,384]{2,1,0:T(8,128)(2,1)S(1)}, bf16[2,64,384]{2,1,0:T(8,128)(2,1)}, u32[]{:S(2)}) %copy-start) | copy-done | bytes 98328
  43.0 0.0 copy-start.2
  43.0 0.8 %copy-done.2 = bf16[64,384]{1,0:T(8,128)(2,1)S(1)} copy-done((bf16[64,384]{1,0:T(8,128)(2,1)S(1)}, bf16[64,384]{1,0:T(8,128)(2,1)}, u32[]{:S(2)}) %copy-start.2) | copy-done | bytes 49176
  43.8 1.1 %attend.1 = (bf16[64,384]{1,0:T(8,128)(2,1)S(1)}, bf16[64,384]{1,0:T(8,128)(2,1)S(1)}, bf16[64,384]{1,0:T(8,128)(2,1)S(1)}, bf16[64,384]{1,0:T(8,128)(2,1)S(1)}) custom-call(bf16[64,384]{1,0:T(8,128)(2,1)S(1)} %copy-done.2, bf16[64,384]{1,0:T(8,128)(2,1)S(1)} %collective-permute-done.refs_1_, bf16[64,384]{1,0:T(8,128)(2,1)S(1)} %collective-permute-done.1.refs_2_, ...), custom_call_target="tpu_custom_call" | custom-call | flops 201326592 | bytes 1179648 | tf_op jit(solution)/shard_map/attend/pallas_call | solution.py:174
  44.9 0.0 copy-start.1
  44.9 0.6 copy-done.1
  45.5 0.0 collective-permute-start.10
  45.5 3.0 %collective-permute-start.11 = (bf16[64,384]{1,0:T(8,128)(2,1)S(1)}, bf16[64,384]{1,0:T(8,128)(2,1)S(1)}, u32[]{:S(2)}, u32[]{:S(2)}) collective-permute-start(bf16[64,384]{1,0:T(8,128)(2,1)S(1)} %get-tuple-element.27), channel_id=1, source_target_pairs={{0,8},{4,12},{8,0},{12,4},{1,9},{5,13},{9,1},{13,5},{2,10},{6,14},... | collective-permute-start | bytes 147464 | tf_op jit(solution)/shard_map/ppermute | solution.py:160
  48.6 1.3 %collective-permute-start.12 = (bf16[64,384]{1,0:T(8,128)(2,1)S(1)}, bf16[64,384]{1,0:T(8,128)(2,1)S(1)}, u32[]{:S(2)}, u32[]{:S(2)}) collective-permute-start(bf16[64,384]{1,0:T(8,128)(2,1)S(1)} %get-tuple-element.28), channel_id=1, source_target_pairs={{0,12},{4,8},{8,4},{12,0},{1,13},{5,9},{9,5},{13,1},{2,14},{6,10},... | collective-permute-start | bytes 147464 | tf_op jit(solution)/shard_map/ppermute | solution.py:160
  49.9 0.0 collective-permute-done.10.refs_1_
  49.9 0.0 copy-start.3
  49.9 1.1 %collective-permute-done.11.refs_2_ = bf16[64,384]{1,0:T(8,128)(2,1)S(1)} collective-permute-done((bf16[64,384]{1,0:T(8,128)(2,1)S(1)}, bf16[64,384]{1,0:T(8,128)(2,1)S(1)}, u32[]{:S(2)}, u32[]{:S(2)}) %collective-permute-start.11) | collective-permute-done | bytes 49184 | tf_op jit(solution)/shard_map/ppermute | solution.py:160
  51.0 0.0 copy-start.4
  51.0 3.4 %collective-permute-done.12.refs_3_ = bf16[64,384]{1,0:T(8,128)(2,1)S(1)} collective-permute-done((bf16[64,384]{1,0:T(8,128)(2,1)S(1)}, bf16[64,384]{1,0:T(8,128)(2,1)S(1)}, u32[]{:S(2)}, u32[]{:S(2)}) %collective-permute-start.12) | collective-permute-done | bytes 49184 | tf_op jit(solution)/shard_map/ppermute | solution.py:160
  54.5 0.0 copy-start.5
  54.5 0.0 copy-done.3
  54.5 0.0 copy-done.4
  54.5 0.6 copy-done.5
  55.1 7.1 %unpack.1 = bf16[1,64,1536]{2,1,0:T(8,128)(2,1)} custom-call(bf16[64,384]{1,0:T(8,128)(2,1)} %copy-done.1, bf16[64,384]{1,0:T(8,128)(2,1)} %copy-done.3, bf16[64,384]{1,0:T(8,128)(2,1)} %copy-done.4, bf16[64,384]{1,0:T(8,128)(2,1)} %copy-done.5), custom_call_target="tpu_custom_call" | custom-call | bytes 393216 | tf_op jit(solution)/shard_map/unpack/pallas_call | solution.py:189
Async XLA Ops:
  19.1 13.0 %collective-permute-start.3 = (bf16[2,64,384]{2,1,0:T(8,128)(2,1)}, bf16[2,64,384]{2,1,0:T(8,128)(2,1)S(1)}, u32[]{:S(2)}, u32[]{:S(2)}) collective-permute-start(bf16[2,64,384]{2,1,0:T(8,128)(2,1)} %get-tuple-element.22), channel_id=1, source_target_pairs={{0,4},{4,0},{8,12},{12,8},{1,5},{5,1},{9,13},{13,9},{2,6},{6,2},{1... | collective-permute-start | bytes 294920 | tf_op jit(solution)/shard_map/ppermute | solution.py:160
  22.2 11.8 %collective-permute-start.4 = (bf16[2,64,384]{2,1,0:T(8,128)(2,1)}, bf16[2,64,384]{2,1,0:T(8,128)(2,1)S(1)}, u32[]{:S(2)}, u32[]{:S(2)}) collective-permute-start(bf16[2,64,384]{2,1,0:T(8,128)(2,1)} %get-tuple-element.23), channel_id=1, source_target_pairs={{0,8},{4,12},{8,0},{12,4},{1,9},{5,13},{9,1},{13,5},{2,10},{6,14},... | collective-permute-start | bytes 294920 | tf_op jit(solution)/shard_map/ppermute | solution.py:160
  24.8 10.7 %collective-permute-start.5 = (bf16[2,64,384]{2,1,0:T(8,128)(2,1)}, bf16[2,64,384]{2,1,0:T(8,128)(2,1)S(1)}, u32[]{:S(2)}, u32[]{:S(2)}) collective-permute-start(bf16[2,64,384]{2,1,0:T(8,128)(2,1)} %get-tuple-element.24), channel_id=1, source_target_pairs={{0,12},{4,8},{8,4},{12,0},{1,13},{5,9},{9,5},{13,1},{2,14},{6,10},... | collective-permute-start | bytes 294920 | tf_op jit(solution)/shard_map/ppermute | solution.py:160
  24.8 5.8 %collective-permute-start = (bf16[64,384]{1,0:T(8,128)(2,1)}, bf16[64,384]{1,0:T(8,128)(2,1)S(1)}, u32[]{:S(2)}, u32[]{:S(2)}) collective-permute-start(bf16[64,384]{1,0:T(8,128)(2,1)} %get-tuple-element.18), channel_id=1, source_target_pairs={{0,4},{4,0},{8,12},{12,8},{1,5},{5,1},{9,13},{13,9},{2,6},{6,2},{1... | collective-permute-start | bytes 147464 | tf_op jit(solution)/shard_map/ppermute | solution.py:160
  25.7 10.3 %collective-permute-start.1 = (bf16[64,384]{1,0:T(8,128)(2,1)}, bf16[64,384]{1,0:T(8,128)(2,1)S(1)}, u32[]{:S(2)}, u32[]{:S(2)}) collective-permute-start(bf16[64,384]{1,0:T(8,128)(2,1)} %get-tuple-element.19), channel_id=1, source_target_pairs={{0,8},{4,12},{8,0},{12,4},{1,9},{5,13},{9,1},{13,5},{2,10},{6,14},... | collective-permute-start | bytes 147464 | tf_op jit(solution)/shard_map/ppermute | solution.py:160
  30.6 11.5 %collective-permute-start.6 = (bf16[2,64,384]{2,1,0:T(8,128)(2,1)}, bf16[2,64,384]{2,1,0:T(8,128)(2,1)S(1)}, u32[]{:S(2)}, u32[]{:S(2)}) collective-permute-start(bf16[2,64,384]{2,1,0:T(8,128)(2,1)} %get-tuple-element.21.refs_4_), channel_id=1, source_target_pairs={{0,2},{2,0},{1,3},{3,1},{4,6},{6,4},{5,7},{7,5},{8,10},{10,8},{9,1... | collective-permute-start | bytes 294920 | tf_op jit(solution)/shard_map/ppermute | solution.py:163
  32.1 10.0 %collective-permute-start.7 = (bf16[2,64,384]{2,1,0:T(8,128)(2,1)S(1)}, bf16[2,64,384]{2,1,0:T(8,128)(2,1)S(1)}, u32[]{:S(2)}, u32[]{:S(2)}) collective-permute-start(bf16[2,64,384]{2,1,0:T(8,128)(2,1)S(1)} %collective-permute-done.3.refs_5_), channel_id=1, source_target_pairs={{0,2},{2,0},{1,3},{3,1},{4,6},{6,4},{5,7},{7,5},{8,10},{10,8},{9,1... | collective-permute-start | bytes 294920 | tf_op jit(solution)/shard_map/ppermute | solution.py:163
  34.0 8.1 %collective-permute-start.8 = (bf16[2,64,384]{2,1,0:T(8,128)(2,1)S(1)}, bf16[2,64,384]{2,1,0:T(8,128)(2,1)S(1)}, u32[]{:S(2)}, u32[]{:S(2)}) collective-permute-start(bf16[2,64,384]{2,1,0:T(8,128)(2,1)S(1)} %collective-permute-done.4.refs_6_), channel_id=1, source_target_pairs={{0,2},{2,0},{1,3},{3,1},{4,6},{6,4},{5,7},{7,5},{8,10},{10,8},{9,1... | collective-permute-start | bytes 294920 | tf_op jit(solution)/shard_map/ppermute | solution.py:163
  35.4 6.7 %collective-permute-start.9 = (bf16[2,64,384]{2,1,0:T(8,128)(2,1)S(1)}, bf16[2,64,384]{2,1,0:T(8,128)(2,1)S(1)}, u32[]{:S(2)}, u32[]{:S(2)}) collective-permute-start(bf16[2,64,384]{2,1,0:T(8,128)(2,1)S(1)} %collective-permute-done.5.refs_7_), channel_id=1, source_target_pairs={{0,2},{2,0},{1,3},{3,1},{4,6},{6,4},{5,7},{7,5},{8,10},{10,8},{9,1... | collective-permute-start | bytes 294920 | tf_op jit(solution)/shard_map/ppermute | solution.py:163
  36.0 6.1 %collective-permute-start.2 = (bf16[64,384]{1,0:T(8,128)(2,1)}, bf16[64,384]{1,0:T(8,128)(2,1)S(1)}, u32[]{:S(2)}, u32[]{:S(2)}) collective-permute-start(bf16[64,384]{1,0:T(8,128)(2,1)} %get-tuple-element.20), channel_id=1, source_target_pairs={{0,12},{4,8},{8,4},{12,0},{1,13},{5,9},{9,5},{13,1},{2,14},{6,10},... | collective-permute-start | bytes 147464 | tf_op jit(solution)/shard_map/ppermute | solution.py:160
  42.1 0.9 %copy-start = (bf16[2,64,384]{2,1,0:T(8,128)(2,1)S(1)}, bf16[2,64,384]{2,1,0:T(8,128)(2,1)}, u32[]{:S(2)}) copy-start(bf16[2,64,384]{2,1,0:T(8,128)(2,1)} %get-tuple-element.21.refs_4_) | copy-start | bytes 294916
  43.0 0.8 %copy-start.2 = (bf16[64,384]{1,0:T(8,128)(2,1)S(1)}, bf16[64,384]{1,0:T(8,128)(2,1)}, u32[]{:S(2)}) copy-start(bf16[64,384]{1,0:T(8,128)(2,1)} %get-tuple-element.17.refs_0_) | copy-start | bytes 147460
  44.9 0.6 copy-start.1
  45.5 4.4 %collective-permute-start.10 = (bf16[64,384]{1,0:T(8,128)(2,1)S(1)}, bf16[64,384]{1,0:T(8,128)(2,1)S(1)}, u32[]{:S(2)}, u32[]{:S(2)}) collective-permute-start(bf16[64,384]{1,0:T(8,128)(2,1)S(1)} %get-tuple-element.26), channel_id=1, source_target_pairs={{0,4},{4,0},{8,12},{12,8},{1,5},{5,1},{9,13},{13,9},{2,6},{6,2},{1... | collective-permute-start | bytes 147464 | tf_op jit(solution)/shard_map/ppermute | solution.py:160
  45.5 5.5 %collective-permute-start.11 = (bf16[64,384]{1,0:T(8,128)(2,1)S(1)}, bf16[64,384]{1,0:T(8,128)(2,1)S(1)}, u32[]{:S(2)}, u32[]{:S(2)}) collective-permute-start(bf16[64,384]{1,0:T(8,128)(2,1)S(1)} %get-tuple-element.27), channel_id=1, source_target_pairs={{0,8},{4,12},{8,0},{12,4},{1,9},{5,13},{9,1},{13,5},{2,10},{6,14},... | collective-permute-start | bytes 147464 | tf_op jit(solution)/shard_map/ppermute | solution.py:160
  48.6 5.9 %collective-permute-start.12 = (bf16[64,384]{1,0:T(8,128)(2,1)S(1)}, bf16[64,384]{1,0:T(8,128)(2,1)S(1)}, u32[]{:S(2)}, u32[]{:S(2)}) collective-permute-start(bf16[64,384]{1,0:T(8,128)(2,1)S(1)} %get-tuple-element.28), channel_id=1, source_target_pairs={{0,12},{4,8},{8,4},{12,0},{1,13},{5,9},{9,5},{13,1},{2,14},{6,10},... | collective-permute-start | bytes 147464 | tf_op jit(solution)/shard_map/ppermute | solution.py:160
  49.9 4.5 %copy-start.3 = (bf16[64,384]{1,0:T(8,128)(2,1)}, bf16[64,384]{1,0:T(8,128)(2,1)S(1)}, u32[]{:S(2)}) copy-start(bf16[64,384]{1,0:T(8,128)(2,1)S(1)} %collective-permute-done.10.refs_1_) | copy-start | bytes 147460
  51.0 3.4 %copy-start.4 = (bf16[64,384]{1,0:T(8,128)(2,1)}, bf16[64,384]{1,0:T(8,128)(2,1)S(1)}, u32[]{:S(2)}) copy-start(bf16[64,384]{1,0:T(8,128)(2,1)S(1)} %collective-permute-done.11.refs_2_) | copy-start | bytes 147460
  54.5 0.6 copy-start.5

commit v2 on v1

--- a/solution.py
+++ b/solution.py
@@ -77,34 +77,38 @@
     return merged.reshape(1, tokens, width)
 
 
-def pack_kernel(blocks, part, q_ref, k_ref, v_ref, *refs):
-    outs, sems = refs[:-1], refs[-1]
-    me = lax.axis_index("blk")
-    copies = []
-    for s in range(blocks):
-        columns = pl.ds(pl.multiple_of((me ^ s) * part, 128), part)
-        kv_out, q_out = outs[2 * s], outs[2 * s + 1]
-        copies.append((k_ref.at[0, :, columns], kv_out.at[0]))
-        copies.append((v_ref.at[0, :, columns], kv_out.at[1]))
-        copies.append((q_ref.at[0, :, columns], q_out))
-    started = [
-        pltpu.make_async_copy(src, dst, sems.at[at]) for at, (src, dst) in enumerate(copies)
-    ]
+def run_copies(pairs, sems):
+    started = [pltpu.make_async_copy(src, dst, sems.at[at]) for at, (src, dst) in enumerate(pairs)]
     for copy in started:
         copy.start()
     for copy in started:
         copy.wait()
 
 
-def attend_kernel(blocks, columns_of, *refs):
-    q_refs = refs[:blocks]
-    kv_refs = refs[blocks : blocks + blocks * columns_of]
-    out_refs = refs[blocks + blocks * columns_of :]
-    tokens, part = q_refs[0].shape
+def pack_kernel(partners, part, with_query, q_ref, k_ref, v_ref, *refs):
+    outs, sems = refs[:-1], refs[-1]
+    me = lax.axis_index("blk")
+    pairs = []
+    for s, query, out in zip(partners, with_query, outs):
+        columns = pl.ds(pl.multiple_of((me ^ s) * part, 128), part)
+        sources = {"kv": (k_ref, v_ref), "kvq": (k_ref, v_ref, q_ref), "q": (q_ref,)}[query]
+        for at, ref in enumerate(sources):
+            pairs.append((ref.at[0, :, columns], out.at[at]))
+    run_copies(pairs, sems)
+
+
+def attend_kernel(query_places, key_places, *refs):
+    query_count, key_count = len(query_places), len(key_places)
+    q_refs = refs[:query_count]
+    kv_refs = refs[query_count : query_count + key_count]
+    out_refs = refs[query_count + key_count :]
+    tokens, part = out_refs[0].shape
     scale = 1.0 / math.sqrt(HD)
     for head in range(part // HD):
         lanes = slice(head * HD, (head + 1) * HD)
-        queries = jnp.concatenate([ref[:, lanes] for ref in q_refs], axis=0)
+        queries = jnp.concatenate(
+            [ref[at, :, lanes] for ref, at in zip(q_refs, query_places)], axis=0
+        )
         keys = jnp.concatenate([ref[0, :, lanes] for ref in kv_refs], axis=0)
         values = jnp.concatenate([ref[1, :, lanes] for ref in kv_refs], axis=0)
         scores = (
@@ -126,14 +130,11 @@
 def unpack_kernel(blocks, part, *refs):
     ins, out_ref, sems = refs[:blocks], refs[blocks], refs[-1]
     me = lax.axis_index("blk")
-    started = []
+    pairs = []
     for s in range(blocks):
         columns = pl.ds(pl.multiple_of((me ^ s) * part, 128), part)
-        started.append(pltpu.make_async_copy(ins[s], out_ref.at[0, :, columns], sems.at[s]))
-    for copy in started:
-        copy.start()
-    for copy in started:
-        copy.wait()
+        pairs.append((ins[s], out_ref.at[0, :, columns]))
+    run_copies(pairs, sems)
 
 
 def local_blocks(query_rows, key_rows, value_rows):
@@ -142,54 +143,63 @@
     part = width // blocks
     heads = part // HD
     kind = query_rows.dtype
-    kv_shape = jax.ShapeDtypeStruct((2, tokens, part), kind)
-    q_shape = jax.ShapeDtypeStruct((tokens, part), kind)
-
+    far = list(range(2, blocks))
+
+    partners = far + [1, 0] + far + [0]
+    contents = ["kv"] * len(far) + ["kvq", "kv"] + ["q"] * len(far) + ["q"]
+    deep = {"kv": 2, "kvq": 3, "q": 1}
     packed = pl.pallas_call(
-        functools.partial(pack_kernel, blocks, part),
-        out_shape=[kv_shape, q_shape] * blocks,
+        functools.partial(pack_kernel, partners, part, contents),
+        out_shape=[jax.ShapeDtypeStruct((deep[c], tokens, part), kind) for c in contents],
         in_specs=[ANY] * 3,
-        out_specs=[ANY] * (2 * blocks),
+        out_specs=[VMEM] * len(partners),
         scratch_shapes=[pltpu.SemaphoreType.DMA((3 * blocks,))],
         cost_estimate=pl.CostEstimate(flops=0, bytes_accessed=6 * tokens * width * 2, transcendentals=0),
         name="pack",
     )(query_rows, key_rows, value_rows)
-    own_kv, own_q = packed[0::2], packed[1::2]
 
     def to_block(array, s):
-        return lax.ppermute(array, "blk", [(i, i ^ s) for i in range(blocks)]) if s else array
+        return lax.ppermute(array, "blk", [(i, i ^ s) for i in range(blocks)])
 
     def to_column(array, t):
         return lax.ppermute(array, "uly", [(i, (i + t) % columns_of) for i in range(columns_of)])
 
-    order = list(range(blocks))[::-1]
-    kv = {s: to_block(own_kv[s], s) for s in order}
-    queries = {s: to_block(own_q[s], s) for s in order}
+    own = packed[len(far) + 1]
+    kv = {s: to_block(packed[at], s) for at, s in enumerate(far)}
+    kv[1] = to_block(packed[len(far)], 1)
+    kv[0] = own
+    far_q = {s: to_block(packed[len(far) + 2 + at], s) for at, s in enumerate(far)}
     all_kv = [kv[s] for s in range(blocks)]
     for t in range(1, columns_of):
-        all_kv += [to_column(kv[s], t) for s in range(blocks)]
+        for s in range(blocks):
+            all_kv.append(to_column(kv[s][:2] if s == 1 else kv[s], t))
 
     all_tokens = tokens * blocks * columns_of
-    pairs = heads * tokens * blocks * all_tokens
-    mixed = pl.pallas_call(
-        functools.partial(attend_kernel, blocks, columns_of),
-        out_shape=[q_shape] * blocks,
-        in_specs=[VMEM] * (blocks + blocks * columns_of),
-        out_specs=[VMEM] * blocks,
-        compiler_params=pltpu.CompilerParams(vmem_limit_bytes=32 * 1024 * 1024),
-        cost_estimate=pl.CostEstimate(
-            flops=4 * HD * pairs,
-            bytes_accessed=2 * part * (2 * all_tokens + 2 * tokens * blocks),
-            transcendentals=pairs,
-        ),
-        name="attend",
-    )(*[queries[s] for s in range(blocks)], *all_kv)
-
-    back = [to_block(mixed[s], s) for s in range(blocks)]
+
+    def attend_blocks(query_arrays, places):
+        pairs = heads * tokens * len(places) * all_tokens
+        return pl.pallas_call(
+            functools.partial(attend_kernel, places, [0] * len(all_kv)),
+            out_shape=[jax.ShapeDtypeStruct((tokens, part), kind)] * len(places),
+            in_specs=[VMEM] * (len(places) + len(all_kv)),
+            out_specs=[VMEM] * len(places),
+            compiler_params=pltpu.CompilerParams(vmem_limit_bytes=32 * 1024 * 1024),
+            cost_estimate=pl.CostEstimate(
+                flops=4 * HD * pairs,
+                bytes_accessed=2 * part * (2 * all_tokens + 2 * tokens * len(places)),
+                transcendentals=pairs,
+            ),
+            name="attend",
+        )(*query_arrays, *all_kv)
+
+    mixed = dict(zip((0, 1), attend_blocks([packed[-1], kv[1]], [0, 2])))
+    for s in far:
+        mixed[s] = attend_blocks([far_q[s]], [0])[0]
+    back = [mixed[0]] + [to_block(mixed[s], s) for s in range(1, blocks)]
     return pl.pallas_call(
         functools.partial(unpack_kernel, blocks, part),
         out_shape=jax.ShapeDtypeStruct((1, tokens, width), kind),
-        in_specs=[ANY] * blocks,
+        in_specs=[VMEM] * blocks,
         out_specs=ANY,
         scratch_shapes=[pltpu.SemaphoreType.DMA((blocks,))],
         cost_estimate=pl.CostEstimate(flops=0, bytes_accessed=2 * tokens * width * 2, transcendentals=0),
@@ -200,7 +210,7 @@
 def local(query_rows, key_rows, value_rows):
     blocks = lax.axis_size("blk")
     heads = query_rows.shape[2] // HD
-    few = heads % blocks == 0 and blocks & (blocks - 1) == 0
+    few = blocks >= 2 and heads % blocks == 0 and blocks & (blocks - 1) == 0
     plan = local_blocks if few else local_generic
     return plan(query_rows, key_rows, value_rows)
 

time: 62.3 us -> 40.5 us (0.65)
  Pallas kernels: 27.3 us -> 6.25 us
  waiting for transfers between devices: 10.9 us -> 14.4 us
  starting transfers between devices: 21 us -> 18.2 us
  local copies, waits for them, and re-layouts: 2.9 us -> 1.26 us
    pallas_call x2 -> x4, Pallas kernels: 20.2 us -> 4.68 us  [the longest x3 2.73 us: attend_blocks(): pl.pallas_call(functools.partial(attend_kernel, places, [0] * len(all_kv)...]
    pallas_call x1, Pallas kernels: 7.09 us -> 1.57 us  [local_blocks(): pl.pallas_call(functools.partial(unpack_kernel, blocks, part), out_shape=...]
    ppermute x9 -> x8, starting transfers between devices: 16.9 us -> 13 us  [to_block(): return lax.ppermute(array, 'blk', [(i, i ^ s) for i in range(blocks)])]
    ppermute x9 -> x8, waiting for transfers between devices: 10.9 us -> 14.4 us  [to_block(): return lax.ppermute(array, 'blk', [(i, i ^ s) for i in range(blocks)])]
    unnamed x12 -> x16, local copies, waits for them, and re-layouts: 2.9 us -> 1.25 us
    ppermute x4, starting transfers between devices: 4.05 us -> 5.29 us  [to_column(): lax.ppermute(array, 'uly', [(i, (i + t) % columns_of) for i in range(colu...]
  transfers between devices with their start and end apart: 13 -> 12, of which waited for: 5 -> 5; matrix products, arithmetic and copies ran while one was open for 0% -> 0% of each run, Pallas kernels for 0% -> 7%
where the time goes in v2:
time: 40.5 us; the launch traced here: 40.2 us
  starting transfers between devices  18.2 us (45%)
  waiting for transfers between devices  14.4 us (36%)
  Pallas kernels  6.25 us (15%)
  local copies, waits for them, and re-layouts  1.26 us (3%)
    ppermute x8, waiting for transfers between devices, to_block(): return lax.ppermute(array, 'blk', [(i, i ^ s) for i in range(blocks)])  14.4 us
    ppermute x8, starting transfers between devices, to_block(): return lax.ppermute(array, 'blk', [(i, i ^ s) for i in range(blocks)])  13 us
    ppermute x4, starting transfers between devices, to_column(): lax.ppermute(array, 'uly', [(i, (i + t) % columns_of) for i in range(colu...  5.29 us
    pallas_call x3, Pallas kernels, attend_blocks(): pl.pallas_call(functools.partial(attend_kernel, places, [0] * len(all_kv)...  2.73 us
    pallas_call x1, Pallas kernels, local_blocks(): pl.pallas_call(functools.partial(pack_kernel, partners, part, contents),...  1.96 us
    pallas_call x1, Pallas kernels, local_blocks(): pl.pallas_call(functools.partial(unpack_kernel, blocks, part), out_shape=...  1.57 us
    unnamed x16, local copies, waits for them, and re-layouts  1.25 us
  transfers between devices with their start and end apart: 12, of which 5 were waited for; matrix products, arithmetic and copies ran while one was open for 0% of the time, Pallas kernels for 7%

profile of v2, /device:TPU:0, one launch (start us, length us, event | category | flops | bytes accessed | tf_op | source)
XLA Modules:
  0.0 40.2 jit_solution(182847230182794417)
XLA Ops:
  0.0 2.0 %pack.1 = (bf16[2,64,384]{2,1,0:T(8,128)(2,1)}, bf16[2,64,384]{2,1,0:T(8,128)(2,1)}, bf16[3,64,384]{2,1,0:T(8,128)(2,1)}, bf16[2,64,384]{2,1,0:T(8,128)(2,1)}, b...) custom-call(bf16[1,64,1536]{2,1,0:T(8,128)(2,1)} %q_ref.1, ...), custom_call_target="tpu_custom_call" | custom-call | bytes 1179648 | tf_op jit(solution)/shard_map/pack/pallas_call | solution.py:151
  2.0 3.1 %collective-permute-start = (bf16[3,64,384]{2,1,0:T(8,128)(2,1)}, bf16[3,64,384]{2,1,0:T(8,128)(2,1)S(1)}, u32[]{:S(2)}, u32[]{:S(2)}) collective-permute-start(bf16[3,64,384]{2,1,0:T(8,128)(2,1)} %get-tuple-element.15), channel_id=1, source_target_pairs={{0,4},{4,0},{8,12},{12,8},{1,5},{5,1},{9,13},{13,9},{2,6},{6,2},{1... | collective-permute-start | bytes 442376 | tf_op jit(solution)/shard_map/ppermute | solution.py:162
  5.1 2.6 %collective-permute-start.1 = (bf16[2,64,384]{2,1,0:T(8,128)(2,1)}, bf16[2,64,384]{2,1,0:T(8,128)(2,1)S(1)}, u32[]{:S(2)}, u32[]{:S(2)}) collective-permute-start(bf16[2,64,384]{2,1,0:T(8,128)(2,1)} %get-tuple-element.17), channel_id=1, source_target_pairs={{0,8},{4,12},{8,0},{12,4},{1,9},{5,13},{9,1},{13,5},{2,10},{6,14},... | collective-permute-start | bytes 294920 | tf_op jit(solution)/shard_map/ppermute | solution.py:162
  7.6 0.0 collective-permute-start.2
  7.6 0.0 copy-start.7
  7.7 0.0 copy-start.6
  7.7 0.0 copy-start
  7.7 1.7 %collective-permute-start.3 = (bf16[2,64,384]{2,1,0:T(8,128)(2,1)}, bf16[2,64,384]{2,1,0:T(8,128)(2,1)S(1)}, u32[]{:S(2)}, u32[]{:S(2)}) collective-permute-start(bf16[2,64,384]{2,1,0:T(8,128)(2,1)} %get-tuple-element.16.refs_2_.refs_1_), channel_id=1, source_target_pairs={{0,2},{2,0},{1,3},{3,1},{4,6},{6,4},{5,7},{7,5},{8,10},{10,8},{9,1... | collective-permute-start | bytes 294920 | tf_op jit(solution)/shard_map/ppermute | solution.py:165
  9.4 6.6 %collective-permute-done.1.refs_4_.refs_3_ = bf16[2,64,384]{2,1,0:T(8,128)(2,1)S(1)} collective-permute-done((bf16[2,64,384]{2,1,0:T(8,128)(2,1)}, bf16[2,64,384]{2,1,0:T(8,128)(2,1)S(1)}, u32[]{:S(2)}, u32[]{:S(2)}) %collective-permute-start.1) | collective-permute-done | bytes 98336 | tf_op jit(solution)/shard_map/ppermute | solution.py:162
  15.9 1.5 %collective-permute-start.5 = (bf16[2,64,384]{2,1,0:T(8,128)(2,1)S(1)}, bf16[2,64,384]{2,1,0:T(8,128)(2,1)S(1)}, u32[]{:S(2)}, u32[]{:S(2)}) collective-permute-start(bf16[2,64,384]{2,1,0:T(8,128)(2,1)S(1)} %collective-permute-done.1.refs_4_.refs_3_), channel_id=1, source_target_pairs={{0,2},{2,0},{1,3},{3,1},{4,6},{6,4},{5,7},{7,5},{8,10},{10,8},{9,1... | collective-permute-start | bytes 294920 | tf_op jit(solution)/shard_map/ppermute | solution.py:165
  17.4 0.0 collective-permute-done.2.refs_5_.refs_4_
  17.4 0.5 %collective-permute-start.6 = (bf16[2,64,384]{2,1,0:T(8,128)(2,1)S(1)}, bf16[2,64,384]{2,1,0:T(8,128)(2,1)S(1)}, u32[]{:S(2)}, u32[]{:S(2)}) collective-permute-start(bf16[2,64,384]{2,1,0:T(8,128)(2,1)S(1)} %collective-permute-done.2.refs_5_.refs_4_), channel_id=1, source_target_pairs={{0,2},{2,0},{1,3},{3,1},{4,6},{6,4},{5,7},{7,5},{8,10},{10,8},{9,1... | collective-permute-start | bytes 294920 | tf_op jit(solution)/shard_map/ppermute | solution.py:165
  18.0 0.0 collective-permute-done.refs_1_.refs_3_.refs_2_
  18.0 1.6 %collective-permute-start.4 = (bf16[2,64,384]{2,1,0:T(8,128)(2,1)S(1)}, bf16[2,64,384]{2,1,0:T(8,128)(2,1)S(1)}, u32[]{:S(2)}, u32[]{:S(2)}) collective-permute-start(bf16[2,64,384]{2,1,0:T(8,128)(2,1)S(1)} %slice.4), channel_id=1, source_target_pairs={{0,2},{2,0},{1,3},{3,1},{4,6},{6,4},{5,7},{7,5},{8,10},{10,8},{9,1... | collective-permute-start | bytes 294920 | tf_op jit(solution)/shard_map/ppermute | solution.py:165
  19.5 0.0 copy-done.7
  19.5 2.3 %collective-permute-start.10 = (bf16[1,64,384]{2,1,0:T(8,128)(2,1)S(1)}, bf16[1,64,384]{2,1,0:T(8,128)(2,1)S(1)}, u32[]{:S(2)}, u32[]{:S(2)}) collective-permute-start(bf16[1,64,384]{2,1,0:T(8,128)(2,1)S(1)} %copy-done.7), channel_id=1, source_target_pairs={{0,12},{4,8},{8,4},{12,0},{1,13},{5,9},{9,5},{13,1},{2,14},{6,10},... | collective-permute-start | bytes 147464 | tf_op jit(solution)/shard_map/ppermute | solution.py:162
  21.8 3.6 %collective-permute-done.10.refs_0_ = bf16[1,64,384]{2,1,0:T(8,128)(2,1)S(1)} collective-permute-done((bf16[1,64,384]{2,1,0:T(8,128)(2,1)S(1)}, bf16[1,64,384]{2,1,0:T(8,128)(2,1)S(1)}, u32[]{:S(2)}, u32[]{:S(2)}) %collective-permute-start.10) | collective-permute-done | bytes 49184 | tf_op jit(solution)/shard_map/ppermute | solution.py:162
  25.4 0.0 copy-done.6
  25.4 0.0 collective-permute-start.8
  25.4 0.0 collective-permute-done.3.refs_6_.refs_5_
  25.4 0.0 collective-permute-done.5.refs_8_.refs_7_
  25.5 0.0 collective-permute-done.6.refs_9_.refs_8_
  25.5 0.0 collective-permute-done.4.refs_7_.refs_6_
  25.5 0.0 copy-done
  25.5 0.9 %attend.5 = bf16[64,384]{1,0:T(8,128)(2,1)S(1)} custom-call(bf16[1,64,384]{2,1,0:T(8,128)(2,1)S(1)} %collective-permute-done.10.refs_0_, bf16[2,64,384]{2,1,0:T(8,128)(2,1)S(1)} %copy-done, bf16[3,64,384]{2,1,0:T(8,128)(2,1)S(1)} %collective-permute-done.refs_1_.refs_3_.refs_2_, bf16[2,64,384]{2,1,0:T(8,128)(2,1)S(1)} %collective-permute-done.1.refs_4_.refs_3_, ...), custom_call_target="tpu_custom_call" | custom-call | flops 50331648 | bytes 884736 | tf_op jit(solution)/shard_map/attend/pallas_call | solution.py:181
  26.4 0.0 copy-start.1
  26.4 2.3 %collective-permute-start.11 = (bf16[64,384]{1,0:T(8,128)(2,1)S(1)}, bf16[64,384]{1,0:T(8,128)(2,1)S(1)}, u32[]{:S(2)}, u32[]{:S(2)}) collective-permute-start(bf16[64,384]{1,0:T(8,128)(2,1)S(1)} %attend.5), channel_id=1, source_target_pairs={{0,12},{4,8},{8,4},{12,0},{1,13},{5,9},{9,5},{13,1},{2,14},{6,10},... | collective-permute-start | bytes 147464 | tf_op jit(solution)/shard_map/ppermute | solution.py:162
  28.7 2.1 %collective-permute-done.8.refs_0_ = bf16[1,64,384]{2,1,0:T(8,128)(2,1)S(1)} collective-permute-done((bf16[1,64,384]{2,1,0:T(8,128)(2,1)S(1)}, bf16[1,64,384]{2,1,0:T(8,128)(2,1)S(1)}, u32[]{:S(2)}, u32[]{:S(2)}) %collective-permute-start.8) | collective-permute-done | bytes 49184 | tf_op jit(solution)/shard_map/ppermute | solution.py:162
  30.9 0.9 %attend.4 = bf16[64,384]{1,0:T(8,128)(2,1)S(1)} custom-call(bf16[1,64,384]{2,1,0:T(8,128)(2,1)S(1)} %collective-permute-done.8.refs_0_, bf16[2,64,384]{2,1,0:T(8,128)(2,1)S(1)} %copy-done, bf16[3,64,384]{2,1,0:T(8,128)(2,1)S(1)} %collective-permute-done.refs_1_.refs_3_.refs_2_, bf16[2,64,384]{2,1,0:T(8,128)(2,1)S(1)} %collective-permute-done.1.refs_4_.refs_3_, ...), custom_call_target="tpu_custom_call" | custom-call | flops 50331648 | bytes 884736 | tf_op jit(solution)/shard_map/attend/pallas_call | solution.py:181
  31.7 0.1 collective-permute-start.9
  31.8 0.0 copy-done.1
  31.8 0.9 %attend.3 = (bf16[64,384]{1,0:T(8,128)(2,1)S(1)}, bf16[64,384]{1,0:T(8,128)(2,1)S(1)}) custom-call(bf16[1,64,384]{2,1,0:T(8,128)(2,1)S(1)} %copy-done.1, bf16[3,64,384]{2,1,0:T(8,128)(2,1)S(1)} %collective-permute-done.refs_1_.refs_3_.refs_2_, bf16[2,64,384]{2,1,0:T(8,128)(2,1)S(1)} %copy-done, ...), custom_call_target="tpu_custom_call" | custom-call | flops 100663296 | bytes 983040 | tf_op jit(solution)/shard_map/attend/pallas_call | solution.py:181
  32.8 0.0 copy-start.2
  32.8 0.6 %copy-done.2 = bf16[64,384]{1,0:T(8,128)(2,1)} copy-done((bf16[64,384]{1,0:T(8,128)(2,1)}, bf16[64,384]{1,0:T(8,128)(2,1)S(1)}, u32[]{:S(2)}) %copy-start.2) | copy-done | bytes 49176
  33.4 2.6 %collective-permute-start.7 = (bf16[64,384]{1,0:T(8,128)(2,1)S(1)}, bf16[64,384]{1,0:T(8,128)(2,1)S(1)}, u32[]{:S(2)}, u32[]{:S(2)}) collective-permute-start(bf16[64,384]{1,0:T(8,128)(2,1)S(1)} %get-tuple-element.20), channel_id=1, source_target_pairs={{0,4},{4,0},{8,12},{12,8},{1,5},{5,1},{9,13},{13,9},{2,6},{6,2},{1... | collective-permute-start | bytes 147464 | tf_op jit(solution)/shard_map/ppermute | solution.py:162
  36.0 0.0 collective-permute-done.11.refs_3_
  36.0 0.0 copy-start.3
  36.0 0.8 %collective-permute-done.9.refs_2_ = bf16[64,384]{1,0:T(8,128)(2,1)S(1)} collective-permute-done((bf16[64,384]{1,0:T(8,128)(2,1)S(1)}, bf16[64,384]{1,0:T(8,128)(2,1)S(1)}, u32[]{:S(2)}, u32[]{:S(2)}) %collective-permute-start.9) | collective-permute-done | bytes 49184 | tf_op jit(solution)/shard_map/ppermute | solution.py:162
  36.8 0.0 copy-start.4
  36.8 1.2 %collective-permute-done.7.refs_1_ = bf16[64,384]{1,0:T(8,128)(2,1)S(1)} collective-permute-done((bf16[64,384]{1,0:T(8,128)(2,1)S(1)}, bf16[64,384]{1,0:T(8,128)(2,1)S(1)}, u32[]{:S(2)}, u32[]{:S(2)}) %collective-permute-start.7) | collective-permute-done | bytes 49184 | tf_op jit(solution)/shard_map/ppermute | solution.py:162
  38.0 0.0 copy-start.5
  38.0 0.0 copy-done.3
  38.1 0.0 copy-done.4
  38.1 0.6 %copy-done.5 = bf16[64,384]{1,0:T(8,128)(2,1)} copy-done((bf16[64,384]{1,0:T(8,128)(2,1)}, bf16[64,384]{1,0:T(8,128)(2,1)S(1)}, u32[]{:S(2)}) %copy-start.5) | copy-done | bytes 49176
  38.7 1.6 %unpack.1 = bf16[1,64,1536]{2,1,0:T(8,128)(2,1)} custom-call(bf16[64,384]{1,0:T(8,128)(2,1)} %copy-done.2, bf16[64,384]{1,0:T(8,128)(2,1)} %copy-done.5, bf16[64,384]{1,0:T(8,128)(2,1)} %copy-done.4, bf16[64,384]{1,0:T(8,128)(2,1)} %copy-done.3), custom_call_target="tpu_custom_call" | custom-call | bytes 393216 | tf_op jit(solution)/shard_map/unpack/pallas_call | solution.py:199
  (1 shorter events, 0.0 us)
Async XLA Ops:
  2.0 16.0 %collective-permute-start = (bf16[3,64,384]{2,1,0:T(8,128)(2,1)}, bf16[3,64,384]{2,1,0:T(8,128)(2,1)S(1)}, u32[]{:S(2)}, u32[]{:S(2)}) collective-permute-start(bf16[3,64,384]{2,1,0:T(8,128)(2,1)} %get-tuple-element.15), channel_id=1, source_target_pairs={{0,4},{4,0},{8,12},{12,8},{1,5},{5,1},{9,13},{13,9},{2,6},{6,2},{1... | collective-permute-start | bytes 442376 | tf_op jit(solution)/shard_map/ppermute | solution.py:162
  5.1 10.9 %collective-permute-start.1 = (bf16[2,64,384]{2,1,0:T(8,128)(2,1)}, bf16[2,64,384]{2,1,0:T(8,128)(2,1)S(1)}, u32[]{:S(2)}, u32[]{:S(2)}) collective-permute-start(bf16[2,64,384]{2,1,0:T(8,128)(2,1)} %get-tuple-element.17), channel_id=1, source_target_pairs={{0,8},{4,12},{8,0},{12,4},{1,9},{5,13},{9,1},{13,5},{2,10},{6,14},... | collective-permute-start | bytes 294920 | tf_op jit(solution)/shard_map/ppermute | solution.py:162
  7.6 9.8 %collective-permute-start.2 = (bf16[2,64,384]{2,1,0:T(8,128)(2,1)}, bf16[2,64,384]{2,1,0:T(8,128)(2,1)S(1)}, u32[]{:S(2)}, u32[]{:S(2)}) collective-permute-start(bf16[2,64,384]{2,1,0:T(8,128)(2,1)} %get-tuple-element.18), channel_id=1, source_target_pairs={{0,12},{4,8},{8,4},{12,0},{1,13},{5,9},{9,5},{13,1},{2,14},{6,10},... | collective-permute-start | bytes 294920 | tf_op jit(solution)/shard_map/ppermute | solution.py:162
  7.6 11.9 %copy-start.7 = (bf16[1,64,384]{2,1,0:T(8,128)(2,1)S(1)}, bf16[1,64,384]{2,1,0:T(8,128)(2,1)}, u32[]{:S(2)}) copy-start(bf16[1,64,384]{2,1,0:T(8,128)(2,1)} %get-tuple-element.22) | copy-start | bytes 147460
  7.7 17.8 %copy-start.6 = (bf16[1,64,384]{2,1,0:T(8,128)(2,1)S(1)}, bf16[1,64,384]{2,1,0:T(8,128)(2,1)}, u32[]{:S(2)}) copy-start(bf16[1,64,384]{2,1,0:T(8,128)(2,1)} %get-tuple-element.21) | copy-start | bytes 147460
  7.7 17.8 %copy-start = (bf16[2,64,384]{2,1,0:T(8,128)(2,1)S(1)}, bf16[2,64,384]{2,1,0:T(8,128)(2,1)}, u32[]{:S(2)}) copy-start(bf16[2,64,384]{2,1,0:T(8,128)(2,1)} %get-tuple-element.16.refs_2_.refs_1_) | copy-start | bytes 294916
  7.7 17.8 %collective-permute-start.3 = (bf16[2,64,384]{2,1,0:T(8,128)(2,1)}, bf16[2,64,384]{2,1,0:T(8,128)(2,1)S(1)}, u32[]{:S(2)}, u32[]{:S(2)}) collective-permute-start(bf16[2,64,384]{2,1,0:T(8,128)(2,1)} %get-tuple-element.16.refs_2_.refs_1_), channel_id=1, source_target_pairs={{0,2},{2,0},{1,3},{3,1},{4,6},{6,4},{5,7},{7,5},{8,10},{10,8},{9,1... | collective-permute-start | bytes 294920 | tf_op jit(solution)/shard_map/ppermute | solution.py:165
  15.9 9.5 %collective-permute-start.5 = (bf16[2,64,384]{2,1,0:T(8,128)(2,1)S(1)}, bf16[2,64,384]{2,1,0:T(8,128)(2,1)S(1)}, u32[]{:S(2)}, u32[]{:S(2)}) collective-permute-start(bf16[2,64,384]{2,1,0:T(8,128)(2,1)S(1)} %collective-permute-done.1.refs_4_.refs_3_), channel_id=1, source_target_pairs={{0,2},{2,0},{1,3},{3,1},{4,6},{6,4},{5,7},{7,5},{8,10},{10,8},{9,1... | collective-permute-start | bytes 294920 | tf_op jit(solution)/shard_map/ppermute | solution.py:165
  17.4 8.0 %collective-permute-start.6 = (bf16[2,64,384]{2,1,0:T(8,128)(2,1)S(1)}, bf16[2,64,384]{2,1,0:T(8,128)(2,1)S(1)}, u32[]{:S(2)}, u32[]{:S(2)}) collective-permute-start(bf16[2,64,384]{2,1,0:T(8,128)(2,1)S(1)} %collective-permute-done.2.refs_5_.refs_4_), channel_id=1, source_target_pairs={{0,2},{2,0},{1,3},{3,1},{4,6},{6,4},{5,7},{7,5},{8,10},{10,8},{9,1... | collective-permute-start | bytes 294920 | tf_op jit(solution)/shard_map/ppermute | solution.py:165
  18.0 7.5 %collective-permute-start.4 = (bf16[2,64,384]{2,1,0:T(8,128)(2,1)S(1)}, bf16[2,64,384]{2,1,0:T(8,128)(2,1)S(1)}, u32[]{:S(2)}, u32[]{:S(2)}) collective-permute-start(bf16[2,64,384]{2,1,0:T(8,128)(2,1)S(1)} %slice.4), channel_id=1, source_target_pairs={{0,2},{2,0},{1,3},{3,1},{4,6},{6,4},{5,7},{7,5},{8,10},{10,8},{9,1... | collective-permute-start | bytes 294920 | tf_op jit(solution)/shard_map/ppermute | solution.py:165
  19.5 5.9 %collective-permute-start.10 = (bf16[1,64,384]{2,1,0:T(8,128)(2,1)S(1)}, bf16[1,64,384]{2,1,0:T(8,128)(2,1)S(1)}, u32[]{:S(2)}, u32[]{:S(2)}) collective-permute-start(bf16[1,64,384]{2,1,0:T(8,128)(2,1)S(1)} %copy-done.7), channel_id=1, source_target_pairs={{0,12},{4,8},{8,4},{12,0},{1,13},{5,9},{9,5},{13,1},{2,14},{6,10},... | collective-permute-start | bytes 147464 | tf_op jit(solution)/shard_map/ppermute | solution.py:162
  25.4 5.4 %collective-permute-start.8 = (bf16[1,64,384]{2,1,0:T(8,128)(2,1)S(1)}, bf16[1,64,384]{2,1,0:T(8,128)(2,1)S(1)}, u32[]{:S(2)}, u32[]{:S(2)}) collective-permute-start(bf16[1,64,384]{2,1,0:T(8,128)(2,1)S(1)} %copy-done.6), channel_id=1, source_target_pairs={{0,8},{4,12},{8,0},{12,4},{1,9},{5,13},{9,1},{13,5},{2,10},{6,14},... | collective-permute-start | bytes 147464 | tf_op jit(solution)/shard_map/ppermute | solution.py:162
  26.4 5.4 %copy-start.1 = (bf16[1,64,384]{2,1,0:T(8,128)(2,1)S(1)}, bf16[1,64,384]{2,1,0:T(8,128)(2,1)}, u32[]{:S(2)}) copy-start(bf16[1,64,384]{2,1,0:T(8,128)(2,1)} %get-tuple-element.14.refs_0_) | copy-start | bytes 147460
  26.4 9.6 %collective-permute-start.11 = (bf16[64,384]{1,0:T(8,128)(2,1)S(1)}, bf16[64,384]{1,0:T(8,128)(2,1)S(1)}, u32[]{:S(2)}, u32[]{:S(2)}) collective-permute-start(bf16[64,384]{1,0:T(8,128)(2,1)S(1)} %attend.5), channel_id=1, source_target_pairs={{0,12},{4,8},{8,4},{12,0},{1,13},{5,9},{9,5},{13,1},{2,14},{6,10},... | collective-permute-start | bytes 147464 | tf_op jit(solution)/shard_map/ppermute | solution.py:162
  31.7 5.0 %collective-permute-start.9 = (bf16[64,384]{1,0:T(8,128)(2,1)S(1)}, bf16[64,384]{1,0:T(8,128)(2,1)S(1)}, u32[]{:S(2)}, u32[]{:S(2)}) collective-permute-start(bf16[64,384]{1,0:T(8,128)(2,1)S(1)} %attend.4), channel_id=1, source_target_pairs={{0,8},{4,12},{8,0},{12,4},{1,9},{5,13},{9,1},{13,5},{2,10},{6,14},... | collective-permute-start | bytes 147464 | tf_op jit(solution)/shard_map/ppermute | solution.py:162
  32.8 0.6 %copy-start.2 = (bf16[64,384]{1,0:T(8,128)(2,1)}, bf16[64,384]{1,0:T(8,128)(2,1)S(1)}, u32[]{:S(2)}) copy-start(bf16[64,384]{1,0:T(8,128)(2,1)S(1)} %get-tuple-element.19.refs_0_) | copy-start | bytes 147460
  33.4 4.7 %collective-permute-start.7 = (bf16[64,384]{1,0:T(8,128)(2,1)S(1)}, bf16[64,384]{1,0:T(8,128)(2,1)S(1)}, u32[]{:S(2)}, u32[]{:S(2)}) collective-permute-start(bf16[64,384]{1,0:T(8,128)(2,1)S(1)} %get-tuple-element.20), channel_id=1, source_target_pairs={{0,4},{4,0},{8,12},{12,8},{1,5},{5,1},{9,13},{13,9},{2,6},{6,2},{1... | collective-permute-start | bytes 147464 | tf_op jit(solution)/shard_map/ppermute | solution.py:162
  36.0 2.1 %copy-start.3 = (bf16[64,384]{1,0:T(8,128)(2,1)}, bf16[64,384]{1,0:T(8,128)(2,1)S(1)}, u32[]{:S(2)}) copy-start(bf16[64,384]{1,0:T(8,128)(2,1)S(1)} %collective-permute-done.11.refs_3_) | copy-start | bytes 147460
  36.8 1.3 %copy-start.4 = (bf16[64,384]{1,0:T(8,128)(2,1)}, bf16[64,384]{1,0:T(8,128)(2,1)S(1)}, u32[]{:S(2)}) copy-start(bf16[64,384]{1,0:T(8,128)(2,1)S(1)} %collective-permute-done.9.refs_2_) | copy-start | bytes 147460
  38.0 0.6 %copy-start.5 = (bf16[64,384]{1,0:T(8,128)(2,1)}, bf16[64,384]{1,0:T(8,128)(2,1)S(1)}, u32[]{:S(2)}) copy-start(bf16[64,384]{1,0:T(8,128)(2,1)S(1)} %collective-permute-done.7.refs_1_) | copy-start | bytes 147460

commit v3 on v2

--- a/solution.py
+++ b/solution.py
@@ -9,8 +9,9 @@
 from jax.sharding import PartitionSpec as P
 
 HD = 128
-ANY = pl.BlockSpec(memory_space=pl.ANY)
+HBM = pl.BlockSpec(memory_space=pltpu.HBM)
 VMEM = pl.BlockSpec(memory_space=pltpu.VMEM)
+SMALL = pltpu.CompilerParams(vmem_limit_bytes=4 * 1024 * 1024)
 
 
 def attend(queries, key_part, value_part):
@@ -85,32 +86,48 @@
         copy.wait()
 
 
-def pack_kernel(partners, part, with_query, q_ref, k_ref, v_ref, *refs):
+def pack_kernel(messages, part, q_ref, k_ref, v_ref, *refs):
     outs, sems = refs[:-1], refs[-1]
+    sources = {"q": q_ref, "k": k_ref, "v": v_ref}
     me = lax.axis_index("blk")
     pairs = []
-    for s, query, out in zip(partners, with_query, outs):
+    for (s, names), out in zip(messages, outs):
         columns = pl.ds(pl.multiple_of((me ^ s) * part, 128), part)
-        sources = {"kv": (k_ref, v_ref), "kvq": (k_ref, v_ref, q_ref), "q": (q_ref,)}[query]
-        for at, ref in enumerate(sources):
-            pairs.append((ref.at[0, :, columns], out.at[at]))
+        for at, name in enumerate(names):
+            pairs.append((sources[name].at[0, :, columns], out.at[at]))
     run_copies(pairs, sems)
 
 
-def attend_kernel(query_places, key_places, *refs):
-    query_count, key_count = len(query_places), len(key_places)
-    q_refs = refs[:query_count]
-    kv_refs = refs[query_count : query_count + key_count]
-    out_refs = refs[query_count + key_count :]
+def join_kernel(places, *refs):
+    for at, (source, place) in enumerate(places):
+        refs[-1][at] = refs[source][place]
+
+
+def join(arrays, places):
+    shape = (len(places),) + arrays[0].shape[1:]
+    size = math.prod(shape) * 2
+    return pl.pallas_call(
+        functools.partial(join_kernel, places),
+        out_shape=jax.ShapeDtypeStruct(shape, arrays[0].dtype),
+        in_specs=[VMEM] * len(arrays),
+        out_specs=VMEM,
+        compiler_params=SMALL,
+        cost_estimate=pl.CostEstimate(flops=0, bytes_accessed=2 * size, transcendentals=0),
+        name="join",
+    )(*arrays)
+
+
+def attend_kernel(query_places, key_places, value_places, *refs):
+    blocks = len(query_places)
+    ins, out_refs = refs[:-blocks], refs[-blocks:]
     tokens, part = out_refs[0].shape
     scale = 1.0 / math.sqrt(HD)
     for head in range(part // HD):
         lanes = slice(head * HD, (head + 1) * HD)
-        queries = jnp.concatenate(
-            [ref[at, :, lanes] for ref, at in zip(q_refs, query_places)], axis=0
-        )
-        keys = jnp.concatenate([ref[0, :, lanes] for ref in kv_refs], axis=0)
-        values = jnp.concatenate([ref[1, :, lanes] for ref in kv_refs], axis=0)
+        queries, keys, values = (
+            jnp.concatenate([ins[source][at, :, lanes] for source, at in places], axis=0)
+            for places in (query_places, key_places, value_places)
+        )
         scores = (
             lax.dot_general(
                 queries, keys, (((1,), (1,)), ((), ())), preferred_element_type=jnp.float32
@@ -145,16 +162,18 @@
     kind = query_rows.dtype
     far = list(range(2, blocks))
 
-    partners = far + [1, 0] + far + [0]
-    contents = ["kv"] * len(far) + ["kvq", "kv"] + ["q"] * len(far) + ["q"]
-    deep = {"kv": 2, "kvq": 3, "q": 1}
+    messages = [(s, "k") for s in far] + [(1, "kvq")] + [(s, "vq") for s in far]
+    messages += [(0, "kv"), (0, "q")]
     packed = pl.pallas_call(
-        functools.partial(pack_kernel, partners, part, contents),
-        out_shape=[jax.ShapeDtypeStruct((deep[c], tokens, part), kind) for c in contents],
-        in_specs=[ANY] * 3,
-        out_specs=[VMEM] * len(partners),
+        functools.partial(pack_kernel, messages, part),
+        out_shape=[jax.ShapeDtypeStruct((len(m), tokens, part), kind) for s, m in messages],
+        in_specs=[HBM] * 3,
+        out_specs=[VMEM] * len(messages),
         scratch_shapes=[pltpu.SemaphoreType.DMA((3 * blocks,))],
-        cost_estimate=pl.CostEstimate(flops=0, bytes_accessed=6 * tokens * width * 2, transcendentals=0),
+        compiler_params=SMALL,
+        cost_estimate=pl.CostEstimate(
+            flops=0, bytes_accessed=6 * tokens * width * 2, transcendentals=0
+        ),
         name="pack",
     )(query_rows, key_rows, value_rows)
 
@@ -164,53 +183,60 @@
     def to_column(array, t):
         return lax.ppermute(array, "uly", [(i, (i + t) % columns_of) for i in range(columns_of)])
 
-    own = packed[len(far) + 1]
-    kv = {s: to_block(packed[at], s) for at, s in enumerate(far)}
-    kv[1] = to_block(packed[len(far)], 1)
-    kv[0] = own
-    far_q = {s: to_block(packed[len(far) + 2 + at], s) for at, s in enumerate(far)}
-    all_kv = [kv[s] for s in range(blocks)]
+    sent = {message: array for message, array in zip(messages, packed)}
+    held = [sent[0, "kv"], sent[0, "q"]]
+    held += [to_block(sent[m], m[0]) for m in messages[:-2]]
+    at_near = 2 + len(far)
+    at_keys = {s: 2 + at for at, s in enumerate(far)}
+    at_values = {s: 3 + len(far) + at for at, s in enumerate(far)}
+    query_places = [(1, 0), (at_near, 2)] + [(at_values[s], 1) for s in far]
+    key_places = [(0, 0), (at_near, 0)] + [(at_keys[s], 0) for s in far]
+    value_places = [(0, 1), (at_near, 1)] + [(at_values[s], 0) for s in far]
+    near = join([held[0], held[at_near]], [(0, 0), (0, 1), (1, 0), (1, 1)])
+    far_places = [(at, 0) for at in range(len(far))]
+    far_keys = join([held[at_keys[s]] for s in far], far_places)
+    far_values = join([held[at_values[s]] for s in far], far_places)
     for t in range(1, columns_of):
-        for s in range(blocks):
-            all_kv.append(to_column(kv[s][:2] if s == 1 else kv[s], t))
+        base = len(held)
+        held += [to_column(array, t) for array in (near, far_keys, far_values)]
+        key_places += [(base, 0), (base, 2)] + [(base + 1, at) for at in range(len(far))]
+        value_places += [(base, 1), (base, 3)] + [(base + 2, at) for at in range(len(far))]
 
     all_tokens = tokens * blocks * columns_of
-
-    def attend_blocks(query_arrays, places):
-        pairs = heads * tokens * len(places) * all_tokens
-        return pl.pallas_call(
-            functools.partial(attend_kernel, places, [0] * len(all_kv)),
-            out_shape=[jax.ShapeDtypeStruct((tokens, part), kind)] * len(places),
-            in_specs=[VMEM] * (len(places) + len(all_kv)),
-            out_specs=[VMEM] * len(places),
-            compiler_params=pltpu.CompilerParams(vmem_limit_bytes=32 * 1024 * 1024),
-            cost_estimate=pl.CostEstimate(
-                flops=4 * HD * pairs,
-                bytes_accessed=2 * part * (2 * all_tokens + 2 * tokens * len(places)),
-                transcendentals=pairs,
-            ),
-            name="attend",
-        )(*query_arrays, *all_kv)
-
-    mixed = dict(zip((0, 1), attend_blocks([packed[-1], kv[1]], [0, 2])))
-    for s in far:
-        mixed[s] = attend_blocks([far_q[s]], [0])[0]
-    back = [mixed[0]] + [to_block(mixed[s], s) for s in range(1, blocks)]
+    pairs = heads * tokens * blocks * all_tokens
+    mixed = pl.pallas_call(
+        functools.partial(attend_kernel, query_places, key_places, value_places),
+        out_shape=[jax.ShapeDtypeStruct((tokens, part), kind)] * blocks,
+        in_specs=[VMEM] * len(held),
+        out_specs=[VMEM] * blocks,
+        compiler_params=pltpu.CompilerParams(vmem_limit_bytes=24 * 1024 * 1024),
+        cost_estimate=pl.CostEstimate(
+            flops=4 * HD * pairs,
+            bytes_accessed=2 * part * (2 * all_tokens + 2 * tokens * blocks),
+            transcendentals=pairs,
+        ),
+        name="attend",
+    )(*held)
+
+    back = {s: to_block(mixed[s], s) for s in range(blocks - 1, 0, -1)}
     return pl.pallas_call(
         functools.partial(unpack_kernel, blocks, part),
         out_shape=jax.ShapeDtypeStruct((1, tokens, width), kind),
         in_specs=[VMEM] * blocks,
-        out_specs=ANY,
+        out_specs=HBM,
         scratch_shapes=[pltpu.SemaphoreType.DMA((blocks,))],
-        cost_estimate=pl.CostEstimate(flops=0, bytes_accessed=2 * tokens * width * 2, transcendentals=0),
+        compiler_params=SMALL,
+        cost_estimate=pl.CostEstimate(
+            flops=0, bytes_accessed=2 * tokens * width * 2, transcendentals=0
+        ),
         name="unpack",
-    )(*back)
+    )(mixed[0], *[back[s] for s in range(1, blocks)])
 
 
 def local(query_rows, key_rows, value_rows):
     blocks = lax.axis_size("blk")
     heads = query_rows.shape[2] // HD
-    few = blocks >= 2 and heads % blocks == 0 and blocks & (blocks - 1) == 0
+    few = blocks >= 4 and heads % blocks == 0 and blocks & (blocks - 1) == 0
     plan = local_blocks if few else local_generic
     return plan(query_rows, key_rows, value_rows)
 

time: 40.5 us -> 38.5 us (0.951)
  Pallas kernels: 6.25 us -> 2.03 us
  local copies, waits for them, and re-layouts: 1.26 us -> 2.78 us
  waiting for transfers between devices: 14.4 us -> 15.6 us
    ppermute x4 -> x3, waiting for transfers between devices: 0.01 us -> 4.08 us  [to_column(): lax.ppermute(array, 'uly', [(i, (i + t) % columns_of) for i in range(colu...]
    pallas_call x4 -> x5, Pallas kernels: 4.68 us -> 1.33 us  [the longest x1 1.08 us: local_blocks(): pl.pallas_call(functools.partial(attend_kernel, query_places, key_places,...]
    ppermute x8, waiting for transfers between devices: 14.4 us -> 11.5 us  [to_block(): return lax.ppermute(array, 'blk', [(i, i ^ s) for i in range(blocks)])]
    unnamed x16 -> x6, local copies, waits for them, and re-layouts: 1.25 us -> 2.78 us
    ppermute x4 -> x3, starting transfers between devices: 5.29 us -> 3.93 us  [to_column(): lax.ppermute(array, 'uly', [(i, (i + t) % columns_of) for i in range(colu...]
    ppermute x8, starting transfers between devices: 13 us -> 14 us  [to_block(): return lax.ppermute(array, 'blk', [(i, i ^ s) for i in range(blocks)])]
    pallas_call x1, Pallas kernels: 1.57 us -> 0.7 us  [local_blocks(): pl.pallas_call(functools.partial(unpack_kernel, blocks, part), out_shape=...]
  transfers between devices with their start and end apart: 12 -> 11, of which waited for: 5 -> 6; matrix products, arithmetic and copies ran while one was open for 0% -> 0% of each run, Pallas kernels for 7% -> 0%
where the time goes in v3:
time: 38.5 us; the launch traced here: 38.4 us
  starting transfers between devices  17.9 us (46%)
  waiting for transfers between devices  15.6 us (41%)
  local copies, waits for them, and re-layouts  2.78 us (7%)
  Pallas kernels  2.03 us (5%)
    ppermute x8, starting transfers between devices, to_block(): return lax.ppermute(array, 'blk', [(i, i ^ s) for i in range(blocks)])  14 us
    ppermute x8, waiting for transfers between devices, to_block(): return lax.ppermute(array, 'blk', [(i, i ^ s) for i in range(blocks)])  11.5 us
    ppermute x3, waiting for transfers between devices, to_column(): lax.ppermute(array, 'uly', [(i, (i + t) % columns_of) for i in range(colu...  4.08 us
    ppermute x3, starting transfers between devices, to_column(): lax.ppermute(array, 'uly', [(i, (i + t) % columns_of) for i in range(colu...  3.93 us
    unnamed x6, local copies, waits for them, and re-layouts  2.78 us
    pallas_call x1, Pallas kernels, local_blocks(): pl.pallas_call(functools.partial(attend_kernel, query_places, key_places,...  1.08 us
  transfers between devices with their start and end apart: 11, of which 6 were waited for; matrix products, arithmetic and copies ran while one was open for 0% of the time, Pallas kernels for 0%

profile of v3, /device:TPU:0, one launch (start us, length us, event | category | flops | bytes accessed | tf_op | source)
XLA Modules:
  0.0 38.4 jit_solution(1966992892729712567)
XLA Ops:
  0.0 0.0 copy-start
  0.0 0.9 %copy-done = bf16[1,64,1536]{2,1,0:T(8,128)(2,1)S(1)} copy-done((bf16[1,64,1536]{2,1,0:T(8,128)(2,1)S(1)}, bf16[1,64,1536]{2,1,0:T(8,128)(2,1)}, u32[]{:S(2)}) %copy-start) | copy-done | bytes 196632
  0.9 0.0 copy-start.1
  0.9 0.9 %copy-done.1 = bf16[1,64,1536]{2,1,0:T(8,128)(2,1)S(1)} copy-done((bf16[1,64,1536]{2,1,0:T(8,128)(2,1)S(1)}, bf16[1,64,1536]{2,1,0:T(8,128)(2,1)}, u32[]{:S(2)}) %copy-start.1) | copy-done | bytes 196632
  1.9 0.0 copy-start.2
  1.9 0.9 %copy-done.2 = bf16[1,64,1536]{2,1,0:T(8,128)(2,1)S(1)} copy-done((bf16[1,64,1536]{2,1,0:T(8,128)(2,1)S(1)}, bf16[1,64,1536]{2,1,0:T(8,128)(2,1)}, u32[]{:S(2)}) %copy-start.2) | copy-done | bytes 196632
  2.8 0.2 pack.1
  3.0 3.1 %collective-permute-start.2 = (bf16[3,64,384]{2,1,0:T(8,128)(2,1)S(1)}, bf16[3,64,384]{2,1,0:T(8,128)(2,1)S(1)}, u32[]{:S(2)}, u32[]{:S(2)}) collective-permute-start(bf16[3,64,384]{2,1,0:T(8,128)(2,1)S(1)} %get-tuple-element.20), channel_id=1, source_target_pairs={{0,4},{4,0},{8,12},{12,8},{1,5},{5,1},{9,13},{13,9},{2,6},{6,2},{1... | collective-permute-start | bytes 442376 | tf_op jit(solution)/shard_map/ppermute | solution.py:181
  6.1 2.6 %collective-permute-start.3 = (bf16[2,64,384]{2,1,0:T(8,128)(2,1)S(1)}, bf16[2,64,384]{2,1,0:T(8,128)(2,1)S(1)}, u32[]{:S(2)}, u32[]{:S(2)}) collective-permute-start(bf16[2,64,384]{2,1,0:T(8,128)(2,1)S(1)} %get-tuple-element.21), channel_id=1, source_target_pairs={{0,8},{4,12},{8,0},{12,4},{1,9},{5,13},{9,1},{13,5},{2,10},{6,14},... | collective-permute-start | bytes 294920 | tf_op jit(solution)/shard_map/ppermute | solution.py:181
  8.7 0.0 collective-permute-start.4
  8.7 2.6 %collective-permute-done.2.refs_1_.refs_4_ = bf16[3,64,384]{2,1,0:T(8,128)(2,1)S(1)} collective-permute-done((bf16[3,64,384]{2,1,0:T(8,128)(2,1)S(1)}, bf16[3,64,384]{2,1,0:T(8,128)(2,1)S(1)}, u32[]{:S(2)}, u32[]{:S(2)}) %collective-permute-start.2) | collective-permute-done | bytes 147488 | tf_op jit(solution)/shard_map/ppermute | solution.py:181
  11.3 1.8 %collective-permute-start.5 = (bf16[4,64,384]{2,1,0:T(8,128)(2,1)S(1)}, bf16[4,64,384]{2,1,0:T(8,128)(2,1)S(1)}, u32[]{:S(2)}, u32[]{:S(2)}) collective-permute-start(bf16[4,64,384]{2,1,0:T(8,128)(2,1)S(1)} %join.3), channel_id=1, source_target_pairs={{0,2},{2,0},{1,3},{3,1},{4,6},{6,4},{5,7},{7,5},{8,10},{10,8},{9,1... | collective-permute-start | bytes 589832 | tf_op jit(solution)/shard_map/ppermute | solution.py:184
  13.1 2.3 %collective-permute-start = (bf16[1,64,384]{2,1,0:T(8,128)(2,1)S(1)}, bf16[1,64,384]{2,1,0:T(8,128)(2,1)S(1)}, u32[]{:S(2)}, u32[]{:S(2)}) collective-permute-start(bf16[1,64,384]{2,1,0:T(8,128)(2,1)S(1)} %get-tuple-element.18), channel_id=1, source_target_pairs={{0,8},{4,12},{8,0},{12,4},{1,9},{5,13},{9,1},{13,5},{2,10},{6,14},... | collective-permute-start | bytes 147464 | tf_op jit(solution)/shard_map/ppermute | solution.py:181
  15.4 1.5 %collective-permute-start.1 = (bf16[1,64,384]{2,1,0:T(8,128)(2,1)S(1)}, bf16[1,64,384]{2,1,0:T(8,128)(2,1)S(1)}, u32[]{:S(2)}, u32[]{:S(2)}) collective-permute-start(bf16[1,64,384]{2,1,0:T(8,128)(2,1)S(1)} %get-tuple-element.19), channel_id=1, source_target_pairs={{0,12},{4,8},{8,4},{12,0},{1,13},{5,9},{9,5},{13,1},{2,14},{6,10},... | collective-permute-start | bytes 147464 | tf_op jit(solution)/shard_map/ppermute | solution.py:181
  16.9 4.6 %collective-permute-done.refs_0_.refs_2_ = bf16[1,64,384]{2,1,0:T(8,128)(2,1)S(1)} collective-permute-done((bf16[1,64,384]{2,1,0:T(8,128)(2,1)S(1)}, bf16[1,64,384]{2,1,0:T(8,128)(2,1)S(1)}, u32[]{:S(2)}, u32[]{:S(2)}) %collective-permute-start) | collective-permute-done | bytes 49184 | tf_op jit(solution)/shard_map/ppermute | solution.py:181
  21.5 0.0 collective-permute-done.1.refs_1_.refs_3_
  21.5 1.6 %collective-permute-start.6 = (bf16[2,64,384]{2,1,0:T(8,128)(2,1)S(1)}, bf16[2,64,384]{2,1,0:T(8,128)(2,1)S(1)}, u32[]{:S(2)}, u32[]{:S(2)}) collective-permute-start(bf16[2,64,384]{2,1,0:T(8,128)(2,1)S(1)} %join.4), channel_id=1, source_target_pairs={{0,2},{2,0},{1,3},{3,1},{4,6},{6,4},{5,7},{7,5},{8,10},{10,8},{9,1... | collective-permute-start | bytes 294920 | tf_op jit(solution)/shard_map/ppermute | solution.py:184
  23.1 0.0 collective-permute-done.3.refs_0_.refs_5_
  23.1 0.0 collective-permute-done.4.refs_1_.refs_6_
  23.1 0.6 %collective-permute-start.7 = (bf16[2,64,384]{2,1,0:T(8,128)(2,1)S(1)}, bf16[2,64,384]{2,1,0:T(8,128)(2,1)S(1)}, u32[]{:S(2)}, u32[]{:S(2)}) collective-permute-start(bf16[2,64,384]{2,1,0:T(8,128)(2,1)S(1)} %join.5), channel_id=1, source_target_pairs={{0,2},{2,0},{1,3},{3,1},{4,6},{6,4},{5,7},{7,5},{8,10},{10,8},{9,1... | collective-permute-start | bytes 294920 | tf_op jit(solution)/shard_map/ppermute | solution.py:184
  23.7 2.5 %collective-permute-done.6.refs_8_ = bf16[2,64,384]{2,1,0:T(8,128)(2,1)S(1)} collective-permute-done((bf16[2,64,384]{2,1,0:T(8,128)(2,1)S(1)}, bf16[2,64,384]{2,1,0:T(8,128)(2,1)S(1)}, u32[]{:S(2)}, u32[]{:S(2)}) %collective-permute-start.6) | collective-permute-done | bytes 98336 | tf_op jit(solution)/shard_map/ppermute | solution.py:184
  26.2 1.6 %collective-permute-done.7.refs_9_ = bf16[2,64,384]{2,1,0:T(8,128)(2,1)S(1)} collective-permute-done((bf16[2,64,384]{2,1,0:T(8,128)(2,1)S(1)}, bf16[2,64,384]{2,1,0:T(8,128)(2,1)S(1)}, u32[]{:S(2)}, u32[]{:S(2)}) %collective-permute-start.7) | collective-permute-done | bytes 98336 | tf_op jit(solution)/shard_map/ppermute | solution.py:184
  27.8 0.0 collective-permute-done.5.refs_7_
  27.8 1.1 %attend.1 = (bf16[64,384]{1,0:T(8,128)(2,1)S(1)}, bf16[64,384]{1,0:T(8,128)(2,1)S(1)}, bf16[64,384]{1,0:T(8,128)(2,1)S(1)}, bf16[64,384]{1,0:T(8,128)(2,1)S(1)}) custom-call(bf16[2,64,384]{2,1,0:T(8,128)(2,1)S(1)} %get-tuple-element.16.refs_0_, bf16[1,64,384]{2,1,0:T(8,128)(2,1)S(1)} %get-tuple-element.17.refs_1_, ...), custom_call_target="tpu_custom_call" | custom-call | flops 201326592 | bytes 1179648 | tf_op jit(solution)/shard_map/attend/pallas_call | solution.py:207
  28.9 1.2 %collective-permute-start.8 = (bf16[64,384]{1,0:T(8,128)(2,1)S(1)}, bf16[64,384]{1,0:T(8,128)(2,1)S(1)}, u32[]{:S(2)}, u32[]{:S(2)}) collective-permute-start(bf16[64,384]{1,0:T(8,128)(2,1)S(1)} %get-tuple-element.24), channel_id=1, source_target_pairs={{0,4},{4,0},{8,12},{12,8},{1,5},{5,1},{9,13},{13,9},{2,6},{6,2},{1... | collective-permute-start | bytes 147464 | tf_op jit(solution)/shard_map/ppermute | solution.py:181
  30.0 1.7 %collective-permute-start.9 = (bf16[64,384]{1,0:T(8,128)(2,1)S(1)}, bf16[64,384]{1,0:T(8,128)(2,1)S(1)}, u32[]{:S(2)}, u32[]{:S(2)}) collective-permute-start(bf16[64,384]{1,0:T(8,128)(2,1)S(1)} %get-tuple-element.25), channel_id=1, source_target_pairs={{0,8},{4,12},{8,0},{12,4},{1,9},{5,13},{9,1},{13,5},{2,10},{6,14},... | collective-permute-start | bytes 147464 | tf_op jit(solution)/shard_map/ppermute | solution.py:181
  31.8 1.5 %collective-permute-start.10 = (bf16[64,384]{1,0:T(8,128)(2,1)S(1)}, bf16[64,384]{1,0:T(8,128)(2,1)S(1)}, u32[]{:S(2)}, u32[]{:S(2)}) collective-permute-start(bf16[64,384]{1,0:T(8,128)(2,1)S(1)} %get-tuple-element.26), channel_id=1, source_target_pairs={{0,12},{4,8},{8,4},{12,0},{1,13},{5,9},{9,5},{13,1},{2,14},{6,10},... | collective-permute-start | bytes 147464 | tf_op jit(solution)/shard_map/ppermute | solution.py:181
  33.3 0.0 collective-permute-done.8.refs_1_
  33.3 2.2 %collective-permute-done.9.refs_2_ = bf16[64,384]{1,0:T(8,128)(2,1)S(1)} collective-permute-done((bf16[64,384]{1,0:T(8,128)(2,1)S(1)}, bf16[64,384]{1,0:T(8,128)(2,1)S(1)}, u32[]{:S(2)}, u32[]{:S(2)}) %collective-permute-start.9) | collective-permute-done | bytes 49184 | tf_op jit(solution)/shard_map/ppermute | solution.py:181
  35.5 2.1 %collective-permute-done.10.refs_3_ = bf16[64,384]{1,0:T(8,128)(2,1)S(1)} collective-permute-done((bf16[64,384]{1,0:T(8,128)(2,1)S(1)}, bf16[64,384]{1,0:T(8,128)(2,1)S(1)}, u32[]{:S(2)}, u32[]{:S(2)}) %collective-permute-start.10) | collective-permute-done | bytes 49184 | tf_op jit(solution)/shard_map/ppermute | solution.py:181
  37.7 0.7 %unpack.1 = bf16[1,64,1536]{2,1,0:T(8,128)(2,1)} custom-call(bf16[64,384]{1,0:T(8,128)(2,1)S(1)} %get-tuple-element.23.refs_0_, bf16[64,384]{1,0:T(8,128)(2,1)S(1)} %collective-permute-done.8.refs_1_, bf16[64,384]{1,0:T(8,128)(2,1)S(1)} %collective-permute-done.9.refs_2_, bf16[64,384]{1,0:T(8,128)(2,1)S(1)} %collective-permute-done.10.refs_3_), custom_call_target="tpu_custom_call" | custom-call | bytes 393216 | tf_op jit(solution)/shard_map/unpack/pallas_call | solution.py:222
  (3 shorter events, 0.0 us)
Async XLA Ops:
  0.0 0.9 %copy-start = (bf16[1,64,1536]{2,1,0:T(8,128)(2,1)S(1)}, bf16[1,64,1536]{2,1,0:T(8,128)(2,1)}, u32[]{:S(2)}) copy-start(bf16[1,64,1536]{2,1,0:T(8,128)(2,1)} %q_ref.1) | copy-start | bytes 589828
  0.9 0.9 %copy-start.1 = (bf16[1,64,1536]{2,1,0:T(8,128)(2,1)S(1)}, bf16[1,64,1536]{2,1,0:T(8,128)(2,1)}, u32[]{:S(2)}) copy-start(bf16[1,64,1536]{2,1,0:T(8,128)(2,1)} %k_ref.1) | copy-start | bytes 589828
  1.9 0.9 %copy-start.2 = (bf16[1,64,1536]{2,1,0:T(8,128)(2,1)S(1)}, bf16[1,64,1536]{2,1,0:T(8,128)(2,1)}, u32[]{:S(2)}) copy-start(bf16[1,64,1536]{2,1,0:T(8,128)(2,1)} %v_ref.1) | copy-start | bytes 589828
  3.0 8.3 %collective-permute-start.2 = (bf16[3,64,384]{2,1,0:T(8,128)(2,1)S(1)}, bf16[3,64,384]{2,1,0:T(8,128)(2,1)S(1)}, u32[]{:S(2)}, u32[]{:S(2)}) collective-permute-start(bf16[3,64,384]{2,1,0:T(8,128)(2,1)S(1)} %get-tuple-element.20), channel_id=1, source_target_pairs={{0,4},{4,0},{8,12},{12,8},{1,5},{5,1},{9,13},{13,9},{2,6},{6,2},{1... | collective-permute-start | bytes 442376 | tf_op jit(solution)/shard_map/ppermute | solution.py:181
  6.1 17.0 %collective-permute-start.3 = (bf16[2,64,384]{2,1,0:T(8,128)(2,1)S(1)}, bf16[2,64,384]{2,1,0:T(8,128)(2,1)S(1)}, u32[]{:S(2)}, u32[]{:S(2)}) collective-permute-start(bf16[2,64,384]{2,1,0:T(8,128)(2,1)S(1)} %get-tuple-element.21), channel_id=1, source_target_pairs={{0,8},{4,12},{8,0},{12,4},{1,9},{5,13},{9,1},{13,5},{2,10},{6,14},... | collective-permute-start | bytes 294920 | tf_op jit(solution)/shard_map/ppermute | solution.py:181
  8.7 14.4 %collective-permute-start.4 = (bf16[2,64,384]{2,1,0:T(8,128)(2,1)S(1)}, bf16[2,64,384]{2,1,0:T(8,128)(2,1)S(1)}, u32[]{:S(2)}, u32[]{:S(2)}) collective-permute-start(bf16[2,64,384]{2,1,0:T(8,128)(2,1)S(1)} %get-tuple-element.22), channel_id=1, source_target_pairs={{0,12},{4,8},{8,4},{12,0},{1,13},{5,9},{9,5},{13,1},{2,14},{6,10},... | collective-permute-start | bytes 294920 | tf_op jit(solution)/shard_map/ppermute | solution.py:181
  11.3 16.5 %collective-permute-start.5 = (bf16[4,64,384]{2,1,0:T(8,128)(2,1)S(1)}, bf16[4,64,384]{2,1,0:T(8,128)(2,1)S(1)}, u32[]{:S(2)}, u32[]{:S(2)}) collective-permute-start(bf16[4,64,384]{2,1,0:T(8,128)(2,1)S(1)} %join.3), channel_id=1, source_target_pairs={{0,2},{2,0},{1,3},{3,1},{4,6},{6,4},{5,7},{7,5},{8,10},{10,8},{9,1... | collective-permute-start | bytes 589832 | tf_op jit(solution)/shard_map/ppermute | solution.py:184
  13.1 8.4 %collective-permute-start = (bf16[1,64,384]{2,1,0:T(8,128)(2,1)S(1)}, bf16[1,64,384]{2,1,0:T(8,128)(2,1)S(1)}, u32[]{:S(2)}, u32[]{:S(2)}) collective-permute-start(bf16[1,64,384]{2,1,0:T(8,128)(2,1)S(1)} %get-tuple-element.18), channel_id=1, source_target_pairs={{0,8},{4,12},{8,0},{12,4},{1,9},{5,13},{9,1},{13,5},{2,10},{6,14},... | collective-permute-start | bytes 147464 | tf_op jit(solution)/shard_map/ppermute | solution.py:181
  15.4 6.1 %collective-permute-start.1 = (bf16[1,64,384]{2,1,0:T(8,128)(2,1)S(1)}, bf16[1,64,384]{2,1,0:T(8,128)(2,1)S(1)}, u32[]{:S(2)}, u32[]{:S(2)}) collective-permute-start(bf16[1,64,384]{2,1,0:T(8,128)(2,1)S(1)} %get-tuple-element.19), channel_id=1, source_target_pairs={{0,12},{4,8},{8,4},{12,0},{1,13},{5,9},{9,5},{13,1},{2,14},{6,10},... | collective-permute-start | bytes 147464 | tf_op jit(solution)/shard_map/ppermute | solution.py:181
  21.5 4.7 %collective-permute-start.6 = (bf16[2,64,384]{2,1,0:T(8,128)(2,1)S(1)}, bf16[2,64,384]{2,1,0:T(8,128)(2,1)S(1)}, u32[]{:S(2)}, u32[]{:S(2)}) collective-permute-start(bf16[2,64,384]{2,1,0:T(8,128)(2,1)S(1)} %join.4), channel_id=1, source_target_pairs={{0,2},{2,0},{1,3},{3,1},{4,6},{6,4},{5,7},{7,5},{8,10},{10,8},{9,1... | collective-permute-start | bytes 294920 | tf_op jit(solution)/shard_map/ppermute | solution.py:184
  23.1 4.7 %collective-permute-start.7 = (bf16[2,64,384]{2,1,0:T(8,128)(2,1)S(1)}, bf16[2,64,384]{2,1,0:T(8,128)(2,1)S(1)}, u32[]{:S(2)}, u32[]{:S(2)}) collective-permute-start(bf16[2,64,384]{2,1,0:T(8,128)(2,1)S(1)} %join.5), channel_id=1, source_target_pairs={{0,2},{2,0},{1,3},{3,1},{4,6},{6,4},{5,7},{7,5},{8,10},{10,8},{9,1... | collective-permute-start | bytes 294920 | tf_op jit(solution)/shard_map/ppermute | solution.py:184
  28.9 4.5 %collective-permute-start.8 = (bf16[64,384]{1,0:T(8,128)(2,1)S(1)}, bf16[64,384]{1,0:T(8,128)(2,1)S(1)}, u32[]{:S(2)}, u32[]{:S(2)}) collective-permute-start(bf16[64,384]{1,0:T(8,128)(2,1)S(1)} %get-tuple-element.24), channel_id=1, source_target_pairs={{0,4},{4,0},{8,12},{12,8},{1,5},{5,1},{9,13},{13,9},{2,6},{6,2},{1... | collective-permute-start | bytes 147464 | tf_op jit(solution)/shard_map/ppermute | solution.py:181
  30.0 5.5 %collective-permute-start.9 = (bf16[64,384]{1,0:T(8,128)(2,1)S(1)}, bf16[64,384]{1,0:T(8,128)(2,1)S(1)}, u32[]{:S(2)}, u32[]{:S(2)}) collective-permute-start(bf16[64,384]{1,0:T(8,128)(2,1)S(1)} %get-tuple-element.25), channel_id=1, source_target_pairs={{0,8},{4,12},{8,0},{12,4},{1,9},{5,13},{9,1},{13,5},{2,10},{6,14},... | collective-permute-start | bytes 147464 | tf_op jit(solution)/shard_map/ppermute | solution.py:181
  31.8 5.9 %collective-permute-start.10 = (bf16[64,384]{1,0:T(8,128)(2,1)S(1)}, bf16[64,384]{1,0:T(8,128)(2,1)S(1)}, u32[]{:S(2)}, u32[]{:S(2)}) collective-permute-start(bf16[64,384]{1,0:T(8,128)(2,1)S(1)} %get-tuple-element.26), channel_id=1, source_target_pairs={{0,12},{4,8},{8,4},{12,0},{1,13},{5,9},{9,5},{13,1},{2,14},{6,10},... | collective-permute-start | bytes 147464 | tf_op jit(solution)/shard_map/ppermute | solution.py:181

commit v4 on v3

--- a/solution.py
+++ b/solution.py
@@ -9,6 +9,7 @@
 from jax.sharding import PartitionSpec as P
 
 HD = 128
+ANY = pl.BlockSpec(memory_space=pl.ANY)
 HBM = pl.BlockSpec(memory_space=pltpu.HBM)
 VMEM = pl.BlockSpec(memory_space=pltpu.VMEM)
 SMALL = pltpu.CompilerParams(vmem_limit_bytes=4 * 1024 * 1024)
@@ -117,6 +118,22 @@
     )(*arrays)
 
 
+def hold_kernel(array_ref, until_ref, out_ref):
+    pass
+
+
+def hold(array, until):
+    return pl.pallas_call(
+        hold_kernel,
+        out_shape=jax.ShapeDtypeStruct(array.shape, array.dtype),
+        in_specs=[ANY, ANY],
+        out_specs=ANY,
+        input_output_aliases={0: 0},
+        compiler_params=SMALL,
+        name="hold",
+    )(array, until)
+
+
 def attend_kernel(query_places, key_places, value_places, *refs):
     blocks = len(query_places)
     ins, out_refs = refs[:-blocks], refs[-blocks:]
@@ -144,13 +161,13 @@
             ref[:, lanes] = result[at * tokens : (at + 1) * tokens]
 
 
-def unpack_kernel(blocks, part, *refs):
-    ins, out_ref, sems = refs[:blocks], refs[blocks], refs[-1]
+def unpack_kernel(order, part, *refs):
+    ins, out_ref, sems = refs[:-2], refs[-2], refs[-1]
     me = lax.axis_index("blk")
     pairs = []
-    for s in range(blocks):
+    for s, ref in zip(order, ins):
         columns = pl.ds(pl.multiple_of((me ^ s) * part, 128), part)
-        pairs.append((ins[s], out_ref.at[0, :, columns]))
+        pairs.append((ref, out_ref.at[0, :, columns]))
     run_copies(pairs, sems)
 
 
@@ -160,10 +177,7 @@
     part = width // blocks
     heads = part // HD
     kind = query_rows.dtype
-    far = list(range(2, blocks))
-
-    messages = [(s, "k") for s in far] + [(1, "kvq")] + [(s, "vq") for s in far]
-    messages += [(0, "kv"), (0, "q")]
+    messages = [(s, "kvq") for s in range(blocks - 1, 0, -1)] + [(0, "kv"), (0, "q")]
     packed = pl.pallas_call(
         functools.partial(pack_kernel, messages, part),
         out_shape=[jax.ShapeDtypeStruct((len(m), tokens, part), kind) for s, m in messages],
@@ -175,7 +189,7 @@
             flops=0, bytes_accessed=6 * tokens * width * 2, transcendentals=0
         ),
         name="pack",
-    )(query_rows, key_rows, value_rows)
+    )(*[pltpu.with_memory_space_constraint(x, pltpu.HBM) for x in (query_rows, key_rows, value_rows)])
 
     def to_block(array, s):
         return lax.ppermute(array, "blk", [(i, i ^ s) for i in range(blocks)])
@@ -183,24 +197,22 @@
     def to_column(array, t):
         return lax.ppermute(array, "uly", [(i, (i + t) % columns_of) for i in range(columns_of)])
 
-    sent = {message: array for message, array in zip(messages, packed)}
-    held = [sent[0, "kv"], sent[0, "q"]]
-    held += [to_block(sent[m], m[0]) for m in messages[:-2]]
-    at_near = 2 + len(far)
-    at_keys = {s: 2 + at for at, s in enumerate(far)}
-    at_values = {s: 3 + len(far) + at for at, s in enumerate(far)}
-    query_places = [(1, 0), (at_near, 2)] + [(at_values[s], 1) for s in far]
-    key_places = [(0, 0), (at_near, 0)] + [(at_keys[s], 0) for s in far]
-    value_places = [(0, 1), (at_near, 1)] + [(at_values[s], 0) for s in far]
-    near = join([held[0], held[at_near]], [(0, 0), (0, 1), (1, 0), (1, 1)])
-    far_places = [(at, 0) for at in range(len(far))]
-    far_keys = join([held[at_keys[s]] for s in far], far_places)
-    far_values = join([held[at_values[s]] for s in far], far_places)
+    sent = {message[0]: array for message, array in zip(messages, packed)}
+    own_kv, own_q = packed[-2:]
+    got = {s: to_block(sent[s], s) for s in (1, 3)}
+    got[2] = to_block(hold(sent[2], got[1]), 2)
+    held = [own_kv, own_q] + [got[s] for s in range(1, blocks)]
+    query_places = [(1, 0)] + [(1 + s, 2) for s in range(1, blocks)]
+    key_places = [(0, 0)] + [(1 + s, 0) for s in range(1, blocks)]
+    value_places = [(0, 1)] + [(1 + s, 1) for s in range(1, blocks)]
+    groups = [join([own_kv, got[1]], [(0, 0), (0, 1), (1, 0), (1, 1)])]
+    groups += [join([got[s]], [(0, 0), (0, 1)]) for s in range(blocks - 1, 1, -1)]
     for t in range(1, columns_of):
-        base = len(held)
-        held += [to_column(array, t) for array in (near, far_keys, far_values)]
-        key_places += [(base, 0), (base, 2)] + [(base + 1, at) for at in range(len(far))]
-        value_places += [(base, 1), (base, 3)] + [(base + 2, at) for at in range(len(far))]
+        for group in groups:
+            for at in range(0, group.shape[0], 2):
+                key_places.append((len(held), at))
+                value_places.append((len(held), at + 1))
+            held.append(to_column(group, t))
 
     all_tokens = tokens * blocks * columns_of
     pairs = heads * tokens * blocks * all_tokens
@@ -218,9 +230,10 @@
         name="attend",
     )(*held)
 
-    back = {s: to_block(mixed[s], s) for s in range(blocks - 1, 0, -1)}
+    order = [0] + list(range(blocks - 1, 0, -1))
+    back = [to_block(mixed[s], s) if s else mixed[0] for s in order]
     return pl.pallas_call(
-        functools.partial(unpack_kernel, blocks, part),
+        functools.partial(unpack_kernel, order, part),
         out_shape=jax.ShapeDtypeStruct((1, tokens, width), kind),
         in_specs=[VMEM] * blocks,
         out_specs=HBM,
@@ -230,13 +243,13 @@
             flops=0, bytes_accessed=2 * tokens * width * 2, transcendentals=0
         ),
         name="unpack",
-    )(mixed[0], *[back[s] for s in range(1, blocks)])
+    )(*back)
 
 
 def local(query_rows, key_rows, value_rows):
     blocks = lax.axis_size("blk")
     heads = query_rows.shape[2] // HD
-    few = blocks >= 4 and heads % blocks == 0 and blocks & (blocks - 1) == 0
+    few = blocks == 4 and heads % blocks == 0
     plan = local_blocks if few else local_generic
     return plan(query_rows, key_rows, value_rows)
 

time: 38.5 us -> 34.3 us (0.89)
  waiting for transfers between devices: 15.6 us -> 12.7 us
  local copies, waits for them, and re-layouts: 2.78 us -> 0 us
  Pallas kernels: 2.03 us -> 3.01 us
  starting transfers between devices: 17.9 us -> 18.4 us
    unnamed x6 -> x0, local copies, waits for them, and re-layouts: 2.78 us -> none
    ppermute x8 -> x6, waiting for transfers between devices: 11.5 us -> 9.56 us  [to_block(): return lax.ppermute(array, 'blk', [(i, i ^ s) for i in range(blocks)])]
    ppermute x3, waiting for transfers between devices: 4.08 us -> 3.12 us  [to_column(): lax.ppermute(array, 'uly', [(i, (i + t) % columns_of) for i in range(colu...]
    pallas_call x1, Pallas kernels: 0.21 us -> 1.17 us  [local_blocks(): pl.pallas_call(functools.partial(pack_kernel, messages, part), out_shape=...]
    ppermute x3, starting transfers between devices: 3.93 us -> 4.67 us  [to_column(): lax.ppermute(array, 'uly', [(i, (i + t) % columns_of) for i in range(colu...]
    ppermute x8 -> x6, starting transfers between devices: 14 us -> 13.7 us  [to_block(): return lax.ppermute(array, 'blk', [(i, i ^ s) for i in range(blocks)])]
  transfers between devices with their start and end apart: 11 -> 9, of which waited for: 6 -> 6; matrix products, arithmetic and copies ran while one was open for 0% -> 0% of each run, Pallas kernels for 0% -> 0%
where the time goes in v4:
time: 34.3 us; the launch traced here: 34.1 us
  starting transfers between devices  18.4 us (54%)
  waiting for transfers between devices  12.7 us (37%)
  Pallas kernels  3.01 us (9%)
    ppermute x6, starting transfers between devices, to_block(): return lax.ppermute(array, 'blk', [(i, i ^ s) for i in range(blocks)])  13.7 us
    ppermute x6, waiting for transfers between devices, to_block(): return lax.ppermute(array, 'blk', [(i, i ^ s) for i in range(blocks)])  9.56 us
    ppermute x3, starting transfers between devices, to_column(): lax.ppermute(array, 'uly', [(i, (i + t) % columns_of) for i in range(colu...  4.67 us
    ppermute x3, waiting for transfers between devices, to_column(): lax.ppermute(array, 'uly', [(i, (i + t) % columns_of) for i in range(colu...  3.12 us
    pallas_call x1, Pallas kernels, local_blocks(): pl.pallas_call(functools.partial(pack_kernel, messages, part), out_shape=...  1.17 us
    pallas_call x1, Pallas kernels, local_blocks(): pl.pallas_call(functools.partial(attend_kernel, query_places, key_places,...  1.1 us
    pallas_call x1, Pallas kernels, local_blocks(): pl.pallas_call(functools.partial(unpack_kernel, order, part), out_shape=j...  0.7 us
  transfers between devices with their start and end apart: 9, of which 6 were waited for; matrix products, arithmetic and copies ran while one was open for 0% of the time, Pallas kernels for 0%

profile of v4, /device:TPU:0, one launch (start us, length us, event | category | flops | bytes accessed | tf_op | source)
XLA Modules:
  0.0 34.1 jit_solution(7385187584714971367)
XLA Ops:
  0.0 1.2 %pack.1 = (bf16[3,64,384]{2,1,0:T(8,128)(2,1)S(1)}, bf16[3,64,384]{2,1,0:T(8,128)(2,1)S(1)}, bf16[3,64,384]{2,1,0:T(8,128)(2,1)S(1)}, bf16[2,64,384]{2,1,0:T(8,128)(2,1)S(1)}, bf16[1,64,384]{2,1,0:T(8,128)(2,1)S(1)}) custom-call(bf16[1,64,1536]{2,1,0:T(8,128)(2,1)} %q_ref.1, bf16[1,64,1536]{2,1,0:T(8,128)(2,1)} %k_ref.1, bf16[1,64,1536]{2,1,0:T(8,128)(2,1)} %v_ref.1), custom_call_target="tpu_custom_call" | custom-call | bytes 1179648 | tf_op jit(solution)/shard_map/pack/pallas_call | solution.py:181
  1.2 3.1 %collective-permute-start = (bf16[3,64,384]{2,1,0:T(8,128)(2,1)S(1)}, bf16[3,64,384]{2,1,0:T(8,128)(2,1)S(1)}, u32[]{:S(2)}, u32[]{:S(2)}) collective-permute-start(bf16[3,64,384]{2,1,0:T(8,128)(2,1)S(1)} %get-tuple-element.16), channel_id=1, source_target_pairs={{0,4},{4,0},{8,12},{12,8},{1,5},{5,1},{9,13},{13,9},{2,6},{6,2},{1... | collective-permute-start | bytes 442376 | tf_op jit(solution)/shard_map/ppermute | solution.py:195
  4.3 2.5 %collective-permute-start.2 = (bf16[3,64,384]{2,1,0:T(8,128)(2,1)S(1)}, bf16[3,64,384]{2,1,0:T(8,128)(2,1)S(1)}, u32[]{:S(2)}, u32[]{:S(2)}) collective-permute-start(bf16[3,64,384]{2,1,0:T(8,128)(2,1)S(1)} %get-tuple-element.18), channel_id=1, source_target_pairs={{0,12},{4,8},{8,4},{12,0},{1,13},{5,9},{9,5},{13,1},{2,14},{6,10},... | collective-permute-start | bytes 442376 | tf_op jit(solution)/shard_map/ppermute | solution.py:195
  6.7 1.6 %collective-permute-done.until_ref.refs_1_.refs_2_ = bf16[3,64,384]{2,1,0:T(8,128)(2,1)S(1)} collective-permute-done((bf16[3,64,384]{2,1,0:T(8,128)(2,1)S(1)}, bf16[3,64,384]{2,1,0:T(8,128)(2,1)S(1)}, u32[]{:S(2)}, u32[]{:S(2)}) %collective-permute-start) | collective-permute-done | bytes 147488 | tf_op jit(solution)/shard_map/ppermute | solution.py:195
  8.3 3.7 %collective-permute-start.1 = (bf16[3,64,384]{2,1,0:T(8,128)(2,1)S(1)}, bf16[3,64,384]{2,1,0:T(8,128)(2,1)S(1)}, u32[]{:S(2)}, u32[]{:S(2)}) collective-permute-start(bf16[3,64,384]{2,1,0:T(8,128)(2,1)S(1)} %hold.1), channel_id=1, source_target_pairs={{0,8},{4,12},{8,0},{12,4},{1,9},{5,13},{9,1},{13,5},{2,10},{6,14},... | collective-permute-start | bytes 442376 | tf_op jit(solution)/shard_map/ppermute | solution.py:195
  12.0 1.6 %collective-permute-start.3 = (bf16[4,64,384]{2,1,0:T(8,128)(2,1)S(1)}, bf16[4,64,384]{2,1,0:T(8,128)(2,1)S(1)}, u32[]{:S(2)}, u32[]{:S(2)}) collective-permute-start(bf16[4,64,384]{2,1,0:T(8,128)(2,1)S(1)} %join.3), channel_id=1, source_target_pairs={{0,2},{2,0},{1,3},{3,1},{4,6},{6,4},{5,7},{7,5},{8,10},{10,8},{9,1... | collective-permute-start | bytes 589832 | tf_op jit(solution)/shard_map/ppermute | solution.py:198
  13.6 1.1 %collective-permute-done.2.refs_0_.refs_4_ = bf16[3,64,384]{2,1,0:T(8,128)(2,1)S(1)} collective-permute-done((bf16[3,64,384]{2,1,0:T(8,128)(2,1)S(1)}, bf16[3,64,384]{2,1,0:T(8,128)(2,1)S(1)}, u32[]{:S(2)}, u32[]{:S(2)}) %collective-permute-start.2) | collective-permute-done | bytes 147488 | tf_op jit(solution)/shard_map/ppermute | solution.py:195
  14.7 1.6 %collective-permute-start.4 = (bf16[2,64,384]{2,1,0:T(8,128)(2,1)S(1)}, bf16[2,64,384]{2,1,0:T(8,128)(2,1)S(1)}, u32[]{:S(2)}, u32[]{:S(2)}) collective-permute-start(bf16[2,64,384]{2,1,0:T(8,128)(2,1)S(1)} %join.4), channel_id=1, source_target_pairs={{0,2},{2,0},{1,3},{3,1},{4,6},{6,4},{5,7},{7,5},{8,10},{10,8},{9,1... | collective-permute-start | bytes 294920 | tf_op jit(solution)/shard_map/ppermute | solution.py:198
  16.3 3.6 %collective-permute-done.1.refs_0_.refs_3_ = bf16[3,64,384]{2,1,0:T(8,128)(2,1)S(1)} collective-permute-done((bf16[3,64,384]{2,1,0:T(8,128)(2,1)S(1)}, bf16[3,64,384]{2,1,0:T(8,128)(2,1)S(1)}, u32[]{:S(2)}, u32[]{:S(2)}) %collective-permute-start.1) | collective-permute-done | bytes 147488 | tf_op jit(solution)/shard_map/ppermute | solution.py:195
  19.9 1.6 %collective-permute-start.5 = (bf16[2,64,384]{2,1,0:T(8,128)(2,1)S(1)}, bf16[2,64,384]{2,1,0:T(8,128)(2,1)S(1)}, u32[]{:S(2)}, u32[]{:S(2)}) collective-permute-start(bf16[2,64,384]{2,1,0:T(8,128)(2,1)S(1)} %join.5), channel_id=1, source_target_pairs={{0,2},{2,0},{1,3},{3,1},{4,6},{6,4},{5,7},{7,5},{8,10},{10,8},{9,1... | collective-permute-start | bytes 294920 | tf_op jit(solution)/shard_map/ppermute | solution.py:198
  21.5 0.0 collective-permute-done.4.refs_6_
  21.5 0.0 collective-permute-done.3.refs_5_
  21.5 3.1 %collective-permute-done.5.refs_7_ = bf16[2,64,384]{2,1,0:T(8,128)(2,1)S(1)} collective-permute-done((bf16[2,64,384]{2,1,0:T(8,128)(2,1)S(1)}, bf16[2,64,384]{2,1,0:T(8,128)(2,1)S(1)}, u32[]{:S(2)}, u32[]{:S(2)}) %collective-permute-start.5) | collective-permute-done | bytes 98336 | tf_op jit(solution)/shard_map/ppermute | solution.py:198
  24.6 1.1 %attend.1 = (bf16[64,384]{1,0:T(8,128)(2,1)S(1)}, bf16[64,384]{1,0:T(8,128)(2,1)S(1)}, bf16[64,384]{1,0:T(8,128)(2,1)S(1)}, bf16[64,384]{1,0:T(8,128)(2,1)S(1)}) custom-call(bf16[2,64,384]{2,1,0:T(8,128)(2,1)S(1)} %get-tuple-element.14.refs_0_, bf16[1,64,384]{2,1,0:T(8,128)(2,1)S(1)} %get-tuple-element.15.refs_1_, ...), custom_call_target="tpu_custom_call" | custom-call | flops 201326592 | bytes 1179648 | tf_op jit(solution)/shard_map/attend/pallas_call | solution.py:219
  25.7 2.7 %collective-permute-start.6 = (bf16[64,384]{1,0:T(8,128)(2,1)S(1)}, bf16[64,384]{1,0:T(8,128)(2,1)S(1)}, u32[]{:S(2)}, u32[]{:S(2)}) collective-permute-start(bf16[64,384]{1,0:T(8,128)(2,1)S(1)} %get-tuple-element.20), channel_id=1, source_target_pairs={{0,12},{4,8},{8,4},{12,0},{1,13},{5,9},{9,5},{13,1},{2,14},{6,10},... | collective-permute-start | bytes 147464 | tf_op jit(solution)/shard_map/ppermute | solution.py:195
  28.4 0.0 collective-permute-start.7
  28.4 1.8 %collective-permute-start.8 = (bf16[64,384]{1,0:T(8,128)(2,1)S(1)}, bf16[64,384]{1,0:T(8,128)(2,1)S(1)}, u32[]{:S(2)}, u32[]{:S(2)}) collective-permute-start(bf16[64,384]{1,0:T(8,128)(2,1)S(1)} %get-tuple-element.22), channel_id=1, source_target_pairs={{0,4},{4,0},{8,12},{12,8},{1,5},{5,1},{9,13},{13,9},{2,6},{6,2},{1... | collective-permute-start | bytes 147464 | tf_op jit(solution)/shard_map/ppermute | solution.py:195
  30.2 1.5 %collective-permute-done.6.refs_1_ = bf16[64,384]{1,0:T(8,128)(2,1)S(1)} collective-permute-done((bf16[64,384]{1,0:T(8,128)(2,1)S(1)}, bf16[64,384]{1,0:T(8,128)(2,1)S(1)}, u32[]{:S(2)}, u32[]{:S(2)}) %collective-permute-start.6) | collective-permute-done | bytes 49184 | tf_op jit(solution)/shard_map/ppermute | solution.py:195
  31.7 1.7 %collective-permute-done.7.refs_2_ = bf16[64,384]{1,0:T(8,128)(2,1)S(1)} collective-permute-done((bf16[64,384]{1,0:T(8,128)(2,1)S(1)}, bf16[64,384]{1,0:T(8,128)(2,1)S(1)}, u32[]{:S(2)}, u32[]{:S(2)}) %collective-permute-start.7) | collective-permute-done | bytes 49184 | tf_op jit(solution)/shard_map/ppermute | solution.py:195
  33.4 0.0 collective-permute-done.8.refs_3_
  33.4 0.7 %unpack.1 = bf16[1,64,1536]{2,1,0:T(8,128)(2,1)} custom-call(bf16[64,384]{1,0:T(8,128)(2,1)S(1)} %get-tuple-element.19.refs_0_, bf16[64,384]{1,0:T(8,128)(2,1)S(1)} %collective-permute-done.6.refs_1_, bf16[64,384]{1,0:T(8,128)(2,1)S(1)} %collective-permute-done.7.refs_2_, bf16[64,384]{1,0:T(8,128)(2,1)S(1)} %collective-permute-done.8.refs_3_), custom_call_target="tpu_custom_call" | custom-call | bytes 393216 | tf_op jit(solution)/shard_map/unpack/pallas_call | solution.py:235
  (4 shorter events, 0.0 us)
Async XLA Ops:
  1.2 7.2 %collective-permute-start = (bf16[3,64,384]{2,1,0:T(8,128)(2,1)S(1)}, bf16[3,64,384]{2,1,0:T(8,128)(2,1)S(1)}, u32[]{:S(2)}, u32[]{:S(2)}) collective-permute-start(bf16[3,64,384]{2,1,0:T(8,128)(2,1)S(1)} %get-tuple-element.16), channel_id=1, source_target_pairs={{0,4},{4,0},{8,12},{12,8},{1,5},{5,1},{9,13},{13,9},{2,6},{6,2},{1... | collective-permute-start | bytes 442376 | tf_op jit(solution)/shard_map/ppermute | solution.py:195
  4.3 10.4 %collective-permute-start.2 = (bf16[3,64,384]{2,1,0:T(8,128)(2,1)S(1)}, bf16[3,64,384]{2,1,0:T(8,128)(2,1)S(1)}, u32[]{:S(2)}, u32[]{:S(2)}) collective-permute-start(bf16[3,64,384]{2,1,0:T(8,128)(2,1)S(1)} %get-tuple-element.18), channel_id=1, source_target_pairs={{0,12},{4,8},{8,4},{12,0},{1,13},{5,9},{9,5},{13,1},{2,14},{6,10},... | collective-permute-start | bytes 442376 | tf_op jit(solution)/shard_map/ppermute | solution.py:195
  8.3 11.6 %collective-permute-start.1 = (bf16[3,64,384]{2,1,0:T(8,128)(2,1)S(1)}, bf16[3,64,384]{2,1,0:T(8,128)(2,1)S(1)}, u32[]{:S(2)}, u32[]{:S(2)}) collective-permute-start(bf16[3,64,384]{2,1,0:T(8,128)(2,1)S(1)} %hold.1), channel_id=1, source_target_pairs={{0,8},{4,12},{8,0},{12,4},{1,9},{5,13},{9,1},{13,5},{2,10},{6,14},... | collective-permute-start | bytes 442376 | tf_op jit(solution)/shard_map/ppermute | solution.py:195
  12.0 9.4 %collective-permute-start.3 = (bf16[4,64,384]{2,1,0:T(8,128)(2,1)S(1)}, bf16[4,64,384]{2,1,0:T(8,128)(2,1)S(1)}, u32[]{:S(2)}, u32[]{:S(2)}) collective-permute-start(bf16[4,64,384]{2,1,0:T(8,128)(2,1)S(1)} %join.3), channel_id=1, source_target_pairs={{0,2},{2,0},{1,3},{3,1},{4,6},{6,4},{5,7},{7,5},{8,10},{10,8},{9,1... | collective-permute-start | bytes 589832 | tf_op jit(solution)/shard_map/ppermute | solution.py:198
  14.7 6.7 %collective-permute-start.4 = (bf16[2,64,384]{2,1,0:T(8,128)(2,1)S(1)}, bf16[2,64,384]{2,1,0:T(8,128)(2,1)S(1)}, u32[]{:S(2)}, u32[]{:S(2)}) collective-permute-start(bf16[2,64,384]{2,1,0:T(8,128)(2,1)S(1)} %join.4), channel_id=1, source_target_pairs={{0,2},{2,0},{1,3},{3,1},{4,6},{6,4},{5,7},{7,5},{8,10},{10,8},{9,1... | collective-permute-start | bytes 294920 | tf_op jit(solution)/shard_map/ppermute | solution.py:198
  19.9 4.7 %collective-permute-start.5 = (bf16[2,64,384]{2,1,0:T(8,128)(2,1)S(1)}, bf16[2,64,384]{2,1,0:T(8,128)(2,1)S(1)}, u32[]{:S(2)}, u32[]{:S(2)}) collective-permute-start(bf16[2,64,384]{2,1,0:T(8,128)(2,1)S(1)} %join.5), channel_id=1, source_target_pairs={{0,2},{2,0},{1,3},{3,1},{4,6},{6,4},{5,7},{7,5},{8,10},{10,8},{9,1... | collective-permute-start | bytes 294920 | tf_op jit(solution)/shard_map/ppermute | solution.py:198
  25.7 6.0 %collective-permute-start.6 = (bf16[64,384]{1,0:T(8,128)(2,1)S(1)}, bf16[64,384]{1,0:T(8,128)(2,1)S(1)}, u32[]{:S(2)}, u32[]{:S(2)}) collective-permute-start(bf16[64,384]{1,0:T(8,128)(2,1)S(1)} %get-tuple-element.20), channel_id=1, source_target_pairs={{0,12},{4,8},{8,4},{12,0},{1,13},{5,9},{9,5},{13,1},{2,14},{6,10},... | collective-permute-start | bytes 147464 | tf_op jit(solution)/shard_map/ppermute | solution.py:195
  28.4 5.0 %collective-permute-start.7 = (bf16[64,384]{1,0:T(8,128)(2,1)S(1)}, bf16[64,384]{1,0:T(8,128)(2,1)S(1)}, u32[]{:S(2)}, u32[]{:S(2)}) collective-permute-start(bf16[64,384]{1,0:T(8,128)(2,1)S(1)} %get-tuple-element.21), channel_id=1, source_target_pairs={{0,8},{4,12},{8,0},{12,4},{1,9},{5,13},{9,1},{13,5},{2,10},{6,14},... | collective-permute-start | bytes 147464 | tf_op jit(solution)/shard_map/ppermute | solution.py:195
  28.4 5.0 %collective-permute-start.8 = (bf16[64,384]{1,0:T(8,128)(2,1)S(1)}, bf16[64,384]{1,0:T(8,128)(2,1)S(1)}, u32[]{:S(2)}, u32[]{:S(2)}) collective-permute-start(bf16[64,384]{1,0:T(8,128)(2,1)S(1)} %get-tuple-element.22), channel_id=1, source_target_pairs={{0,4},{4,0},{8,12},{12,8},{1,5},{5,1},{9,13},{13,9},{2,6},{6,2},{1... | collective-permute-start | bytes 147464 | tf_op jit(solution)/shard_map/ppermute | solution.py:195

commit v5 on v4

--- a/solution.py
+++ b/solution.py
@@ -9,6 +9,7 @@
 from jax.sharding import PartitionSpec as P
 
 HD = 128
+EFFORT = 15 * 10**8
 ANY = pl.BlockSpec(memory_space=pl.ANY)
 HBM = pl.BlockSpec(memory_space=pltpu.HBM)
 VMEM = pl.BlockSpec(memory_space=pltpu.VMEM)
@@ -92,30 +93,34 @@
     sources = {"q": q_ref, "k": k_ref, "v": v_ref}
     me = lax.axis_index("blk")
     pairs = []
-    for (s, names), out in zip(messages, outs):
-        columns = pl.ds(pl.multiple_of((me ^ s) * part, 128), part)
-        for at, name in enumerate(names):
-            pairs.append((sources[name].at[0, :, columns], out.at[at]))
+    for (s, pieces), out in zip(messages, outs):
+        start = 0
+        for name, first, lanes in pieces:
+            columns = pl.ds(pl.multiple_of((me ^ s) * part + first, 128), lanes)
+            pairs.append((sources[name].at[0, :, columns], out.at[:, pl.ds(start, lanes)]))
+            start += lanes
     run_copies(pairs, sems)
 
 
-def join_kernel(places, *refs):
-    for at, (source, place) in enumerate(places):
-        refs[-1][at] = refs[source][place]
-
-
-def join(arrays, places):
-    shape = (len(places),) + arrays[0].shape[1:]
-    size = math.prod(shape) * 2
+def join_kernel(pieces, *refs):
+    lanes = refs[-1].shape[2]
+    for at, (source, start) in enumerate(pieces):
+        refs[-1][at] = refs[source][:, start : start + lanes]
+
+
+def join(arrays, starts, lanes, effort=0, after=()):
+    shape = (len(arrays), arrays[0].shape[0], lanes)
     return pl.pallas_call(
-        functools.partial(join_kernel, places),
+        functools.partial(join_kernel, list(enumerate(starts))),
         out_shape=jax.ShapeDtypeStruct(shape, arrays[0].dtype),
-        in_specs=[VMEM] * len(arrays),
+        in_specs=[VMEM] * (len(arrays) + len(after)),
         out_specs=VMEM,
         compiler_params=SMALL,
-        cost_estimate=pl.CostEstimate(flops=0, bytes_accessed=2 * size, transcendentals=0),
+        cost_estimate=pl.CostEstimate(
+            flops=effort, bytes_accessed=4 * math.prod(shape), transcendentals=0
+        ),
         name="join",
-    )(*arrays)
+    )(*arrays, *after)
 
 
 def hold_kernel(array_ref, until_ref, out_ref):
@@ -134,16 +139,20 @@
     )(array, until)
 
 
-def attend_kernel(query_places, key_places, value_places, *refs):
-    blocks = len(query_places)
+def attend_kernel(plan, *refs):
+    blocks = len(plan[0][0])
     ins, out_refs = refs[:-blocks], refs[-blocks:]
-    tokens, part = out_refs[0].shape
+    tokens = out_refs[0].shape[0]
     scale = 1.0 / math.sqrt(HD)
-    for head in range(part // HD):
-        lanes = slice(head * HD, (head + 1) * HD)
+
+    def load(place):
+        source, row, first = place
+        lanes = slice(first, first + HD)
+        return ins[source][:, lanes] if row is None else ins[source][row, :, lanes]
+
+    for head, all_places in enumerate(plan):
         queries, keys, values = (
-            jnp.concatenate([ins[source][at, :, lanes] for source, at in places], axis=0)
-            for places in (query_places, key_places, value_places)
+            jnp.concatenate([load(place) for place in places], axis=0) for places in all_places
         )
         scores = (
             lax.dot_general(
@@ -157,8 +166,8 @@
             weights.astype(jnp.bfloat16), values, preferred_element_type=jnp.float32
         )
         result = (mixed / totals).astype(jnp.bfloat16)
-        for at, ref in enumerate(out_refs):
-            ref[:, lanes] = result[at * tokens : (at + 1) * tokens]
+        for block, ref in enumerate(out_refs):
+            ref[:, head * HD : (head + 1) * HD] = result[block * tokens : (block + 1) * tokens]
 
 
 def unpack_kernel(order, part, *refs):
@@ -177,13 +186,19 @@
     part = width // blocks
     heads = part // HD
     kind = query_rows.dtype
-    messages = [(s, "kvq") for s in range(blocks - 1, 0, -1)] + [(0, "kv"), (0, "q")]
+    far = list(range(blocks - 1, 1, -1))
+
+    kv, q = (("k", 0, part), ("v", 0, part)), (("q", 0, part),)
+    messages = [(s, kv) for s in far] + [(1, kv + q)] + [(s, q) for s in far] + [(0, kv), (0, q)]
     packed = pl.pallas_call(
         functools.partial(pack_kernel, messages, part),
-        out_shape=[jax.ShapeDtypeStruct((len(m), tokens, part), kind) for s, m in messages],
+        out_shape=[
+            jax.ShapeDtypeStruct((tokens, sum(piece[2] for piece in pieces)), kind)
+            for s, pieces in messages
+        ],
         in_specs=[HBM] * 3,
         out_specs=[VMEM] * len(messages),
-        scratch_shapes=[pltpu.SemaphoreType.DMA((3 * blocks,))],
+        scratch_shapes=[pltpu.SemaphoreType.DMA((sum(len(m[1]) for m in messages),))],
         compiler_params=SMALL,
         cost_estimate=pl.CostEstimate(
             flops=0, bytes_accessed=6 * tokens * width * 2, transcendentals=0
@@ -197,40 +212,49 @@
     def to_column(array, t):
         return lax.ppermute(array, "uly", [(i, (i + t) % columns_of) for i in range(columns_of)])
 
-    sent = {message[0]: array for message, array in zip(messages, packed)}
+    sent = {message: array for message, array in zip(messages, packed)}
     own_kv, own_q = packed[-2:]
-    got = {s: to_block(sent[s], s) for s in (1, 3)}
-    got[2] = to_block(hold(sent[2], got[1]), 2)
-    held = [own_kv, own_q] + [got[s] for s in range(1, blocks)]
-    query_places = [(1, 0)] + [(1 + s, 2) for s in range(1, blocks)]
-    key_places = [(0, 0)] + [(1 + s, 0) for s in range(1, blocks)]
-    value_places = [(0, 1)] + [(1 + s, 1) for s in range(1, blocks)]
-    groups = [join([own_kv, got[1]], [(0, 0), (0, 1), (1, 0), (1, 1)])]
-    groups += [join([got[s]], [(0, 0), (0, 1)]) for s in range(blocks - 1, 1, -1)]
-    for t in range(1, columns_of):
-        for group in groups:
-            for at in range(0, group.shape[0], 2):
-                key_places.append((len(held), at))
-                value_places.append((len(held), at + 1))
-            held.append(to_column(group, t))
-
+    far_kv = [to_block(sent[s, kv], s) for s in far]
+    near_kvq = to_block(sent[1, kv + q], 1)
+    near_kv = join([own_kv, near_kvq], [0, 0], 2 * part)
+    far_q = [to_block(hold(sent[s, q], near_kv), s) for s in far]
+    groups = [near_kv, join(far_kv, [0] * len(far), 2 * part)]
+    crossed = [to_column(group, t) for group in groups for t in range(1, columns_of)]
+    far_q = join(far_q, [0] * len(far), part, EFFORT)
+    near_q = join([own_q, near_kvq], [0, 2 * part], part, EFFORT, crossed[: columns_of - 1])
+    arrays = [near_q, far_q, near_kvq, own_kv] + far_kv
+    key_places = [(at, None, 0) for at in range(2, len(arrays))]
+    for array in crossed:
+        key_places += [(len(arrays), at, 0) for at in range(array.shape[0])]
+        arrays.append(array)
+    query_places = [(0, 0, 0), (0, 1, 0)]
+    query_places += [(1, far.index(s), 0) for s in range(2, blocks)]
+
+    def moved(places, lanes):
+        return [(source, row, first + lanes) for source, row, first in places]
+
+    plan = [
+        (moved(query_places, lane), moved(key_places, lane), moved(key_places, part + lane))
+        for lane in range(0, part, HD)
+    ]
     all_tokens = tokens * blocks * columns_of
+
     pairs = heads * tokens * blocks * all_tokens
     mixed = pl.pallas_call(
-        functools.partial(attend_kernel, query_places, key_places, value_places),
+        functools.partial(attend_kernel, plan),
         out_shape=[jax.ShapeDtypeStruct((tokens, part), kind)] * blocks,
-        in_specs=[VMEM] * len(held),
+        in_specs=[VMEM] * len(arrays),
         out_specs=[VMEM] * blocks,
         compiler_params=pltpu.CompilerParams(vmem_limit_bytes=24 * 1024 * 1024),
         cost_estimate=pl.CostEstimate(
             flops=4 * HD * pairs,
-            bytes_accessed=2 * part * (2 * all_tokens + 2 * tokens * blocks),
+            bytes_accessed=4 * part * (all_tokens + tokens * blocks),
             transcendentals=pairs,
         ),
         name="attend",
-    )(*held)
-
-    order = [0] + list(range(blocks - 1, 0, -1))
+    )(*arrays)
+
+    order = [0] + far + [1]
     back = [to_block(mixed[s], s) if s else mixed[0] for s in order]
     return pl.pallas_call(
         functools.partial(unpack_kernel, order, part),

time: 34.3 us -> 33.7 us (0.983)
  waiting for transfers between devices: 12.7 us -> 11.5 us
  starting transfers between devices: 18.4 us -> 19 us
    ppermute x6 -> x8, starting transfers between devices: 13.7 us -> 15.9 us  [to_block(): return lax.ppermute(array, 'blk', [(i, i ^ s) for i in range(blocks)])]
    ppermute x6 -> x8, waiting for transfers between devices: 9.56 us -> 7.78 us  [to_block(): return lax.ppermute(array, 'blk', [(i, i ^ s) for i in range(blocks)])]
    ppermute x3 -> x2, starting transfers between devices: 4.67 us -> 3.11 us  [to_column(): lax.ppermute(array, 'uly', [(i, (i + t) % columns_of) for i in range(colu...]
    ppermute x3 -> x2, waiting for transfers between devices: 3.12 us -> 3.76 us  [to_column(): lax.ppermute(array, 'uly', [(i, (i + t) % columns_of) for i in range(colu...]
    pallas_call x4 -> x5, Pallas kernels: 1.13 us -> 1.13 us  [the longest x1 1.08 us: local_blocks(): pl.pallas_call(functools.partial(attend_kernel, plan), out_shape=[jax.Sha...]
  transfers between devices with their start and end apart: 9 -> 10, of which waited for: 6 -> 6; matrix products, arithmetic and copies ran while one was open for 0% -> 0% of each run, Pallas kernels for 0% -> 0%
where the time goes in v5:
time: 33.7 us; the launch traced here: 33.6 us
  starting transfers between devices  19 us (56%)
  waiting for transfers between devices  11.5 us (34%)
  Pallas kernels  3 us (9%)
    ppermute x8, starting transfers between devices, to_block(): return lax.ppermute(array, 'blk', [(i, i ^ s) for i in range(blocks)])  15.9 us
    ppermute x8, waiting for transfers between devices, to_block(): return lax.ppermute(array, 'blk', [(i, i ^ s) for i in range(blocks)])  7.78 us
    ppermute x2, waiting for transfers between devices, to_column(): lax.ppermute(array, 'uly', [(i, (i + t) % columns_of) for i in range(colu...  3.76 us
    ppermute x2, starting transfers between devices, to_column(): lax.ppermute(array, 'uly', [(i, (i + t) % columns_of) for i in range(colu...  3.11 us
    pallas_call x1, Pallas kernels, local_blocks(): pl.pallas_call(functools.partial(pack_kernel, messages, part), out_shape=...  1.17 us
    pallas_call x1, Pallas kernels, local_blocks(): pl.pallas_call(functools.partial(attend_kernel, plan), out_shape=[jax.Sha...  1.08 us
    pallas_call x1, Pallas kernels, local_blocks(): pl.pallas_call(functools.partial(unpack_kernel, order, part), out_shape=j...  0.7 us
  transfers between devices with their start and end apart: 10, of which 6 were waited for; matrix products, arithmetic and copies ran while one was open for 0% of the time, Pallas kernels for 0%

profile of v5, /device:TPU:0, one launch (start us, length us, event | category | flops | bytes accessed | tf_op | source)
XLA Modules:
  0.0 33.6 jit_solution(1291114909797450137)
XLA Ops:
  0.0 1.2 %pack.1 = (bf16[64,768]{1,0:T(8,128)(2,1)S(1)}, bf16[64,768]{1,0:T(8,128)(2,1)S(1)}, bf16[64,1152]{1,0:T(8,128)(2,1)S(1)}, bf16[64,384]{1,0:T(8,128)(2,1)S(1)}, ...) custom-call(bf16[1,64,1536]{2,1,0:T(8,128)(2,1)} %q_ref.1, ...), custom_call_target="tpu_custom_call" | custom-call | bytes 1179648 | tf_op jit(solution)/shard_map/pack/pallas_call | solution.py:193
  1.2 3.1 %collective-permute-start = (bf16[64,1152]{1,0:T(8,128)(2,1)S(1)}, bf16[64,1152]{1,0:T(8,128)(2,1)S(1)}, u32[]{:S(2)}, u32[]{:S(2)}) collective-permute-start(bf16[64,1152]{1,0:T(8,128)(2,1)S(1)} %get-tuple-element.17), channel_id=1, source_target_pairs={{0,4},{4,0},{8,12},{12,8},{1,5},{5,1},{9,13},{13,9},{2,6},{6,2},{1... | collective-permute-start | bytes 442376 | tf_op jit(solution)/shard_map/ppermute | solution.py:210
  4.3 2.5 %collective-permute-start.4 = (bf16[64,768]{1,0:T(8,128)(2,1)S(1)}, bf16[64,768]{1,0:T(8,128)(2,1)S(1)}, u32[]{:S(2)}, u32[]{:S(2)}) collective-permute-start(bf16[64,768]{1,0:T(8,128)(2,1)S(1)} %get-tuple-element.21), channel_id=1, source_target_pairs={{0,12},{4,8},{8,4},{12,0},{1,13},{5,9},{9,5},{13,1},{2,14},{6,10},... | collective-permute-start | bytes 294920 | tf_op jit(solution)/shard_map/ppermute | solution.py:210
  6.7 0.1 collective-permute-start.5
  6.9 1.5 %collective-permute-done.refs_1_.refs_2_ = bf16[64,1152]{1,0:T(8,128)(2,1)S(1)} collective-permute-done((bf16[64,1152]{1,0:T(8,128)(2,1)S(1)}, bf16[64,1152]{1,0:T(8,128)(2,1)S(1)}, u32[]{:S(2)}, u32[]{:S(2)}) %collective-permute-start) | collective-permute-done | bytes 147488 | tf_op jit(solution)/shard_map/ppermute | solution.py:210
  8.3 1.6 %collective-permute-start.1 = (bf16[2,64,768]{2,1,0:T(8,128)(2,1)S(1)}, bf16[2,64,768]{2,1,0:T(8,128)(2,1)S(1)}, u32[]{:S(2)}, u32[]{:S(2)}) collective-permute-start(bf16[2,64,768]{2,1,0:T(8,128)(2,1)S(1)} %join.4.until_ref), channel_id=1, source_target_pairs={{0,2},{2,0},{1,3},{3,1},{4,6},{6,4},{5,7},{7,5},{8,10},{10,8},{9,1... | collective-permute-start | bytes 589832 | tf_op jit(solution)/shard_map/ppermute | solution.py:213
  9.9 5.7 %collective-permute-start.2 = (bf16[64,384]{1,0:T(8,128)(2,1)S(1)}, bf16[64,384]{1,0:T(8,128)(2,1)S(1)}, u32[]{:S(2)}, u32[]{:S(2)}) collective-permute-start(bf16[64,384]{1,0:T(8,128)(2,1)S(1)} %hold.2), channel_id=1, source_target_pairs={{0,12},{4,8},{8,4},{12,0},{1,13},{5,9},{9,5},{13,1},{2,14},{6,10},... | collective-permute-start | bytes 147464 | tf_op jit(solution)/shard_map/ppermute | solution.py:210
  15.6 0.0 collective-permute-start.3
  15.6 0.0 collective-permute-done.4.refs_0_.refs_4_
  15.6 3.0 %collective-permute-done.5.refs_1_.refs_5_ = bf16[64,768]{1,0:T(8,128)(2,1)S(1)} collective-permute-done((bf16[64,768]{1,0:T(8,128)(2,1)S(1)}, bf16[64,768]{1,0:T(8,128)(2,1)S(1)}, u32[]{:S(2)}, u32[]{:S(2)}) %collective-permute-start.5) | collective-permute-done | bytes 98336 | tf_op jit(solution)/shard_map/ppermute | solution.py:210
  18.7 1.6 %collective-permute-start.6 = (bf16[2,64,768]{2,1,0:T(8,128)(2,1)S(1)}, bf16[2,64,768]{2,1,0:T(8,128)(2,1)S(1)}, u32[]{:S(2)}, u32[]{:S(2)}) collective-permute-start(bf16[2,64,768]{2,1,0:T(8,128)(2,1)S(1)} %join.7), channel_id=1, source_target_pairs={{0,2},{2,0},{1,3},{3,1},{4,6},{6,4},{5,7},{7,5},{8,10},{10,8},{9,1... | collective-permute-start | bytes 589832 | tf_op jit(solution)/shard_map/ppermute | solution.py:213
  20.2 0.0 collective-permute-done.2.refs_0_
  20.2 0.4 %collective-permute-done.3.refs_1_ = bf16[64,384]{1,0:T(8,128)(2,1)S(1)} collective-permute-done((bf16[64,384]{1,0:T(8,128)(2,1)S(1)}, bf16[64,384]{1,0:T(8,128)(2,1)S(1)}, u32[]{:S(2)}, u32[]{:S(2)}) %collective-permute-start.3) | collective-permute-done | bytes 49184 | tf_op jit(solution)/shard_map/ppermute | solution.py:210
  20.6 0.0 collective-permute-done.1.refs_2_.refs_6_
  20.7 3.8 %collective-permute-done.6.refs_7_ = bf16[2,64,768]{2,1,0:T(8,128)(2,1)S(1)} collective-permute-done((bf16[2,64,768]{2,1,0:T(8,128)(2,1)S(1)}, bf16[2,64,768]{2,1,0:T(8,128)(2,1)S(1)}, u32[]{:S(2)}, u32[]{:S(2)}) %collective-permute-start.6) | collective-permute-done | bytes 196640 | tf_op jit(solution)/shard_map/ppermute | solution.py:213
  24.4 1.1 %attend.1 = (bf16[64,384]{1,0:T(8,128)(2,1)S(1)}, bf16[64,384]{1,0:T(8,128)(2,1)S(1)}, bf16[64,384]{1,0:T(8,128)(2,1)S(1)}, bf16[64,384]{1,0:T(8,128)(2,1)S(1)}) custom-call(bf16[2,64,384]{2,1,0:T(8,128)(2,1)S(1)} %join.5.refs_0_, bf16[2,64,384]{2,1,0:T(8,128)(2,1)S(1)} %join.6.refs_1_, bf16[64,1152]{1,0:T(8,128)(2,1)S(1)} %collective-permute-done.refs_1_.refs_2_, ...), custom_call_target="tpu_custom_call" | custom-call | flops 201326592 | bytes 1179648 | tf_op jit(solution)/shard_map/attend/pallas_call | solution.py:243
  25.5 2.4 %collective-permute-start.7 = (bf16[64,384]{1,0:T(8,128)(2,1)S(1)}, bf16[64,384]{1,0:T(8,128)(2,1)S(1)}, u32[]{:S(2)}, u32[]{:S(2)}) collective-permute-start(bf16[64,384]{1,0:T(8,128)(2,1)S(1)} %get-tuple-element.24), channel_id=1, source_target_pairs={{0,12},{4,8},{8,4},{12,0},{1,13},{5,9},{9,5},{13,1},{2,14},{6,10},... | collective-permute-start | bytes 147464 | tf_op jit(solution)/shard_map/ppermute | solution.py:210
  27.9 0.0 collective-permute-start.8
  27.9 2.1 %collective-permute-start.9 = (bf16[64,384]{1,0:T(8,128)(2,1)S(1)}, bf16[64,384]{1,0:T(8,128)(2,1)S(1)}, u32[]{:S(2)}, u32[]{:S(2)}) collective-permute-start(bf16[64,384]{1,0:T(8,128)(2,1)S(1)} %get-tuple-element.26), channel_id=1, source_target_pairs={{0,4},{4,0},{8,12},{12,8},{1,5},{5,1},{9,13},{13,9},{2,6},{6,2},{1... | collective-permute-start | bytes 147464 | tf_op jit(solution)/shard_map/ppermute | solution.py:210
  30.0 1.5 %collective-permute-done.7.refs_1_ = bf16[64,384]{1,0:T(8,128)(2,1)S(1)} collective-permute-done((bf16[64,384]{1,0:T(8,128)(2,1)S(1)}, bf16[64,384]{1,0:T(8,128)(2,1)S(1)}, u32[]{:S(2)}, u32[]{:S(2)}) %collective-permute-start.7) | collective-permute-done | bytes 49184 | tf_op jit(solution)/shard_map/ppermute | solution.py:210
  31.5 1.4 %collective-permute-done.8.refs_2_ = bf16[64,384]{1,0:T(8,128)(2,1)S(1)} collective-permute-done((bf16[64,384]{1,0:T(8,128)(2,1)S(1)}, bf16[64,384]{1,0:T(8,128)(2,1)S(1)}, u32[]{:S(2)}, u32[]{:S(2)}) %collective-permute-start.8) | collective-permute-done | bytes 49184 | tf_op jit(solution)/shard_map/ppermute | solution.py:210
  32.9 0.0 collective-permute-done.9.refs_3_
  32.9 0.7 %unpack.1 = bf16[1,64,1536]{2,1,0:T(8,128)(2,1)} custom-call(bf16[64,384]{1,0:T(8,128)(2,1)S(1)} %get-tuple-element.23.refs_0_, bf16[64,384]{1,0:T(8,128)(2,1)S(1)} %collective-permute-done.7.refs_1_, bf16[64,384]{1,0:T(8,128)(2,1)S(1)} %collective-permute-done.8.refs_2_, bf16[64,384]{1,0:T(8,128)(2,1)S(1)} %collective-permute-done.9.refs_3_), custom_call_target="tpu_custom_call" | custom-call | bytes 393216 | tf_op jit(solution)/shard_map/unpack/pallas_call | solution.py:259
  (6 shorter events, 0.0 us)
Async XLA Ops:
  1.2 7.2 %collective-permute-start = (bf16[64,1152]{1,0:T(8,128)(2,1)S(1)}, bf16[64,1152]{1,0:T(8,128)(2,1)S(1)}, u32[]{:S(2)}, u32[]{:S(2)}) collective-permute-start(bf16[64,1152]{1,0:T(8,128)(2,1)S(1)} %get-tuple-element.17), channel_id=1, source_target_pairs={{0,4},{4,0},{8,12},{12,8},{1,5},{5,1},{9,13},{13,9},{2,6},{6,2},{1... | collective-permute-start | bytes 442376 | tf_op jit(solution)/shard_map/ppermute | solution.py:210
  4.3 11.4 %collective-permute-start.4 = (bf16[64,768]{1,0:T(8,128)(2,1)S(1)}, bf16[64,768]{1,0:T(8,128)(2,1)S(1)}, u32[]{:S(2)}, u32[]{:S(2)}) collective-permute-start(bf16[64,768]{1,0:T(8,128)(2,1)S(1)} %get-tuple-element.21), channel_id=1, source_target_pairs={{0,12},{4,8},{8,4},{12,0},{1,13},{5,9},{9,5},{13,1},{2,14},{6,10},... | collective-permute-start | bytes 294920 | tf_op jit(solution)/shard_map/ppermute | solution.py:210
  6.7 11.9 %collective-permute-start.5 = (bf16[64,768]{1,0:T(8,128)(2,1)S(1)}, bf16[64,768]{1,0:T(8,128)(2,1)S(1)}, u32[]{:S(2)}, u32[]{:S(2)}) collective-permute-start(bf16[64,768]{1,0:T(8,128)(2,1)S(1)} %get-tuple-element.22), channel_id=1, source_target_pairs={{0,8},{4,12},{8,0},{12,4},{1,9},{5,13},{9,1},{13,5},{2,10},{6,14},... | collective-permute-start | bytes 294920 | tf_op jit(solution)/shard_map/ppermute | solution.py:210
  8.3 12.3 %collective-permute-start.1 = (bf16[2,64,768]{2,1,0:T(8,128)(2,1)S(1)}, bf16[2,64,768]{2,1,0:T(8,128)(2,1)S(1)}, u32[]{:S(2)}, u32[]{:S(2)}) collective-permute-start(bf16[2,64,768]{2,1,0:T(8,128)(2,1)S(1)} %join.4.until_ref), channel_id=1, source_target_pairs={{0,2},{2,0},{1,3},{3,1},{4,6},{6,4},{5,7},{7,5},{8,10},{10,8},{9,1... | collective-permute-start | bytes 589832 | tf_op jit(solution)/shard_map/ppermute | solution.py:213
  9.9 10.3 %collective-permute-start.2 = (bf16[64,384]{1,0:T(8,128)(2,1)S(1)}, bf16[64,384]{1,0:T(8,128)(2,1)S(1)}, u32[]{:S(2)}, u32[]{:S(2)}) collective-permute-start(bf16[64,384]{1,0:T(8,128)(2,1)S(1)} %hold.2), channel_id=1, source_target_pairs={{0,12},{4,8},{8,4},{12,0},{1,13},{5,9},{9,5},{13,1},{2,14},{6,10},... | collective-permute-start | bytes 147464 | tf_op jit(solution)/shard_map/ppermute | solution.py:210
  15.6 5.0 %collective-permute-start.3 = (bf16[64,384]{1,0:T(8,128)(2,1)S(1)}, bf16[64,384]{1,0:T(8,128)(2,1)S(1)}, u32[]{:S(2)}, u32[]{:S(2)}) collective-permute-start(bf16[64,384]{1,0:T(8,128)(2,1)S(1)} %hold.3), channel_id=1, source_target_pairs={{0,8},{4,12},{8,0},{12,4},{1,9},{5,13},{9,1},{13,5},{2,10},{6,14},... | collective-permute-start | bytes 147464 | tf_op jit(solution)/shard_map/ppermute | solution.py:210
  18.7 5.7 %collective-permute-start.6 = (bf16[2,64,768]{2,1,0:T(8,128)(2,1)S(1)}, bf16[2,64,768]{2,1,0:T(8,128)(2,1)S(1)}, u32[]{:S(2)}, u32[]{:S(2)}) collective-permute-start(bf16[2,64,768]{2,1,0:T(8,128)(2,1)S(1)} %join.7), channel_id=1, source_target_pairs={{0,2},{2,0},{1,3},{3,1},{4,6},{6,4},{5,7},{7,5},{8,10},{10,8},{9,1... | collective-permute-start | bytes 589832 | tf_op jit(solution)/shard_map/ppermute | solution.py:213
  25.5 6.0 %collective-permute-start.7 = (bf16[64,384]{1,0:T(8,128)(2,1)S(1)}, bf16[64,384]{1,0:T(8,128)(2,1)S(1)}, u32[]{:S(2)}, u32[]{:S(2)}) collective-permute-start(bf16[64,384]{1,0:T(8,128)(2,1)S(1)} %get-tuple-element.24), channel_id=1, source_target_pairs={{0,12},{4,8},{8,4},{12,0},{1,13},{5,9},{9,5},{13,1},{2,14},{6,10},... | collective-permute-start | bytes 147464 | tf_op jit(solution)/shard_map/ppermute | solution.py:210
  27.9 5.0 %collective-permute-start.8 = (bf16[64,384]{1,0:T(8,128)(2,1)S(1)}, bf16[64,384]{1,0:T(8,128)(2,1)S(1)}, u32[]{:S(2)}, u32[]{:S(2)}) collective-permute-start(bf16[64,384]{1,0:T(8,128)(2,1)S(1)} %get-tuple-element.25), channel_id=1, source_target_pairs={{0,8},{4,12},{8,0},{12,4},{1,9},{5,13},{9,1},{13,5},{2,10},{6,14},... | collective-permute-start | bytes 147464 | tf_op jit(solution)/shard_map/ppermute | solution.py:210
  27.9 5.0 %collective-permute-start.9 = (bf16[64,384]{1,0:T(8,128)(2,1)S(1)}, bf16[64,384]{1,0:T(8,128)(2,1)S(1)}, u32[]{:S(2)}, u32[]{:S(2)}) collective-permute-start(bf16[64,384]{1,0:T(8,128)(2,1)S(1)} %get-tuple-element.26), channel_id=1, source_target_pairs={{0,4},{4,0},{8,12},{12,8},{1,5},{5,1},{9,13},{13,9},{2,6},{6,2},{1... | collective-permute-start | bytes 147464 | tf_op jit(solution)/shard_map/ppermute | solution.py:210

commit v6 on v0

--- a/solution.py
+++ b/solution.py
@@ -1,11 +1,17 @@
+import functools
 import math
 
 import jax
 import jax.numpy as jnp
 from jax import lax
+from jax.experimental import pallas as pl
+from jax.experimental.pallas import tpu as pltpu
 from jax.sharding import PartitionSpec as P
 
 HD = 128
+HBM = pl.BlockSpec(memory_space=pltpu.HBM)
+VMEM = pl.BlockSpec(memory_space=pltpu.VMEM)
+SMALL = pltpu.CompilerParams(vmem_limit_bytes=4 * 1024 * 1024)
 
 
 def attend(queries, key_part, value_part):
@@ -57,31 +63,152 @@
     return output.reshape(1, row_count, 1, head_count, head_size)
 
 
-def regroup_back(attended_part):
-    return lax.all_to_all(attended_part, "uly", split_axis=1, concat_axis=2, tiled=True)
-
-
-def whole_pass(triple):
-    return regroup_back(attend(triple[0], triple[1], triple[2]))
-
-
-def local(query_rows, key_rows, value_rows):
+def local_generic(query_rows, key_rows, value_rows):
     ulysses = lax.axis_size("uly")
     tokens = query_rows.shape[1]
     width = query_rows.shape[2]
     heads_local = width // HD // ulysses
 
     def split_heads(array):
-        return array.reshape(1, tokens, ulysses, heads_local, HD)
-
-    sectioned = (split_heads(query_rows), split_heads(key_rows), split_heads(value_rows))
-    moved = (
-        lax.all_to_all(sectioned[0], "uly", split_axis=2, concat_axis=1, tiled=True),
-        lax.all_to_all(sectioned[1], "uly", split_axis=2, concat_axis=1, tiled=True),
-        lax.all_to_all(sectioned[2], "uly", split_axis=2, concat_axis=1, tiled=True),
-    )
-    merged = whole_pass(moved)
+        array = array.reshape(1, tokens, ulysses, heads_local, HD)
+        return lax.all_to_all(array, "uly", split_axis=2, concat_axis=1, tiled=True)
+
+    mixed = attend(split_heads(query_rows), split_heads(key_rows), split_heads(value_rows))
+    merged = lax.all_to_all(mixed, "uly", split_axis=1, concat_axis=2, tiled=True)
     return merged.reshape(1, tokens, width)
+
+
+AXES = ("blk", "uly")
+
+
+def place_of(mask, members):
+    here = lax.axis_index("blk") * lax.axis_size("uly") + lax.axis_index("uly")
+    return lax.rem(here ^ mask, members)
+
+
+def run_copies(pairs, sems):
+    started = [pltpu.make_async_copy(src, dst, sems.at[at]) for at, (src, dst) in enumerate(pairs)]
+    for copy in started:
+        copy.start()
+    for copy in started:
+        copy.wait()
+
+
+def pack_kernel(messages, members, part, q_ref, k_ref, v_ref, *refs):
+    outs, sems = refs[:-1], refs[-1]
+    sources = {"q": q_ref, "k": k_ref, "v": v_ref}
+    pairs = []
+    for (mask, names), out in zip(messages, outs):
+        columns = pl.ds(pl.multiple_of(place_of(mask, members) * part, 128), part)
+        for at, name in enumerate(names):
+            pairs.append((sources[name].at[0, :, columns], out.at[:, pl.ds(at * part, part)]))
+    run_copies(pairs, sems)
+
+
+def attend_kernel(members, *refs):
+    ins, out_refs = refs[:-members], refs[-members:]
+    tokens, part = out_refs[0].shape
+    scale = 1.0 / math.sqrt(HD)
+
+    def rows(sources, first):
+        return jnp.concatenate([ref[:, first : first + HD] for ref in sources], axis=0)
+
+    for lane in range(0, part, HD):
+        queries = rows(ins[:members], 2 * part + lane)
+        keys = rows(ins, lane)
+        values = rows(ins, part + lane)
+        scores = (
+            lax.dot_general(
+                queries, keys, (((1,), (1,)), ((), ())), preferred_element_type=jnp.float32
+            )
+            * scale
+        )
+        weights = jnp.exp(scores - jnp.max(scores, axis=1, keepdims=True))
+        totals = jnp.sum(weights, axis=1, keepdims=True)
+        mixed = jnp.dot(
+            weights.astype(jnp.bfloat16), values, preferred_element_type=jnp.float32
+        )
+        result = (mixed / totals).astype(jnp.bfloat16)
+        for at, ref in enumerate(out_refs):
+            ref[:, lane : lane + HD] = result[at * tokens : (at + 1) * tokens]
+
+
+def unpack_kernel(members, part, *refs):
+    ins, out_ref, sems = refs[:-2], refs[-2], refs[-1]
+    pairs = []
+    for mask, ref in enumerate(ins):
+        columns = pl.ds(pl.multiple_of(place_of(mask, members) * part, 128), part)
+        pairs.append((ref, out_ref.at[0, :, columns]))
+    run_copies(pairs, sems)
+
+
+def local_halves(query_rows, key_rows, value_rows):
+    devices = lax.axis_size("blk") * lax.axis_size("uly")
+    members = devices // 2
+    tokens, width = query_rows.shape[1:]
+    part = width // members
+    heads = part // HD
+    kind = query_rows.dtype
+
+    messages = [(mask, "kv") for mask in range(members, devices)]
+    messages += [(mask, "kvq") for mask in range(members)]
+    packed = pl.pallas_call(
+        functools.partial(pack_kernel, messages, members, part),
+        out_shape=[jax.ShapeDtypeStruct((tokens, len(m[1]) * part), kind) for m in messages],
+        in_specs=[HBM] * 3,
+        out_specs=[VMEM] * len(messages),
+        scratch_shapes=[pltpu.SemaphoreType.DMA((sum(len(m[1]) for m in messages),))],
+        compiler_params=SMALL,
+        cost_estimate=pl.CostEstimate(
+            flops=0, bytes_accessed=6 * tokens * width * 2, transcendentals=0
+        ),
+        name="pack",
+    )(*[pltpu.with_memory_space_constraint(x, pltpu.HBM) for x in (query_rows, key_rows, value_rows)])
+
+    def swap(array, mask):
+        return lax.ppermute(array, AXES, [(i, i ^ mask) for i in range(devices)]) if mask else array
+
+    got = [swap(array, mask) for (mask, names), array in zip(messages, packed)]
+    arrays = got[members:] + got[:members]
+
+    pairs = heads * tokens * members * tokens * devices
+    mixed = pl.pallas_call(
+        functools.partial(attend_kernel, members),
+        out_shape=[jax.ShapeDtypeStruct((tokens, part), kind)] * members,
+        in_specs=[VMEM] * devices,
+        out_specs=[VMEM] * members,
+        compiler_params=pltpu.CompilerParams(vmem_limit_bytes=24 * 1024 * 1024),
+        cost_estimate=pl.CostEstimate(
+            flops=4 * HD * pairs,
+            bytes_accessed=4 * part * tokens * (devices + members),
+            transcendentals=pairs,
+        ),
+        name="attend",
+    )(*arrays)
+
+    back = [swap(array, mask) for mask, array in enumerate(mixed)]
+    return pl.pallas_call(
+        functools.partial(unpack_kernel, members, part),
+        out_shape=jax.ShapeDtypeStruct((1, tokens, width), kind),
+        in_specs=[VMEM] * members,
+        out_specs=HBM,
+        scratch_shapes=[pltpu.SemaphoreType.DMA((members,))],
+        compiler_params=SMALL,
+        cost_estimate=pl.CostEstimate(
+            flops=0, bytes_accessed=2 * tokens * width * 2, transcendentals=0
+        ),
+        name="unpack",
+    )(*back)
+
+
+def local(query_rows, key_rows, value_rows):
+    blocks, columns = lax.axis_size("blk"), lax.axis_size("uly")
+    heads = query_rows.shape[2] // HD
+    devices = blocks * columns
+    powers = devices & (devices - 1) == 0 and blocks > 1
+    few = powers and devices <= 8 and heads % (devices // 2) == 0
+    plan = local_halves if few else local_generic
+    return plan(query_rows, key_rows, value_rows)
 
 
 def solution(mesh):

time: 69.7 us -> 33.3 us (0.48)
  blocking collectives: 44.7 us -> 0 us
  starting transfers between devices: 11.1 us -> 18.9 us
  local copies, waits for them, and re-layouts: 5.94 us -> 0 us
  waiting for transfers between devices: 6.09 us -> 11.1 us
  Pallas kernels: 0 us -> 3.16 us
  matrix products: 0.99 us -> 0 us
    all_gather x2 -> x0, blocking collectives: 37.1 us -> none  [the longest x1 20 us: attend(): lax.all_gather(key_part, 'blk', axis=1, tiled=True)]
    ppermute x0 -> x10, starting transfers between devices: none -> 18.9 us  [swap(): lax.ppermute(array, AXES, [(i, i ^ mask) for i in range(devices)])]
    all_to_all x3 -> x0, starting transfers between devices: 11.1 us -> none  [the longest x1 4.21 us: local(): lax.all_to_all(sectioned[1], 'uly', split_axis=2, concat_axis=1, tiled=True)]
    ppermute x0 -> x10, waiting for transfers between devices: none -> 11.1 us  [swap(): lax.ppermute(array, AXES, [(i, i ^ mask) for i in range(devices)])]
    all_to_all x1 -> x0, blocking collectives: 7.56 us -> none  [regroup_back(): lax.all_to_all(attended_part, 'uly', split_axis=1, concat_axis=2, tiled=T...]
    all_to_all x3 -> x0, waiting for transfers between devices: 6.09 us -> none  [the longest x1 3.81 us: local(): lax.all_to_all(sectioned[2], 'uly', split_axis=2, concat_axis=1, tiled=True)]
    reshape x8 -> x0, local copies, waits for them, and re-layouts: 5.84 us -> none  [the longest x6 4.8 us: split_heads(): return array.reshape(1, tokens, ulysses, heads_local, HD)]
    pallas_call x0 -> x3, Pallas kernels: none -> 3.16 us  [the longest x1 1.36 us: local_halves(): pl.pallas_call(functools.partial(pack_kernel, messages, members, part), o...]
  transfers between devices with their start and end apart: 3 -> 10, of which waited for: 2 -> 6; matrix products, arithmetic and copies ran while one was open for 6% -> 0% of each run, Pallas kernels for 0% -> 0%
where the time goes in v6:
time: 33.3 us; the launch traced here: 33.1 us
  starting transfers between devices  18.9 us (57%)
  waiting for transfers between devices  11.1 us (33%)
  Pallas kernels  3.16 us (9%)
    ppermute x10, starting transfers between devices, swap(): lax.ppermute(array, AXES, [(i, i ^ mask) for i in range(devices)])  18.9 us
    ppermute x10, waiting for transfers between devices, swap(): lax.ppermute(array, AXES, [(i, i ^ mask) for i in range(devices)])  11.1 us
    pallas_call x1, Pallas kernels, local_halves(): pl.pallas_call(functools.partial(pack_kernel, messages, members, part), o...  1.36 us
    pallas_call x1, Pallas kernels, local_halves(): pl.pallas_call(functools.partial(attend_kernel, members), out_shape=[jax....  1.09 us
    pallas_call x1, Pallas kernels, local_halves(): pl.pallas_call(functools.partial(unpack_kernel, members, part), out_shape...  0.7 us
  transfers between devices with their start and end apart: 10, of which 6 were waited for; matrix products, arithmetic and copies ran while one was open for 0% of the time, Pallas kernels for 0%

profile of v6, /device:TPU:0, one launch (start us, length us, event | category | flops | bytes accessed | tf_op | source)
XLA Modules:
  0.0 33.1 jit_solution(1654232236739416089)
XLA Ops:
  0.0 1.4 %pack.1 = (bf16[64,768]{1,0:T(8,128)(2,1)S(1)}, bf16[64,768]{1,0:T(8,128)(2,1)S(1)}, bf16[64,768]{1,0:T(8,128)(2,1)S(1)}, bf16[64,768]{1,0:T(8,128)(2,1)S(1)}, b...) custom-call(bf16[1,64,1536]{2,1,0:T(8,128)(2,1)} %q_ref.1, ...), custom_call_target="tpu_custom_call" | custom-call | bytes 1179648 | tf_op jit(solution)/shard_map/pack/pallas_call | solution.py:155
  1.4 4.1 %collective-permute-start.3 = (bf16[64,768]{1,0:T(8,128)(2,1)S(1)}, bf16[64,768]{1,0:T(8,128)(2,1)S(1)}, u32[]{:S(2)}, u32[]{:S(2)}) collective-permute-start(bf16[64,768]{1,0:T(8,128)(2,1)S(1)} %get-tuple-element.21), channel_id=1, source_target_pairs={{0,8},{2,10},{4,12},{6,14},{8,0},{10,2},{12,4},{14,6},{1,9},{3,11}... | collective-permute-start | bytes 294920 | tf_op jit(solution)/shard_map/ppermute | solution.py:169
  5.5 1.3 %collective-permute-start.4 = (bf16[64,768]{1,0:T(8,128)(2,1)S(1)}, bf16[64,768]{1,0:T(8,128)(2,1)S(1)}, u32[]{:S(2)}, u32[]{:S(2)}) collective-permute-start(bf16[64,768]{1,0:T(8,128)(2,1)S(1)} %get-tuple-element.22), channel_id=1, source_target_pairs={{0,10},{2,8},{4,14},{6,12},{8,2},{10,0},{12,6},{14,4},{1,11},{3,9}... | collective-permute-start | bytes 294920 | tf_op jit(solution)/shard_map/ppermute | solution.py:169
  6.7 0.3 collective-permute-start
  7.0 1.8 %collective-permute-start.1 = (bf16[64,1152]{1,0:T(8,128)(2,1)S(1)}, bf16[64,1152]{1,0:T(8,128)(2,1)S(1)}, u32[]{:S(2)}, u32[]{:S(2)}) collective-permute-start(bf16[64,1152]{1,0:T(8,128)(2,1)S(1)} %get-tuple-element.19), channel_id=1, source_target_pairs={{0,4},{2,6},{4,0},{6,2},{8,12},{10,14},{12,8},{14,10},{1,5},{3,7},... | collective-permute-start | bytes 442376 | tf_op jit(solution)/shard_map/ppermute | solution.py:169
  8.9 1.4 %collective-permute-start.2 = (bf16[64,1152]{1,0:T(8,128)(2,1)S(1)}, bf16[64,1152]{1,0:T(8,128)(2,1)S(1)}, u32[]{:S(2)}, u32[]{:S(2)}) collective-permute-start(bf16[64,1152]{1,0:T(8,128)(2,1)S(1)} %get-tuple-element.20), channel_id=1, source_target_pairs={{0,6},{2,4},{4,2},{6,0},{8,14},{10,12},{12,10},{14,8},{1,7},{3,5},... | collective-permute-start | bytes 442376 | tf_op jit(solution)/shard_map/ppermute | solution.py:169
  10.2 2.4 %collective-permute-done.3.refs_4_ = bf16[64,768]{1,0:T(8,128)(2,1)S(1)} collective-permute-done((bf16[64,768]{1,0:T(8,128)(2,1)S(1)}, bf16[64,768]{1,0:T(8,128)(2,1)S(1)}, u32[]{:S(2)}, u32[]{:S(2)}) %collective-permute-start.3) | collective-permute-done | bytes 98336 | tf_op jit(solution)/shard_map/ppermute | solution.py:169
  12.7 3.5 %collective-permute-start.5 = (bf16[64,768]{1,0:T(8,128)(2,1)S(1)}, bf16[64,768]{1,0:T(8,128)(2,1)S(1)}, u32[]{:S(2)}, u32[]{:S(2)}) collective-permute-start(bf16[64,768]{1,0:T(8,128)(2,1)S(1)} %get-tuple-element.23), channel_id=1, source_target_pairs={{0,12},{2,14},{4,8},{6,10},{8,4},{10,6},{12,0},{14,2},{1,13},{3,15... | collective-permute-start | bytes 294920 | tf_op jit(solution)/shard_map/ppermute | solution.py:169
  16.2 0.0 collective-permute-done.4.refs_5_
  16.2 2.9 %collective-permute-start.6 = (bf16[64,768]{1,0:T(8,128)(2,1)S(1)}, bf16[64,768]{1,0:T(8,128)(2,1)S(1)}, u32[]{:S(2)}, u32[]{:S(2)}) collective-permute-start(bf16[64,768]{1,0:T(8,128)(2,1)S(1)} %get-tuple-element.24), channel_id=1, source_target_pairs={{0,14},{2,12},{4,10},{6,8},{8,6},{10,4},{12,2},{14,0},{1,15},{3,13... | collective-permute-start | bytes 294920 | tf_op jit(solution)/shard_map/ppermute | solution.py:169
  19.2 2.0 %collective-permute-done.5.refs_6_ = bf16[64,768]{1,0:T(8,128)(2,1)S(1)} collective-permute-done((bf16[64,768]{1,0:T(8,128)(2,1)S(1)}, bf16[64,768]{1,0:T(8,128)(2,1)S(1)}, u32[]{:S(2)}, u32[]{:S(2)}) %collective-permute-start.5) | collective-permute-done | bytes 98336 | tf_op jit(solution)/shard_map/ppermute | solution.py:169
  21.1 2.4 %collective-permute-done.6.refs_7_ = bf16[64,768]{1,0:T(8,128)(2,1)S(1)} collective-permute-done((bf16[64,768]{1,0:T(8,128)(2,1)S(1)}, bf16[64,768]{1,0:T(8,128)(2,1)S(1)}, u32[]{:S(2)}, u32[]{:S(2)}) %collective-permute-start.6) | collective-permute-done | bytes 98336 | tf_op jit(solution)/shard_map/ppermute | solution.py:169
  23.5 0.0 collective-permute-done.refs_1_
  23.5 0.0 collective-permute-done.1.refs_2_
  23.5 0.0 collective-permute-done.2.refs_3_
  23.6 1.1 %attend.1 = (bf16[64,384]{1,0:T(8,128)(2,1)S(1)}, bf16[64,384]{1,0:T(8,128)(2,1)S(1)}, bf16[64,384]{1,0:T(8,128)(2,1)S(1)}, bf16[64,384]{1,0:T(8,128)(2,1)S(1)}) custom-call(bf16[64,1152]{1,0:T(8,128)(2,1)S(1)} %get-tuple-element.17.refs_0_, bf16[64,1152]{1,0:T(8,128)(2,1)S(1)} %collective-permute-done.refs_1_, ...), custom_call_target="tpu_custom_call" | custom-call | flops 201326592 | bytes 1179648 | tf_op jit(solution)/shard_map/attend/pallas_call | solution.py:175
  24.6 1.6 %collective-permute-start.7 = (bf16[64,384]{1,0:T(8,128)(2,1)S(1)}, bf16[64,384]{1,0:T(8,128)(2,1)S(1)}, u32[]{:S(2)}, u32[]{:S(2)}) collective-permute-start(bf16[64,384]{1,0:T(8,128)(2,1)S(1)} %get-tuple-element.26), channel_id=1, source_target_pairs={{0,2},{2,0},{4,6},{6,4},{8,10},{10,8},{12,14},{14,12},{1,3},{3,1},... | collective-permute-start | bytes 147464 | tf_op jit(solution)/shard_map/ppermute | solution.py:169
  26.2 1.2 %collective-permute-start.8 = (bf16[64,384]{1,0:T(8,128)(2,1)S(1)}, bf16[64,384]{1,0:T(8,128)(2,1)S(1)}, u32[]{:S(2)}, u32[]{:S(2)}) collective-permute-start(bf16[64,384]{1,0:T(8,128)(2,1)S(1)} %get-tuple-element.27), channel_id=1, source_target_pairs={{0,4},{2,6},{4,0},{6,2},{8,12},{10,14},{12,8},{14,10},{1,5},{3,7},... | collective-permute-start | bytes 147464 | tf_op jit(solution)/shard_map/ppermute | solution.py:169
  27.4 0.8 %collective-permute-start.9 = (bf16[64,384]{1,0:T(8,128)(2,1)S(1)}, bf16[64,384]{1,0:T(8,128)(2,1)S(1)}, u32[]{:S(2)}, u32[]{:S(2)}) collective-permute-start(bf16[64,384]{1,0:T(8,128)(2,1)S(1)} %get-tuple-element.28), channel_id=1, source_target_pairs={{0,6},{2,4},{4,2},{6,0},{8,14},{10,12},{12,10},{14,8},{1,7},{3,5},... | collective-permute-start | bytes 147464 | tf_op jit(solution)/shard_map/ppermute | solution.py:169
  28.2 0.6 %collective-permute-done.7.refs_1_ = bf16[64,384]{1,0:T(8,128)(2,1)S(1)} collective-permute-done((bf16[64,384]{1,0:T(8,128)(2,1)S(1)}, bf16[64,384]{1,0:T(8,128)(2,1)S(1)}, u32[]{:S(2)}, u32[]{:S(2)}) %collective-permute-start.7) | collective-permute-done | bytes 49184 | tf_op jit(solution)/shard_map/ppermute | solution.py:169
  28.8 1.8 %collective-permute-done.8.refs_2_ = bf16[64,384]{1,0:T(8,128)(2,1)S(1)} collective-permute-done((bf16[64,384]{1,0:T(8,128)(2,1)S(1)}, bf16[64,384]{1,0:T(8,128)(2,1)S(1)}, u32[]{:S(2)}, u32[]{:S(2)}) %collective-permute-start.8) | collective-permute-done | bytes 49184 | tf_op jit(solution)/shard_map/ppermute | solution.py:169
  30.6 1.9 %collective-permute-done.9.refs_3_ = bf16[64,384]{1,0:T(8,128)(2,1)S(1)} collective-permute-done((bf16[64,384]{1,0:T(8,128)(2,1)S(1)}, bf16[64,384]{1,0:T(8,128)(2,1)S(1)}, u32[]{:S(2)}, u32[]{:S(2)}) %collective-permute-start.9) | collective-permute-done | bytes 49184 | tf_op jit(solution)/shard_map/ppermute | solution.py:169
  32.4 0.7 %unpack.1 = bf16[1,64,1536]{2,1,0:T(8,128)(2,1)} custom-call(bf16[64,384]{1,0:T(8,128)(2,1)S(1)} %get-tuple-element.25.refs_0_, bf16[64,384]{1,0:T(8,128)(2,1)S(1)} %collective-permute-done.7.refs_1_, bf16[64,384]{1,0:T(8,128)(2,1)S(1)} %collective-permute-done.8.refs_2_, bf16[64,384]{1,0:T(8,128)(2,1)S(1)} %collective-permute-done.9.refs_3_), custom_call_target="tpu_custom_call" | custom-call | bytes 393216 | tf_op jit(solution)/shard_map/unpack/pallas_call | solution.py:190
Async XLA Ops:
  1.4 11.3 %collective-permute-start.3 = (bf16[64,768]{1,0:T(8,128)(2,1)S(1)}, bf16[64,768]{1,0:T(8,128)(2,1)S(1)}, u32[]{:S(2)}, u32[]{:S(2)}) collective-permute-start(bf16[64,768]{1,0:T(8,128)(2,1)S(1)} %get-tuple-element.21), channel_id=1, source_target_pairs={{0,8},{2,10},{4,12},{6,14},{8,0},{10,2},{12,4},{14,6},{1,9},{3,11}... | collective-permute-start | bytes 294920 | tf_op jit(solution)/shard_map/ppermute | solution.py:169
  5.5 10.7 %collective-permute-start.4 = (bf16[64,768]{1,0:T(8,128)(2,1)S(1)}, bf16[64,768]{1,0:T(8,128)(2,1)S(1)}, u32[]{:S(2)}, u32[]{:S(2)}) collective-permute-start(bf16[64,768]{1,0:T(8,128)(2,1)S(1)} %get-tuple-element.22), channel_id=1, source_target_pairs={{0,10},{2,8},{4,14},{6,12},{8,2},{10,0},{12,6},{14,4},{1,11},{3,9}... | collective-permute-start | bytes 294920 | tf_op jit(solution)/shard_map/ppermute | solution.py:169
  6.7 16.8 %collective-permute-start = (bf16[64,1152]{1,0:T(8,128)(2,1)S(1)}, bf16[64,1152]{1,0:T(8,128)(2,1)S(1)}, u32[]{:S(2)}, u32[]{:S(2)}) collective-permute-start(bf16[64,1152]{1,0:T(8,128)(2,1)S(1)} %get-tuple-element.18), channel_id=1, source_target_pairs={{0,2},{2,0},{4,6},{6,4},{8,10},{10,8},{12,14},{14,12},{1,3},{3,1},... | collective-permute-start | bytes 442376 | tf_op jit(solution)/shard_map/ppermute | solution.py:169
  7.0 16.5 %collective-permute-start.1 = (bf16[64,1152]{1,0:T(8,128)(2,1)S(1)}, bf16[64,1152]{1,0:T(8,128)(2,1)S(1)}, u32[]{:S(2)}, u32[]{:S(2)}) collective-permute-start(bf16[64,1152]{1,0:T(8,128)(2,1)S(1)} %get-tuple-element.19), channel_id=1, source_target_pairs={{0,4},{2,6},{4,0},{6,2},{8,12},{10,14},{12,8},{14,10},{1,5},{3,7},... | collective-permute-start | bytes 442376 | tf_op jit(solution)/shard_map/ppermute | solution.py:169
  8.9 14.7 %collective-permute-start.2 = (bf16[64,1152]{1,0:T(8,128)(2,1)S(1)}, bf16[64,1152]{1,0:T(8,128)(2,1)S(1)}, u32[]{:S(2)}, u32[]{:S(2)}) collective-permute-start(bf16[64,1152]{1,0:T(8,128)(2,1)S(1)} %get-tuple-element.20), channel_id=1, source_target_pairs={{0,6},{2,4},{4,2},{6,0},{8,14},{10,12},{12,10},{14,8},{1,7},{3,5},... | collective-permute-start | bytes 442376 | tf_op jit(solution)/shard_map/ppermute | solution.py:169
  12.7 8.5 %collective-permute-start.5 = (bf16[64,768]{1,0:T(8,128)(2,1)S(1)}, bf16[64,768]{1,0:T(8,128)(2,1)S(1)}, u32[]{:S(2)}, u32[]{:S(2)}) collective-permute-start(bf16[64,768]{1,0:T(8,128)(2,1)S(1)} %get-tuple-element.23), channel_id=1, source_target_pairs={{0,12},{2,14},{4,8},{6,10},{8,4},{10,6},{12,0},{14,2},{1,13},{3,15... | collective-permute-start | bytes 294920 | tf_op jit(solution)/shard_map/ppermute | solution.py:169
  16.2 7.3 %collective-permute-start.6 = (bf16[64,768]{1,0:T(8,128)(2,1)S(1)}, bf16[64,768]{1,0:T(8,128)(2,1)S(1)}, u32[]{:S(2)}, u32[]{:S(2)}) collective-permute-start(bf16[64,768]{1,0:T(8,128)(2,1)S(1)} %get-tuple-element.24), channel_id=1, source_target_pairs={{0,14},{2,12},{4,10},{6,8},{8,6},{10,4},{12,2},{14,0},{1,15},{3,13... | collective-permute-start | bytes 294920 | tf_op jit(solution)/shard_map/ppermute | solution.py:169
  24.6 4.2 %collective-permute-start.7 = (bf16[64,384]{1,0:T(8,128)(2,1)S(1)}, bf16[64,384]{1,0:T(8,128)(2,1)S(1)}, u32[]{:S(2)}, u32[]{:S(2)}) collective-permute-start(bf16[64,384]{1,0:T(8,128)(2,1)S(1)} %get-tuple-element.26), channel_id=1, source_target_pairs={{0,2},{2,0},{4,6},{6,4},{8,10},{10,8},{12,14},{14,12},{1,3},{3,1},... | collective-permute-start | bytes 147464 | tf_op jit(solution)/shard_map/ppermute | solution.py:169
  26.2 4.4 %collective-permute-start.8 = (bf16[64,384]{1,0:T(8,128)(2,1)S(1)}, bf16[64,384]{1,0:T(8,128)(2,1)S(1)}, u32[]{:S(2)}, u32[]{:S(2)}) collective-permute-start(bf16[64,384]{1,0:T(8,128)(2,1)S(1)} %get-tuple-element.27), channel_id=1, source_target_pairs={{0,4},{2,6},{4,0},{6,2},{8,12},{10,14},{12,8},{14,10},{1,5},{3,7},... | collective-permute-start | bytes 147464 | tf_op jit(solution)/shard_map/ppermute | solution.py:169
  27.4 5.0 %collective-permute-start.9 = (bf16[64,384]{1,0:T(8,128)(2,1)S(1)}, bf16[64,384]{1,0:T(8,128)(2,1)S(1)}, u32[]{:S(2)}, u32[]{:S(2)}) collective-permute-start(bf16[64,384]{1,0:T(8,128)(2,1)S(1)} %get-tuple-element.28), channel_id=1, source_target_pairs={{0,6},{2,4},{4,2},{6,0},{8,14},{10,12},{12,10},{14,8},{1,7},{3,5},... | collective-permute-start | bytes 147464 | tf_op jit(solution)/shard_map/ppermute | solution.py:169

commit v7 on v5

--- a/solution.py
+++ b/solution.py
@@ -9,7 +9,7 @@
 from jax.sharding import PartitionSpec as P
 
 HD = 128
-EFFORT = 15 * 10**8
+EFFORT = 10**8
 ANY = pl.BlockSpec(memory_space=pl.ANY)
 HBM = pl.BlockSpec(memory_space=pltpu.HBM)
 VMEM = pl.BlockSpec(memory_space=pltpu.VMEM)
@@ -220,7 +220,7 @@
     far_q = [to_block(hold(sent[s, q], near_kv), s) for s in far]
     groups = [near_kv, join(far_kv, [0] * len(far), 2 * part)]
     crossed = [to_column(group, t) for group in groups for t in range(1, columns_of)]
-    far_q = join(far_q, [0] * len(far), part, EFFORT)
+    far_q = join(far_q, [0] * len(far), part)
     near_q = join([own_q, near_kvq], [0, 2 * part], part, EFFORT, crossed[: columns_of - 1])
     arrays = [near_q, far_q, near_kvq, own_kv] + far_kv
     key_places = [(at, None, 0) for at in range(2, len(arrays))]

time: 33.7 us -> 34 us (level)
  waiting for transfers between devices: 11.5 us -> 14.9 us
  starting transfers between devices: 19 us -> 15.8 us
    ppermute x8, waiting for transfers between devices: 7.78 us -> 14.9 us  [to_block(): return lax.ppermute(array, 'blk', [(i, i ^ s) for i in range(blocks)])]
    ppermute x2, waiting for transfers between devices: 3.76 us -> 0.01 us  [to_column(): lax.ppermute(array, 'uly', [(i, (i + t) % columns_of) for i in range(colu...]
    ppermute x8, starting transfers between devices: 15.9 us -> 12.7 us  [to_block(): return lax.ppermute(array, 'blk', [(i, i ^ s) for i in range(blocks)])]
  transfers between devices with their start and end apart: 10 -> 10, of which waited for: 6 -> 7; matrix products, arithmetic and copies ran while one was open for 0% -> 0% of each run, Pallas kernels for 0% -> 0%
where the time goes in v7:
time: 34 us; the launch traced here: 33.8 us
  starting transfers between devices  15.8 us (46%)
  waiting for transfers between devices  14.9 us (44%)
  Pallas kernels  3.01 us (9%)
    ppermute x8, waiting for transfers between devices, to_block(): return lax.ppermute(array, 'blk', [(i, i ^ s) for i in range(blocks)])  14.9 us
    ppermute x8, starting transfers between devices, to_block(): return lax.ppermute(array, 'blk', [(i, i ^ s) for i in range(blocks)])  12.7 us
    ppermute x2, starting transfers between devices, to_column(): lax.ppermute(array, 'uly', [(i, (i + t) % columns_of) for i in range(colu...  3.11 us
    pallas_call x1, Pallas kernels, local_blocks(): pl.pallas_call(functools.partial(pack_kernel, messages, part), out_shape=...  1.17 us
    pallas_call x1, Pallas kernels, local_blocks(): pl.pallas_call(functools.partial(attend_kernel, plan), out_shape=[jax.Sha...  1.09 us
    pallas_call x1, Pallas kernels, local_blocks(): pl.pallas_call(functools.partial(unpack_kernel, order, part), out_shape=j...  0.7 us
  transfers between devices with their start and end apart: 10, of which 7 were waited for; matrix products, arithmetic and copies ran while one was open for 0% of the time, Pallas kernels for 0%

profile of v7, /device:TPU:0, one launch (start us, length us, event | category | flops | bytes accessed | tf_op | source)
XLA Modules:
  0.0 33.8 jit_solution(4402494431191288512)
XLA Ops:
  0.0 1.2 %pack.1 = (bf16[64,768]{1,0:T(8,128)(2,1)S(1)}, bf16[64,768]{1,0:T(8,128)(2,1)S(1)}, bf16[64,1152]{1,0:T(8,128)(2,1)S(1)}, bf16[64,384]{1,0:T(8,128)(2,1)S(1)}, ...) custom-call(bf16[1,64,1536]{2,1,0:T(8,128)(2,1)} %q_ref.1, ...), custom_call_target="tpu_custom_call" | custom-call | bytes 1179648 | tf_op jit(solution)/shard_map/pack/pallas_call | solution.py:193
  1.2 3.1 %collective-permute-start = (bf16[64,1152]{1,0:T(8,128)(2,1)S(1)}, bf16[64,1152]{1,0:T(8,128)(2,1)S(1)}, u32[]{:S(2)}, u32[]{:S(2)}) collective-permute-start(bf16[64,1152]{1,0:T(8,128)(2,1)S(1)} %get-tuple-element.17), channel_id=1, source_target_pairs={{0,4},{4,0},{8,12},{12,8},{1,5},{5,1},{9,13},{13,9},{2,6},{6,2},{1... | collective-permute-start | bytes 442376 | tf_op jit(solution)/shard_map/ppermute | solution.py:210
  4.3 2.5 %collective-permute-start.4 = (bf16[64,768]{1,0:T(8,128)(2,1)S(1)}, bf16[64,768]{1,0:T(8,128)(2,1)S(1)}, u32[]{:S(2)}, u32[]{:S(2)}) collective-permute-start(bf16[64,768]{1,0:T(8,128)(2,1)S(1)} %get-tuple-element.21), channel_id=1, source_target_pairs={{0,12},{4,8},{8,4},{12,0},{1,13},{5,9},{9,5},{13,1},{2,14},{6,10},... | collective-permute-start | bytes 294920 | tf_op jit(solution)/shard_map/ppermute | solution.py:210
  6.7 0.1 collective-permute-start.5
  6.9 1.5 %collective-permute-done.refs_1_.refs_2_ = bf16[64,1152]{1,0:T(8,128)(2,1)S(1)} collective-permute-done((bf16[64,1152]{1,0:T(8,128)(2,1)S(1)}, bf16[64,1152]{1,0:T(8,128)(2,1)S(1)}, u32[]{:S(2)}, u32[]{:S(2)}) %collective-permute-start) | collective-permute-done | bytes 147488 | tf_op jit(solution)/shard_map/ppermute | solution.py:210
  8.3 1.6 %collective-permute-start.1 = (bf16[2,64,768]{2,1,0:T(8,128)(2,1)S(1)}, bf16[2,64,768]{2,1,0:T(8,128)(2,1)S(1)}, u32[]{:S(2)}, u32[]{:S(2)}) collective-permute-start(bf16[2,64,768]{2,1,0:T(8,128)(2,1)S(1)} %join.4.until_ref), channel_id=1, source_target_pairs={{0,2},{2,0},{1,3},{3,1},{4,6},{6,4},{5,7},{7,5},{8,10},{10,8},{9,1... | collective-permute-start | bytes 589832 | tf_op jit(solution)/shard_map/ppermute | solution.py:213
  9.9 3.7 %collective-permute-done.4.refs_0_.refs_4_ = bf16[64,768]{1,0:T(8,128)(2,1)S(1)} collective-permute-done((bf16[64,768]{1,0:T(8,128)(2,1)S(1)}, bf16[64,768]{1,0:T(8,128)(2,1)S(1)}, u32[]{:S(2)}, u32[]{:S(2)}) %collective-permute-start.4) | collective-permute-done | bytes 98336 | tf_op jit(solution)/shard_map/ppermute | solution.py:210
  13.6 2.2 %collective-permute-done.5.refs_1_.refs_5_ = bf16[64,768]{1,0:T(8,128)(2,1)S(1)} collective-permute-done((bf16[64,768]{1,0:T(8,128)(2,1)S(1)}, bf16[64,768]{1,0:T(8,128)(2,1)S(1)}, u32[]{:S(2)}, u32[]{:S(2)}) %collective-permute-start.5) | collective-permute-done | bytes 98336 | tf_op jit(solution)/shard_map/ppermute | solution.py:210
  15.8 1.6 %collective-permute-start.6 = (bf16[2,64,768]{2,1,0:T(8,128)(2,1)S(1)}, bf16[2,64,768]{2,1,0:T(8,128)(2,1)S(1)}, u32[]{:S(2)}, u32[]{:S(2)}) collective-permute-start(bf16[2,64,768]{2,1,0:T(8,128)(2,1)S(1)} %join.7), channel_id=1, source_target_pairs={{0,2},{2,0},{1,3},{3,1},{4,6},{6,4},{5,7},{7,5},{8,10},{10,8},{9,1... | collective-permute-start | bytes 589832 | tf_op jit(solution)/shard_map/ppermute | solution.py:213
  17.3 2.6 %collective-permute-start.2 = (bf16[64,384]{1,0:T(8,128)(2,1)S(1)}, bf16[64,384]{1,0:T(8,128)(2,1)S(1)}, u32[]{:S(2)}, u32[]{:S(2)}) collective-permute-start(bf16[64,384]{1,0:T(8,128)(2,1)S(1)} %hold.2), channel_id=1, source_target_pairs={{0,12},{4,8},{8,4},{12,0},{1,13},{5,9},{9,5},{13,1},{2,14},{6,10},... | collective-permute-start | bytes 147464 | tf_op jit(solution)/shard_map/ppermute | solution.py:210
  19.9 0.0 collective-permute-start.3
  19.9 3.3 %collective-permute-done.2.refs_0_ = bf16[64,384]{1,0:T(8,128)(2,1)S(1)} collective-permute-done((bf16[64,384]{1,0:T(8,128)(2,1)S(1)}, bf16[64,384]{1,0:T(8,128)(2,1)S(1)}, u32[]{:S(2)}, u32[]{:S(2)}) %collective-permute-start.2) | collective-permute-done | bytes 49184 | tf_op jit(solution)/shard_map/ppermute | solution.py:210
  23.2 1.7 %collective-permute-done.3.refs_1_ = bf16[64,384]{1,0:T(8,128)(2,1)S(1)} collective-permute-done((bf16[64,384]{1,0:T(8,128)(2,1)S(1)}, bf16[64,384]{1,0:T(8,128)(2,1)S(1)}, u32[]{:S(2)}, u32[]{:S(2)}) %collective-permute-start.3) | collective-permute-done | bytes 49184 | tf_op jit(solution)/shard_map/ppermute | solution.py:210
  24.9 0.0 collective-permute-done.1.refs_2_.refs_6_
  24.9 0.0 collective-permute-done.6.refs_7_
  24.9 1.1 %attend.1 = (bf16[64,384]{1,0:T(8,128)(2,1)S(1)}, bf16[64,384]{1,0:T(8,128)(2,1)S(1)}, bf16[64,384]{1,0:T(8,128)(2,1)S(1)}, bf16[64,384]{1,0:T(8,128)(2,1)S(1)}) custom-call(bf16[2,64,384]{2,1,0:T(8,128)(2,1)S(1)} %join.5.refs_0_, bf16[2,64,384]{2,1,0:T(8,128)(2,1)S(1)} %join.6.refs_1_, bf16[64,1152]{1,0:T(8,128)(2,1)S(1)} %collective-permute-done.refs_1_.refs_2_, ...), custom_call_target="tpu_custom_call" | custom-call | flops 201326592 | bytes 1179648 | tf_op jit(solution)/shard_map/attend/pallas_call | solution.py:243
  26.0 2.0 %collective-permute-start.7 = (bf16[64,384]{1,0:T(8,128)(2,1)S(1)}, bf16[64,384]{1,0:T(8,128)(2,1)S(1)}, u32[]{:S(2)}, u32[]{:S(2)}) collective-permute-start(bf16[64,384]{1,0:T(8,128)(2,1)S(1)} %get-tuple-element.24), channel_id=1, source_target_pairs={{0,12},{4,8},{8,4},{12,0},{1,13},{5,9},{9,5},{13,1},{2,14},{6,10},... | collective-permute-start | bytes 147464 | tf_op jit(solution)/shard_map/ppermute | solution.py:210
  28.1 0.0 collective-permute-start.8
  28.1 2.4 %collective-permute-start.9 = (bf16[64,384]{1,0:T(8,128)(2,1)S(1)}, bf16[64,384]{1,0:T(8,128)(2,1)S(1)}, u32[]{:S(2)}, u32[]{:S(2)}) collective-permute-start(bf16[64,384]{1,0:T(8,128)(2,1)S(1)} %get-tuple-element.26), channel_id=1, source_target_pairs={{0,4},{4,0},{8,12},{12,8},{1,5},{5,1},{9,13},{13,9},{2,6},{6,2},{1... | collective-permute-start | bytes 147464 | tf_op jit(solution)/shard_map/ppermute | solution.py:210
  30.5 1.5 %collective-permute-done.7.refs_1_ = bf16[64,384]{1,0:T(8,128)(2,1)S(1)} collective-permute-done((bf16[64,384]{1,0:T(8,128)(2,1)S(1)}, bf16[64,384]{1,0:T(8,128)(2,1)S(1)}, u32[]{:S(2)}, u32[]{:S(2)}) %collective-permute-start.7) | collective-permute-done | bytes 49184 | tf_op jit(solution)/shard_map/ppermute | solution.py:210
  32.0 1.1 %collective-permute-done.8.refs_2_ = bf16[64,384]{1,0:T(8,128)(2,1)S(1)} collective-permute-done((bf16[64,384]{1,0:T(8,128)(2,1)S(1)}, bf16[64,384]{1,0:T(8,128)(2,1)S(1)}, u32[]{:S(2)}, u32[]{:S(2)}) %collective-permute-start.8) | collective-permute-done | bytes 49184 | tf_op jit(solution)/shard_map/ppermute | solution.py:210
  33.1 0.0 collective-permute-done.9.refs_3_
  33.1 0.7 %unpack.1 = bf16[1,64,1536]{2,1,0:T(8,128)(2,1)} custom-call(bf16[64,384]{1,0:T(8,128)(2,1)S(1)} %get-tuple-element.23.refs_0_, bf16[64,384]{1,0:T(8,128)(2,1)S(1)} %collective-permute-done.7.refs_1_, bf16[64,384]{1,0:T(8,128)(2,1)S(1)} %collective-permute-done.8.refs_2_, bf16[64,384]{1,0:T(8,128)(2,1)S(1)} %collective-permute-done.9.refs_3_), custom_call_target="tpu_custom_call" | custom-call | bytes 393216 | tf_op jit(solution)/shard_map/unpack/pallas_call | solution.py:259
  (6 shorter events, 0.0 us)
Async XLA Ops:
  1.2 7.2 %collective-permute-start = (bf16[64,1152]{1,0:T(8,128)(2,1)S(1)}, bf16[64,1152]{1,0:T(8,128)(2,1)S(1)}, u32[]{:S(2)}, u32[]{:S(2)}) collective-permute-start(bf16[64,1152]{1,0:T(8,128)(2,1)S(1)} %get-tuple-element.17), channel_id=1, source_target_pairs={{0,4},{4,0},{8,12},{12,8},{1,5},{5,1},{9,13},{13,9},{2,6},{6,2},{1... | collective-permute-start | bytes 442376 | tf_op jit(solution)/shard_map/ppermute | solution.py:210
  4.3 9.3 %collective-permute-start.4 = (bf16[64,768]{1,0:T(8,128)(2,1)S(1)}, bf16[64,768]{1,0:T(8,128)(2,1)S(1)}, u32[]{:S(2)}, u32[]{:S(2)}) collective-permute-start(bf16[64,768]{1,0:T(8,128)(2,1)S(1)} %get-tuple-element.21), channel_id=1, source_target_pairs={{0,12},{4,8},{8,4},{12,0},{1,13},{5,9},{9,5},{13,1},{2,14},{6,10},... | collective-permute-start | bytes 294920 | tf_op jit(solution)/shard_map/ppermute | solution.py:210
  6.7 9.0 %collective-permute-start.5 = (bf16[64,768]{1,0:T(8,128)(2,1)S(1)}, bf16[64,768]{1,0:T(8,128)(2,1)S(1)}, u32[]{:S(2)}, u32[]{:S(2)}) collective-permute-start(bf16[64,768]{1,0:T(8,128)(2,1)S(1)} %get-tuple-element.22), channel_id=1, source_target_pairs={{0,8},{4,12},{8,0},{12,4},{1,9},{5,13},{9,1},{13,5},{2,10},{6,14},... | collective-permute-start | bytes 294920 | tf_op jit(solution)/shard_map/ppermute | solution.py:210
  8.3 16.6 %collective-permute-start.1 = (bf16[2,64,768]{2,1,0:T(8,128)(2,1)S(1)}, bf16[2,64,768]{2,1,0:T(8,128)(2,1)S(1)}, u32[]{:S(2)}, u32[]{:S(2)}) collective-permute-start(bf16[2,64,768]{2,1,0:T(8,128)(2,1)S(1)} %join.4.until_ref), channel_id=1, source_target_pairs={{0,2},{2,0},{1,3},{3,1},{4,6},{6,4},{5,7},{7,5},{8,10},{10,8},{9,1... | collective-permute-start | bytes 589832 | tf_op jit(solution)/shard_map/ppermute | solution.py:213
  15.8 9.2 %collective-permute-start.6 = (bf16[2,64,768]{2,1,0:T(8,128)(2,1)S(1)}, bf16[2,64,768]{2,1,0:T(8,128)(2,1)S(1)}, u32[]{:S(2)}, u32[]{:S(2)}) collective-permute-start(bf16[2,64,768]{2,1,0:T(8,128)(2,1)S(1)} %join.7), channel_id=1, source_target_pairs={{0,2},{2,0},{1,3},{3,1},{4,6},{6,4},{5,7},{7,5},{8,10},{10,8},{9,1... | collective-permute-start | bytes 589832 | tf_op jit(solution)/shard_map/ppermute | solution.py:213
  17.3 5.9 %collective-permute-start.2 = (bf16[64,384]{1,0:T(8,128)(2,1)S(1)}, bf16[64,384]{1,0:T(8,128)(2,1)S(1)}, u32[]{:S(2)}, u32[]{:S(2)}) collective-permute-start(bf16[64,384]{1,0:T(8,128)(2,1)S(1)} %hold.2), channel_id=1, source_target_pairs={{0,12},{4,8},{8,4},{12,0},{1,13},{5,9},{9,5},{13,1},{2,14},{6,10},... | collective-permute-start | bytes 147464 | tf_op jit(solution)/shard_map/ppermute | solution.py:210
  19.9 5.0 %collective-permute-start.3 = (bf16[64,384]{1,0:T(8,128)(2,1)S(1)}, bf16[64,384]{1,0:T(8,128)(2,1)S(1)}, u32[]{:S(2)}, u32[]{:S(2)}) collective-permute-start(bf16[64,384]{1,0:T(8,128)(2,1)S(1)} %hold.3), channel_id=1, source_target_pairs={{0,8},{4,12},{8,0},{12,4},{1,9},{5,13},{9,1},{13,5},{2,10},{6,14},... | collective-permute-start | bytes 147464 | tf_op jit(solution)/shard_map/ppermute | solution.py:210
  26.0 6.0 %collective-permute-start.7 = (bf16[64,384]{1,0:T(8,128)(2,1)S(1)}, bf16[64,384]{1,0:T(8,128)(2,1)S(1)}, u32[]{:S(2)}, u32[]{:S(2)}) collective-permute-start(bf16[64,384]{1,0:T(8,128)(2,1)S(1)} %get-tuple-element.24), channel_id=1, source_target_pairs={{0,12},{4,8},{8,4},{12,0},{1,13},{5,9},{9,5},{13,1},{2,14},{6,10},... | collective-permute-start | bytes 147464 | tf_op jit(solution)/shard_map/ppermute | solution.py:210
  28.1 5.0 %collective-permute-start.8 = (bf16[64,384]{1,0:T(8,128)(2,1)S(1)}, bf16[64,384]{1,0:T(8,128)(2,1)S(1)}, u32[]{:S(2)}, u32[]{:S(2)}) collective-permute-start(bf16[64,384]{1,0:T(8,128)(2,1)S(1)} %get-tuple-element.25), channel_id=1, source_target_pairs={{0,8},{4,12},{8,0},{12,4},{1,9},{5,13},{9,1},{13,5},{2,10},{6,14},... | collective-permute-start | bytes 147464 | tf_op jit(solution)/shard_map/ppermute | solution.py:210
  28.1 5.0 %collective-permute-start.9 = (bf16[64,384]{1,0:T(8,128)(2,1)S(1)}, bf16[64,384]{1,0:T(8,128)(2,1)S(1)}, u32[]{:S(2)}, u32[]{:S(2)}) collective-permute-start(bf16[64,384]{1,0:T(8,128)(2,1)S(1)} %get-tuple-element.26), channel_id=1, source_target_pairs={{0,4},{4,0},{8,12},{12,8},{1,5},{5,1},{9,13},{13,9},{2,6},{6,2},{1... | collective-permute-start | bytes 147464 | tf_op jit(solution)/shard_map/ppermute | solution.py:210

commit v8 on v6

--- a/solution.py
+++ b/solution.py
@@ -9,6 +9,8 @@
 from jax.sharding import PartitionSpec as P
 
 HD = 128
+EFFORT = 4 * 10**9
+ANY = pl.BlockSpec(memory_space=pl.ANY)
 HBM = pl.BlockSpec(memory_space=pltpu.HBM)
 VMEM = pl.BlockSpec(memory_space=pltpu.VMEM)
 SMALL = pltpu.CompilerParams(vmem_limit_bytes=4 * 1024 * 1024)
@@ -105,38 +107,78 @@
     run_copies(pairs, sems)
 
 
-def attend_kernel(members, *refs):
-    ins, out_refs = refs[:-members], refs[-members:]
+def hold_kernel(*refs):
+    pass
+
+
+def hold(arrays, until=(), effort=0):
+    return pl.pallas_call(
+        hold_kernel,
+        out_shape=[jax.ShapeDtypeStruct(array.shape, array.dtype) for array in arrays],
+        in_specs=[ANY] * (len(arrays) + len(until)),
+        out_specs=[ANY] * len(arrays),
+        input_output_aliases={at: at for at in range(len(arrays))},
+        compiler_params=SMALL,
+        cost_estimate=pl.CostEstimate(flops=effort, bytes_accessed=0, transcendentals=0),
+        name="hold",
+    )(*arrays, *until)
+
+
+def rows(sources, first):
+    return jnp.concatenate([ref[:, first : first + HD] for ref in sources], axis=0)
+
+
+def scores_of(query_refs, key_refs, lane, part):
+    scores = lax.dot_general(
+        rows(query_refs, 2 * part + lane),
+        rows(key_refs, lane),
+        (((1,), (1,)), ((), ())),
+        preferred_element_type=jnp.float32,
+    )
+    return scores * (1.0 / math.sqrt(HD))
+
+
+def mix(weights, key_refs, lane, part):
+    values = rows(key_refs, part + lane)
+    return jnp.dot(weights.astype(jnp.bfloat16), values, preferred_element_type=jnp.float32)
+
+
+def first_kernel(members, *refs):
+    ins, (largest_ref, totals_ref, mixed_ref) = refs[:-3], refs[-3:]
+    part = mixed_ref.shape[0] * HD
+    for head in range(part // HD):
+        scores = scores_of(ins[:members], ins, head * HD, part)
+        largest = jnp.max(scores, axis=1, keepdims=True)
+        weights = jnp.exp(scores - largest)
+        totals = jnp.sum(weights, axis=1, keepdims=True)
+        largest_ref[head] = jnp.broadcast_to(largest, largest_ref.shape[1:])
+        totals_ref[head] = jnp.broadcast_to(totals, totals_ref.shape[1:])
+        mixed_ref[head] = mix(weights, ins, head * HD, part)
+
+
+def last_kernel(members, *refs):
+    query_refs, key_refs = refs[:members], refs[members:-3 - members]
+    largest_ref, totals_ref, mixed_ref = refs[-3 - members : -members]
+    out_refs = refs[-members:]
     tokens, part = out_refs[0].shape
-    scale = 1.0 / math.sqrt(HD)
-
-    def rows(sources, first):
-        return jnp.concatenate([ref[:, first : first + HD] for ref in sources], axis=0)
-
-    for lane in range(0, part, HD):
-        queries = rows(ins[:members], 2 * part + lane)
-        keys = rows(ins, lane)
-        values = rows(ins, part + lane)
-        scores = (
-            lax.dot_general(
-                queries, keys, (((1,), (1,)), ((), ())), preferred_element_type=jnp.float32
-            )
-            * scale
-        )
-        weights = jnp.exp(scores - jnp.max(scores, axis=1, keepdims=True))
-        totals = jnp.sum(weights, axis=1, keepdims=True)
-        mixed = jnp.dot(
-            weights.astype(jnp.bfloat16), values, preferred_element_type=jnp.float32
-        )
+    for head in range(part // HD):
+        lane = head * HD
+        scores = scores_of(query_refs, key_refs, lane, part)
+        before = largest_ref[head][:, :1]
+        largest = jnp.maximum(before, jnp.max(scores, axis=1, keepdims=True))
+        weights = jnp.exp(scores - largest)
+        factor = jnp.exp(before - largest)
+        totals = totals_ref[head][:, :1] * factor + jnp.sum(weights, axis=1, keepdims=True)
+        mixed = mixed_ref[head] * factor + mix(weights, key_refs, lane, part)
         result = (mixed / totals).astype(jnp.bfloat16)
         for at, ref in enumerate(out_refs):
             ref[:, lane : lane + HD] = result[at * tokens : (at + 1) * tokens]
 
 
-def unpack_kernel(members, part, *refs):
+def unpack_kernel(members, order, part, *refs):
     ins, out_ref, sems = refs[:-2], refs[-2], refs[-1]
     pairs = []
-    for mask, ref in enumerate(ins):
+    for mask, ref in zip(order, ins):
         columns = pl.ds(pl.multiple_of(place_of(mask, members) * part, 128), part)
         pairs.append((ref, out_ref.at[0, :, columns]))
     run_copies(pairs, sems)
@@ -150,7 +192,7 @@
     heads = part // HD
     kind = query_rows.dtype
 
-    messages = [(mask, "kv") for mask in range(members, devices)]
+    messages = [(mask, "kv") for mask in range(devices - 1, members - 1, -1)]
     messages += [(mask, "kvq") for mask in range(members)]
     packed = pl.pallas_call(
         functools.partial(pack_kernel, messages, members, part),
@@ -168,27 +210,45 @@
     def swap(array, mask):
         return lax.ppermute(array, AXES, [(i, i ^ mask) for i in range(devices)]) if mask else array
 
-    got = [swap(array, mask) for (mask, names), array in zip(messages, packed)]
-    arrays = got[members:] + got[:members]
-
-    pairs = heads * tokens * members * tokens * devices
+    far = [swap(array, mask) for (mask, names), array in zip(messages[:members], packed)]
+    near = [packed[members]]
+    for mask in range(1, members):
+        ready = hold([packed[members + mask]], near[1:2])[0] if mask > 1 else packed[members + 1]
+        near.append(swap(ready, mask))
+    soon, late = near + list(hold(far[: members // 2], effort=EFFORT)), far[members // 2 :]
+
+    def cost_of(keys):
+        pairs = heads * tokens * members * tokens * len(keys)
+        return pl.CostEstimate(
+            flops=4 * HD * pairs,
+            bytes_accessed=4 * part * tokens * (members + len(keys)),
+            transcendentals=pairs,
+        )
+
+    roomy = pltpu.CompilerParams(vmem_limit_bytes=24 * 1024 * 1024)
+    state = pl.pallas_call(
+        functools.partial(first_kernel, members),
+        out_shape=[jax.ShapeDtypeStruct((heads, tokens * members, HD), jnp.float32)] * 3,
+        in_specs=[VMEM] * len(soon),
+        out_specs=[VMEM] * 3,
+        compiler_params=roomy,
+        cost_estimate=cost_of(soon),
+        name="first",
+    )(*soon)
     mixed = pl.pallas_call(
-        functools.partial(attend_kernel, members),
+        functools.partial(last_kernel, members),
         out_shape=[jax.ShapeDtypeStruct((tokens, part), kind)] * members,
-        in_specs=[VMEM] * devices,
+        in_specs=[VMEM] * (members + len(late) + 3),
         out_specs=[VMEM] * members,
-        compiler_params=pltpu.CompilerParams(vmem_limit_bytes=24 * 1024 * 1024),
-        cost_estimate=pl.CostEstimate(
-            flops=4 * HD * pairs,
-            bytes_accessed=4 * part * tokens * (devices + members),
-            transcendentals=pairs,
-        ),
-        name="attend",
-    )(*arrays)
-
-    back = [swap(array, mask) for mask, array in enumerate(mixed)]
+        compiler_params=roomy,
+        cost_estimate=cost_of(late),
+        name="last",
+    )(*near, *late, *state)
+
+    order = list(range(members))[::-1]
+    back = [swap(mixed[mask], mask) for mask in order]
     return pl.pallas_call(
-        functools.partial(unpack_kernel, members, part),
+        functools.partial(unpack_kernel, members, order, part),
         out_shape=jax.ShapeDtypeStruct((1, tokens, width), kind),
         in_specs=[VMEM] * members,
         out_specs=HBM,

time: 33.3 us -> 35.9 us (1.078)
  starting transfers between devices: 18.9 us -> 22.4 us
  waiting for transfers between devices: 11.1 us -> 9.21 us
  Pallas kernels: 3.16 us -> 4.02 us
    ppermute x10, starting transfers between devices: 18.9 us -> 22.4 us  [swap(): lax.ppermute(array, AXES, [(i, i ^ mask) for i in range(devices)])]
    ppermute x10, waiting for transfers between devices: 11.1 us -> 9.21 us  [swap(): lax.ppermute(array, AXES, [(i, i ^ mask) for i in range(devices)])]
    pallas_call x2 -> x6, Pallas kernels: 1.8 us -> 2.66 us  [the longest x1 1.02 us: local_halves(): pl.pallas_call(functools.partial(first_kernel, members), out_shape=[jax.S...]
  transfers between devices with their start and end apart: 10 -> 10, of which waited for: 6 -> 4; matrix products, arithmetic and copies ran while one was open for 0% -> 0% of each run, Pallas kernels for 0% -> 3%
where the time goes in v8:
time: 35.9 us; the launch traced here: 35.7 us
  starting transfers between devices  22.4 us (62%)
  waiting for transfers between devices  9.21 us (26%)
  Pallas kernels  4.02 us (11%)
    ppermute x10, starting transfers between devices, swap(): lax.ppermute(array, AXES, [(i, i ^ mask) for i in range(devices)])  22.4 us
    ppermute x10, waiting for transfers between devices, swap(): lax.ppermute(array, AXES, [(i, i ^ mask) for i in range(devices)])  9.21 us
    pallas_call x1, Pallas kernels, local_halves(): pl.pallas_call(functools.partial(pack_kernel, messages, members, part), o...  1.36 us
    pallas_call x1, Pallas kernels, local_halves(): pl.pallas_call(functools.partial(first_kernel, members), out_shape=[jax.S...  1.02 us
    pallas_call x1, Pallas kernels, local_halves(): pl.pallas_call(functools.partial(last_kernel, members), out_shape=[jax.Sh...  0.94 us
  transfers between devices with their start and end apart: 10, of which 4 were waited for; matrix products, arithmetic and copies ran while one was open for 0% of the time, Pallas kernels for 3%

profile of v8, /device:TPU:0, one launch (start us, length us, event | category | flops | bytes accessed | tf_op | source)
XLA Modules:
  0.0 35.7 jit_solution(4352026536383954535)
XLA Ops:
  0.0 1.4 %pack.1 = (bf16[64,768]{1,0:T(8,128)(2,1)S(1)}, bf16[64,768]{1,0:T(8,128)(2,1)S(1)}, bf16[64,768]{1,0:T(8,128)(2,1)S(1)}, bf16[64,768]{1,0:T(8,128)(2,1)S(1)}, b...) custom-call(bf16[1,64,1536]{2,1,0:T(8,128)(2,1)} %q_ref.1, ...), custom_call_target="tpu_custom_call" | custom-call | bytes 1179648 | tf_op jit(solution)/shard_map/pack/pallas_call | solution.py:197
  1.4 3.0 %collective-permute-start = (bf16[64,1152]{1,0:T(8,128)(2,1)S(1)}, bf16[64,1152]{1,0:T(8,128)(2,1)S(1)}, u32[]{:S(2)}, u32[]{:S(2)}) collective-permute-start(bf16[64,1152]{1,0:T(8,128)(2,1)S(1)} %get-tuple-element.23), channel_id=1, source_target_pairs={{0,2},{2,0},{4,6},{6,4},{8,10},{10,8},{12,14},{14,12},{1,3},{3,1},... | collective-permute-start | bytes 442376 | tf_op jit(solution)/shard_map/ppermute | solution.py:211
  4.4 3.6 %collective-permute-start.5 = (bf16[64,768]{1,0:T(8,128)(2,1)S(1)}, bf16[64,768]{1,0:T(8,128)(2,1)S(1)}, u32[]{:S(2)}, u32[]{:S(2)}) collective-permute-start(bf16[64,768]{1,0:T(8,128)(2,1)S(1)} %get-tuple-element.28), channel_id=1, source_target_pairs={{0,14},{2,12},{4,10},{6,8},{8,6},{10,4},{12,2},{14,0},{1,15},{3,13... | collective-permute-start | bytes 294920 | tf_op jit(solution)/shard_map/ppermute | solution.py:211
  8.0 0.0 collective-permute-start.6
  8.0 1.9 %collective-permute-start.3 = (bf16[64,768]{1,0:T(8,128)(2,1)S(1)}, bf16[64,768]{1,0:T(8,128)(2,1)S(1)}, u32[]{:S(2)}, u32[]{:S(2)}) collective-permute-start(bf16[64,768]{1,0:T(8,128)(2,1)S(1)} %get-tuple-element.26), channel_id=1, source_target_pairs={{0,10},{2,8},{4,14},{6,12},{8,2},{10,0},{12,6},{14,4},{1,11},{3,9}... | collective-permute-start | bytes 294920 | tf_op jit(solution)/shard_map/ppermute | solution.py:211
  9.9 2.1 %collective-permute-start.4 = (bf16[64,768]{1,0:T(8,128)(2,1)S(1)}, bf16[64,768]{1,0:T(8,128)(2,1)S(1)}, u32[]{:S(2)}, u32[]{:S(2)}) collective-permute-start(bf16[64,768]{1,0:T(8,128)(2,1)S(1)} %get-tuple-element.27), channel_id=1, source_target_pairs={{0,8},{2,10},{4,12},{6,14},{8,0},{10,2},{12,4},{14,6},{1,9},{3,11}... | collective-permute-start | bytes 294920 | tf_op jit(solution)/shard_map/ppermute | solution.py:211
  12.0 0.0 collective-permute-done.refs_1_
  12.0 1.2 %collective-permute-start.1 = (bf16[64,1152]{1,0:T(8,128)(2,1)S(1)}, bf16[64,1152]{1,0:T(8,128)(2,1)S(1)}, u32[]{:S(2)}, u32[]{:S(2)}) collective-permute-start(bf16[64,1152]{1,0:T(8,128)(2,1)S(1)} %hold.3), channel_id=1, source_target_pairs={{0,4},{2,6},{4,0},{6,2},{8,12},{10,14},{12,8},{14,10},{1,5},{3,7},... | collective-permute-start | bytes 442376 | tf_op jit(solution)/shard_map/ppermute | solution.py:211
  13.3 0.0 collective-permute-done.5.refs_0_
  13.3 7.0 %collective-permute-start.2 = (bf16[64,1152]{1,0:T(8,128)(2,1)S(1)}, bf16[64,1152]{1,0:T(8,128)(2,1)S(1)}, u32[]{:S(2)}, u32[]{:S(2)}) collective-permute-start(bf16[64,1152]{1,0:T(8,128)(2,1)S(1)} %hold.4), channel_id=1, source_target_pairs={{0,6},{2,4},{4,2},{6,0},{8,14},{10,12},{12,10},{14,8},{1,7},{3,5},... | collective-permute-start | bytes 442376 | tf_op jit(solution)/shard_map/ppermute | solution.py:211
  20.3 0.0 collective-permute-done.6.refs_1_
  20.3 0.4 %collective-permute-done.1.refs_2_ = bf16[64,1152]{1,0:T(8,128)(2,1)S(1)} collective-permute-done((bf16[64,1152]{1,0:T(8,128)(2,1)S(1)}, bf16[64,1152]{1,0:T(8,128)(2,1)S(1)}, u32[]{:S(2)}, u32[]{:S(2)}) %collective-permute-start.1) | collective-permute-done | bytes 147488 | tf_op jit(solution)/shard_map/ppermute | solution.py:211
  20.7 6.1 %collective-permute-done.2.refs_3_ = bf16[64,1152]{1,0:T(8,128)(2,1)S(1)} collective-permute-done((bf16[64,1152]{1,0:T(8,128)(2,1)S(1)}, bf16[64,1152]{1,0:T(8,128)(2,1)S(1)}, u32[]{:S(2)}, u32[]{:S(2)}) %collective-permute-start.2) | collective-permute-done | bytes 147488 | tf_op jit(solution)/shard_map/ppermute | solution.py:211
  26.8 1.0 %first.1 = (f32[3,256,128]{2,1,0:T(8,128)S(1)}, f32[3,256,128]{2,1,0:T(8,128)S(1)}, f32[3,256,128]{2,1,0:T(8,128)S(1)}) custom-call(bf16[64,1152]{1,0:T(8,128)(2,1)S(1)} %get-tuple-element.22.refs_0_, bf16[64,1152]{1,0:T(8,128)(2,1)S(1)} %collective-permute-done.refs_1_, bf16[64,1152]{1,0:T(8,128)(2,1)S(1)} %collective-permute-done.1.refs_2_, ...), custom_call_target="tpu_custom_call" | custom-call | flops 150994944 | bytes 983040 | tf_op jit(solution)/shard_map/first/pallas_call | solution.py:229
  27.8 0.0 collective-permute-done.3.refs_4_
  27.8 0.0 collective-permute-done.4.refs_5_
  27.8 0.9 %last.1 = (bf16[64,384]{1,0:T(8,128)(2,1)S(1)}, bf16[64,384]{1,0:T(8,128)(2,1)S(1)}, bf16[64,384]{1,0:T(8,128)(2,1)S(1)}, bf16[64,384]{1,0:T(8,128)(2,1)S(1)}) custom-call(bf16[64,1152]{1,0:T(8,128)(2,1)S(1)} %get-tuple-element.22.refs_0_, bf16[64,1152]{1,0:T(8,128)(2,1)S(1)} %collective-permute-done.refs_1_, ...), custom_call_target="tpu_custom_call" | custom-call | flops 50331648 | bytes 589824 | tf_op jit(solution)/shard_map/last/pallas_call | solution.py:238
  28.8 0.1 collective-permute-start.7
  28.8 2.1 %collective-permute-start.8 = (bf16[64,384]{1,0:T(8,128)(2,1)S(1)}, bf16[64,384]{1,0:T(8,128)(2,1)S(1)}, u32[]{:S(2)}, u32[]{:S(2)}) collective-permute-start(bf16[64,384]{1,0:T(8,128)(2,1)S(1)} %get-tuple-element.36), channel_id=1, source_target_pairs={{0,4},{2,6},{4,0},{6,2},{8,12},{10,14},{12,8},{14,10},{1,5},{3,7},... | collective-permute-start | bytes 147464 | tf_op jit(solution)/shard_map/ppermute | solution.py:211
  30.9 1.4 %collective-permute-start.9 = (bf16[64,384]{1,0:T(8,128)(2,1)S(1)}, bf16[64,384]{1,0:T(8,128)(2,1)S(1)}, u32[]{:S(2)}, u32[]{:S(2)}) collective-permute-start(bf16[64,384]{1,0:T(8,128)(2,1)S(1)} %get-tuple-element.37), channel_id=1, source_target_pairs={{0,2},{2,0},{4,6},{6,4},{8,10},{10,8},{12,14},{14,12},{1,3},{3,1},... | collective-permute-start | bytes 147464 | tf_op jit(solution)/shard_map/ppermute | solution.py:211
  32.3 1.5 %collective-permute-done.7.refs_0_ = bf16[64,384]{1,0:T(8,128)(2,1)S(1)} collective-permute-done((bf16[64,384]{1,0:T(8,128)(2,1)S(1)}, bf16[64,384]{1,0:T(8,128)(2,1)S(1)}, u32[]{:S(2)}, u32[]{:S(2)}) %collective-permute-start.7) | collective-permute-done | bytes 49184 | tf_op jit(solution)/shard_map/ppermute | solution.py:211
  33.8 0.0 collective-permute-done.8.refs_1_
  33.8 1.2 %collective-permute-done.9.refs_2_ = bf16[64,384]{1,0:T(8,128)(2,1)S(1)} collective-permute-done((bf16[64,384]{1,0:T(8,128)(2,1)S(1)}, bf16[64,384]{1,0:T(8,128)(2,1)S(1)}, u32[]{:S(2)}, u32[]{:S(2)}) %collective-permute-start.9) | collective-permute-done | bytes 49184 | tf_op jit(solution)/shard_map/ppermute | solution.py:211
  35.0 0.7 %unpack.1 = bf16[1,64,1536]{2,1,0:T(8,128)(2,1)} custom-call(bf16[64,384]{1,0:T(8,128)(2,1)S(1)} %collective-permute-done.7.refs_0_, bf16[64,384]{1,0:T(8,128)(2,1)S(1)} %collective-permute-done.8.refs_1_, bf16[64,384]{1,0:T(8,128)(2,1)S(1)} %collective-permute-done.9.refs_2_, bf16[64,384]{1,0:T(8,128)(2,1)S(1)} %get-tuple-element.38.refs_3_), custom_call_target="tpu_custom_call" | custom-call | bytes 393216 | tf_op jit(solution)/shard_map/unpack/pallas_call | solution.py:250
  (3 shorter events, 0.0 us)
Async XLA Ops:
  1.4 10.7 %collective-permute-start = (bf16[64,1152]{1,0:T(8,128)(2,1)S(1)}, bf16[64,1152]{1,0:T(8,128)(2,1)S(1)}, u32[]{:S(2)}, u32[]{:S(2)}) collective-permute-start(bf16[64,1152]{1,0:T(8,128)(2,1)S(1)} %get-tuple-element.23), channel_id=1, source_target_pairs={{0,2},{2,0},{4,6},{6,4},{8,10},{10,8},{12,14},{14,12},{1,3},{3,1},... | collective-permute-start | bytes 442376 | tf_op jit(solution)/shard_map/ppermute | solution.py:211
  4.4 8.9 %collective-permute-start.5 = (bf16[64,768]{1,0:T(8,128)(2,1)S(1)}, bf16[64,768]{1,0:T(8,128)(2,1)S(1)}, u32[]{:S(2)}, u32[]{:S(2)}) collective-permute-start(bf16[64,768]{1,0:T(8,128)(2,1)S(1)} %get-tuple-element.28), channel_id=1, source_target_pairs={{0,14},{2,12},{4,10},{6,8},{8,6},{10,4},{12,2},{14,0},{1,15},{3,13... | collective-permute-start | bytes 294920 | tf_op jit(solution)/shard_map/ppermute | solution.py:211
  8.0 12.3 %collective-permute-start.6 = (bf16[64,768]{1,0:T(8,128)(2,1)S(1)}, bf16[64,768]{1,0:T(8,128)(2,1)S(1)}, u32[]{:S(2)}, u32[]{:S(2)}) collective-permute-start(bf16[64,768]{1,0:T(8,128)(2,1)S(1)} %get-tuple-element.29), channel_id=1, source_target_pairs={{0,12},{2,14},{4,8},{6,10},{8,4},{10,6},{12,0},{14,2},{1,13},{3,15... | collective-permute-start | bytes 294920 | tf_op jit(solution)/shard_map/ppermute | solution.py:211
  8.0 19.8 %collective-permute-start.3 = (bf16[64,768]{1,0:T(8,128)(2,1)S(1)}, bf16[64,768]{1,0:T(8,128)(2,1)S(1)}, u32[]{:S(2)}, u32[]{:S(2)}) collective-permute-start(bf16[64,768]{1,0:T(8,128)(2,1)S(1)} %get-tuple-element.26), channel_id=1, source_target_pairs={{0,10},{2,8},{4,14},{6,12},{8,2},{10,0},{12,6},{14,4},{1,11},{3,9}... | collective-permute-start | bytes 294920 | tf_op jit(solution)/shard_map/ppermute | solution.py:211
  9.9 17.9 %collective-permute-start.4 = (bf16[64,768]{1,0:T(8,128)(2,1)S(1)}, bf16[64,768]{1,0:T(8,128)(2,1)S(1)}, u32[]{:S(2)}, u32[]{:S(2)}) collective-permute-start(bf16[64,768]{1,0:T(8,128)(2,1)S(1)} %get-tuple-element.27), channel_id=1, source_target_pairs={{0,8},{2,10},{4,12},{6,14},{8,0},{10,2},{12,4},{14,6},{1,9},{3,11}... | collective-permute-start | bytes 294920 | tf_op jit(solution)/shard_map/ppermute | solution.py:211
  12.0 8.6 %collective-permute-start.1 = (bf16[64,1152]{1,0:T(8,128)(2,1)S(1)}, bf16[64,1152]{1,0:T(8,128)(2,1)S(1)}, u32[]{:S(2)}, u32[]{:S(2)}) collective-permute-start(bf16[64,1152]{1,0:T(8,128)(2,1)S(1)} %hold.3), channel_id=1, source_target_pairs={{0,4},{2,6},{4,0},{6,2},{8,12},{10,14},{12,8},{14,10},{1,5},{3,7},... | collective-permute-start | bytes 442376 | tf_op jit(solution)/shard_map/ppermute | solution.py:211
  13.3 13.5 %collective-permute-start.2 = (bf16[64,1152]{1,0:T(8,128)(2,1)S(1)}, bf16[64,1152]{1,0:T(8,128)(2,1)S(1)}, u32[]{:S(2)}, u32[]{:S(2)}) collective-permute-start(bf16[64,1152]{1,0:T(8,128)(2,1)S(1)} %hold.4), channel_id=1, source_target_pairs={{0,6},{2,4},{4,2},{6,0},{8,14},{10,12},{12,10},{14,8},{1,7},{3,5},... | collective-permute-start | bytes 442376 | tf_op jit(solution)/shard_map/ppermute | solution.py:211
  28.8 5.1 %collective-permute-start.7 = (bf16[64,384]{1,0:T(8,128)(2,1)S(1)}, bf16[64,384]{1,0:T(8,128)(2,1)S(1)}, u32[]{:S(2)}, u32[]{:S(2)}) collective-permute-start(bf16[64,384]{1,0:T(8,128)(2,1)S(1)} %get-tuple-element.35), channel_id=1, source_target_pairs={{0,6},{2,4},{4,2},{6,0},{8,14},{10,12},{12,10},{14,8},{1,7},{3,5},... | collective-permute-start | bytes 147464 | tf_op jit(solution)/shard_map/ppermute | solution.py:211
  28.8 5.0 %collective-permute-start.8 = (bf16[64,384]{1,0:T(8,128)(2,1)S(1)}, bf16[64,384]{1,0:T(8,128)(2,1)S(1)}, u32[]{:S(2)}, u32[]{:S(2)}) collective-permute-start(bf16[64,384]{1,0:T(8,128)(2,1)S(1)} %get-tuple-element.36), channel_id=1, source_target_pairs={{0,4},{2,6},{4,0},{6,2},{8,12},{10,14},{12,8},{14,10},{1,5},{3,7},... | collective-permute-start | bytes 147464 | tf_op jit(solution)/shard_map/ppermute | solution.py:211
  30.9 4.1 %collective-permute-start.9 = (bf16[64,384]{1,0:T(8,128)(2,1)S(1)}, bf16[64,384]{1,0:T(8,128)(2,1)S(1)}, u32[]{:S(2)}, u32[]{:S(2)}) collective-permute-start(bf16[64,384]{1,0:T(8,128)(2,1)S(1)} %get-tuple-element.37), channel_id=1, source_target_pairs={{0,2},{2,0},{4,6},{6,4},{8,10},{10,8},{12,14},{14,12},{1,3},{3,1},... | collective-permute-start | bytes 147464 | tf_op jit(solution)/shard_map/ppermute | solution.py:211

commit v9 on v7

--- a/solution.py
+++ b/solution.py
@@ -9,7 +9,7 @@
 from jax.sharding import PartitionSpec as P
 
 HD = 128
-EFFORT = 10**8
+EFFORT = 10**9
 ANY = pl.BlockSpec(memory_space=pl.ANY)
 HBM = pl.BlockSpec(memory_space=pltpu.HBM)
 VMEM = pl.BlockSpec(memory_space=pltpu.VMEM)
@@ -150,22 +150,23 @@
         lanes = slice(first, first + HD)
         return ins[source][:, lanes] if row is None else ins[source][row, :, lanes]
 
-    for head, all_places in enumerate(plan):
-        queries, keys, values = (
-            jnp.concatenate([load(place) for place in places], axis=0) for places in all_places
+    def rows(places):
+        return jnp.concatenate([load(place) for place in places], axis=0)
+
+    scores = [
+        lax.dot_general(
+            rows(queries), rows(keys), (((1,), (1,)), ((), ())), preferred_element_type=jnp.float32
         )
-        scores = (
-            lax.dot_general(
-                queries, keys, (((1,), (1,)), ((), ())), preferred_element_type=jnp.float32
-            )
-            * scale
-        )
-        weights = jnp.exp(scores - jnp.max(scores, axis=1, keepdims=True))
-        totals = jnp.sum(weights, axis=1, keepdims=True)
-        mixed = jnp.dot(
-            weights.astype(jnp.bfloat16), values, preferred_element_type=jnp.float32
-        )
-        result = (mixed / totals).astype(jnp.bfloat16)
+        * scale
+        for queries, keys, values in plan
+    ]
+    weights = [jnp.exp(s - jnp.max(s, axis=1, keepdims=True)) for s in scores]
+    mixed = [
+        jnp.dot(w.astype(jnp.bfloat16), rows(values), preferred_element_type=jnp.float32)
+        for w, (queries, keys, values) in zip(weights, plan)
+    ]
+    for head, (w, m) in enumerate(zip(weights, mixed)):
+        result = (m / jnp.sum(w, axis=1, keepdims=True)).astype(jnp.bfloat16)
         for block, ref in enumerate(out_refs):
             ref[:, head * HD : (head + 1) * HD] = result[block * tokens : (block + 1) * tokens]
 
@@ -217,18 +218,19 @@
     far_kv = [to_block(sent[s, kv], s) for s in far]
     near_kvq = to_block(sent[1, kv + q], 1)
     near_kv = join([own_kv, near_kvq], [0, 0], 2 * part)
-    far_q = [to_block(hold(sent[s, q], near_kv), s) for s in far]
     groups = [near_kv, join(far_kv, [0] * len(far), 2 * part)]
+    far_q = [to_block(hold(sent[s, q], far_kv[0] if s == far[0] else groups[1]), s) for s in far]
     crossed = [to_column(group, t) for group in groups for t in range(1, columns_of)]
-    far_q = join(far_q, [0] * len(far), part)
+    far_q[0] = join(far_q[:1], [0], part, EFFORT)
     near_q = join([own_q, near_kvq], [0, 2 * part], part, EFFORT, crossed[: columns_of - 1])
-    arrays = [near_q, far_q, near_kvq, own_kv] + far_kv
-    key_places = [(at, None, 0) for at in range(2, len(arrays))]
+    arrays = [near_q] + far_q
+    query_places = [(0, 0, 0), (0, 1, 0)]
+    query_places += [(1 + far.index(s), 0 if s == far[0] else None, 0) for s in range(2, blocks)]
+    key_places = [(len(arrays) + at, None, 0) for at in range(blocks)]
+    arrays += [near_kvq, own_kv] + far_kv
     for array in crossed:
         key_places += [(len(arrays), at, 0) for at in range(array.shape[0])]
         arrays.append(array)
-    query_places = [(0, 0, 0), (0, 1, 0)]
-    query_places += [(1, far.index(s), 0) for s in range(2, blocks)]
 
     def moved(places, lanes):
         return [(source, row, first + lanes) for source, row, first in places]

time: 34 us -> 33.2 us (0.976)
  starting transfers between devices: 15.8 us -> 15.3 us
    ppermute x8, starting transfers between devices: 12.7 us -> 12.2 us  [to_block(): return lax.ppermute(array, 'blk', [(i, i ^ s) for i in range(blocks)])]
where the time goes in v9:
time: 33.2 us; the launch traced here: 33 us
  starting transfers between devices  15.3 us (46%)
  waiting for transfers between devices  14.9 us (45%)
  Pallas kernels  2.67 us (8%)
    ppermute x8, waiting for transfers between devices, to_block(): return lax.ppermute(array, 'blk', [(i, i ^ s) for i in range(blocks)])  14.9 us
    ppermute x8, starting transfers between devices, to_block(): return lax.ppermute(array, 'blk', [(i, i ^ s) for i in range(blocks)])  12.2 us
    ppermute x2, starting transfers between devices, to_column(): lax.ppermute(array, 'uly', [(i, (i + t) % columns_of) for i in range(colu...  3.11 us
    pallas_call x1, Pallas kernels, local_blocks(): pl.pallas_call(functools.partial(pack_kernel, messages, part), out_shape=...  1.17 us
    pallas_call x1, Pallas kernels, local_blocks(): pl.pallas_call(functools.partial(attend_kernel, plan), out_shape=[jax.Sha...  0.76 us
    pallas_call x1, Pallas kernels, local_blocks(): pl.pallas_call(functools.partial(unpack_kernel, order, part), out_shape=j...  0.7 us
  transfers between devices with their start and end apart: 10, of which 7 were waited for; matrix products, arithmetic and copies ran while one was open for 0% of the time, Pallas kernels for 0%

profile of v9, /device:TPU:0, one launch (start us, length us, event | category | flops | bytes accessed | tf_op | source)
XLA Modules:
  0.0 33.0 jit_solution(7275199298595424857)
XLA Ops:
  0.0 1.2 %pack.1 = (bf16[64,768]{1,0:T(8,128)(2,1)S(1)}, bf16[64,768]{1,0:T(8,128)(2,1)S(1)}, bf16[64,1152]{1,0:T(8,128)(2,1)S(1)}, bf16[64,384]{1,0:T(8,128)(2,1)S(1)}, ...) custom-call(bf16[1,64,1536]{2,1,0:T(8,128)(2,1)} %q_ref.1, ...), custom_call_target="tpu_custom_call" | custom-call | bytes 1179648 | tf_op jit(solution)/shard_map/pack/pallas_call | solution.py:194
  1.2 3.1 %collective-permute-start = (bf16[64,1152]{1,0:T(8,128)(2,1)S(1)}, bf16[64,1152]{1,0:T(8,128)(2,1)S(1)}, u32[]{:S(2)}, u32[]{:S(2)}) collective-permute-start(bf16[64,1152]{1,0:T(8,128)(2,1)S(1)} %get-tuple-element.17), channel_id=1, source_target_pairs={{0,4},{4,0},{8,12},{12,8},{1,5},{5,1},{9,13},{13,9},{2,6},{6,2},{1... | collective-permute-start | bytes 442376 | tf_op jit(solution)/shard_map/ppermute | solution.py:211
  4.3 2.5 %collective-permute-start.2 = (bf16[64,768]{1,0:T(8,128)(2,1)S(1)}, bf16[64,768]{1,0:T(8,128)(2,1)S(1)}, u32[]{:S(2)}, u32[]{:S(2)}) collective-permute-start(bf16[64,768]{1,0:T(8,128)(2,1)S(1)} %get-tuple-element.20), channel_id=1, source_target_pairs={{0,12},{4,8},{8,4},{12,0},{1,13},{5,9},{9,5},{13,1},{2,14},{6,10},... | collective-permute-start | bytes 294920 | tf_op jit(solution)/shard_map/ppermute | solution.py:211
  6.7 0.1 collective-permute-start.4
  6.9 1.5 %collective-permute-done.refs_1_.refs_3_ = bf16[64,1152]{1,0:T(8,128)(2,1)S(1)} collective-permute-done((bf16[64,1152]{1,0:T(8,128)(2,1)S(1)}, bf16[64,1152]{1,0:T(8,128)(2,1)S(1)}, u32[]{:S(2)}, u32[]{:S(2)}) %collective-permute-start) | collective-permute-done | bytes 147488 | tf_op jit(solution)/shard_map/ppermute | solution.py:211
  8.3 1.6 %collective-permute-start.1 = (bf16[2,64,768]{2,1,0:T(8,128)(2,1)S(1)}, bf16[2,64,768]{2,1,0:T(8,128)(2,1)S(1)}, u32[]{:S(2)}, u32[]{:S(2)}) collective-permute-start(bf16[2,64,768]{2,1,0:T(8,128)(2,1)S(1)} %join.4), channel_id=1, source_target_pairs={{0,2},{2,0},{1,3},{3,1},{4,6},{6,4},{5,7},{7,5},{8,10},{10,8},{9,1... | collective-permute-start | bytes 589832 | tf_op jit(solution)/shard_map/ppermute | solution.py:214
  9.9 3.7 %collective-permute-done.2.until_ref.refs_0_.refs_5_ = bf16[64,768]{1,0:T(8,128)(2,1)S(1)} collective-permute-done((bf16[64,768]{1,0:T(8,128)(2,1)S(1)}, bf16[64,768]{1,0:T(8,128)(2,1)S(1)}, u32[]{:S(2)}, u32[]{:S(2)}) %collective-permute-start.2) | collective-permute-done | bytes 98336 | tf_op jit(solution)/shard_map/ppermute | solution.py:211
  13.6 2.1 %collective-permute-start.3 = (bf16[64,384]{1,0:T(8,128)(2,1)S(1)}, bf16[64,384]{1,0:T(8,128)(2,1)S(1)}, u32[]{:S(2)}, u32[]{:S(2)}) collective-permute-start(bf16[64,384]{1,0:T(8,128)(2,1)S(1)} %hold.2), channel_id=1, source_target_pairs={{0,12},{4,8},{8,4},{12,0},{1,13},{5,9},{9,5},{13,1},{2,14},{6,10},... | collective-permute-start | bytes 147464 | tf_op jit(solution)/shard_map/ppermute | solution.py:211
  15.6 1.2 %collective-permute-done.4.refs_1_.refs_6_ = bf16[64,768]{1,0:T(8,128)(2,1)S(1)} collective-permute-done((bf16[64,768]{1,0:T(8,128)(2,1)S(1)}, bf16[64,768]{1,0:T(8,128)(2,1)S(1)}, u32[]{:S(2)}, u32[]{:S(2)}) %collective-permute-start.4) | collective-permute-done | bytes 98336 | tf_op jit(solution)/shard_map/ppermute | solution.py:211
  16.8 1.6 %collective-permute-start.6 = (bf16[2,64,768]{2,1,0:T(8,128)(2,1)S(1)}, bf16[2,64,768]{2,1,0:T(8,128)(2,1)S(1)}, u32[]{:S(2)}, u32[]{:S(2)}) collective-permute-start(bf16[2,64,768]{2,1,0:T(8,128)(2,1)S(1)} %join.7.until_ref), channel_id=1, source_target_pairs={{0,2},{2,0},{1,3},{3,1},{4,6},{6,4},{5,7},{7,5},{8,10},{10,8},{9,1... | collective-permute-start | bytes 589832 | tf_op jit(solution)/shard_map/ppermute | solution.py:214
  18.4 0.0 collective-permute-start.5
  18.4 1.4 %collective-permute-done.3.refs_0_ = bf16[64,384]{1,0:T(8,128)(2,1)S(1)} collective-permute-done((bf16[64,384]{1,0:T(8,128)(2,1)S(1)}, bf16[64,384]{1,0:T(8,128)(2,1)S(1)}, u32[]{:S(2)}, u32[]{:S(2)}) %collective-permute-start.3) | collective-permute-done | bytes 49184 | tf_op jit(solution)/shard_map/ppermute | solution.py:211
  19.8 0.0 collective-permute-done.1.refs_2_.refs_7_
  19.8 4.1 %collective-permute-done.5.refs_2_ = bf16[64,384]{1,0:T(8,128)(2,1)S(1)} collective-permute-done((bf16[64,384]{1,0:T(8,128)(2,1)S(1)}, bf16[64,384]{1,0:T(8,128)(2,1)S(1)}, u32[]{:S(2)}, u32[]{:S(2)}) %collective-permute-start.5) | collective-permute-done | bytes 49184 | tf_op jit(solution)/shard_map/ppermute | solution.py:211
  23.9 0.0 collective-permute-done.6.refs_8_
  23.9 0.8 %attend.1 = (bf16[64,384]{1,0:T(8,128)(2,1)S(1)}, bf16[64,384]{1,0:T(8,128)(2,1)S(1)}, bf16[64,384]{1,0:T(8,128)(2,1)S(1)}, bf16[64,384]{1,0:T(8,128)(2,1)S(1)}) custom-call(bf16[2,64,384]{2,1,0:T(8,128)(2,1)S(1)} %join.5.refs_0_, bf16[1,64,384]{2,1,0:T(8,128)(2,1)S(1)} %join.6.refs_1_, bf16[64,384]{1,0:T(8,128)(2,1)S(1)} %collective-permute-done.5.refs_2_, ...), custom_call_target="tpu_custom_call" | custom-call | flops 201326592 | bytes 1179648 | tf_op jit(solution)/shard_map/attend/pallas_call | solution.py:245
  24.7 2.6 %collective-permute-start.7 = (bf16[64,384]{1,0:T(8,128)(2,1)S(1)}, bf16[64,384]{1,0:T(8,128)(2,1)S(1)}, u32[]{:S(2)}, u32[]{:S(2)}) collective-permute-start(bf16[64,384]{1,0:T(8,128)(2,1)S(1)} %get-tuple-element.24), channel_id=1, source_target_pairs={{0,12},{4,8},{8,4},{12,0},{1,13},{5,9},{9,5},{13,1},{2,14},{6,10},... | collective-permute-start | bytes 147464 | tf_op jit(solution)/shard_map/ppermute | solution.py:211
  27.3 0.0 collective-permute-start.8
  27.3 1.9 %collective-permute-start.9 = (bf16[64,384]{1,0:T(8,128)(2,1)S(1)}, bf16[64,384]{1,0:T(8,128)(2,1)S(1)}, u32[]{:S(2)}, u32[]{:S(2)}) collective-permute-start(bf16[64,384]{1,0:T(8,128)(2,1)S(1)} %get-tuple-element.26), channel_id=1, source_target_pairs={{0,4},{4,0},{8,12},{12,8},{1,5},{5,1},{9,13},{13,9},{2,6},{6,2},{1... | collective-permute-start | bytes 147464 | tf_op jit(solution)/shard_map/ppermute | solution.py:211
  29.1 1.5 %collective-permute-done.7.refs_1_ = bf16[64,384]{1,0:T(8,128)(2,1)S(1)} collective-permute-done((bf16[64,384]{1,0:T(8,128)(2,1)S(1)}, bf16[64,384]{1,0:T(8,128)(2,1)S(1)}, u32[]{:S(2)}, u32[]{:S(2)}) %collective-permute-start.7) | collective-permute-done | bytes 49184 | tf_op jit(solution)/shard_map/ppermute | solution.py:211
  30.6 1.6 %collective-permute-done.8.refs_2_ = bf16[64,384]{1,0:T(8,128)(2,1)S(1)} collective-permute-done((bf16[64,384]{1,0:T(8,128)(2,1)S(1)}, bf16[64,384]{1,0:T(8,128)(2,1)S(1)}, u32[]{:S(2)}, u32[]{:S(2)}) %collective-permute-start.8) | collective-permute-done | bytes 49184 | tf_op jit(solution)/shard_map/ppermute | solution.py:211
  32.3 0.0 collective-permute-done.9.refs_3_
  32.3 0.7 %unpack.1 = bf16[1,64,1536]{2,1,0:T(8,128)(2,1)} custom-call(bf16[64,384]{1,0:T(8,128)(2,1)S(1)} %get-tuple-element.23.refs_0_, bf16[64,384]{1,0:T(8,128)(2,1)S(1)} %collective-permute-done.7.refs_1_, bf16[64,384]{1,0:T(8,128)(2,1)S(1)} %collective-permute-done.8.refs_2_, bf16[64,384]{1,0:T(8,128)(2,1)S(1)} %collective-permute-done.9.refs_3_), custom_call_target="tpu_custom_call" | custom-call | bytes 393216 | tf_op jit(solution)/shard_map/unpack/pallas_call | solution.py:261
  (6 shorter events, 0.0 us)
Async XLA Ops:
  1.2 7.2 %collective-permute-start = (bf16[64,1152]{1,0:T(8,128)(2,1)S(1)}, bf16[64,1152]{1,0:T(8,128)(2,1)S(1)}, u32[]{:S(2)}, u32[]{:S(2)}) collective-permute-start(bf16[64,1152]{1,0:T(8,128)(2,1)S(1)} %get-tuple-element.17), channel_id=1, source_target_pairs={{0,4},{4,0},{8,12},{12,8},{1,5},{5,1},{9,13},{13,9},{2,6},{6,2},{1... | collective-permute-start | bytes 442376 | tf_op jit(solution)/shard_map/ppermute | solution.py:211
  4.3 9.3 %collective-permute-start.2 = (bf16[64,768]{1,0:T(8,128)(2,1)S(1)}, bf16[64,768]{1,0:T(8,128)(2,1)S(1)}, u32[]{:S(2)}, u32[]{:S(2)}) collective-permute-start(bf16[64,768]{1,0:T(8,128)(2,1)S(1)} %get-tuple-element.20), channel_id=1, source_target_pairs={{0,12},{4,8},{8,4},{12,0},{1,13},{5,9},{9,5},{13,1},{2,14},{6,10},... | collective-permute-start | bytes 294920 | tf_op jit(solution)/shard_map/ppermute | solution.py:211
  6.7 10.1 %collective-permute-start.4 = (bf16[64,768]{1,0:T(8,128)(2,1)S(1)}, bf16[64,768]{1,0:T(8,128)(2,1)S(1)}, u32[]{:S(2)}, u32[]{:S(2)}) collective-permute-start(bf16[64,768]{1,0:T(8,128)(2,1)S(1)} %get-tuple-element.22), channel_id=1, source_target_pairs={{0,8},{4,12},{8,0},{12,4},{1,9},{5,13},{9,1},{13,5},{2,10},{6,14},... | collective-permute-start | bytes 294920 | tf_op jit(solution)/shard_map/ppermute | solution.py:211
  8.3 11.4 %collective-permute-start.1 = (bf16[2,64,768]{2,1,0:T(8,128)(2,1)S(1)}, bf16[2,64,768]{2,1,0:T(8,128)(2,1)S(1)}, u32[]{:S(2)}, u32[]{:S(2)}) collective-permute-start(bf16[2,64,768]{2,1,0:T(8,128)(2,1)S(1)} %join.4), channel_id=1, source_target_pairs={{0,2},{2,0},{1,3},{3,1},{4,6},{6,4},{5,7},{7,5},{8,10},{10,8},{9,1... | collective-permute-start | bytes 589832 | tf_op jit(solution)/shard_map/ppermute | solution.py:214
  13.6 6.2 %collective-permute-start.3 = (bf16[64,384]{1,0:T(8,128)(2,1)S(1)}, bf16[64,384]{1,0:T(8,128)(2,1)S(1)}, u32[]{:S(2)}, u32[]{:S(2)}) collective-permute-start(bf16[64,384]{1,0:T(8,128)(2,1)S(1)} %hold.2), channel_id=1, source_target_pairs={{0,12},{4,8},{8,4},{12,0},{1,13},{5,9},{9,5},{13,1},{2,14},{6,10},... | collective-permute-start | bytes 147464 | tf_op jit(solution)/shard_map/ppermute | solution.py:211
  16.8 7.1 %collective-permute-start.6 = (bf16[2,64,768]{2,1,0:T(8,128)(2,1)S(1)}, bf16[2,64,768]{2,1,0:T(8,128)(2,1)S(1)}, u32[]{:S(2)}, u32[]{:S(2)}) collective-permute-start(bf16[2,64,768]{2,1,0:T(8,128)(2,1)S(1)} %join.7.until_ref), channel_id=1, source_target_pairs={{0,2},{2,0},{1,3},{3,1},{4,6},{6,4},{5,7},{7,5},{8,10},{10,8},{9,1... | collective-permute-start | bytes 589832 | tf_op jit(solution)/shard_map/ppermute | solution.py:214
  18.4 5.5 %collective-permute-start.5 = (bf16[64,384]{1,0:T(8,128)(2,1)S(1)}, bf16[64,384]{1,0:T(8,128)(2,1)S(1)}, u32[]{:S(2)}, u32[]{:S(2)}) collective-permute-start(bf16[64,384]{1,0:T(8,128)(2,1)S(1)} %hold.3), channel_id=1, source_target_pairs={{0,8},{4,12},{8,0},{12,4},{1,9},{5,13},{9,1},{13,5},{2,10},{6,14},... | collective-permute-start | bytes 147464 | tf_op jit(solution)/shard_map/ppermute | solution.py:211
  24.7 6.0 %collective-permute-start.7 = (bf16[64,384]{1,0:T(8,128)(2,1)S(1)}, bf16[64,384]{1,0:T(8,128)(2,1)S(1)}, u32[]{:S(2)}, u32[]{:S(2)}) collective-permute-start(bf16[64,384]{1,0:T(8,128)(2,1)S(1)} %get-tuple-element.24), channel_id=1, source_target_pairs={{0,12},{4,8},{8,4},{12,0},{1,13},{5,9},{9,5},{13,1},{2,14},{6,10},... | collective-permute-start | bytes 147464 | tf_op jit(solution)/shard_map/ppermute | solution.py:211
  27.3 5.0 %collective-permute-start.8 = (bf16[64,384]{1,0:T(8,128)(2,1)S(1)}, bf16[64,384]{1,0:T(8,128)(2,1)S(1)}, u32[]{:S(2)}, u32[]{:S(2)}) collective-permute-start(bf16[64,384]{1,0:T(8,128)(2,1)S(1)} %get-tuple-element.25), channel_id=1, source_target_pairs={{0,8},{4,12},{8,0},{12,4},{1,9},{5,13},{9,1},{13,5},{2,10},{6,14},... | collective-permute-start | bytes 147464 | tf_op jit(solution)/shard_map/ppermute | solution.py:211
  27.3 5.0 %collective-permute-start.9 = (bf16[64,384]{1,0:T(8,128)(2,1)S(1)}, bf16[64,384]{1,0:T(8,128)(2,1)S(1)}, u32[]{:S(2)}, u32[]{:S(2)}) collective-permute-start(bf16[64,384]{1,0:T(8,128)(2,1)S(1)} %get-tuple-element.26), channel_id=1, source_target_pairs={{0,4},{4,0},{8,12},{12,8},{1,5},{5,1},{9,13},{13,9},{2,6},{6,2},{1... | collective-permute-start | bytes 147464 | tf_op jit(solution)/shard_map/ppermute | solution.py:211

commit v10 on v9

--- a/solution.py
+++ b/solution.py
@@ -123,52 +123,60 @@
     )(*arrays, *after)
 
 
-def hold_kernel(array_ref, until_ref, out_ref):
+def hold_kernel(*refs):
     pass
 
 
-def hold(array, until):
+def hold(arrays, until=(), effort=0):
     return pl.pallas_call(
         hold_kernel,
-        out_shape=jax.ShapeDtypeStruct(array.shape, array.dtype),
-        in_specs=[ANY, ANY],
-        out_specs=ANY,
-        input_output_aliases={0: 0},
-        compiler_params=SMALL,
+        out_shape=[jax.ShapeDtypeStruct(array.shape, array.dtype) for array in arrays],
+        in_specs=[ANY] * (len(arrays) + len(until)),
+        out_specs=[ANY] * len(arrays),
+        input_output_aliases={at: at for at in range(len(arrays))},
+        compiler_params=SMALL,
+        cost_estimate=pl.CostEstimate(flops=effort, bytes_accessed=0, transcendentals=0),
         name="hold",
-    )(array, until)
-
-
-def attend_kernel(plan, *refs):
-    blocks = len(plan[0][0])
-    ins, out_refs = refs[:-blocks], refs[-blocks:]
-    tokens = out_refs[0].shape[0]
+    )(*arrays, *until)
+
+
+def attend_kernel(held, keys, queries, *refs):
+    key_refs, query_refs, out_refs = refs[:held], refs[held : -len(queries)], refs[-len(queries) :]
+    tokens, part = out_refs[0].shape
     scale = 1.0 / math.sqrt(HD)
 
-    def load(place):
-        source, row, first = place
+    def rows(sources, places, first):
         lanes = slice(first, first + HD)
-        return ins[source][:, lanes] if row is None else ins[source][row, :, lanes]
-
-    def rows(places):
-        return jnp.concatenate([load(place) for place in places], axis=0)
-
+        pieces = [
+            sources[at][:, lanes] if row is None else sources[at][row, :, lanes]
+            for at, row in places
+        ]
+        return jnp.concatenate(pieces, axis=0)
+
+    lanes = range(0, part, HD)
     scores = [
         lax.dot_general(
-            rows(queries), rows(keys), (((1,), (1,)), ((), ())), preferred_element_type=jnp.float32
+            rows(query_refs, queries, lane),
+            rows(key_refs, keys, lane),
+            (((1,), (1,)), ((), ())),
+            preferred_element_type=jnp.float32,
         )
         * scale
-        for queries, keys, values in plan
+        for lane in lanes
     ]
     weights = [jnp.exp(s - jnp.max(s, axis=1, keepdims=True)) for s in scores]
     mixed = [
-        jnp.dot(w.astype(jnp.bfloat16), rows(values), preferred_element_type=jnp.float32)
-        for w, (queries, keys, values) in zip(weights, plan)
+        jnp.dot(
+            w.astype(jnp.bfloat16),
+            rows(key_refs, keys, part + lane),
+            preferred_element_type=jnp.float32,
+        )
+        for w, lane in zip(weights, lanes)
     ]
-    for head, (w, m) in enumerate(zip(weights, mixed)):
+    for w, m, lane in zip(weights, mixed, lanes):
         result = (m / jnp.sum(w, axis=1, keepdims=True)).astype(jnp.bfloat16)
         for block, ref in enumerate(out_refs):
-            ref[:, head * HD : (head + 1) * HD] = result[block * tokens : (block + 1) * tokens]
+            ref[:, lane : lane + HD] = result[block * tokens : (block + 1) * tokens]
 
 
 def unpack_kernel(order, part, *refs):
@@ -219,45 +227,43 @@
     near_kvq = to_block(sent[1, kv + q], 1)
     near_kv = join([own_kv, near_kvq], [0, 0], 2 * part)
     groups = [near_kv, join(far_kv, [0] * len(far), 2 * part)]
-    far_q = [to_block(hold(sent[s, q], far_kv[0] if s == far[0] else groups[1]), s) for s in far]
+    far_q = [to_block(hold([sent[s, q]], [far_kv[0] if s == far[0] else groups[1]])[0], s) for s in far]
     crossed = [to_column(group, t) for group in groups for t in range(1, columns_of)]
     far_q[0] = join(far_q[:1], [0], part, EFFORT)
     near_q = join([own_q, near_kvq], [0, 2 * part], part, EFFORT, crossed[: columns_of - 1])
-    arrays = [near_q] + far_q
-    query_places = [(0, 0, 0), (0, 1, 0)]
-    query_places += [(1 + far.index(s), 0 if s == far[0] else None, 0) for s in range(2, blocks)]
-    key_places = [(len(arrays) + at, None, 0) for at in range(blocks)]
-    arrays += [near_kvq, own_kv] + far_kv
+
+    holders = [near_kvq, own_kv] + far_kv
+    keys = [(at, None) for at in range(len(holders))]
     for array in crossed:
-        key_places += [(len(arrays), at, 0) for at in range(array.shape[0])]
-        arrays.append(array)
-
-    def moved(places, lanes):
-        return [(source, row, first + lanes) for source, row, first in places]
-
-    plan = [
-        (moved(query_places, lane), moved(key_places, lane), moved(key_places, part + lane))
-        for lane in range(0, part, HD)
-    ]
-    all_tokens = tokens * blocks * columns_of
-
-    pairs = heads * tokens * blocks * all_tokens
-    mixed = pl.pallas_call(
-        functools.partial(attend_kernel, plan),
-        out_shape=[jax.ShapeDtypeStruct((tokens, part), kind)] * blocks,
-        in_specs=[VMEM] * len(arrays),
-        out_specs=[VMEM] * blocks,
-        compiler_params=pltpu.CompilerParams(vmem_limit_bytes=24 * 1024 * 1024),
-        cost_estimate=pl.CostEstimate(
-            flops=4 * HD * pairs,
-            bytes_accessed=4 * part * (all_tokens + tokens * blocks),
-            transcendentals=pairs,
-        ),
-        name="attend",
-    )(*arrays)
-
+        keys += [(len(holders), at) for at in range(array.shape[0])]
+        holders.append(array)
+
+    def attend(query_arrays, query_places):
+        rows = tokens * len(query_places)
+        pairs = heads * rows * tokens * len(keys)
+        return pl.pallas_call(
+            functools.partial(attend_kernel, len(holders), keys, query_places),
+            out_shape=[jax.ShapeDtypeStruct((tokens, part), kind)] * len(query_places),
+            in_specs=[VMEM] * (len(holders) + len(query_arrays)),
+            out_specs=[VMEM] * len(query_places),
+            compiler_params=pltpu.CompilerParams(vmem_limit_bytes=24 * 1024 * 1024),
+            cost_estimate=pl.CostEstimate(
+                flops=4 * HD * pairs,
+                bytes_accessed=4 * part * (rows + tokens * len(keys)),
+                transcendentals=pairs,
+            ),
+            name="attend",
+        )(*holders, *query_arrays)
+
+    mixed = dict(zip([0, 1] + far[:-1], attend([near_q] + far_q[:-1], [(0, 0), (0, 1), (1, 0)])))
+    last_q = hold([far_q[-1]], [mixed[0]])
+    mixed[far[-1]] = attend(last_q, [(0, None)])[0]
+    back = {s: to_block(mixed[s], s) for s in far + [1]}
+    early = [1] + far[:-1]
+    back.update(zip(early, hold([back[s] for s in early], effort=EFFORT)))
+    back[0] = mixed[0]
     order = [0] + far + [1]
-    back = [to_block(mixed[s], s) if s else mixed[0] for s in order]
+    back = [back[s] for s in order]
     return pl.pallas_call(
         functools.partial(unpack_kernel, order, part),
         out_shape=jax.ShapeDtypeStruct((1, tokens, width), kind),

time: 33.2 us -> 32.4 us (0.976)
  starting transfers between devices: 15.3 us -> 14.5 us
  Pallas kernels: 2.67 us -> 3.05 us
    ppermute x8, waiting for transfers between devices: 14.9 us -> 11.8 us  [to_block(): return lax.ppermute(array, 'blk', [(i, i ^ s) for i in range(blocks)])]
    ppermute x2, waiting for transfers between devices: 0.01 us -> 2.78 us  [to_column(): lax.ppermute(array, 'uly', [(i, (i + t) % columns_of) for i in range(colu...]
    ppermute x8, starting transfers between devices: 12.2 us -> 11.4 us  [to_block(): return lax.ppermute(array, 'blk', [(i, i ^ s) for i in range(blocks)])]
    pallas_call x3 -> x6, Pallas kernels: 0.76 us -> 1.13 us  [the longest x2 1.13 us: attend(): pl.pallas_call(functools.partial(attend_kernel, len(holders), keys, query...]
  transfers between devices with their start and end apart: 10 -> 10, of which waited for: 7 -> 8; matrix products, arithmetic and copies ran while one was open for 0% -> 0% of each run, Pallas kernels for 0% -> 4%
where the time goes in v10:
time: 32.4 us; the launch traced here: 32.2 us
  waiting for transfers between devices  14.6 us (45%)
  starting transfers between devices  14.5 us (45%)
  Pallas kernels  3.05 us (9%)
    ppermute x8, waiting for transfers between devices, to_block(): return lax.ppermute(array, 'blk', [(i, i ^ s) for i in range(blocks)])  11.8 us
    ppermute x8, starting transfers between devices, to_block(): return lax.ppermute(array, 'blk', [(i, i ^ s) for i in range(blocks)])  11.4 us
    ppermute x2, starting transfers between devices, to_column(): lax.ppermute(array, 'uly', [(i, (i + t) % columns_of) for i in range(colu...  3.11 us
    ppermute x2, waiting for transfers between devices, to_column(): lax.ppermute(array, 'uly', [(i, (i + t) % columns_of) for i in range(colu...  2.78 us
    pallas_call x1, Pallas kernels, local_blocks(): pl.pallas_call(functools.partial(pack_kernel, messages, part), out_shape=...  1.17 us
    pallas_call x2, Pallas kernels, attend(): pl.pallas_call(functools.partial(attend_kernel, len(holders), keys, query...  1.13 us
    pallas_call x1, Pallas kernels, local_blocks(): pl.pallas_call(functools.partial(unpack_kernel, order, part), out_shape=j...  0.7 us
  transfers between devices with their start and end apart: 10, of which 8 were waited for; matrix products, arithmetic and copies ran while one was open for 0% of the time, Pallas kernels for 4%

profile of v10, /device:TPU:0, one launch (start us, length us, event | category | flops | bytes accessed | tf_op | source)
XLA Modules:
  0.0 32.2 jit_solution(10855062971064268161)
XLA Ops:
  0.0 1.2 %pack.1 = (bf16[64,768]{1,0:T(8,128)(2,1)S(1)}, bf16[64,768]{1,0:T(8,128)(2,1)S(1)}, bf16[64,1152]{1,0:T(8,128)(2,1)S(1)}, bf16[64,384]{1,0:T(8,128)(2,1)S(1)}, ...) custom-call(bf16[1,64,1536]{2,1,0:T(8,128)(2,1)} %q_ref.1, ...), custom_call_target="tpu_custom_call" | custom-call | bytes 1179648 | tf_op jit(solution)/shard_map/pack/pallas_call | solution.py:202
  1.2 3.1 %collective-permute-start = (bf16[64,1152]{1,0:T(8,128)(2,1)S(1)}, bf16[64,1152]{1,0:T(8,128)(2,1)S(1)}, u32[]{:S(2)}, u32[]{:S(2)}) collective-permute-start(bf16[64,1152]{1,0:T(8,128)(2,1)S(1)} %get-tuple-element.17), channel_id=1, source_target_pairs={{0,4},{4,0},{8,12},{12,8},{1,5},{5,1},{9,13},{13,9},{2,6},{6,2},{1... | collective-permute-start | bytes 442376 | tf_op jit(solution)/shard_map/ppermute | solution.py:219
  4.3 2.5 %collective-permute-start.1 = (bf16[64,768]{1,0:T(8,128)(2,1)S(1)}, bf16[64,768]{1,0:T(8,128)(2,1)S(1)}, u32[]{:S(2)}, u32[]{:S(2)}) collective-permute-start(bf16[64,768]{1,0:T(8,128)(2,1)S(1)} %get-tuple-element.19), channel_id=1, source_target_pairs={{0,12},{4,8},{8,4},{12,0},{1,13},{5,9},{9,5},{13,1},{2,14},{6,10},... | collective-permute-start | bytes 294920 | tf_op jit(solution)/shard_map/ppermute | solution.py:219
  6.7 0.1 collective-permute-start.2
  6.9 1.5 %collective-permute-done.refs_1_.refs_0_ = bf16[64,1152]{1,0:T(8,128)(2,1)S(1)} collective-permute-done((bf16[64,1152]{1,0:T(8,128)(2,1)S(1)}, bf16[64,1152]{1,0:T(8,128)(2,1)S(1)}, u32[]{:S(2)}, u32[]{:S(2)}) %collective-permute-start) | collective-permute-done | bytes 147488 | tf_op jit(solution)/shard_map/ppermute | solution.py:219
  8.3 1.6 %collective-permute-start.3 = (bf16[2,64,768]{2,1,0:T(8,128)(2,1)S(1)}, bf16[2,64,768]{2,1,0:T(8,128)(2,1)S(1)}, u32[]{:S(2)}, u32[]{:S(2)}) collective-permute-start(bf16[2,64,768]{2,1,0:T(8,128)(2,1)S(1)} %join.4), channel_id=1, source_target_pairs={{0,2},{2,0},{1,3},{3,1},{4,6},{6,4},{5,7},{7,5},{8,10},{10,8},{9,1... | collective-permute-start | bytes 589832 | tf_op jit(solution)/shard_map/ppermute | solution.py:222
  9.9 3.7 %collective-permute-done.1.refs_0_.refs_1_.refs_2_ = bf16[64,768]{1,0:T(8,128)(2,1)S(1)} collective-permute-done((bf16[64,768]{1,0:T(8,128)(2,1)S(1)}, bf16[64,768]{1,0:T(8,128)(2,1)S(1)}, u32[]{:S(2)}, u32[]{:S(2)}) %collective-permute-start.1) | collective-permute-done | bytes 98336 | tf_op jit(solution)/shard_map/ppermute | solution.py:219
  13.6 2.1 %collective-permute-start.5 = (bf16[64,384]{1,0:T(8,128)(2,1)S(1)}, bf16[64,384]{1,0:T(8,128)(2,1)S(1)}, u32[]{:S(2)}, u32[]{:S(2)}) collective-permute-start(bf16[64,384]{1,0:T(8,128)(2,1)S(1)} %hold.4), channel_id=1, source_target_pairs={{0,12},{4,8},{8,4},{12,0},{1,13},{5,9},{9,5},{13,1},{2,14},{6,10},... | collective-permute-start | bytes 147464 | tf_op jit(solution)/shard_map/ppermute | solution.py:219
  15.6 1.2 %collective-permute-done.2.refs_1_.refs_3_ = bf16[64,768]{1,0:T(8,128)(2,1)S(1)} collective-permute-done((bf16[64,768]{1,0:T(8,128)(2,1)S(1)}, bf16[64,768]{1,0:T(8,128)(2,1)S(1)}, u32[]{:S(2)}, u32[]{:S(2)}) %collective-permute-start.2) | collective-permute-done | bytes 98336 | tf_op jit(solution)/shard_map/ppermute | solution.py:219
  16.8 1.6 %collective-permute-start.4 = (bf16[2,64,768]{2,1,0:T(8,128)(2,1)S(1)}, bf16[2,64,768]{2,1,0:T(8,128)(2,1)S(1)}, u32[]{:S(2)}, u32[]{:S(2)}) collective-permute-start(bf16[2,64,768]{2,1,0:T(8,128)(2,1)S(1)} %join.5.refs_1_), channel_id=1, source_target_pairs={{0,2},{2,0},{1,3},{3,1},{4,6},{6,4},{5,7},{7,5},{8,10},{10,8},{9,1... | collective-permute-start | bytes 589832 | tf_op jit(solution)/shard_map/ppermute | solution.py:222
  18.4 0.0 collective-permute-start.8
  18.4 1.4 %collective-permute-done.5.refs_0_ = bf16[64,384]{1,0:T(8,128)(2,1)S(1)} collective-permute-done((bf16[64,384]{1,0:T(8,128)(2,1)S(1)}, bf16[64,384]{1,0:T(8,128)(2,1)S(1)}, u32[]{:S(2)}, u32[]{:S(2)}) %collective-permute-start.5) | collective-permute-done | bytes 49184 | tf_op jit(solution)/shard_map/ppermute | solution.py:219
  19.8 0.0 collective-permute-done.3.refs_2_.refs_4_
  19.8 2.8 %collective-permute-done.4.refs_5_ = bf16[2,64,768]{2,1,0:T(8,128)(2,1)S(1)} collective-permute-done((bf16[2,64,768]{2,1,0:T(8,128)(2,1)S(1)}, bf16[2,64,768]{2,1,0:T(8,128)(2,1)S(1)}, u32[]{:S(2)}, u32[]{:S(2)}) %collective-permute-start.4) | collective-permute-done | bytes 196640 | tf_op jit(solution)/shard_map/ppermute | solution.py:222
  22.6 0.6 %attend.2 = (bf16[64,384]{1,0:T(8,128)(2,1)S(1)}, bf16[64,384]{1,0:T(8,128)(2,1)S(1)}, bf16[64,384]{1,0:T(8,128)(2,1)S(1)}) custom-call(bf16[64,1152]{1,0:T(8,128)(2,1)S(1)} %collective-permute-done.refs_1_.refs_0_, bf16[64,768]{1,0:T(8,128)(2,1)S(1)} %get-tuple-element.18.refs_0_.refs_1_, ...), custom_call_target="tpu_custom_call" | custom-call | flops 150994944 | bytes 1081344 | tf_op jit(solution)/shard_map/attend/pallas_call | solution.py:244
  23.2 0.3 collective-permute-start.6
  23.5 2.4 %collective-permute-start.7 = (bf16[64,384]{1,0:T(8,128)(2,1)S(1)}, bf16[64,384]{1,0:T(8,128)(2,1)S(1)}, u32[]{:S(2)}, u32[]{:S(2)}) collective-permute-start(bf16[64,384]{1,0:T(8,128)(2,1)S(1)} %get-tuple-element.25), channel_id=1, source_target_pairs={{0,12},{4,8},{8,4},{12,0},{1,13},{5,9},{9,5},{13,1},{2,14},{6,10},... | collective-permute-start | bytes 147464 | tf_op jit(solution)/shard_map/ppermute | solution.py:219
  25.9 0.0 collective-permute-done.8.refs_0_
  25.9 0.5 %attend.3 = bf16[64,384]{1,0:T(8,128)(2,1)S(1)} custom-call(bf16[64,1152]{1,0:T(8,128)(2,1)S(1)} %collective-permute-done.refs_1_.refs_0_, bf16[64,768]{1,0:T(8,128)(2,1)S(1)} %get-tuple-element.18.refs_0_.refs_1_, bf16[64,768]{1,0:T(8,128)(2,1)S(1)} %collective-permute-done.1.refs_0_.refs_1_.refs_2_, ...), custom_call_target="tpu_custom_call" | custom-call | flops 50331648 | bytes 884736 | tf_op jit(solution)/shard_map/attend/pallas_call | solution.py:244
  26.4 0.9 %collective-permute-start.9 = (bf16[64,384]{1,0:T(8,128)(2,1)S(1)}, bf16[64,384]{1,0:T(8,128)(2,1)S(1)}, u32[]{:S(2)}, u32[]{:S(2)}) collective-permute-start(bf16[64,384]{1,0:T(8,128)(2,1)S(1)} %attend.3), channel_id=1, source_target_pairs={{0,8},{4,12},{8,0},{12,4},{1,9},{5,13},{9,1},{13,5},{2,10},{6,14},... | collective-permute-start | bytes 147464 | tf_op jit(solution)/shard_map/ppermute | solution.py:219
  27.3 0.1 collective-permute-done.6.refs_0_
  27.4 2.0 %collective-permute-done.7.refs_1_ = bf16[64,384]{1,0:T(8,128)(2,1)S(1)} collective-permute-done((bf16[64,384]{1,0:T(8,128)(2,1)S(1)}, bf16[64,384]{1,0:T(8,128)(2,1)S(1)}, u32[]{:S(2)}, u32[]{:S(2)}) %collective-permute-start.7) | collective-permute-done | bytes 49184 | tf_op jit(solution)/shard_map/ppermute | solution.py:219
  29.4 2.1 %collective-permute-done.9.refs_2_ = bf16[64,384]{1,0:T(8,128)(2,1)S(1)} collective-permute-done((bf16[64,384]{1,0:T(8,128)(2,1)S(1)}, bf16[64,384]{1,0:T(8,128)(2,1)S(1)}, u32[]{:S(2)}, u32[]{:S(2)}) %collective-permute-start.9) | collective-permute-done | bytes 49184 | tf_op jit(solution)/shard_map/ppermute | solution.py:219
  31.5 0.7 %unpack.1 = bf16[1,64,1536]{2,1,0:T(8,128)(2,1)} custom-call(bf16[64,384]{1,0:T(8,128)(2,1)S(1)} %get-tuple-element.23.refs_1_.refs_0_, bf16[64,384]{1,0:T(8,128)(2,1)S(1)} %get-tuple-element.26.refs_1_, bf16[64,384]{1,0:T(8,128)(2,1)S(1)} %collective-permute-done.9.refs_2_, bf16[64,384]{1,0:T(8,128)(2,1)S(1)} %get-tuple-element.28.refs_3_), custom_call_target="tpu_custom_call" | custom-call | bytes 393216 | tf_op jit(solution)/shard_map/unpack/pallas_call | solution.py:267
  (8 shorter events, 0.0 us)
Async XLA Ops:
  1.2 7.2 %collective-permute-start = (bf16[64,1152]{1,0:T(8,128)(2,1)S(1)}, bf16[64,1152]{1,0:T(8,128)(2,1)S(1)}, u32[]{:S(2)}, u32[]{:S(2)}) collective-permute-start(bf16[64,1152]{1,0:T(8,128)(2,1)S(1)} %get-tuple-element.17), channel_id=1, source_target_pairs={{0,4},{4,0},{8,12},{12,8},{1,5},{5,1},{9,13},{13,9},{2,6},{6,2},{1... | collective-permute-start | bytes 442376 | tf_op jit(solution)/shard_map/ppermute | solution.py:219
  4.3 9.3 %collective-permute-start.1 = (bf16[64,768]{1,0:T(8,128)(2,1)S(1)}, bf16[64,768]{1,0:T(8,128)(2,1)S(1)}, u32[]{:S(2)}, u32[]{:S(2)}) collective-permute-start(bf16[64,768]{1,0:T(8,128)(2,1)S(1)} %get-tuple-element.19), channel_id=1, source_target_pairs={{0,12},{4,8},{8,4},{12,0},{1,13},{5,9},{9,5},{13,1},{2,14},{6,10},... | collective-permute-start | bytes 294920 | tf_op jit(solution)/shard_map/ppermute | solution.py:219
  6.7 10.1 %collective-permute-start.2 = (bf16[64,768]{1,0:T(8,128)(2,1)S(1)}, bf16[64,768]{1,0:T(8,128)(2,1)S(1)}, u32[]{:S(2)}, u32[]{:S(2)}) collective-permute-start(bf16[64,768]{1,0:T(8,128)(2,1)S(1)} %get-tuple-element.20), channel_id=1, source_target_pairs={{0,8},{4,12},{8,0},{12,4},{1,9},{5,13},{9,1},{13,5},{2,10},{6,14},... | collective-permute-start | bytes 294920 | tf_op jit(solution)/shard_map/ppermute | solution.py:219
  8.3 11.4 %collective-permute-start.3 = (bf16[2,64,768]{2,1,0:T(8,128)(2,1)S(1)}, bf16[2,64,768]{2,1,0:T(8,128)(2,1)S(1)}, u32[]{:S(2)}, u32[]{:S(2)}) collective-permute-start(bf16[2,64,768]{2,1,0:T(8,128)(2,1)S(1)} %join.4), channel_id=1, source_target_pairs={{0,2},{2,0},{1,3},{3,1},{4,6},{6,4},{5,7},{7,5},{8,10},{10,8},{9,1... | collective-permute-start | bytes 589832 | tf_op jit(solution)/shard_map/ppermute | solution.py:222
  13.6 6.2 %collective-permute-start.5 = (bf16[64,384]{1,0:T(8,128)(2,1)S(1)}, bf16[64,384]{1,0:T(8,128)(2,1)S(1)}, u32[]{:S(2)}, u32[]{:S(2)}) collective-permute-start(bf16[64,384]{1,0:T(8,128)(2,1)S(1)} %hold.4), channel_id=1, source_target_pairs={{0,12},{4,8},{8,4},{12,0},{1,13},{5,9},{9,5},{13,1},{2,14},{6,10},... | collective-permute-start | bytes 147464 | tf_op jit(solution)/shard_map/ppermute | solution.py:219
  16.8 5.7 %collective-permute-start.4 = (bf16[2,64,768]{2,1,0:T(8,128)(2,1)S(1)}, bf16[2,64,768]{2,1,0:T(8,128)(2,1)S(1)}, u32[]{:S(2)}, u32[]{:S(2)}) collective-permute-start(bf16[2,64,768]{2,1,0:T(8,128)(2,1)S(1)} %join.5.refs_1_), channel_id=1, source_target_pairs={{0,2},{2,0},{1,3},{3,1},{4,6},{6,4},{5,7},{7,5},{8,10},{10,8},{9,1... | collective-permute-start | bytes 589832 | tf_op jit(solution)/shard_map/ppermute | solution.py:222
  18.4 7.5 %collective-permute-start.8 = (bf16[64,384]{1,0:T(8,128)(2,1)S(1)}, bf16[64,384]{1,0:T(8,128)(2,1)S(1)}, u32[]{:S(2)}, u32[]{:S(2)}) collective-permute-start(bf16[64,384]{1,0:T(8,128)(2,1)S(1)} %hold.6), channel_id=1, source_target_pairs={{0,8},{4,12},{8,0},{12,4},{1,9},{5,13},{9,1},{13,5},{2,10},{6,14},... | collective-permute-start | bytes 147464 | tf_op jit(solution)/shard_map/ppermute | solution.py:219
  23.2 4.2 %collective-permute-start.6 = (bf16[64,384]{1,0:T(8,128)(2,1)S(1)}, bf16[64,384]{1,0:T(8,128)(2,1)S(1)}, u32[]{:S(2)}, u32[]{:S(2)}) collective-permute-start(bf16[64,384]{1,0:T(8,128)(2,1)S(1)} %get-tuple-element.24), channel_id=1, source_target_pairs={{0,4},{4,0},{8,12},{12,8},{1,5},{5,1},{9,13},{13,9},{2,6},{6,2},{1... | collective-permute-start | bytes 147464 | tf_op jit(solution)/shard_map/ppermute | solution.py:219
  23.5 5.9 %collective-permute-start.7 = (bf16[64,384]{1,0:T(8,128)(2,1)S(1)}, bf16[64,384]{1,0:T(8,128)(2,1)S(1)}, u32[]{:S(2)}, u32[]{:S(2)}) collective-permute-start(bf16[64,384]{1,0:T(8,128)(2,1)S(1)} %get-tuple-element.25), channel_id=1, source_target_pairs={{0,12},{4,8},{8,4},{12,0},{1,13},{5,9},{9,5},{13,1},{2,14},{6,10},... | collective-permute-start | bytes 147464 | tf_op jit(solution)/shard_map/ppermute | solution.py:219
  26.4 5.1 %collective-permute-start.9 = (bf16[64,384]{1,0:T(8,128)(2,1)S(1)}, bf16[64,384]{1,0:T(8,128)(2,1)S(1)}, u32[]{:S(2)}, u32[]{:S(2)}) collective-permute-start(bf16[64,384]{1,0:T(8,128)(2,1)S(1)} %attend.3), channel_id=1, source_target_pairs={{0,8},{4,12},{8,0},{12,4},{1,9},{5,13},{9,1},{13,5},{2,10},{6,14},... | collective-permute-start | bytes 147464 | tf_op jit(solution)/shard_map/ppermute | solution.py:219

commit v11 on v10

--- a/solution.py
+++ b/solution.py
@@ -9,7 +9,7 @@
 from jax.sharding import PartitionSpec as P
 
 HD = 128
-EFFORT = 10**9
+EFFORT = 15 * 10**8
 ANY = pl.BlockSpec(memory_space=pl.ANY)
 HBM = pl.BlockSpec(memory_space=pltpu.HBM)
 VMEM = pl.BlockSpec(memory_space=pltpu.VMEM)
@@ -226,8 +226,8 @@
     far_kv = [to_block(sent[s, kv], s) for s in far]
     near_kvq = to_block(sent[1, kv + q], 1)
     near_kv = join([own_kv, near_kvq], [0, 0], 2 * part)
-    groups = [near_kv, join(far_kv, [0] * len(far), 2 * part)]
-    far_q = [to_block(hold([sent[s, q]], [far_kv[0] if s == far[0] else groups[1]])[0], s) for s in far]
+    groups = [near_kv] + [join([array], [0], 2 * part) for array in far_kv]
+    far_q = [to_block(hold([sent[s, q]], [group])[0], s) for s, group in zip(far, groups[1:])]
     crossed = [to_column(group, t) for group in groups for t in range(1, columns_of)]
     far_q[0] = join(far_q[:1], [0], part, EFFORT)
     near_q = join([own_q, near_kvq], [0, 2 * part], part, EFFORT, crossed[: columns_of - 1])
@@ -258,8 +258,9 @@
     mixed = dict(zip([0, 1] + far[:-1], attend([near_q] + far_q[:-1], [(0, 0), (0, 1), (1, 0)])))
     last_q = hold([far_q[-1]], [mixed[0]])
     mixed[far[-1]] = attend(last_q, [(0, None)])[0]
+    mixed[1] = hold([mixed[1]], [mixed[far[-1]]])[0]
     back = {s: to_block(mixed[s], s) for s in far + [1]}
-    early = [1] + far[:-1]
+    early = far[:-1]
     back.update(zip(early, hold([back[s] for s in early], effort=EFFORT)))
     back[0] = mixed[0]
     order = [0] + far + [1]

time: 32.4 us -> 31.5 us (0.972)
  waiting for transfers between devices: 14.6 us -> 12 us
  starting transfers between devices: 14.5 us -> 16.3 us
    ppermute x8, waiting for transfers between devices: 11.8 us -> 10.4 us  [to_block(): return lax.ppermute(array, 'blk', [(i, i ^ s) for i in range(blocks)])]
    ppermute x2 -> x3, waiting for transfers between devices: 2.78 us -> 1.54 us  [to_column(): lax.ppermute(array, 'uly', [(i, (i + t) % columns_of) for i in range(colu...]
    ppermute x8, starting transfers between devices: 11.4 us -> 12.5 us  [to_block(): return lax.ppermute(array, 'blk', [(i, i ^ s) for i in range(blocks)])]
    ppermute x2 -> x3, starting transfers between devices: 3.11 us -> 3.79 us  [to_column(): lax.ppermute(array, 'uly', [(i, (i + t) % columns_of) for i in range(colu...]
  transfers between devices with their start and end apart: 10 -> 11, of which waited for: 8 -> 9; matrix products, arithmetic and copies ran while one was open for 0% -> 0% of each run, Pallas kernels for 4% -> 4%
where the time goes in v11:
time: 31.5 us; the launch traced here: 31.4 us
  starting transfers between devices  16.3 us (52%)
  waiting for transfers between devices  12 us (38%)
  Pallas kernels  3.05 us (10%)
    ppermute x8, starting transfers between devices, to_block(): return lax.ppermute(array, 'blk', [(i, i ^ s) for i in range(blocks)])  12.5 us
    ppermute x8, waiting for transfers between devices, to_block(): return lax.ppermute(array, 'blk', [(i, i ^ s) for i in range(blocks)])  10.4 us
    ppermute x3, starting transfers between devices, to_column(): lax.ppermute(array, 'uly', [(i, (i + t) % columns_of) for i in range(colu...  3.79 us
    ppermute x3, waiting for transfers between devices, to_column(): lax.ppermute(array, 'uly', [(i, (i + t) % columns_of) for i in range(colu...  1.54 us
    pallas_call x1, Pallas kernels, local_blocks(): pl.pallas_call(functools.partial(pack_kernel, messages, part), out_shape=...  1.17 us
    pallas_call x2, Pallas kernels, attend(): pl.pallas_call(functools.partial(attend_kernel, len(holders), keys, query...  1.13 us
    pallas_call x1, Pallas kernels, local_blocks(): pl.pallas_call(functools.partial(unpack_kernel, order, part), out_shape=j...  0.7 us
  transfers between devices with their start and end apart: 11, of which 9 were waited for; matrix products, arithmetic and copies ran while one was open for 0% of the time, Pallas kernels for 4%

profile of v11, /device:TPU:0, one launch (start us, length us, event | category | flops | bytes accessed | tf_op | source)
XLA Modules:
  0.0 31.4 jit_solution(6914423686542488353)
XLA Ops:
  0.0 1.2 %pack.1 = (bf16[64,768]{1,0:T(8,128)(2,1)S(1)}, bf16[64,768]{1,0:T(8,128)(2,1)S(1)}, bf16[64,1152]{1,0:T(8,128)(2,1)S(1)}, bf16[64,384]{1,0:T(8,128)(2,1)S(1)}, ...) custom-call(bf16[1,64,1536]{2,1,0:T(8,128)(2,1)} %q_ref.1, ...), custom_call_target="tpu_custom_call" | custom-call | bytes 1179648 | tf_op jit(solution)/shard_map/pack/pallas_call | solution.py:202
  1.2 3.1 %collective-permute-start = (bf16[64,1152]{1,0:T(8,128)(2,1)S(1)}, bf16[64,1152]{1,0:T(8,128)(2,1)S(1)}, u32[]{:S(2)}, u32[]{:S(2)}) collective-permute-start(bf16[64,1152]{1,0:T(8,128)(2,1)S(1)} %get-tuple-element.15), channel_id=1, source_target_pairs={{0,4},{4,0},{8,12},{12,8},{1,5},{5,1},{9,13},{13,9},{2,6},{6,2},{1... | collective-permute-start | bytes 442376 | tf_op jit(solution)/shard_map/ppermute | solution.py:219
  4.3 2.5 %collective-permute-start.1 = (bf16[64,768]{1,0:T(8,128)(2,1)S(1)}, bf16[64,768]{1,0:T(8,128)(2,1)S(1)}, u32[]{:S(2)}, u32[]{:S(2)}) collective-permute-start(bf16[64,768]{1,0:T(8,128)(2,1)S(1)} %get-tuple-element.17), channel_id=1, source_target_pairs={{0,12},{4,8},{8,4},{12,0},{1,13},{5,9},{9,5},{13,1},{2,14},{6,10},... | collective-permute-start | bytes 294920 | tf_op jit(solution)/shard_map/ppermute | solution.py:219
  6.7 0.1 collective-permute-start.2
  6.9 1.5 %collective-permute-done.refs_1_.refs_0_ = bf16[64,1152]{1,0:T(8,128)(2,1)S(1)} collective-permute-done((bf16[64,1152]{1,0:T(8,128)(2,1)S(1)}, bf16[64,1152]{1,0:T(8,128)(2,1)S(1)}, u32[]{:S(2)}, u32[]{:S(2)}) %collective-permute-start) | collective-permute-done | bytes 147488 | tf_op jit(solution)/shard_map/ppermute | solution.py:219
  8.3 1.6 %collective-permute-start.3 = (bf16[2,64,768]{2,1,0:T(8,128)(2,1)S(1)}, bf16[2,64,768]{2,1,0:T(8,128)(2,1)S(1)}, u32[]{:S(2)}, u32[]{:S(2)}) collective-permute-start(bf16[2,64,768]{2,1,0:T(8,128)(2,1)S(1)} %join.5), channel_id=1, source_target_pairs={{0,2},{2,0},{1,3},{3,1},{4,6},{6,4},{5,7},{7,5},{8,10},{10,8},{9,1... | collective-permute-start | bytes 589832 | tf_op jit(solution)/shard_map/ppermute | solution.py:222
  9.9 3.7 %collective-permute-done.1.refs_0_.refs_2_ = bf16[64,768]{1,0:T(8,128)(2,1)S(1)} collective-permute-done((bf16[64,768]{1,0:T(8,128)(2,1)S(1)}, bf16[64,768]{1,0:T(8,128)(2,1)S(1)}, u32[]{:S(2)}, u32[]{:S(2)}) %collective-permute-start.1) | collective-permute-done | bytes 98336 | tf_op jit(solution)/shard_map/ppermute | solution.py:219
  13.6 2.1 %collective-permute-start.6 = (bf16[64,384]{1,0:T(8,128)(2,1)S(1)}, bf16[64,384]{1,0:T(8,128)(2,1)S(1)}, u32[]{:S(2)}, u32[]{:S(2)}) collective-permute-start(bf16[64,384]{1,0:T(8,128)(2,1)S(1)} %hold.5), channel_id=1, source_target_pairs={{0,12},{4,8},{8,4},{12,0},{1,13},{5,9},{9,5},{13,1},{2,14},{6,10},... | collective-permute-start | bytes 147464 | tf_op jit(solution)/shard_map/ppermute | solution.py:219
  15.7 0.7 %collective-permute-start.4 = (bf16[1,64,768]{2,1,0:T(8,128)(2,1)S(1)}, bf16[1,64,768]{2,1,0:T(8,128)(2,1)S(1)}, u32[]{:S(2)}, u32[]{:S(2)}) collective-permute-start(bf16[1,64,768]{2,1,0:T(8,128)(2,1)S(1)} %join.6.refs_1_), channel_id=1, source_target_pairs={{0,2},{2,0},{1,3},{3,1},{4,6},{6,4},{5,7},{7,5},{8,10},{10,8},{9,1... | collective-permute-start | bytes 294920 | tf_op jit(solution)/shard_map/ppermute | solution.py:222
  16.4 0.4 %collective-permute-done.2.refs_0_.refs_3_ = bf16[64,768]{1,0:T(8,128)(2,1)S(1)} collective-permute-done((bf16[64,768]{1,0:T(8,128)(2,1)S(1)}, bf16[64,768]{1,0:T(8,128)(2,1)S(1)}, u32[]{:S(2)}, u32[]{:S(2)}) %collective-permute-start.2) | collective-permute-done | bytes 98336 | tf_op jit(solution)/shard_map/ppermute | solution.py:219
  16.8 1.6 %collective-permute-start.5 = (bf16[1,64,768]{2,1,0:T(8,128)(2,1)S(1)}, bf16[1,64,768]{2,1,0:T(8,128)(2,1)S(1)}, u32[]{:S(2)}, u32[]{:S(2)}) collective-permute-start(bf16[1,64,768]{2,1,0:T(8,128)(2,1)S(1)} %join.7.refs_1_), channel_id=1, source_target_pairs={{0,2},{2,0},{1,3},{3,1},{4,6},{6,4},{5,7},{7,5},{8,10},{10,8},{9,1... | collective-permute-start | bytes 294920 | tf_op jit(solution)/shard_map/ppermute | solution.py:222
  18.4 0.4 %collective-permute-start.8 = (bf16[64,384]{1,0:T(8,128)(2,1)S(1)}, bf16[64,384]{1,0:T(8,128)(2,1)S(1)}, u32[]{:S(2)}, u32[]{:S(2)}) collective-permute-start(bf16[64,384]{1,0:T(8,128)(2,1)S(1)} %hold.7), channel_id=1, source_target_pairs={{0,8},{4,12},{8,0},{12,4},{1,9},{5,13},{9,1},{13,5},{2,10},{6,14},... | collective-permute-start | bytes 147464 | tf_op jit(solution)/shard_map/ppermute | solution.py:219
  18.7 1.2 %collective-permute-done.6.refs_0_ = bf16[64,384]{1,0:T(8,128)(2,1)S(1)} collective-permute-done((bf16[64,384]{1,0:T(8,128)(2,1)S(1)}, bf16[64,384]{1,0:T(8,128)(2,1)S(1)}, u32[]{:S(2)}, u32[]{:S(2)}) %collective-permute-start.6) | collective-permute-done | bytes 49184 | tf_op jit(solution)/shard_map/ppermute | solution.py:219
  20.0 0.0 collective-permute-done.3.refs_2_.refs_4_
  20.0 0.4 %collective-permute-done.4.refs_5_ = bf16[1,64,768]{2,1,0:T(8,128)(2,1)S(1)} collective-permute-done((bf16[1,64,768]{2,1,0:T(8,128)(2,1)S(1)}, bf16[1,64,768]{2,1,0:T(8,128)(2,1)S(1)}, u32[]{:S(2)}, u32[]{:S(2)}) %collective-permute-start.4) | collective-permute-done | bytes 98336 | tf_op jit(solution)/shard_map/ppermute | solution.py:222
  20.3 1.2 %collective-permute-done.5.refs_6_ = bf16[1,64,768]{2,1,0:T(8,128)(2,1)S(1)} collective-permute-done((bf16[1,64,768]{2,1,0:T(8,128)(2,1)S(1)}, bf16[1,64,768]{2,1,0:T(8,128)(2,1)S(1)}, u32[]{:S(2)}, u32[]{:S(2)}) %collective-permute-start.5) | collective-permute-done | bytes 98336 | tf_op jit(solution)/shard_map/ppermute | solution.py:222
  21.5 0.6 %attend.2 = (bf16[64,384]{1,0:T(8,128)(2,1)S(1)}, bf16[64,384]{1,0:T(8,128)(2,1)S(1)}, bf16[64,384]{1,0:T(8,128)(2,1)S(1)}) custom-call(bf16[64,1152]{1,0:T(8,128)(2,1)S(1)} %collective-permute-done.refs_1_.refs_0_, bf16[64,768]{1,0:T(8,128)(2,1)S(1)} %get-tuple-element.16.refs_0_.refs_1_, bf16[64,768]{1,0:T(8,128)(2,1)S(1)} %collective-permute-done.1.refs_0_.refs_2_, ...), custom_call_target="tpu_custom_call" | custom-call | flops 150994944 | bytes 1081344 | tf_op jit(solution)/shard_map/attend/pallas_call | solution.py:244
  22.2 2.6 %collective-permute-start.7 = (bf16[64,384]{1,0:T(8,128)(2,1)S(1)}, bf16[64,384]{1,0:T(8,128)(2,1)S(1)}, u32[]{:S(2)}, u32[]{:S(2)}) collective-permute-start(bf16[64,384]{1,0:T(8,128)(2,1)S(1)} %get-tuple-element.22), channel_id=1, source_target_pairs={{0,12},{4,8},{8,4},{12,0},{1,13},{5,9},{9,5},{13,1},{2,14},{6,10},... | collective-permute-start | bytes 147464 | tf_op jit(solution)/shard_map/ppermute | solution.py:219
  24.8 0.2 collective-permute-done.8.refs_0_
  25.0 0.5 %attend.3.refs_1_ = bf16[64,384]{1,0:T(8,128)(2,1)S(1)} custom-call(bf16[64,1152]{1,0:T(8,128)(2,1)S(1)} %collective-permute-done.refs_1_.refs_0_, bf16[64,768]{1,0:T(8,128)(2,1)S(1)} %get-tuple-element.16.refs_0_.refs_1_, bf16[64,768]{1,0:T(8,128)(2,1)S(1)} %collective-permute-done.1.refs_0_.refs_2_, ...), custom_call_target="tpu_custom_call" | custom-call | flops 50331648 | bytes 884736 | tf_op jit(solution)/shard_map/attend/pallas_call | solution.py:244
  25.5 0.6 %collective-permute-start.9 = (bf16[64,384]{1,0:T(8,128)(2,1)S(1)}, bf16[64,384]{1,0:T(8,128)(2,1)S(1)}, u32[]{:S(2)}, u32[]{:S(2)}) collective-permute-start(bf16[64,384]{1,0:T(8,128)(2,1)S(1)} %attend.3.refs_1_), channel_id=1, source_target_pairs={{0,8},{4,12},{8,0},{12,4},{1,9},{5,13},{9,1},{13,5},{2,10},{6,14},... | collective-permute-start | bytes 147464 | tf_op jit(solution)/shard_map/ppermute | solution.py:219
  26.0 1.1 %collective-permute-start.10 = (bf16[64,384]{1,0:T(8,128)(2,1)S(1)}, bf16[64,384]{1,0:T(8,128)(2,1)S(1)}, u32[]{:S(2)}, u32[]{:S(2)}) collective-permute-start(bf16[64,384]{1,0:T(8,128)(2,1)S(1)} %hold.9), channel_id=1, source_target_pairs={{0,4},{4,0},{8,12},{12,8},{1,5},{5,1},{9,13},{13,9},{2,6},{6,2},{1... | collective-permute-start | bytes 147464 | tf_op jit(solution)/shard_map/ppermute | solution.py:219
  27.2 1.4 %collective-permute-done.7.refs_0_ = bf16[64,384]{1,0:T(8,128)(2,1)S(1)} collective-permute-done((bf16[64,384]{1,0:T(8,128)(2,1)S(1)}, bf16[64,384]{1,0:T(8,128)(2,1)S(1)}, u32[]{:S(2)}, u32[]{:S(2)}) %collective-permute-start.7) | collective-permute-done | bytes 49184 | tf_op jit(solution)/shard_map/ppermute | solution.py:219
  28.6 2.1 %collective-permute-done.10.refs_3_ = bf16[64,384]{1,0:T(8,128)(2,1)S(1)} collective-permute-done((bf16[64,384]{1,0:T(8,128)(2,1)S(1)}, bf16[64,384]{1,0:T(8,128)(2,1)S(1)}, u32[]{:S(2)}, u32[]{:S(2)}) %collective-permute-start.10) | collective-permute-done | bytes 49184 | tf_op jit(solution)/shard_map/ppermute | solution.py:219
  30.7 0.0 collective-permute-done.9.refs_2_
  30.7 0.7 %unpack.1 = bf16[1,64,1536]{2,1,0:T(8,128)(2,1)} custom-call(bf16[64,384]{1,0:T(8,128)(2,1)S(1)} %get-tuple-element.21.refs_1_.refs_0_, bf16[64,384]{1,0:T(8,128)(2,1)S(1)} %hold.6.refs_1_, bf16[64,384]{1,0:T(8,128)(2,1)S(1)} %collective-permute-done.9.refs_2_, bf16[64,384]{1,0:T(8,128)(2,1)S(1)} %collective-permute-done.10.refs_3_), custom_call_target="tpu_custom_call" | custom-call | bytes 393216 | tf_op jit(solution)/shard_map/unpack/pallas_call | solution.py:268
  (10 shorter events, 0.0 us)
Async XLA Ops:
  1.2 7.2 %collective-permute-start = (bf16[64,1152]{1,0:T(8,128)(2,1)S(1)}, bf16[64,1152]{1,0:T(8,128)(2,1)S(1)}, u32[]{:S(2)}, u32[]{:S(2)}) collective-permute-start(bf16[64,1152]{1,0:T(8,128)(2,1)S(1)} %get-tuple-element.15), channel_id=1, source_target_pairs={{0,4},{4,0},{8,12},{12,8},{1,5},{5,1},{9,13},{13,9},{2,6},{6,2},{1... | collective-permute-start | bytes 442376 | tf_op jit(solution)/shard_map/ppermute | solution.py:219
  4.3 9.3 %collective-permute-start.1 = (bf16[64,768]{1,0:T(8,128)(2,1)S(1)}, bf16[64,768]{1,0:T(8,128)(2,1)S(1)}, u32[]{:S(2)}, u32[]{:S(2)}) collective-permute-start(bf16[64,768]{1,0:T(8,128)(2,1)S(1)} %get-tuple-element.17), channel_id=1, source_target_pairs={{0,12},{4,8},{8,4},{12,0},{1,13},{5,9},{9,5},{13,1},{2,14},{6,10},... | collective-permute-start | bytes 294920 | tf_op jit(solution)/shard_map/ppermute | solution.py:219
  6.7 10.1 %collective-permute-start.2 = (bf16[64,768]{1,0:T(8,128)(2,1)S(1)}, bf16[64,768]{1,0:T(8,128)(2,1)S(1)}, u32[]{:S(2)}, u32[]{:S(2)}) collective-permute-start(bf16[64,768]{1,0:T(8,128)(2,1)S(1)} %get-tuple-element.18), channel_id=1, source_target_pairs={{0,8},{4,12},{8,0},{12,4},{1,9},{5,13},{9,1},{13,5},{2,10},{6,14},... | collective-permute-start | bytes 294920 | tf_op jit(solution)/shard_map/ppermute | solution.py:219
  8.3 11.6 %collective-permute-start.3 = (bf16[2,64,768]{2,1,0:T(8,128)(2,1)S(1)}, bf16[2,64,768]{2,1,0:T(8,128)(2,1)S(1)}, u32[]{:S(2)}, u32[]{:S(2)}) collective-permute-start(bf16[2,64,768]{2,1,0:T(8,128)(2,1)S(1)} %join.5), channel_id=1, source_target_pairs={{0,2},{2,0},{1,3},{3,1},{4,6},{6,4},{5,7},{7,5},{8,10},{10,8},{9,1... | collective-permute-start | bytes 589832 | tf_op jit(solution)/shard_map/ppermute | solution.py:222
  13.6 6.4 %collective-permute-start.6 = (bf16[64,384]{1,0:T(8,128)(2,1)S(1)}, bf16[64,384]{1,0:T(8,128)(2,1)S(1)}, u32[]{:S(2)}, u32[]{:S(2)}) collective-permute-start(bf16[64,384]{1,0:T(8,128)(2,1)S(1)} %hold.5), channel_id=1, source_target_pairs={{0,12},{4,8},{8,4},{12,0},{1,13},{5,9},{9,5},{13,1},{2,14},{6,10},... | collective-permute-start | bytes 147464 | tf_op jit(solution)/shard_map/ppermute | solution.py:219
  15.7 4.6 %collective-permute-start.4 = (bf16[1,64,768]{2,1,0:T(8,128)(2,1)S(1)}, bf16[1,64,768]{2,1,0:T(8,128)(2,1)S(1)}, u32[]{:S(2)}, u32[]{:S(2)}) collective-permute-start(bf16[1,64,768]{2,1,0:T(8,128)(2,1)S(1)} %join.6.refs_1_), channel_id=1, source_target_pairs={{0,2},{2,0},{1,3},{3,1},{4,6},{6,4},{5,7},{7,5},{8,10},{10,8},{9,1... | collective-permute-start | bytes 294920 | tf_op jit(solution)/shard_map/ppermute | solution.py:222
  16.8 4.7 %collective-permute-start.5 = (bf16[1,64,768]{2,1,0:T(8,128)(2,1)S(1)}, bf16[1,64,768]{2,1,0:T(8,128)(2,1)S(1)}, u32[]{:S(2)}, u32[]{:S(2)}) collective-permute-start(bf16[1,64,768]{2,1,0:T(8,128)(2,1)S(1)} %join.7.refs_1_), channel_id=1, source_target_pairs={{0,2},{2,0},{1,3},{3,1},{4,6},{6,4},{5,7},{7,5},{8,10},{10,8},{9,1... | collective-permute-start | bytes 294920 | tf_op jit(solution)/shard_map/ppermute | solution.py:222
  18.4 6.6 %collective-permute-start.8 = (bf16[64,384]{1,0:T(8,128)(2,1)S(1)}, bf16[64,384]{1,0:T(8,128)(2,1)S(1)}, u32[]{:S(2)}, u32[]{:S(2)}) collective-permute-start(bf16[64,384]{1,0:T(8,128)(2,1)S(1)} %hold.7), channel_id=1, source_target_pairs={{0,8},{4,12},{8,0},{12,4},{1,9},{5,13},{9,1},{13,5},{2,10},{6,14},... | collective-permute-start | bytes 147464 | tf_op jit(solution)/shard_map/ppermute | solution.py:219
  22.2 6.5 %collective-permute-start.7 = (bf16[64,384]{1,0:T(8,128)(2,1)S(1)}, bf16[64,384]{1,0:T(8,128)(2,1)S(1)}, u32[]{:S(2)}, u32[]{:S(2)}) collective-permute-start(bf16[64,384]{1,0:T(8,128)(2,1)S(1)} %get-tuple-element.22), channel_id=1, source_target_pairs={{0,12},{4,8},{8,4},{12,0},{1,13},{5,9},{9,5},{13,1},{2,14},{6,10},... | collective-permute-start | bytes 147464 | tf_op jit(solution)/shard_map/ppermute | solution.py:219
  25.5 5.2 %collective-permute-start.9 = (bf16[64,384]{1,0:T(8,128)(2,1)S(1)}, bf16[64,384]{1,0:T(8,128)(2,1)S(1)}, u32[]{:S(2)}, u32[]{:S(2)}) collective-permute-start(bf16[64,384]{1,0:T(8,128)(2,1)S(1)} %attend.3.refs_1_), channel_id=1, source_target_pairs={{0,8},{4,12},{8,0},{12,4},{1,9},{5,13},{9,1},{13,5},{2,10},{6,14},... | collective-permute-start | bytes 147464 | tf_op jit(solution)/shard_map/ppermute | solution.py:219
  26.0 4.6 %collective-permute-start.10 = (bf16[64,384]{1,0:T(8,128)(2,1)S(1)}, bf16[64,384]{1,0:T(8,128)(2,1)S(1)}, u32[]{:S(2)}, u32[]{:S(2)}) collective-permute-start(bf16[64,384]{1,0:T(8,128)(2,1)S(1)} %hold.9), channel_id=1, source_target_pairs={{0,4},{4,0},{8,12},{12,8},{1,5},{5,1},{9,13},{13,9},{2,6},{6,2},{1... | collective-permute-start | bytes 147464 | tf_op jit(solution)/shard_map/ppermute | solution.py:219

commit v12 on v11

--- a/solution.py
+++ b/solution.py
@@ -9,7 +9,10 @@
 from jax.sharding import PartitionSpec as P
 
 HD = 128
-EFFORT = 15 * 10**8
+EFFORT = 10**9
+EFFORT_OWN = 3 * 10**8
+EFFORT_FIRST = 10**9
+EFFORT_SECOND = 2 * 10**9
 ANY = pl.BlockSpec(memory_space=pl.ANY)
 HBM = pl.BlockSpec(memory_space=pltpu.HBM)
 VMEM = pl.BlockSpec(memory_space=pltpu.VMEM)
@@ -225,18 +228,20 @@
     own_kv, own_q = packed[-2:]
     far_kv = [to_block(sent[s, kv], s) for s in far]
     near_kvq = to_block(sent[1, kv + q], 1)
-    near_kv = join([own_kv, near_kvq], [0, 0], 2 * part)
-    groups = [near_kv] + [join([array], [0], 2 * part) for array in far_kv]
+    far_kv[0] = hold(far_kv[:1], effort=EFFORT_FIRST)[0]
+    far_kv[1] = hold(far_kv[1:], effort=EFFORT_SECOND)[0]
+    groups = [own_kv, join([near_kvq, far_kv[0]], [0, 0], 2 * part)] + far_kv[1:]
     far_q = [to_block(hold([sent[s, q]], [group])[0], s) for s, group in zip(far, groups[1:])]
+    hops = columns_of - 1
     crossed = [to_column(group, t) for group in groups for t in range(1, columns_of)]
-    far_q[0] = join(far_q[:1], [0], part, EFFORT)
-    near_q = join([own_q, near_kvq], [0, 2 * part], part, EFFORT, crossed[: columns_of - 1])
-
-    holders = [near_kvq, own_kv] + far_kv
-    keys = [(at, None) for at in range(len(holders))]
-    for array in crossed:
-        keys += [(len(holders), at) for at in range(array.shape[0])]
-        holders.append(array)
+    crossed[:hops] = hold(crossed[:hops], effort=EFFORT_OWN)
+    near_q = join([own_q, near_kvq], [0, 2 * part], part)
+    far_q[0] = join(far_q[:1], [0], part, EFFORT, crossed[: 2 * hops])
+
+    holders = [near_kvq, own_kv] + far_kv + crossed
+    keys = []
+    for at, array in enumerate(holders):
+        keys += [(at, None)] if array.ndim == 2 else [(at, row) for row in range(array.shape[0])]
 
     def attend(query_arrays, query_places):
         rows = tokens * len(query_places)

time: 31.5 us -> 32 us (1.016)
  waiting for transfers between devices: 12 us -> 12.6 us
    ppermute x8, waiting for transfers between devices: 10.4 us -> 11.7 us  [to_block(): return lax.ppermute(array, 'blk', [(i, i ^ s) for i in range(blocks)])]
    ppermute x3, waiting for transfers between devices: 1.54 us -> 0.84 us  [to_column(): lax.ppermute(array, 'uly', [(i, (i + t) % columns_of) for i in range(colu...]
  transfers between devices with their start and end apart: 11 -> 11, of which waited for: 9 -> 6; matrix products, arithmetic and copies ran while one was open for 0% -> 0% of each run, Pallas kernels for 4% -> 4%
where the time goes in v12:
time: 32 us; the launch traced here: 31.8 us
  starting transfers between devices  16.1 us (50%)
  waiting for transfers between devices  12.6 us (39%)
  Pallas kernels  3.03 us (9%)
    ppermute x8, starting transfers between devices, to_block(): return lax.ppermute(array, 'blk', [(i, i ^ s) for i in range(blocks)])  12.3 us
    ppermute x8, waiting for transfers between devices, to_block(): return lax.ppermute(array, 'blk', [(i, i ^ s) for i in range(blocks)])  11.7 us
    ppermute x3, starting transfers between devices, to_column(): lax.ppermute(array, 'uly', [(i, (i + t) % columns_of) for i in range(colu...  3.84 us
    pallas_call x1, Pallas kernels, local_blocks(): pl.pallas_call(functools.partial(pack_kernel, messages, part), out_shape=...  1.17 us
    pallas_call x2, Pallas kernels, attend(): pl.pallas_call(functools.partial(attend_kernel, len(holders), keys, query...  1.13 us
    ppermute x3, waiting for transfers between devices, to_column(): lax.ppermute(array, 'uly', [(i, (i + t) % columns_of) for i in range(colu...  0.84 us
    pallas_call x1, Pallas kernels, local_blocks(): pl.pallas_call(functools.partial(unpack_kernel, order, part), out_shape=j...  0.7 us
  transfers between devices with their start and end apart: 11, of which 6 were waited for; matrix products, arithmetic and copies ran while one was open for 0% of the time, Pallas kernels for 4%

profile of v12, /device:TPU:0, one launch (start us, length us, event | category | flops | bytes accessed | tf_op | source)
XLA Modules:
  0.0 31.8 jit_solution(3760198546394909760)
XLA Ops:
  0.0 1.2 %pack.1 = (bf16[64,768]{1,0:T(8,128)(2,1)S(1)}, bf16[64,768]{1,0:T(8,128)(2,1)S(1)}, bf16[64,1152]{1,0:T(8,128)(2,1)S(1)}, bf16[64,384]{1,0:T(8,128)(2,1)S(1)}, ...) custom-call(bf16[1,64,1536]{2,1,0:T(8,128)(2,1)} %q_ref.1, ...), custom_call_target="tpu_custom_call" | custom-call | bytes 1179648 | tf_op jit(solution)/shard_map/pack/pallas_call | solution.py:205
  1.2 5.1 %collective-permute-start.1 = (bf16[64,768]{1,0:T(8,128)(2,1)S(1)}, bf16[64,768]{1,0:T(8,128)(2,1)S(1)}, u32[]{:S(2)}, u32[]{:S(2)}) collective-permute-start(bf16[64,768]{1,0:T(8,128)(2,1)S(1)} %get-tuple-element.17), channel_id=1, source_target_pairs={{0,12},{4,8},{8,4},{12,0},{1,13},{5,9},{9,5},{13,1},{2,14},{6,10},... | collective-permute-start | bytes 294920 | tf_op jit(solution)/shard_map/ppermute | solution.py:222
  6.3 0.0 collective-permute-start
  6.3 0.6 %collective-permute-start.2 = (bf16[64,768]{1,0:T(8,128)(2,1)S(1)}, bf16[64,768]{1,0:T(8,128)(2,1)S(1)}, u32[]{:S(2)}, u32[]{:S(2)}) collective-permute-start(bf16[64,768]{1,0:T(8,128)(2,1)S(1)} %get-tuple-element.18), channel_id=1, source_target_pairs={{0,8},{4,12},{8,0},{12,4},{1,9},{5,13},{9,1},{13,5},{2,10},{6,14},... | collective-permute-start | bytes 294920 | tf_op jit(solution)/shard_map/ppermute | solution.py:222
  6.9 1.6 %collective-permute-start.3 = (bf16[64,768]{1,0:T(8,128)(2,1)S(1)}, bf16[64,768]{1,0:T(8,128)(2,1)S(1)}, u32[]{:S(2)}, u32[]{:S(2)}) collective-permute-start(bf16[64,768]{1,0:T(8,128)(2,1)S(1)} %get-tuple-element.16.refs_1_), channel_id=1, source_target_pairs={{0,2},{2,0},{1,3},{3,1},{4,6},{6,4},{5,7},{7,5},{8,10},{10,8},{9,1... | collective-permute-start | bytes 294920 | tf_op jit(solution)/shard_map/ppermute | solution.py:225
  8.6 1.4 %collective-permute-done.1.refs_0_ = bf16[64,768]{1,0:T(8,128)(2,1)S(1)} collective-permute-done((bf16[64,768]{1,0:T(8,128)(2,1)S(1)}, bf16[64,768]{1,0:T(8,128)(2,1)S(1)}, u32[]{:S(2)}, u32[]{:S(2)}) %collective-permute-start.1) | collective-permute-done | bytes 98336 | tf_op jit(solution)/shard_map/ppermute | solution.py:222
  10.0 4.4 %collective-permute-done.refs_0_.refs_1_ = bf16[64,1152]{1,0:T(8,128)(2,1)S(1)} collective-permute-done((bf16[64,1152]{1,0:T(8,128)(2,1)S(1)}, bf16[64,1152]{1,0:T(8,128)(2,1)S(1)}, u32[]{:S(2)}, u32[]{:S(2)}) %collective-permute-start) | collective-permute-done | bytes 147488 | tf_op jit(solution)/shard_map/ppermute | solution.py:222
  14.4 1.7 %collective-permute-start.4 = (bf16[2,64,768]{2,1,0:T(8,128)(2,1)S(1)}, bf16[2,64,768]{2,1,0:T(8,128)(2,1)S(1)}, u32[]{:S(2)}, u32[]{:S(2)}) collective-permute-start(bf16[2,64,768]{2,1,0:T(8,128)(2,1)S(1)} %join.3.refs_1_), channel_id=1, source_target_pairs={{0,2},{2,0},{1,3},{3,1},{4,6},{6,4},{5,7},{7,5},{8,10},{10,8},{9,1... | collective-permute-start | bytes 589832 | tf_op jit(solution)/shard_map/ppermute | solution.py:225
  16.1 1.7 %collective-permute-start.6 = (bf16[64,384]{1,0:T(8,128)(2,1)S(1)}, bf16[64,384]{1,0:T(8,128)(2,1)S(1)}, u32[]{:S(2)}, u32[]{:S(2)}) collective-permute-start(bf16[64,384]{1,0:T(8,128)(2,1)S(1)} %hold.11), channel_id=1, source_target_pairs={{0,12},{4,8},{8,4},{12,0},{1,13},{5,9},{9,5},{13,1},{2,14},{6,10},... | collective-permute-start | bytes 147464 | tf_op jit(solution)/shard_map/ppermute | solution.py:222
  17.7 0.0 collective-permute-done.2.refs_0_
  17.8 0.5 %collective-permute-start.5 = (bf16[64,768]{1,0:T(8,128)(2,1)S(1)}, bf16[64,768]{1,0:T(8,128)(2,1)S(1)}, u32[]{:S(2)}, u32[]{:S(2)}) collective-permute-start(bf16[64,768]{1,0:T(8,128)(2,1)S(1)} %hold.9.refs_3_.refs_1_), channel_id=1, source_target_pairs={{0,2},{2,0},{1,3},{3,1},{4,6},{6,4},{5,7},{7,5},{8,10},{10,8},{9,1... | collective-permute-start | bytes 294920 | tf_op jit(solution)/shard_map/ppermute | solution.py:225
  18.3 0.4 %collective-permute-start.8 = (bf16[64,384]{1,0:T(8,128)(2,1)S(1)}, bf16[64,384]{1,0:T(8,128)(2,1)S(1)}, u32[]{:S(2)}, u32[]{:S(2)}) collective-permute-start(bf16[64,384]{1,0:T(8,128)(2,1)S(1)} %hold.13), channel_id=1, source_target_pairs={{0,8},{4,12},{8,0},{12,4},{1,9},{5,13},{9,1},{13,5},{2,10},{6,14},... | collective-permute-start | bytes 147464 | tf_op jit(solution)/shard_map/ppermute | solution.py:222
  18.7 0.0 collective-permute-done.3.refs_0_
  18.7 3.3 %collective-permute-done.6.refs_0_ = bf16[64,384]{1,0:T(8,128)(2,1)S(1)} collective-permute-done((bf16[64,384]{1,0:T(8,128)(2,1)S(1)}, bf16[64,384]{1,0:T(8,128)(2,1)S(1)}, u32[]{:S(2)}, u32[]{:S(2)}) %collective-permute-start.6) | collective-permute-done | bytes 49184 | tf_op jit(solution)/shard_map/ppermute | solution.py:222
  22.0 0.0 collective-permute-done.4.refs_2_.refs_5_
  22.0 0.8 %collective-permute-done.5.refs_6_ = bf16[64,768]{1,0:T(8,128)(2,1)S(1)} collective-permute-done((bf16[64,768]{1,0:T(8,128)(2,1)S(1)}, bf16[64,768]{1,0:T(8,128)(2,1)S(1)}, u32[]{:S(2)}, u32[]{:S(2)}) %collective-permute-start.5) | collective-permute-done | bytes 98336 | tf_op jit(solution)/shard_map/ppermute | solution.py:225
  22.8 0.6 %attend.2 = (bf16[64,384]{1,0:T(8,128)(2,1)S(1)}, bf16[64,384]{1,0:T(8,128)(2,1)S(1)}, bf16[64,384]{1,0:T(8,128)(2,1)S(1)}) custom-call(bf16[64,1152]{1,0:T(8,128)(2,1)S(1)} %collective-permute-done.refs_0_.refs_1_, bf16[64,768]{1,0:T(8,128)(2,1)S(1)} %get-tuple-element.16.refs_1_, bf16[64,768]{1,0:T(8,128)(2,1)S(1)} %hold.8.refs_1_.refs_2_, ...), custom_call_target="tpu_custom_call" | custom-call | flops 150994944 | bytes 1081344 | tf_op jit(solution)/shard_map/attend/pallas_call | solution.py:249
  23.5 1.8 %collective-permute-start.7 = (bf16[64,384]{1,0:T(8,128)(2,1)S(1)}, bf16[64,384]{1,0:T(8,128)(2,1)S(1)}, u32[]{:S(2)}, u32[]{:S(2)}) collective-permute-start(bf16[64,384]{1,0:T(8,128)(2,1)S(1)} %get-tuple-element.22), channel_id=1, source_target_pairs={{0,12},{4,8},{8,4},{12,0},{1,13},{5,9},{9,5},{13,1},{2,14},{6,10},... | collective-permute-start | bytes 147464 | tf_op jit(solution)/shard_map/ppermute | solution.py:222
  25.2 0.0 collective-permute-done.8.refs_0_
  25.2 0.5 %attend.3.refs_1_ = bf16[64,384]{1,0:T(8,128)(2,1)S(1)} custom-call(bf16[64,1152]{1,0:T(8,128)(2,1)S(1)} %collective-permute-done.refs_0_.refs_1_, bf16[64,768]{1,0:T(8,128)(2,1)S(1)} %get-tuple-element.16.refs_1_, bf16[64,768]{1,0:T(8,128)(2,1)S(1)} %hold.8.refs_1_.refs_2_, bf16[64,768]{1,0:T(8,128)(2,1)S(1)} %hold.9.refs_3_.refs_1_, ...), custom_call_target="tpu_custom_call" | custom-call | flops 50331648 | bytes 884736 | tf_op jit(solution)/shard_map/attend/pallas_call | solution.py:249
  25.7 0.1 collective-permute-start.9
  25.8 2.7 %collective-permute-start.10 = (bf16[64,384]{1,0:T(8,128)(2,1)S(1)}, bf16[64,384]{1,0:T(8,128)(2,1)S(1)}, u32[]{:S(2)}, u32[]{:S(2)}) collective-permute-start(bf16[64,384]{1,0:T(8,128)(2,1)S(1)} %hold.15), channel_id=1, source_target_pairs={{0,4},{4,0},{8,12},{12,8},{1,5},{5,1},{9,13},{13,9},{2,6},{6,2},{1... | collective-permute-start | bytes 147464 | tf_op jit(solution)/shard_map/ppermute | solution.py:222
  28.5 1.3 %collective-permute-done.7.refs_0_ = bf16[64,384]{1,0:T(8,128)(2,1)S(1)} collective-permute-done((bf16[64,384]{1,0:T(8,128)(2,1)S(1)}, bf16[64,384]{1,0:T(8,128)(2,1)S(1)}, u32[]{:S(2)}, u32[]{:S(2)}) %collective-permute-start.7) | collective-permute-done | bytes 49184 | tf_op jit(solution)/shard_map/ppermute | solution.py:222
  29.8 1.3 %collective-permute-done.10.refs_3_ = bf16[64,384]{1,0:T(8,128)(2,1)S(1)} collective-permute-done((bf16[64,384]{1,0:T(8,128)(2,1)S(1)}, bf16[64,384]{1,0:T(8,128)(2,1)S(1)}, u32[]{:S(2)}, u32[]{:S(2)}) %collective-permute-start.10) | collective-permute-done | bytes 49184 | tf_op jit(solution)/shard_map/ppermute | solution.py:222
  31.1 0.0 collective-permute-done.9.refs_2_
  31.1 0.7 %unpack.1 = bf16[1,64,1536]{2,1,0:T(8,128)(2,1)} custom-call(bf16[64,384]{1,0:T(8,128)(2,1)S(1)} %get-tuple-element.21.refs_1_.refs_0_, bf16[64,384]{1,0:T(8,128)(2,1)S(1)} %hold.12.refs_1_, bf16[64,384]{1,0:T(8,128)(2,1)S(1)} %collective-permute-done.9.refs_2_, bf16[64,384]{1,0:T(8,128)(2,1)S(1)} %collective-permute-done.10.refs_3_), custom_call_target="tpu_custom_call" | custom-call | bytes 393216 | tf_op jit(solution)/shard_map/unpack/pallas_call | solution.py:273
  (11 shorter events, 0.0 us)
Async XLA Ops:
  1.2 8.8 %collective-permute-start.1 = (bf16[64,768]{1,0:T(8,128)(2,1)S(1)}, bf16[64,768]{1,0:T(8,128)(2,1)S(1)}, u32[]{:S(2)}, u32[]{:S(2)}) collective-permute-start(bf16[64,768]{1,0:T(8,128)(2,1)S(1)} %get-tuple-element.17), channel_id=1, source_target_pairs={{0,12},{4,8},{8,4},{12,0},{1,13},{5,9},{9,5},{13,1},{2,14},{6,10},... | collective-permute-start | bytes 294920 | tf_op jit(solution)/shard_map/ppermute | solution.py:222
  6.3 8.1 %collective-permute-start = (bf16[64,1152]{1,0:T(8,128)(2,1)S(1)}, bf16[64,1152]{1,0:T(8,128)(2,1)S(1)}, u32[]{:S(2)}, u32[]{:S(2)}) collective-permute-start(bf16[64,1152]{1,0:T(8,128)(2,1)S(1)} %get-tuple-element.15), channel_id=1, source_target_pairs={{0,4},{4,0},{8,12},{12,8},{1,5},{5,1},{9,13},{13,9},{2,6},{6,2},{1... | collective-permute-start | bytes 442376 | tf_op jit(solution)/shard_map/ppermute | solution.py:222
  6.3 11.5 %collective-permute-start.2 = (bf16[64,768]{1,0:T(8,128)(2,1)S(1)}, bf16[64,768]{1,0:T(8,128)(2,1)S(1)}, u32[]{:S(2)}, u32[]{:S(2)}) collective-permute-start(bf16[64,768]{1,0:T(8,128)(2,1)S(1)} %get-tuple-element.18), channel_id=1, source_target_pairs={{0,8},{4,12},{8,0},{12,4},{1,9},{5,13},{9,1},{13,5},{2,10},{6,14},... | collective-permute-start | bytes 294920 | tf_op jit(solution)/shard_map/ppermute | solution.py:222
  6.9 11.7 %collective-permute-start.3 = (bf16[64,768]{1,0:T(8,128)(2,1)S(1)}, bf16[64,768]{1,0:T(8,128)(2,1)S(1)}, u32[]{:S(2)}, u32[]{:S(2)}) collective-permute-start(bf16[64,768]{1,0:T(8,128)(2,1)S(1)} %get-tuple-element.16.refs_1_), channel_id=1, source_target_pairs={{0,2},{2,0},{1,3},{3,1},{4,6},{6,4},{5,7},{7,5},{8,10},{10,8},{9,1... | collective-permute-start | bytes 294920 | tf_op jit(solution)/shard_map/ppermute | solution.py:225
  14.4 7.6 %collective-permute-start.4 = (bf16[2,64,768]{2,1,0:T(8,128)(2,1)S(1)}, bf16[2,64,768]{2,1,0:T(8,128)(2,1)S(1)}, u32[]{:S(2)}, u32[]{:S(2)}) collective-permute-start(bf16[2,64,768]{2,1,0:T(8,128)(2,1)S(1)} %join.3.refs_1_), channel_id=1, source_target_pairs={{0,2},{2,0},{1,3},{3,1},{4,6},{6,4},{5,7},{7,5},{8,10},{10,8},{9,1... | collective-permute-start | bytes 589832 | tf_op jit(solution)/shard_map/ppermute | solution.py:225
  16.1 5.9 %collective-permute-start.6 = (bf16[64,384]{1,0:T(8,128)(2,1)S(1)}, bf16[64,384]{1,0:T(8,128)(2,1)S(1)}, u32[]{:S(2)}, u32[]{:S(2)}) collective-permute-start(bf16[64,384]{1,0:T(8,128)(2,1)S(1)} %hold.11), channel_id=1, source_target_pairs={{0,12},{4,8},{8,4},{12,0},{1,13},{5,9},{9,5},{13,1},{2,14},{6,10},... | collective-permute-start | bytes 147464 | tf_op jit(solution)/shard_map/ppermute | solution.py:222
  17.8 5.1 %collective-permute-start.5 = (bf16[64,768]{1,0:T(8,128)(2,1)S(1)}, bf16[64,768]{1,0:T(8,128)(2,1)S(1)}, u32[]{:S(2)}, u32[]{:S(2)}) collective-permute-start(bf16[64,768]{1,0:T(8,128)(2,1)S(1)} %hold.9.refs_3_.refs_1_), channel_id=1, source_target_pairs={{0,2},{2,0},{1,3},{3,1},{4,6},{6,4},{5,7},{7,5},{8,10},{10,8},{9,1... | collective-permute-start | bytes 294920 | tf_op jit(solution)/shard_map/ppermute | solution.py:225
  18.3 7.0 %collective-permute-start.8 = (bf16[64,384]{1,0:T(8,128)(2,1)S(1)}, bf16[64,384]{1,0:T(8,128)(2,1)S(1)}, u32[]{:S(2)}, u32[]{:S(2)}) collective-permute-start(bf16[64,384]{1,0:T(8,128)(2,1)S(1)} %hold.13), channel_id=1, source_target_pairs={{0,8},{4,12},{8,0},{12,4},{1,9},{5,13},{9,1},{13,5},{2,10},{6,14},... | collective-permute-start | bytes 147464 | tf_op jit(solution)/shard_map/ppermute | solution.py:222
  23.5 6.3 %collective-permute-start.7 = (bf16[64,384]{1,0:T(8,128)(2,1)S(1)}, bf16[64,384]{1,0:T(8,128)(2,1)S(1)}, u32[]{:S(2)}, u32[]{:S(2)}) collective-permute-start(bf16[64,384]{1,0:T(8,128)(2,1)S(1)} %get-tuple-element.22), channel_id=1, source_target_pairs={{0,12},{4,8},{8,4},{12,0},{1,13},{5,9},{9,5},{13,1},{2,14},{6,10},... | collective-permute-start | bytes 147464 | tf_op jit(solution)/shard_map/ppermute | solution.py:222
  25.7 5.3 %collective-permute-start.9 = (bf16[64,384]{1,0:T(8,128)(2,1)S(1)}, bf16[64,384]{1,0:T(8,128)(2,1)S(1)}, u32[]{:S(2)}, u32[]{:S(2)}) collective-permute-start(bf16[64,384]{1,0:T(8,128)(2,1)S(1)} %attend.3.refs_1_), channel_id=1, source_target_pairs={{0,8},{4,12},{8,0},{12,4},{1,9},{5,13},{9,1},{13,5},{2,10},{6,14},... | collective-permute-start | bytes 147464 | tf_op jit(solution)/shard_map/ppermute | solution.py:222
  25.8 5.2 %collective-permute-start.10 = (bf16[64,384]{1,0:T(8,128)(2,1)S(1)}, bf16[64,384]{1,0:T(8,128)(2,1)S(1)}, u32[]{:S(2)}, u32[]{:S(2)}) collective-permute-start(bf16[64,384]{1,0:T(8,128)(2,1)S(1)} %hold.15), channel_id=1, source_target_pairs={{0,4},{4,0},{8,12},{12,8},{1,5},{5,1},{9,13},{13,9},{2,6},{6,2},{1... | collective-permute-start | bytes 147464 | tf_op jit(solution)/shard_map/ppermute | solution.py:222

commit v13 on v11

--- a/solution.py
+++ b/solution.py
@@ -9,7 +9,10 @@
 from jax.sharding import PartitionSpec as P
 
 HD = 128
-EFFORT = 15 * 10**8
+EFFORT = 10**9
+EFFORT_OWN = 3 * 10**8
+EFFORT_NEAR = 0
+EFFORT_FAR = (10**9, 2 * 10**9)
 ANY = pl.BlockSpec(memory_space=pl.ANY)
 HBM = pl.BlockSpec(memory_space=pltpu.HBM)
 VMEM = pl.BlockSpec(memory_space=pltpu.VMEM)
@@ -225,18 +228,19 @@
     own_kv, own_q = packed[-2:]
     far_kv = [to_block(sent[s, kv], s) for s in far]
     near_kvq = to_block(sent[1, kv + q], 1)
-    near_kv = join([own_kv, near_kvq], [0, 0], 2 * part)
-    groups = [near_kv] + [join([array], [0], 2 * part) for array in far_kv]
-    far_q = [to_block(hold([sent[s, q]], [group])[0], s) for s, group in zip(far, groups[1:])]
-    crossed = [to_column(group, t) for group in groups for t in range(1, columns_of)]
-    far_q[0] = join(far_q[:1], [0], part, EFFORT)
-    near_q = join([own_q, near_kvq], [0, 2 * part], part, EFFORT, crossed[: columns_of - 1])
-
-    holders = [near_kvq, own_kv] + far_kv
+    far_kv = [hold([array], (), effort)[0] for array, effort in zip(far_kv, EFFORT_FAR)]
+    near_kv = join([near_kvq], [0], 2 * part, EFFORT_NEAR)
+    far_q = [to_block(hold([sent[s, q]], [array])[0], s) for s, array in zip(far, far_kv)]
+    own_kv_x, first_x, near_x, second_x = (
+        [to_column(group, t) for t in range(1, columns_of)]
+        for group in (own_kv, far_kv[0], near_kv[0], far_kv[1])
+    )
+    own_kv_x = hold(own_kv_x, effort=EFFORT_OWN)
+    near_q = join([own_q, near_kvq], [0, 2 * part], part)
+    far_q[0] = join(far_q[:1], [0], part, EFFORT, [*own_kv_x, *first_x, *near_x])
+
+    holders = [near_kvq, own_kv, *far_kv, *own_kv_x, *first_x, *near_x, *second_x]
     keys = [(at, None) for at in range(len(holders))]
-    for array in crossed:
-        keys += [(len(holders), at) for at in range(array.shape[0])]
-        holders.append(array)
 
     def attend(query_arrays, query_places):
         rows = tokens * len(query_places)

time: 31.5 us -> 30.5 us (0.968)
  waiting for transfers between devices: 12 us -> 6.15 us
  starting transfers between devices: 16.3 us -> 21.1 us
    ppermute x8, waiting for transfers between devices: 10.4 us -> 4.29 us  [to_block(): return lax.ppermute(array, 'blk', [(i, i ^ s) for i in range(blocks)])]
    ppermute x8, starting transfers between devices: 12.5 us -> 15.7 us  [to_block(): return lax.ppermute(array, 'blk', [(i, i ^ s) for i in range(blocks)])]
    ppermute x3 -> x4, starting transfers between devices: 3.79 us -> 5.41 us  [to_column(): lax.ppermute(array, 'uly', [(i, (i + t) % columns_of) for i in range(colu...]
    ppermute x3 -> x4, waiting for transfers between devices: 1.54 us -> 1.87 us  [to_column(): lax.ppermute(array, 'uly', [(i, (i + t) % columns_of) for i in range(colu...]
  transfers between devices with their start and end apart: 11 -> 12, of which waited for: 9 -> 5; matrix products, arithmetic and copies ran while one was open for 0% -> 0% of each run, Pallas kernels for 4% -> 4%
where the time goes in v13:
time: 30.5 us; the launch traced here: 30.3 us
  starting transfers between devices  21.1 us (69%)
  waiting for transfers between devices  6.15 us (20%)
  Pallas kernels  3.03 us (10%)
    ppermute x8, starting transfers between devices, to_block(): return lax.ppermute(array, 'blk', [(i, i ^ s) for i in range(blocks)])  15.7 us
    ppermute x4, starting transfers between devices, to_column(): lax.ppermute(array, 'uly', [(i, (i + t) % columns_of) for i in range(colu...  5.41 us
    ppermute x8, waiting for transfers between devices, to_block(): return lax.ppermute(array, 'blk', [(i, i ^ s) for i in range(blocks)])  4.29 us
    ppermute x4, waiting for transfers between devices, to_column(): lax.ppermute(array, 'uly', [(i, (i + t) % columns_of) for i in range(colu...  1.87 us
    pallas_call x1, Pallas kernels, local_blocks(): pl.pallas_call(functools.partial(pack_kernel, messages, part), out_shape=...  1.17 us
    pallas_call x2, Pallas kernels, attend(): pl.pallas_call(functools.partial(attend_kernel, len(holders), keys, query...  1.13 us
    pallas_call x1, Pallas kernels, local_blocks(): pl.pallas_call(functools.partial(unpack_kernel, order, part), out_shape=j...  0.7 us
  transfers between devices with their start and end apart: 12, of which 5 were waited for; matrix products, arithmetic and copies ran while one was open for 0% of the time, Pallas kernels for 4%

profile of v13, /device:TPU:0, one launch (start us, length us, event | category | flops | bytes accessed | tf_op | source)
XLA Modules:
  0.0 30.3 jit_solution(10583319273000431066)
XLA Ops:
  0.0 1.2 %pack.1 = (bf16[64,768]{1,0:T(8,128)(2,1)S(1)}, bf16[64,768]{1,0:T(8,128)(2,1)S(1)}, bf16[64,1152]{1,0:T(8,128)(2,1)S(1)}, bf16[64,384]{1,0:T(8,128)(2,1)S(1)}, ...) custom-call(bf16[1,64,1536]{2,1,0:T(8,128)(2,1)} %q_ref.1, ...), custom_call_target="tpu_custom_call" | custom-call | bytes 1179648 | tf_op jit(solution)/shard_map/pack/pallas_call | solution.py:205
  1.2 5.1 %collective-permute-start.1 = (bf16[64,768]{1,0:T(8,128)(2,1)S(1)}, bf16[64,768]{1,0:T(8,128)(2,1)S(1)}, u32[]{:S(2)}, u32[]{:S(2)}) collective-permute-start(bf16[64,768]{1,0:T(8,128)(2,1)S(1)} %get-tuple-element.17), channel_id=1, source_target_pairs={{0,12},{4,8},{8,4},{12,0},{1,13},{5,9},{9,5},{13,1},{2,14},{6,10},... | collective-permute-start | bytes 294920 | tf_op jit(solution)/shard_map/ppermute | solution.py:222
  6.3 0.0 collective-permute-start
  6.3 0.6 %collective-permute-start.2 = (bf16[64,768]{1,0:T(8,128)(2,1)S(1)}, bf16[64,768]{1,0:T(8,128)(2,1)S(1)}, u32[]{:S(2)}, u32[]{:S(2)}) collective-permute-start(bf16[64,768]{1,0:T(8,128)(2,1)S(1)} %get-tuple-element.18), channel_id=1, source_target_pairs={{0,8},{4,12},{8,0},{12,4},{1,9},{5,13},{9,1},{13,5},{2,10},{6,14},... | collective-permute-start | bytes 294920 | tf_op jit(solution)/shard_map/ppermute | solution.py:222
  6.9 1.6 %collective-permute-start.3 = (bf16[64,768]{1,0:T(8,128)(2,1)S(1)}, bf16[64,768]{1,0:T(8,128)(2,1)S(1)}, u32[]{:S(2)}, u32[]{:S(2)}) collective-permute-start(bf16[64,768]{1,0:T(8,128)(2,1)S(1)} %get-tuple-element.16.refs_1_), channel_id=1, source_target_pairs={{0,2},{2,0},{1,3},{3,1},{4,6},{6,4},{5,7},{7,5},{8,10},{10,8},{9,1... | collective-permute-start | bytes 294920 | tf_op jit(solution)/shard_map/ppermute | solution.py:225
  8.6 1.4 %collective-permute-done.1.refs_0_ = bf16[64,768]{1,0:T(8,128)(2,1)S(1)} collective-permute-done((bf16[64,768]{1,0:T(8,128)(2,1)S(1)}, bf16[64,768]{1,0:T(8,128)(2,1)S(1)}, u32[]{:S(2)}, u32[]{:S(2)}) %collective-permute-start.1) | collective-permute-done | bytes 98336 | tf_op jit(solution)/shard_map/ppermute | solution.py:222
  10.0 1.7 %collective-permute-start.4 = (bf16[64,768]{1,0:T(8,128)(2,1)S(1)}, bf16[64,768]{1,0:T(8,128)(2,1)S(1)}, u32[]{:S(2)}, u32[]{:S(2)}) collective-permute-start(bf16[64,768]{1,0:T(8,128)(2,1)S(1)} %hold.8.refs_1_.refs_2_), channel_id=1, source_target_pairs={{0,2},{2,0},{1,3},{3,1},{4,6},{6,4},{5,7},{7,5},{8,10},{10,8},{9,1... | collective-permute-start | bytes 294920 | tf_op jit(solution)/shard_map/ppermute | solution.py:225
  11.7 3.7 %collective-permute-start.7 = (bf16[64,384]{1,0:T(8,128)(2,1)S(1)}, bf16[64,384]{1,0:T(8,128)(2,1)S(1)}, u32[]{:S(2)}, u32[]{:S(2)}) collective-permute-start(bf16[64,384]{1,0:T(8,128)(2,1)S(1)} %hold.11), channel_id=1, source_target_pairs={{0,12},{4,8},{8,4},{12,0},{1,13},{5,9},{9,5},{13,1},{2,14},{6,10},... | collective-permute-start | bytes 147464 | tf_op jit(solution)/shard_map/ppermute | solution.py:222
  15.3 0.0 collective-permute-done.refs_0_.refs_1_
  15.3 1.0 %collective-permute-start.5 = (bf16[64,768]{1,0:T(8,128)(2,1)S(1)}, bf16[64,768]{1,0:T(8,128)(2,1)S(1)}, u32[]{:S(2)}, u32[]{:S(2)}) collective-permute-start(bf16[64,768]{1,0:T(8,128)(2,1)S(1)} %bitcast.1), channel_id=1, source_target_pairs={{0,2},{2,0},{1,3},{3,1},{4,6},{6,4},{5,7},{7,5},{8,10},{10,8},{9,1... | collective-permute-start | bytes 294920 | tf_op jit(solution)/shard_map/ppermute | solution.py:225
  16.4 0.0 collective-permute-done.2.refs_0_
  16.4 1.1 %collective-permute-start.6 = (bf16[64,768]{1,0:T(8,128)(2,1)S(1)}, bf16[64,768]{1,0:T(8,128)(2,1)S(1)}, u32[]{:S(2)}, u32[]{:S(2)}) collective-permute-start(bf16[64,768]{1,0:T(8,128)(2,1)S(1)} %hold.9.refs_3_.refs_1_), channel_id=1, source_target_pairs={{0,2},{2,0},{1,3},{3,1},{4,6},{6,4},{5,7},{7,5},{8,10},{10,8},{9,1... | collective-permute-start | bytes 294920 | tf_op jit(solution)/shard_map/ppermute | solution.py:225
  17.4 0.0 collective-permute-done.3.refs_0_
  17.4 1.7 %collective-permute-start.9 = (bf16[64,384]{1,0:T(8,128)(2,1)S(1)}, bf16[64,384]{1,0:T(8,128)(2,1)S(1)}, u32[]{:S(2)}, u32[]{:S(2)}) collective-permute-start(bf16[64,384]{1,0:T(8,128)(2,1)S(1)} %hold.13), channel_id=1, source_target_pairs={{0,8},{4,12},{8,0},{12,4},{1,9},{5,13},{9,1},{13,5},{2,10},{6,14},... | collective-permute-start | bytes 147464 | tf_op jit(solution)/shard_map/ppermute | solution.py:222
  19.2 0.0 collective-permute-done.7.refs_0_
  19.2 0.0 collective-permute-done.4.refs_2_.refs_5_
  19.2 0.8 %collective-permute-done.5.refs_3_.refs_6_ = bf16[64,768]{1,0:T(8,128)(2,1)S(1)} collective-permute-done((bf16[64,768]{1,0:T(8,128)(2,1)S(1)}, bf16[64,768]{1,0:T(8,128)(2,1)S(1)}, u32[]{:S(2)}, u32[]{:S(2)}) %collective-permute-start.5) | collective-permute-done | bytes 98336 | tf_op jit(solution)/shard_map/ppermute | solution.py:225
  20.0 1.0 %collective-permute-done.6.refs_7_ = bf16[64,768]{1,0:T(8,128)(2,1)S(1)} collective-permute-done((bf16[64,768]{1,0:T(8,128)(2,1)S(1)}, bf16[64,768]{1,0:T(8,128)(2,1)S(1)}, u32[]{:S(2)}, u32[]{:S(2)}) %collective-permute-start.6) | collective-permute-done | bytes 98336 | tf_op jit(solution)/shard_map/ppermute | solution.py:225
  21.1 0.6 %attend.2 = (bf16[64,384]{1,0:T(8,128)(2,1)S(1)}, bf16[64,384]{1,0:T(8,128)(2,1)S(1)}, bf16[64,384]{1,0:T(8,128)(2,1)S(1)}) custom-call(bf16[64,1152]{1,0:T(8,128)(2,1)S(1)} %collective-permute-done.refs_0_.refs_1_, bf16[64,768]{1,0:T(8,128)(2,1)S(1)} %get-tuple-element.16.refs_1_, bf16[64,768]{1,0:T(8,128)(2,1)S(1)} %hold.8.refs_1_.refs_2_, ...), custom_call_target="tpu_custom_call" | custom-call | flops 150994944 | bytes 1081344 | tf_op jit(solution)/shard_map/attend/pallas_call | solution.py:248
  21.7 1.4 %collective-permute-start.8 = (bf16[64,384]{1,0:T(8,128)(2,1)S(1)}, bf16[64,384]{1,0:T(8,128)(2,1)S(1)}, u32[]{:S(2)}, u32[]{:S(2)}) collective-permute-start(bf16[64,384]{1,0:T(8,128)(2,1)S(1)} %get-tuple-element.22), channel_id=1, source_target_pairs={{0,12},{4,8},{8,4},{12,0},{1,13},{5,9},{9,5},{13,1},{2,14},{6,10},... | collective-permute-start | bytes 147464 | tf_op jit(solution)/shard_map/ppermute | solution.py:222
  23.1 0.0 collective-permute-done.9.refs_0_
  23.1 0.5 %attend.3.refs_1_ = bf16[64,384]{1,0:T(8,128)(2,1)S(1)} custom-call(bf16[64,1152]{1,0:T(8,128)(2,1)S(1)} %collective-permute-done.refs_0_.refs_1_, bf16[64,768]{1,0:T(8,128)(2,1)S(1)} %get-tuple-element.16.refs_1_, bf16[64,768]{1,0:T(8,128)(2,1)S(1)} %hold.8.refs_1_.refs_2_, bf16[64,768]{1,0:T(8,128)(2,1)S(1)} %hold.9.refs_3_.refs_1_, ...), custom_call_target="tpu_custom_call" | custom-call | flops 50331648 | bytes 884736 | tf_op jit(solution)/shard_map/attend/pallas_call | solution.py:248
  23.6 1.7 %collective-permute-start.10 = (bf16[64,384]{1,0:T(8,128)(2,1)S(1)}, bf16[64,384]{1,0:T(8,128)(2,1)S(1)}, u32[]{:S(2)}, u32[]{:S(2)}) collective-permute-start(bf16[64,384]{1,0:T(8,128)(2,1)S(1)} %attend.3.refs_1_), channel_id=1, source_target_pairs={{0,8},{4,12},{8,0},{12,4},{1,9},{5,13},{9,1},{13,5},{2,10},{6,14},... | collective-permute-start | bytes 147464 | tf_op jit(solution)/shard_map/ppermute | solution.py:222
  25.3 1.5 %collective-permute-start.11 = (bf16[64,384]{1,0:T(8,128)(2,1)S(1)}, bf16[64,384]{1,0:T(8,128)(2,1)S(1)}, u32[]{:S(2)}, u32[]{:S(2)}) collective-permute-start(bf16[64,384]{1,0:T(8,128)(2,1)S(1)} %hold.15), channel_id=1, source_target_pairs={{0,4},{4,0},{8,12},{12,8},{1,5},{5,1},{9,13},{13,9},{2,6},{6,2},{1... | collective-permute-start | bytes 147464 | tf_op jit(solution)/shard_map/ppermute | solution.py:222
  26.7 0.9 %collective-permute-done.8.refs_0_ = bf16[64,384]{1,0:T(8,128)(2,1)S(1)} collective-permute-done((bf16[64,384]{1,0:T(8,128)(2,1)S(1)}, bf16[64,384]{1,0:T(8,128)(2,1)S(1)}, u32[]{:S(2)}, u32[]{:S(2)}) %collective-permute-start.8) | collective-permute-done | bytes 49184 | tf_op jit(solution)/shard_map/ppermute | solution.py:222
  27.7 1.9 %collective-permute-done.11.refs_3_ = bf16[64,384]{1,0:T(8,128)(2,1)S(1)} collective-permute-done((bf16[64,384]{1,0:T(8,128)(2,1)S(1)}, bf16[64,384]{1,0:T(8,128)(2,1)S(1)}, u32[]{:S(2)}, u32[]{:S(2)}) %collective-permute-start.11) | collective-permute-done | bytes 49184 | tf_op jit(solution)/shard_map/ppermute | solution.py:222
  29.6 0.0 collective-permute-done.10.refs_2_
  29.6 0.7 %unpack.1 = bf16[1,64,1536]{2,1,0:T(8,128)(2,1)} custom-call(bf16[64,384]{1,0:T(8,128)(2,1)S(1)} %get-tuple-element.21.refs_1_.refs_0_, bf16[64,384]{1,0:T(8,128)(2,1)S(1)} %hold.12.refs_1_, bf16[64,384]{1,0:T(8,128)(2,1)S(1)} %collective-permute-done.10.refs_2_, bf16[64,384]{1,0:T(8,128)(2,1)S(1)} %collective-permute-done.11.refs_3_), custom_call_target="tpu_custom_call" | custom-call | bytes 393216 | tf_op jit(solution)/shard_map/unpack/pallas_call | solution.py:272
  (11 shorter events, 0.0 us)
Async XLA Ops:
  1.2 8.8 %collective-permute-start.1 = (bf16[64,768]{1,0:T(8,128)(2,1)S(1)}, bf16[64,768]{1,0:T(8,128)(2,1)S(1)}, u32[]{:S(2)}, u32[]{:S(2)}) collective-permute-start(bf16[64,768]{1,0:T(8,128)(2,1)S(1)} %get-tuple-element.17), channel_id=1, source_target_pairs={{0,12},{4,8},{8,4},{12,0},{1,13},{5,9},{9,5},{13,1},{2,14},{6,10},... | collective-permute-start | bytes 294920 | tf_op jit(solution)/shard_map/ppermute | solution.py:222
  6.3 9.0 %collective-permute-start = (bf16[64,1152]{1,0:T(8,128)(2,1)S(1)}, bf16[64,1152]{1,0:T(8,128)(2,1)S(1)}, u32[]{:S(2)}, u32[]{:S(2)}) collective-permute-start(bf16[64,1152]{1,0:T(8,128)(2,1)S(1)} %get-tuple-element.15), channel_id=1, source_target_pairs={{0,4},{4,0},{8,12},{12,8},{1,5},{5,1},{9,13},{13,9},{2,6},{6,2},{1... | collective-permute-start | bytes 442376 | tf_op jit(solution)/shard_map/ppermute | solution.py:222
  6.3 10.1 %collective-permute-start.2 = (bf16[64,768]{1,0:T(8,128)(2,1)S(1)}, bf16[64,768]{1,0:T(8,128)(2,1)S(1)}, u32[]{:S(2)}, u32[]{:S(2)}) collective-permute-start(bf16[64,768]{1,0:T(8,128)(2,1)S(1)} %get-tuple-element.18), channel_id=1, source_target_pairs={{0,8},{4,12},{8,0},{12,4},{1,9},{5,13},{9,1},{13,5},{2,10},{6,14},... | collective-permute-start | bytes 294920 | tf_op jit(solution)/shard_map/ppermute | solution.py:222
  6.9 10.5 %collective-permute-start.3 = (bf16[64,768]{1,0:T(8,128)(2,1)S(1)}, bf16[64,768]{1,0:T(8,128)(2,1)S(1)}, u32[]{:S(2)}, u32[]{:S(2)}) collective-permute-start(bf16[64,768]{1,0:T(8,128)(2,1)S(1)} %get-tuple-element.16.refs_1_), channel_id=1, source_target_pairs={{0,2},{2,0},{1,3},{3,1},{4,6},{6,4},{5,7},{7,5},{8,10},{10,8},{9,1... | collective-permute-start | bytes 294920 | tf_op jit(solution)/shard_map/ppermute | solution.py:225
  10.0 9.2 %collective-permute-start.4 = (bf16[64,768]{1,0:T(8,128)(2,1)S(1)}, bf16[64,768]{1,0:T(8,128)(2,1)S(1)}, u32[]{:S(2)}, u32[]{:S(2)}) collective-permute-start(bf16[64,768]{1,0:T(8,128)(2,1)S(1)} %hold.8.refs_1_.refs_2_), channel_id=1, source_target_pairs={{0,2},{2,0},{1,3},{3,1},{4,6},{6,4},{5,7},{7,5},{8,10},{10,8},{9,1... | collective-permute-start | bytes 294920 | tf_op jit(solution)/shard_map/ppermute | solution.py:225
  11.7 7.5 %collective-permute-start.7 = (bf16[64,384]{1,0:T(8,128)(2,1)S(1)}, bf16[64,384]{1,0:T(8,128)(2,1)S(1)}, u32[]{:S(2)}, u32[]{:S(2)}) collective-permute-start(bf16[64,384]{1,0:T(8,128)(2,1)S(1)} %hold.11), channel_id=1, source_target_pairs={{0,12},{4,8},{8,4},{12,0},{1,13},{5,9},{9,5},{13,1},{2,14},{6,10},... | collective-permute-start | bytes 147464 | tf_op jit(solution)/shard_map/ppermute | solution.py:222
  15.3 4.7 %collective-permute-start.5 = (bf16[64,768]{1,0:T(8,128)(2,1)S(1)}, bf16[64,768]{1,0:T(8,128)(2,1)S(1)}, u32[]{:S(2)}, u32[]{:S(2)}) collective-permute-start(bf16[64,768]{1,0:T(8,128)(2,1)S(1)} %bitcast.1), channel_id=1, source_target_pairs={{0,2},{2,0},{1,3},{3,1},{4,6},{6,4},{5,7},{7,5},{8,10},{10,8},{9,1... | collective-permute-start | bytes 294920 | tf_op jit(solution)/shard_map/ppermute | solution.py:225
  16.4 4.7 %collective-permute-start.6 = (bf16[64,768]{1,0:T(8,128)(2,1)S(1)}, bf16[64,768]{1,0:T(8,128)(2,1)S(1)}, u32[]{:S(2)}, u32[]{:S(2)}) collective-permute-start(bf16[64,768]{1,0:T(8,128)(2,1)S(1)} %hold.9.refs_3_.refs_1_), channel_id=1, source_target_pairs={{0,2},{2,0},{1,3},{3,1},{4,6},{6,4},{5,7},{7,5},{8,10},{10,8},{9,1... | collective-permute-start | bytes 294920 | tf_op jit(solution)/shard_map/ppermute | solution.py:225
  17.4 5.6 %collective-permute-start.9 = (bf16[64,384]{1,0:T(8,128)(2,1)S(1)}, bf16[64,384]{1,0:T(8,128)(2,1)S(1)}, u32[]{:S(2)}, u32[]{:S(2)}) collective-permute-start(bf16[64,384]{1,0:T(8,128)(2,1)S(1)} %hold.13), channel_id=1, source_target_pairs={{0,8},{4,12},{8,0},{12,4},{1,9},{5,13},{9,1},{13,5},{2,10},{6,14},... | collective-permute-start | bytes 147464 | tf_op jit(solution)/shard_map/ppermute | solution.py:222
  21.7 6.0 %collective-permute-start.8 = (bf16[64,384]{1,0:T(8,128)(2,1)S(1)}, bf16[64,384]{1,0:T(8,128)(2,1)S(1)}, u32[]{:S(2)}, u32[]{:S(2)}) collective-permute-start(bf16[64,384]{1,0:T(8,128)(2,1)S(1)} %get-tuple-element.22), channel_id=1, source_target_pairs={{0,12},{4,8},{8,4},{12,0},{1,13},{5,9},{9,5},{13,1},{2,14},{6,10},... | collective-permute-start | bytes 147464 | tf_op jit(solution)/shard_map/ppermute | solution.py:222
  23.6 6.0 %collective-permute-start.10 = (bf16[64,384]{1,0:T(8,128)(2,1)S(1)}, bf16[64,384]{1,0:T(8,128)(2,1)S(1)}, u32[]{:S(2)}, u32[]{:S(2)}) collective-permute-start(bf16[64,384]{1,0:T(8,128)(2,1)S(1)} %attend.3.refs_1_), channel_id=1, source_target_pairs={{0,8},{4,12},{8,0},{12,4},{1,9},{5,13},{9,1},{13,5},{2,10},{6,14},... | collective-permute-start | bytes 147464 | tf_op jit(solution)/shard_map/ppermute | solution.py:222
  25.3 4.3 %collective-permute-start.11 = (bf16[64,384]{1,0:T(8,128)(2,1)S(1)}, bf16[64,384]{1,0:T(8,128)(2,1)S(1)}, u32[]{:S(2)}, u32[]{:S(2)}) collective-permute-start(bf16[64,384]{1,0:T(8,128)(2,1)S(1)} %hold.15), channel_id=1, source_target_pairs={{0,4},{4,0},{8,12},{12,8},{1,5},{5,1},{9,13},{13,9},{2,6},{6,2},{1... | collective-permute-start | bytes 147464 | tf_op jit(solution)/shard_map/ppermute | solution.py:222

commit v14 on v13

--- a/solution.py
+++ b/solution.py
@@ -9,10 +9,11 @@
 from jax.sharding import PartitionSpec as P
 
 HD = 128
-EFFORT = 10**9
-EFFORT_OWN = 3 * 10**8
+EFFORT = 0
+EFFORT_OWN = 10**9
+EFFORT_QUERIES = 2 * 10**8
 EFFORT_NEAR = 0
-EFFORT_FAR = (10**9, 2 * 10**9)
+EFFORT_FAR = (10**9, 5 * 10**8)
 ANY = pl.BlockSpec(memory_space=pl.ANY)
 HBM = pl.BlockSpec(memory_space=pltpu.HBM)
 VMEM = pl.BlockSpec(memory_space=pltpu.VMEM)
@@ -230,14 +231,16 @@
     near_kvq = to_block(sent[1, kv + q], 1)
     far_kv = [hold([array], (), effort)[0] for array, effort in zip(far_kv, EFFORT_FAR)]
     near_kv = join([near_kvq], [0], 2 * part, EFFORT_NEAR)
-    far_q = [to_block(hold([sent[s, q]], [array])[0], s) for s, array in zip(far, far_kv)]
+    far_q = [to_block(sent[far[0], q], far[0])]
+    far_q += [to_block(hold([sent[s, q]], [array])[0], s) for s, array in zip(far[1:], far_kv[1:])]
     own_kv_x, first_x, near_x, second_x = (
         [to_column(group, t) for t in range(1, columns_of)]
         for group in (own_kv, far_kv[0], near_kv[0], far_kv[1])
     )
     own_kv_x = hold(own_kv_x, effort=EFFORT_OWN)
     near_q = join([own_q, near_kvq], [0, 2 * part], part)
-    far_q[0] = join(far_q[:1], [0], part, EFFORT, [*own_kv_x, *first_x, *near_x])
+    far_q[:1] = hold(far_q[:1], [*own_kv_x, *first_x, *near_x], EFFORT)
+    far_q[:1] = hold(far_q[:1], (), EFFORT_QUERIES)
 
     holders = [near_kvq, own_kv, *far_kv, *own_kv_x, *first_x, *near_x, *second_x]
     keys = [(at, None) for at in range(len(holders))]
@@ -259,7 +262,7 @@
             name="attend",
         )(*holders, *query_arrays)
 
-    mixed = dict(zip([0, 1] + far[:-1], attend([near_q] + far_q[:-1], [(0, 0), (0, 1), (1, 0)])))
+    mixed = dict(zip([0, 1] + far[:-1], attend([near_q] + far_q[:-1], [(0, 0), (0, 1), (1, None)])))
     last_q = hold([far_q[-1]], [mixed[0]])
     mixed[far[-1]] = attend(last_q, [(0, None)])[0]
     mixed[1] = hold([mixed[1]], [mixed[far[-1]]])[0]

time: 30.5 us -> 30 us (0.984)
  starting transfers between devices: 21.1 us -> 20.6 us
    ppermute x4, starting transfers between devices: 5.41 us -> 5.06 us  [to_column(): lax.ppermute(array, 'uly', [(i, (i + t) % columns_of) for i in range(colu...]
  transfers between devices with their start and end apart: 12 -> 12, of which waited for: 5 -> 6; matrix products, arithmetic and copies ran while one was open for 0% -> 0% of each run, Pallas kernels for 4% -> 4%
where the time goes in v14:
time: 30 us; the launch traced here: 29.8 us
  starting transfers between devices  20.6 us (69%)
  waiting for transfers between devices  6.12 us (20%)
  Pallas kernels  3.02 us (10%)
    ppermute x8, starting transfers between devices, to_block(): return lax.ppermute(array, 'blk', [(i, i ^ s) for i in range(blocks)])  15.6 us
    ppermute x4, starting transfers between devices, to_column(): lax.ppermute(array, 'uly', [(i, (i + t) % columns_of) for i in range(colu...  5.06 us
    ppermute x8, waiting for transfers between devices, to_block(): return lax.ppermute(array, 'blk', [(i, i ^ s) for i in range(blocks)])  4.31 us
    ppermute x4, waiting for transfers between devices, to_column(): lax.ppermute(array, 'uly', [(i, (i + t) % columns_of) for i in range(colu...  1.81 us
    pallas_call x1, Pallas kernels, local_blocks(): pl.pallas_call(functools.partial(pack_kernel, messages, part), out_shape=...  1.17 us
    pallas_call x2, Pallas kernels, attend(): pl.pallas_call(functools.partial(attend_kernel, len(holders), keys, query...  1.13 us
    pallas_call x1, Pallas kernels, local_blocks(): pl.pallas_call(functools.partial(unpack_kernel, order, part), out_shape=j...  0.7 us
  transfers between devices with their start and end apart: 12, of which 6 were waited for; matrix products, arithmetic and copies ran while one was open for 0% of the time, Pallas kernels for 4%

profile of v14, /device:TPU:0, one launch (start us, length us, event | category | flops | bytes accessed | tf_op | source)
XLA Modules:
  0.0 29.8 jit_solution(13159460454871502388)
XLA Ops:
  0.0 1.2 %pack.1 = (bf16[64,768]{1,0:T(8,128)(2,1)S(1)}, bf16[64,768]{1,0:T(8,128)(2,1)S(1)}, bf16[64,1152]{1,0:T(8,128)(2,1)S(1)}, bf16[64,384]{1,0:T(8,128)(2,1)S(1)}, ...) custom-call(bf16[1,64,1536]{2,1,0:T(8,128)(2,1)} %q_ref.1, ...), custom_call_target="tpu_custom_call" | custom-call | bytes 1179648 | tf_op jit(solution)/shard_map/pack/pallas_call | solution.py:206
  1.2 5.1 %collective-permute-start.1 = (bf16[64,768]{1,0:T(8,128)(2,1)S(1)}, bf16[64,768]{1,0:T(8,128)(2,1)S(1)}, u32[]{:S(2)}, u32[]{:S(2)}) collective-permute-start(bf16[64,768]{1,0:T(8,128)(2,1)S(1)} %get-tuple-element.17), channel_id=1, source_target_pairs={{0,12},{4,8},{8,4},{12,0},{1,13},{5,9},{9,5},{13,1},{2,14},{6,10},... | collective-permute-start | bytes 294920 | tf_op jit(solution)/shard_map/ppermute | solution.py:223
  6.3 0.0 collective-permute-start
  6.3 0.6 %collective-permute-start.2 = (bf16[64,768]{1,0:T(8,128)(2,1)S(1)}, bf16[64,768]{1,0:T(8,128)(2,1)S(1)}, u32[]{:S(2)}, u32[]{:S(2)}) collective-permute-start(bf16[64,768]{1,0:T(8,128)(2,1)S(1)} %get-tuple-element.18), channel_id=1, source_target_pairs={{0,8},{4,12},{8,0},{12,4},{1,9},{5,13},{9,1},{13,5},{2,10},{6,14},... | collective-permute-start | bytes 294920 | tf_op jit(solution)/shard_map/ppermute | solution.py:223
  6.9 3.7 %collective-permute-start.7 = (bf16[64,384]{1,0:T(8,128)(2,1)S(1)}, bf16[64,384]{1,0:T(8,128)(2,1)S(1)}, u32[]{:S(2)}, u32[]{:S(2)}) collective-permute-start(bf16[64,384]{1,0:T(8,128)(2,1)S(1)} %get-tuple-element.20), channel_id=1, source_target_pairs={{0,12},{4,8},{8,4},{12,0},{1,13},{5,9},{9,5},{13,1},{2,14},{6,10},... | collective-permute-start | bytes 147464 | tf_op jit(solution)/shard_map/ppermute | solution.py:223
  10.7 1.5 %collective-permute-start.3 = (bf16[64,768]{1,0:T(8,128)(2,1)S(1)}, bf16[64,768]{1,0:T(8,128)(2,1)S(1)}, u32[]{:S(2)}, u32[]{:S(2)}) collective-permute-start(bf16[64,768]{1,0:T(8,128)(2,1)S(1)} %get-tuple-element.16.refs_1_), channel_id=1, source_target_pairs={{0,2},{2,0},{1,3},{3,1},{4,6},{6,4},{5,7},{7,5},{8,10},{10,8},{9,1... | collective-permute-start | bytes 294920 | tf_op jit(solution)/shard_map/ppermute | solution.py:226
  12.2 0.0 collective-permute-done.1.refs_0_
  12.2 0.5 %collective-permute-start.4 = (bf16[64,768]{1,0:T(8,128)(2,1)S(1)}, bf16[64,768]{1,0:T(8,128)(2,1)S(1)}, u32[]{:S(2)}, u32[]{:S(2)}) collective-permute-start(bf16[64,768]{1,0:T(8,128)(2,1)S(1)} %hold.9.refs_2_), channel_id=1, source_target_pairs={{0,2},{2,0},{1,3},{3,1},{4,6},{6,4},{5,7},{7,5},{8,10},{10,8},{9,1... | collective-permute-start | bytes 294920 | tf_op jit(solution)/shard_map/ppermute | solution.py:226
  12.7 1.9 %collective-permute-done.refs_0_.refs_1_ = bf16[64,1152]{1,0:T(8,128)(2,1)S(1)} collective-permute-done((bf16[64,1152]{1,0:T(8,128)(2,1)S(1)}, bf16[64,1152]{1,0:T(8,128)(2,1)S(1)}, u32[]{:S(2)}, u32[]{:S(2)}) %collective-permute-start) | collective-permute-done | bytes 147488 | tf_op jit(solution)/shard_map/ppermute | solution.py:223
  14.6 1.8 %collective-permute-start.5 = (bf16[64,768]{1,0:T(8,128)(2,1)S(1)}, bf16[64,768]{1,0:T(8,128)(2,1)S(1)}, u32[]{:S(2)}, u32[]{:S(2)}) collective-permute-start(bf16[64,768]{1,0:T(8,128)(2,1)S(1)} %bitcast.1), channel_id=1, source_target_pairs={{0,2},{2,0},{1,3},{3,1},{4,6},{6,4},{5,7},{7,5},{8,10},{10,8},{9,1... | collective-permute-start | bytes 294920 | tf_op jit(solution)/shard_map/ppermute | solution.py:226
  16.4 0.0 collective-permute-done.2.refs_0_
  16.4 1.2 %collective-permute-start.6 = (bf16[64,768]{1,0:T(8,128)(2,1)S(1)}, bf16[64,768]{1,0:T(8,128)(2,1)S(1)}, u32[]{:S(2)}, u32[]{:S(2)}) collective-permute-start(bf16[64,768]{1,0:T(8,128)(2,1)S(1)} %hold.10.refs_3_.refs_1_), channel_id=1, source_target_pairs={{0,2},{2,0},{1,3},{3,1},{4,6},{6,4},{5,7},{7,5},{8,10},{10,8},{9,1... | collective-permute-start | bytes 294920 | tf_op jit(solution)/shard_map/ppermute | solution.py:226
  17.6 0.0 collective-permute-done.3.refs_0_
  17.6 1.5 %collective-permute-start.9 = (bf16[64,384]{1,0:T(8,128)(2,1)S(1)}, bf16[64,384]{1,0:T(8,128)(2,1)S(1)}, u32[]{:S(2)}, u32[]{:S(2)}) collective-permute-start(bf16[64,384]{1,0:T(8,128)(2,1)S(1)} %hold.15), channel_id=1, source_target_pairs={{0,8},{4,12},{8,0},{12,4},{1,9},{5,13},{9,1},{13,5},{2,10},{6,14},... | collective-permute-start | bytes 147464 | tf_op jit(solution)/shard_map/ppermute | solution.py:223
  19.2 0.0 collective-permute-done.7.refs_0_
  19.2 0.0 collective-permute-done.4.refs_2_.refs_5_
  19.2 0.8 %collective-permute-done.5.refs_3_.refs_6_ = bf16[64,768]{1,0:T(8,128)(2,1)S(1)} collective-permute-done((bf16[64,768]{1,0:T(8,128)(2,1)S(1)}, bf16[64,768]{1,0:T(8,128)(2,1)S(1)}, u32[]{:S(2)}, u32[]{:S(2)}) %collective-permute-start.5) | collective-permute-done | bytes 98336 | tf_op jit(solution)/shard_map/ppermute | solution.py:226
  20.0 1.1 %collective-permute-done.6.refs_7_ = bf16[64,768]{1,0:T(8,128)(2,1)S(1)} collective-permute-done((bf16[64,768]{1,0:T(8,128)(2,1)S(1)}, bf16[64,768]{1,0:T(8,128)(2,1)S(1)}, u32[]{:S(2)}, u32[]{:S(2)}) %collective-permute-start.6) | collective-permute-done | bytes 98336 | tf_op jit(solution)/shard_map/ppermute | solution.py:226
  21.0 0.6 %attend.2 = (bf16[64,384]{1,0:T(8,128)(2,1)S(1)}, bf16[64,384]{1,0:T(8,128)(2,1)S(1)}, bf16[64,384]{1,0:T(8,128)(2,1)S(1)}) custom-call(bf16[64,1152]{1,0:T(8,128)(2,1)S(1)} %collective-permute-done.refs_0_.refs_1_, bf16[64,768]{1,0:T(8,128)(2,1)S(1)} %get-tuple-element.16.refs_1_, bf16[64,768]{1,0:T(8,128)(2,1)S(1)} %hold.9.refs_2_, ...), custom_call_target="tpu_custom_call" | custom-call | flops 150994944 | bytes 1081344 | tf_op jit(solution)/shard_map/attend/pallas_call | solution.py:251
  21.6 1.4 %collective-permute-start.8 = (bf16[64,384]{1,0:T(8,128)(2,1)S(1)}, bf16[64,384]{1,0:T(8,128)(2,1)S(1)}, u32[]{:S(2)}, u32[]{:S(2)}) collective-permute-start(bf16[64,384]{1,0:T(8,128)(2,1)S(1)} %get-tuple-element.22), channel_id=1, source_target_pairs={{0,12},{4,8},{8,4},{12,0},{1,13},{5,9},{9,5},{13,1},{2,14},{6,10},... | collective-permute-start | bytes 147464 | tf_op jit(solution)/shard_map/ppermute | solution.py:223
  23.1 0.0 collective-permute-done.9.refs_0_
  23.1 0.5 %attend.3.refs_1_ = bf16[64,384]{1,0:T(8,128)(2,1)S(1)} custom-call(bf16[64,1152]{1,0:T(8,128)(2,1)S(1)} %collective-permute-done.refs_0_.refs_1_, bf16[64,768]{1,0:T(8,128)(2,1)S(1)} %get-tuple-element.16.refs_1_, bf16[64,768]{1,0:T(8,128)(2,1)S(1)} %hold.9.refs_2_, bf16[64,768]{1,0:T(8,128)(2,1)S(1)} %hold.10.refs_3_.refs_1_, ...), custom_call_target="tpu_custom_call" | custom-call | flops 50331648 | bytes 884736 | tf_op jit(solution)/shard_map/attend/pallas_call | solution.py:251
  23.6 0.5 %collective-permute-start.11 = (bf16[64,384]{1,0:T(8,128)(2,1)S(1)}, bf16[64,384]{1,0:T(8,128)(2,1)S(1)}, u32[]{:S(2)}, u32[]{:S(2)}) collective-permute-start(bf16[64,384]{1,0:T(8,128)(2,1)S(1)} %hold.17), channel_id=1, source_target_pairs={{0,4},{4,0},{8,12},{12,8},{1,5},{5,1},{9,13},{13,9},{2,6},{6,2},{1... | collective-permute-start | bytes 147464 | tf_op jit(solution)/shard_map/ppermute | solution.py:223
  24.1 2.5 %collective-permute-start.10 = (bf16[64,384]{1,0:T(8,128)(2,1)S(1)}, bf16[64,384]{1,0:T(8,128)(2,1)S(1)}, u32[]{:S(2)}, u32[]{:S(2)}) collective-permute-start(bf16[64,384]{1,0:T(8,128)(2,1)S(1)} %attend.3.refs_1_), channel_id=1, source_target_pairs={{0,8},{4,12},{8,0},{12,4},{1,9},{5,13},{9,1},{13,5},{2,10},{6,14},... | collective-permute-start | bytes 147464 | tf_op jit(solution)/shard_map/ppermute | solution.py:223
  26.7 1.0 %collective-permute-done.8.refs_0_ = bf16[64,384]{1,0:T(8,128)(2,1)S(1)} collective-permute-done((bf16[64,384]{1,0:T(8,128)(2,1)S(1)}, bf16[64,384]{1,0:T(8,128)(2,1)S(1)}, u32[]{:S(2)}, u32[]{:S(2)}) %collective-permute-start.8) | collective-permute-done | bytes 49184 | tf_op jit(solution)/shard_map/ppermute | solution.py:223
  27.6 0.5 %collective-permute-done.11.refs_3_ = bf16[64,384]{1,0:T(8,128)(2,1)S(1)} collective-permute-done((bf16[64,384]{1,0:T(8,128)(2,1)S(1)}, bf16[64,384]{1,0:T(8,128)(2,1)S(1)}, u32[]{:S(2)}, u32[]{:S(2)}) %collective-permute-start.11) | collective-permute-done | bytes 49184 | tf_op jit(solution)/shard_map/ppermute | solution.py:223
  28.1 1.0 %collective-permute-done.10.refs_2_ = bf16[64,384]{1,0:T(8,128)(2,1)S(1)} collective-permute-done((bf16[64,384]{1,0:T(8,128)(2,1)S(1)}, bf16[64,384]{1,0:T(8,128)(2,1)S(1)}, u32[]{:S(2)}, u32[]{:S(2)}) %collective-permute-start.10) | collective-permute-done | bytes 49184 | tf_op jit(solution)/shard_map/ppermute | solution.py:223
  29.1 0.7 %unpack.1 = bf16[1,64,1536]{2,1,0:T(8,128)(2,1)} custom-call(bf16[64,384]{1,0:T(8,128)(2,1)S(1)} %get-tuple-element.21.refs_1_.refs_0_, bf16[64,384]{1,0:T(8,128)(2,1)S(1)} %hold.14.refs_1_, bf16[64,384]{1,0:T(8,128)(2,1)S(1)} %collective-permute-done.10.refs_2_, bf16[64,384]{1,0:T(8,128)(2,1)S(1)} %collective-permute-done.11.refs_3_), custom_call_target="tpu_custom_call" | custom-call | bytes 393216 | tf_op jit(solution)/shard_map/unpack/pallas_call | solution.py:275
  (11 shorter events, 0.0 us)
Async XLA Ops:
  1.2 11.0 %collective-permute-start.1 = (bf16[64,768]{1,0:T(8,128)(2,1)S(1)}, bf16[64,768]{1,0:T(8,128)(2,1)S(1)}, u32[]{:S(2)}, u32[]{:S(2)}) collective-permute-start(bf16[64,768]{1,0:T(8,128)(2,1)S(1)} %get-tuple-element.17), channel_id=1, source_target_pairs={{0,12},{4,8},{8,4},{12,0},{1,13},{5,9},{9,5},{13,1},{2,14},{6,10},... | collective-permute-start | bytes 294920 | tf_op jit(solution)/shard_map/ppermute | solution.py:223
  6.3 8.3 %collective-permute-start = (bf16[64,1152]{1,0:T(8,128)(2,1)S(1)}, bf16[64,1152]{1,0:T(8,128)(2,1)S(1)}, u32[]{:S(2)}, u32[]{:S(2)}) collective-permute-start(bf16[64,1152]{1,0:T(8,128)(2,1)S(1)} %get-tuple-element.15), channel_id=1, source_target_pairs={{0,4},{4,0},{8,12},{12,8},{1,5},{5,1},{9,13},{13,9},{2,6},{6,2},{1... | collective-permute-start | bytes 442376 | tf_op jit(solution)/shard_map/ppermute | solution.py:223
  6.3 10.1 %collective-permute-start.2 = (bf16[64,768]{1,0:T(8,128)(2,1)S(1)}, bf16[64,768]{1,0:T(8,128)(2,1)S(1)}, u32[]{:S(2)}, u32[]{:S(2)}) collective-permute-start(bf16[64,768]{1,0:T(8,128)(2,1)S(1)} %get-tuple-element.18), channel_id=1, source_target_pairs={{0,8},{4,12},{8,0},{12,4},{1,9},{5,13},{9,1},{13,5},{2,10},{6,14},... | collective-permute-start | bytes 294920 | tf_op jit(solution)/shard_map/ppermute | solution.py:223
  6.9 12.2 %collective-permute-start.7 = (bf16[64,384]{1,0:T(8,128)(2,1)S(1)}, bf16[64,384]{1,0:T(8,128)(2,1)S(1)}, u32[]{:S(2)}, u32[]{:S(2)}) collective-permute-start(bf16[64,384]{1,0:T(8,128)(2,1)S(1)} %get-tuple-element.20), channel_id=1, source_target_pairs={{0,12},{4,8},{8,4},{12,0},{1,13},{5,9},{9,5},{13,1},{2,14},{6,10},... | collective-permute-start | bytes 147464 | tf_op jit(solution)/shard_map/ppermute | solution.py:223
  10.7 6.9 %collective-permute-start.3 = (bf16[64,768]{1,0:T(8,128)(2,1)S(1)}, bf16[64,768]{1,0:T(8,128)(2,1)S(1)}, u32[]{:S(2)}, u32[]{:S(2)}) collective-permute-start(bf16[64,768]{1,0:T(8,128)(2,1)S(1)} %get-tuple-element.16.refs_1_), channel_id=1, source_target_pairs={{0,2},{2,0},{1,3},{3,1},{4,6},{6,4},{5,7},{7,5},{8,10},{10,8},{9,1... | collective-permute-start | bytes 294920 | tf_op jit(solution)/shard_map/ppermute | solution.py:226
  12.2 7.0 %collective-permute-start.4 = (bf16[64,768]{1,0:T(8,128)(2,1)S(1)}, bf16[64,768]{1,0:T(8,128)(2,1)S(1)}, u32[]{:S(2)}, u32[]{:S(2)}) collective-permute-start(bf16[64,768]{1,0:T(8,128)(2,1)S(1)} %hold.9.refs_2_), channel_id=1, source_target_pairs={{0,2},{2,0},{1,3},{3,1},{4,6},{6,4},{5,7},{7,5},{8,10},{10,8},{9,1... | collective-permute-start | bytes 294920 | tf_op jit(solution)/shard_map/ppermute | solution.py:226
  14.6 5.4 %collective-permute-start.5 = (bf16[64,768]{1,0:T(8,128)(2,1)S(1)}, bf16[64,768]{1,0:T(8,128)(2,1)S(1)}, u32[]{:S(2)}, u32[]{:S(2)}) collective-permute-start(bf16[64,768]{1,0:T(8,128)(2,1)S(1)} %bitcast.1), channel_id=1, source_target_pairs={{0,2},{2,0},{1,3},{3,1},{4,6},{6,4},{5,7},{7,5},{8,10},{10,8},{9,1... | collective-permute-start | bytes 294920 | tf_op jit(solution)/shard_map/ppermute | solution.py:226
  16.4 4.6 %collective-permute-start.6 = (bf16[64,768]{1,0:T(8,128)(2,1)S(1)}, bf16[64,768]{1,0:T(8,128)(2,1)S(1)}, u32[]{:S(2)}, u32[]{:S(2)}) collective-permute-start(bf16[64,768]{1,0:T(8,128)(2,1)S(1)} %hold.10.refs_3_.refs_1_), channel_id=1, source_target_pairs={{0,2},{2,0},{1,3},{3,1},{4,6},{6,4},{5,7},{7,5},{8,10},{10,8},{9,1... | collective-permute-start | bytes 294920 | tf_op jit(solution)/shard_map/ppermute | solution.py:226
  17.6 5.4 %collective-permute-start.9 = (bf16[64,384]{1,0:T(8,128)(2,1)S(1)}, bf16[64,384]{1,0:T(8,128)(2,1)S(1)}, u32[]{:S(2)}, u32[]{:S(2)}) collective-permute-start(bf16[64,384]{1,0:T(8,128)(2,1)S(1)} %hold.15), channel_id=1, source_target_pairs={{0,8},{4,12},{8,0},{12,4},{1,9},{5,13},{9,1},{13,5},{2,10},{6,14},... | collective-permute-start | bytes 147464 | tf_op jit(solution)/shard_map/ppermute | solution.py:223
  21.6 6.0 %collective-permute-start.8 = (bf16[64,384]{1,0:T(8,128)(2,1)S(1)}, bf16[64,384]{1,0:T(8,128)(2,1)S(1)}, u32[]{:S(2)}, u32[]{:S(2)}) collective-permute-start(bf16[64,384]{1,0:T(8,128)(2,1)S(1)} %get-tuple-element.22), channel_id=1, source_target_pairs={{0,12},{4,8},{8,4},{12,0},{1,13},{5,9},{9,5},{13,1},{2,14},{6,10},... | collective-permute-start | bytes 147464 | tf_op jit(solution)/shard_map/ppermute | solution.py:223
  23.6 4.6 %collective-permute-start.11 = (bf16[64,384]{1,0:T(8,128)(2,1)S(1)}, bf16[64,384]{1,0:T(8,128)(2,1)S(1)}, u32[]{:S(2)}, u32[]{:S(2)}) collective-permute-start(bf16[64,384]{1,0:T(8,128)(2,1)S(1)} %hold.17), channel_id=1, source_target_pairs={{0,4},{4,0},{8,12},{12,8},{1,5},{5,1},{9,13},{13,9},{2,6},{6,2},{1... | collective-permute-start | bytes 147464 | tf_op jit(solution)/shard_map/ppermute | solution.py:223
  24.1 5.0 %collective-permute-start.10 = (bf16[64,384]{1,0:T(8,128)(2,1)S(1)}, bf16[64,384]{1,0:T(8,128)(2,1)S(1)}, u32[]{:S(2)}, u32[]{:S(2)}) collective-permute-start(bf16[64,384]{1,0:T(8,128)(2,1)S(1)} %attend.3.refs_1_), channel_id=1, source_target_pairs={{0,8},{4,12},{8,0},{12,4},{1,9},{5,13},{9,1},{13,5},{2,10},{6,14},... | collective-permute-start | bytes 147464 | tf_op jit(solution)/shard_map/ppermute | solution.py:223

commit v15 on v14

--- a/solution.py
+++ b/solution.py
@@ -9,7 +9,7 @@
 from jax.sharding import PartitionSpec as P
 
 HD = 128
-EFFORT = 0
+EFFORT_BACK = 10**9
 EFFORT_OWN = 10**9
 EFFORT_QUERIES = 2 * 10**8
 EFFORT_NEAR = 0
@@ -106,27 +106,6 @@
     run_copies(pairs, sems)
 
 
-def join_kernel(pieces, *refs):
-    lanes = refs[-1].shape[2]
-    for at, (source, start) in enumerate(pieces):
-        refs[-1][at] = refs[source][:, start : start + lanes]
-
-
-def join(arrays, starts, lanes, effort=0, after=()):
-    shape = (len(arrays), arrays[0].shape[0], lanes)
-    return pl.pallas_call(
-        functools.partial(join_kernel, list(enumerate(starts))),
-        out_shape=jax.ShapeDtypeStruct(shape, arrays[0].dtype),
-        in_specs=[VMEM] * (len(arrays) + len(after)),
-        out_specs=VMEM,
-        compiler_params=SMALL,
-        cost_estimate=pl.CostEstimate(
-            flops=effort, bytes_accessed=4 * math.prod(shape), transcendentals=0
-        ),
-        name="join",
-    )(*arrays, *after)
-
-
 def hold_kernel(*refs):
     pass
 
@@ -202,7 +181,7 @@
     far = list(range(blocks - 1, 1, -1))
 
     kv, q = (("k", 0, part), ("v", 0, part)), (("q", 0, part),)
-    messages = [(s, kv) for s in far] + [(1, kv + q)] + [(s, q) for s in far] + [(0, kv), (0, q)]
+    messages = [(s, names) for names in (kv, q) for s in far + [1, 0]]
     packed = pl.pallas_call(
         functools.partial(pack_kernel, messages, part),
         out_shape=[
@@ -226,23 +205,21 @@
         return lax.ppermute(array, "uly", [(i, (i + t) % columns_of) for i in range(columns_of)])
 
     sent = {message: array for message, array in zip(messages, packed)}
-    own_kv, own_q = packed[-2:]
+    own_kv, own_q = sent[0, kv], sent[0, q]
     far_kv = [to_block(sent[s, kv], s) for s in far]
-    near_kvq = to_block(sent[1, kv + q], 1)
     far_kv = [hold([array], (), effort)[0] for array, effort in zip(far_kv, EFFORT_FAR)]
-    near_kv = join([near_kvq], [0], 2 * part, EFFORT_NEAR)
-    far_q = [to_block(sent[far[0], q], far[0])]
-    far_q += [to_block(hold([sent[s, q]], [array])[0], s) for s, array in zip(far[1:], far_kv[1:])]
+    near_kv = hold([to_block(sent[1, kv], 1)], (), EFFORT_NEAR)[0]
+
     own_kv_x, first_x, near_x, second_x = (
         [to_column(group, t) for t in range(1, columns_of)]
-        for group in (own_kv, far_kv[0], near_kv[0], far_kv[1])
+        for group in (own_kv, far_kv[0], near_kv, far_kv[1])
     )
     own_kv_x = hold(own_kv_x, effort=EFFORT_OWN)
-    near_q = join([own_q, near_kvq], [0, 2 * part], part)
-    far_q[:1] = hold(far_q[:1], [*own_kv_x, *first_x, *near_x], EFFORT)
-    far_q[:1] = hold(far_q[:1], (), EFFORT_QUERIES)
-
-    holders = [near_kvq, own_kv, *far_kv, *own_kv_x, *first_x, *near_x, *second_x]
+    first_q = to_block(sent[far[0], q], far[0])
+    first_q = hold([first_q], [*own_kv_x, *first_x, *near_x], EFFORT_QUERIES)[0]
+    second_q, near_q = (to_block(hold([sent[s, q]], far_kv[1:])[0], s) for s in (far[1], 1))
+
+    holders = [near_kv, own_kv, *far_kv, *own_kv_x, *first_x, *near_x, *second_x]
     keys = [(at, None) for at in range(len(holders))]
 
     def attend(query_arrays, query_places):
@@ -262,13 +239,12 @@
             name="attend",
         )(*holders, *query_arrays)
 
-    mixed = dict(zip([0, 1] + far[:-1], attend([near_q] + far_q[:-1], [(0, 0), (0, 1), (1, None)])))
-    last_q = hold([far_q[-1]], [mixed[0]])
-    mixed[far[-1]] = attend(last_q, [(0, None)])[0]
-    mixed[1] = hold([mixed[1]], [mixed[far[-1]]])[0]
+    mixed = dict(zip((0, far[0]), attend([own_q, first_q], [(0, None), (1, None)])))
+    last_q = hold([second_q, near_q], [mixed[0]])
+    mixed.update(zip((far[1], 1), attend(last_q, [(0, None), (1, None)])))
     back = {s: to_block(mixed[s], s) for s in far + [1]}
     early = far[:-1]
-    back.update(zip(early, hold([back[s] for s in early], effort=EFFORT)))
+    back.update(zip(early, hold([back[s] for s in early], effort=EFFORT_BACK)))
     back[0] = mixed[0]
     order = [0] + far + [1]
     back = [back[s] for s in order]

time: 30 us -> 32.1 us (1.070)
  waiting for transfers between devices: 6.12 us -> 7.63 us
  starting transfers between devices: 20.6 us -> 21.3 us
    ppermute x8 -> x9, waiting for transfers between devices: 4.31 us -> 7.62 us  [to_block(): return lax.ppermute(array, 'blk', [(i, i ^ s) for i in range(blocks)])]
    ppermute x4, waiting for transfers between devices: 1.81 us -> 0.01 us  [to_column(): lax.ppermute(array, 'uly', [(i, (i + t) % columns_of) for i in range(colu...]
    ppermute x8 -> x9, starting transfers between devices: 15.6 us -> 16.3 us  [to_block(): return lax.ppermute(array, 'blk', [(i, i ^ s) for i in range(blocks)])]
  transfers between devices with their start and end apart: 12 -> 13, of which waited for: 6 -> 5; matrix products, arithmetic and copies ran while one was open for 0% -> 0% of each run, Pallas kernels for 4% -> 3%
where the time goes in v15:
time: 32.1 us; the launch traced here: 31.9 us
  starting transfers between devices  21.3 us (66%)
  waiting for transfers between devices  7.63 us (24%)
  Pallas kernels  2.93 us (9%)
    ppermute x9, starting transfers between devices, to_block(): return lax.ppermute(array, 'blk', [(i, i ^ s) for i in range(blocks)])  16.3 us
    ppermute x9, waiting for transfers between devices, to_block(): return lax.ppermute(array, 'blk', [(i, i ^ s) for i in range(blocks)])  7.62 us
    ppermute x4, starting transfers between devices, to_column(): lax.ppermute(array, 'uly', [(i, (i + t) % columns_of) for i in range(colu...  5.01 us
    pallas_call x1, Pallas kernels, local_blocks(): pl.pallas_call(functools.partial(pack_kernel, messages, part), out_shape=...  1.17 us
    pallas_call x2, Pallas kernels, attend(): pl.pallas_call(functools.partial(attend_kernel, len(holders), keys, query...  1.06 us
    pallas_call x1, Pallas kernels, local_blocks(): pl.pallas_call(functools.partial(unpack_kernel, order, part), out_shape=j...  0.7 us
  transfers between devices with their start and end apart: 13, of which 5 were waited for; matrix products, arithmetic and copies ran while one was open for 0% of the time, Pallas kernels for 3%

profile of v15, /device:TPU:0, one launch (start us, length us, event | category | flops | bytes accessed | tf_op | source)
XLA Modules:
  0.0 31.9 jit_solution(454439510823257366)
XLA Ops:
  0.0 1.2 %pack.1 = (bf16[64,768]{1,0:T(8,128)(2,1)S(1)}, bf16[64,768]{1,0:T(8,128)(2,1)S(1)}, bf16[64,768]{1,0:T(8,128)(2,1)S(1)}, bf16[64,768]{1,0:T(8,128)(2,1)S(1)}, b...) custom-call(bf16[1,64,1536]{2,1,0:T(8,128)(2,1)} %q_ref.1, ...), custom_call_target="tpu_custom_call" | custom-call | bytes 1179648 | tf_op jit(solution)/shard_map/pack/pallas_call | solution.py:185
  1.2 3.1 %collective-permute-start = (bf16[64,768]{1,0:T(8,128)(2,1)S(1)}, bf16[64,768]{1,0:T(8,128)(2,1)S(1)}, u32[]{:S(2)}, u32[]{:S(2)}) collective-permute-start(bf16[64,768]{1,0:T(8,128)(2,1)S(1)} %get-tuple-element.19), channel_id=1, source_target_pairs={{0,4},{4,0},{8,12},{12,8},{1,5},{5,1},{9,13},{13,9},{2,6},{6,2},{1... | collective-permute-start | bytes 294920 | tf_op jit(solution)/shard_map/ppermute | solution.py:202
  4.3 2.5 %collective-permute-start.1 = (bf16[64,768]{1,0:T(8,128)(2,1)S(1)}, bf16[64,768]{1,0:T(8,128)(2,1)S(1)}, u32[]{:S(2)}, u32[]{:S(2)}) collective-permute-start(bf16[64,768]{1,0:T(8,128)(2,1)S(1)} %get-tuple-element.21), channel_id=1, source_target_pairs={{0,12},{4,8},{8,4},{12,0},{1,13},{5,9},{9,5},{13,1},{2,14},{6,10},... | collective-permute-start | bytes 294920 | tf_op jit(solution)/shard_map/ppermute | solution.py:202
  6.7 0.1 collective-permute-start.2
  6.9 2.9 %collective-permute-start.7 = (bf16[64,384]{1,0:T(8,128)(2,1)S(1)}, bf16[64,384]{1,0:T(8,128)(2,1)S(1)}, u32[]{:S(2)}, u32[]{:S(2)}) collective-permute-start(bf16[64,384]{1,0:T(8,128)(2,1)S(1)} %get-tuple-element.24), channel_id=1, source_target_pairs={{0,12},{4,8},{8,4},{12,0},{1,13},{5,9},{9,5},{13,1},{2,14},{6,10},... | collective-permute-start | bytes 147464 | tf_op jit(solution)/shard_map/ppermute | solution.py:202
  9.8 1.5 %collective-permute-start.3 = (bf16[64,768]{1,0:T(8,128)(2,1)S(1)}, bf16[64,768]{1,0:T(8,128)(2,1)S(1)}, u32[]{:S(2)}, u32[]{:S(2)}) collective-permute-start(bf16[64,768]{1,0:T(8,128)(2,1)S(1)} %get-tuple-element.20.refs_1_), channel_id=1, source_target_pairs={{0,2},{2,0},{1,3},{3,1},{4,6},{6,4},{5,7},{7,5},{8,10},{10,8},{9,1... | collective-permute-start | bytes 294920 | tf_op jit(solution)/shard_map/ppermute | solution.py:205
  11.3 0.0 collective-permute-done.refs_0_
  11.3 0.5 %collective-permute-start.5 = (bf16[64,768]{1,0:T(8,128)(2,1)S(1)}, bf16[64,768]{1,0:T(8,128)(2,1)S(1)}, u32[]{:S(2)}, u32[]{:S(2)}) collective-permute-start(bf16[64,768]{1,0:T(8,128)(2,1)S(1)} %hold.9.refs_0_), channel_id=1, source_target_pairs={{0,2},{2,0},{1,3},{3,1},{4,6},{6,4},{5,7},{7,5},{8,10},{10,8},{9,1... | collective-permute-start | bytes 294920 | tf_op jit(solution)/shard_map/ppermute | solution.py:205
  11.8 0.7 %collective-permute-done.1.refs_0_ = bf16[64,768]{1,0:T(8,128)(2,1)S(1)} collective-permute-done((bf16[64,768]{1,0:T(8,128)(2,1)S(1)}, bf16[64,768]{1,0:T(8,128)(2,1)S(1)}, u32[]{:S(2)}, u32[]{:S(2)}) %collective-permute-start.1) | collective-permute-done | bytes 98336 | tf_op jit(solution)/shard_map/ppermute | solution.py:202
  12.5 1.5 %collective-permute-start.4 = (bf16[64,768]{1,0:T(8,128)(2,1)S(1)}, bf16[64,768]{1,0:T(8,128)(2,1)S(1)}, u32[]{:S(2)}, u32[]{:S(2)}) collective-permute-start(bf16[64,768]{1,0:T(8,128)(2,1)S(1)} %hold.10.refs_2_), channel_id=1, source_target_pairs={{0,2},{2,0},{1,3},{3,1},{4,6},{6,4},{5,7},{7,5},{8,10},{10,8},{9,1... | collective-permute-start | bytes 294920 | tf_op jit(solution)/shard_map/ppermute | solution.py:205
  14.0 3.3 %collective-permute-done.2.refs_0_ = bf16[64,768]{1,0:T(8,128)(2,1)S(1)} collective-permute-done((bf16[64,768]{1,0:T(8,128)(2,1)S(1)}, bf16[64,768]{1,0:T(8,128)(2,1)S(1)}, u32[]{:S(2)}, u32[]{:S(2)}) %collective-permute-start.2) | collective-permute-done | bytes 98336 | tf_op jit(solution)/shard_map/ppermute | solution.py:202
  17.3 1.5 %collective-permute-start.6 = (bf16[64,768]{1,0:T(8,128)(2,1)S(1)}, bf16[64,768]{1,0:T(8,128)(2,1)S(1)}, u32[]{:S(2)}, u32[]{:S(2)}) collective-permute-start(bf16[64,768]{1,0:T(8,128)(2,1)S(1)} %hold.11.refs_3_.refs_1_), channel_id=1, source_target_pairs={{0,2},{2,0},{1,3},{3,1},{4,6},{6,4},{5,7},{7,5},{8,10},{10,8},{9,1... | collective-permute-start | bytes 294920 | tf_op jit(solution)/shard_map/ppermute | solution.py:205
  18.8 0.0 collective-permute-done.3.refs_0_
  18.8 0.6 %collective-permute-start.9 = (bf16[64,384]{1,0:T(8,128)(2,1)S(1)}, bf16[64,384]{1,0:T(8,128)(2,1)S(1)}, u32[]{:S(2)}, u32[]{:S(2)}) collective-permute-start(bf16[64,384]{1,0:T(8,128)(2,1)S(1)} %hold.15), channel_id=1, source_target_pairs={{0,8},{4,12},{8,0},{12,4},{1,9},{5,13},{9,1},{13,5},{2,10},{6,14},... | collective-permute-start | bytes 147464 | tf_op jit(solution)/shard_map/ppermute | solution.py:202
  19.4 0.0 collective-permute-done.7.refs_0_
  19.4 2.6 %collective-permute-start.10 = (bf16[64,384]{1,0:T(8,128)(2,1)S(1)}, bf16[64,384]{1,0:T(8,128)(2,1)S(1)}, u32[]{:S(2)}, u32[]{:S(2)}) collective-permute-start(bf16[64,384]{1,0:T(8,128)(2,1)S(1)} %hold.16), channel_id=1, source_target_pairs={{0,4},{4,0},{8,12},{12,8},{1,5},{5,1},{9,13},{13,9},{2,6},{6,2},{1... | collective-permute-start | bytes 147464 | tf_op jit(solution)/shard_map/ppermute | solution.py:202
  22.0 0.0 collective-permute-done.5.refs_3_.refs_6_
  22.0 0.0 collective-permute-done.4.refs_2_.refs_5_
  22.0 0.0 collective-permute-done.6.refs_7_
  22.0 0.5 %attend.2 = (bf16[64,384]{1,0:T(8,128)(2,1)S(1)}, bf16[64,384]{1,0:T(8,128)(2,1)S(1)}) custom-call(bf16[64,768]{1,0:T(8,128)(2,1)S(1)} %hold.9.refs_0_, bf16[64,768]{1,0:T(8,128)(2,1)S(1)} %get-tuple-element.20.refs_1_, bf16[64,768]{1,0:T(8,128)(2,1)S(1)} %hold.10.refs_2_, bf16[64,768]{1,0:T(8,128)(2,1)S(1)} %hold.11.refs_3_.refs_1_, ...), custom_call_target="tpu_custom_call" | custom-call | flops 100663296 | bytes 983040 | tf_op jit(solution)/shard_map/attend/pallas_call | solution.py:228
  22.5 2.6 %collective-permute-start.8 = (bf16[64,384]{1,0:T(8,128)(2,1)S(1)}, bf16[64,384]{1,0:T(8,128)(2,1)S(1)}, u32[]{:S(2)}, u32[]{:S(2)}) collective-permute-start(bf16[64,384]{1,0:T(8,128)(2,1)S(1)} %get-tuple-element.26), channel_id=1, source_target_pairs={{0,12},{4,8},{8,4},{12,0},{1,13},{5,9},{9,5},{13,1},{2,14},{6,10},... | collective-permute-start | bytes 147464 | tf_op jit(solution)/shard_map/ppermute | solution.py:202
  25.1 0.0 collective-permute-done.9.refs_0_
  25.1 0.0 collective-permute-done.10.refs_1_
  25.1 0.5 %attend.3 = (bf16[64,384]{1,0:T(8,128)(2,1)S(1)}, bf16[64,384]{1,0:T(8,128)(2,1)S(1)}) custom-call(bf16[64,768]{1,0:T(8,128)(2,1)S(1)} %hold.9.refs_0_, bf16[64,768]{1,0:T(8,128)(2,1)S(1)} %get-tuple-element.20.refs_1_, bf16[64,768]{1,0:T(8,128)(2,1)S(1)} %hold.10.refs_2_, bf16[64,768]{1,0:T(8,128)(2,1)S(1)} %hold.11.refs_3_.refs_1_, ...), custom_call_target="tpu_custom_call" | custom-call | flops 100663296 | bytes 983040 | tf_op jit(solution)/shard_map/attend/pallas_call | solution.py:228
  25.7 1.2 %collective-permute-start.11 = (bf16[64,384]{1,0:T(8,128)(2,1)S(1)}, bf16[64,384]{1,0:T(8,128)(2,1)S(1)}, u32[]{:S(2)}, u32[]{:S(2)}) collective-permute-start(bf16[64,384]{1,0:T(8,128)(2,1)S(1)} %get-tuple-element.31), channel_id=1, source_target_pairs={{0,8},{4,12},{8,0},{12,4},{1,9},{5,13},{9,1},{13,5},{2,10},{6,14},... | collective-permute-start | bytes 147464 | tf_op jit(solution)/shard_map/ppermute | solution.py:202
  26.8 0.8 %collective-permute-start.12 = (bf16[64,384]{1,0:T(8,128)(2,1)S(1)}, bf16[64,384]{1,0:T(8,128)(2,1)S(1)}, u32[]{:S(2)}, u32[]{:S(2)}) collective-permute-start(bf16[64,384]{1,0:T(8,128)(2,1)S(1)} %get-tuple-element.32), channel_id=1, source_target_pairs={{0,4},{4,0},{8,12},{12,8},{1,5},{5,1},{9,13},{13,9},{2,6},{6,2},{1... | collective-permute-start | bytes 147464 | tf_op jit(solution)/shard_map/ppermute | solution.py:202
  27.6 1.1 %collective-permute-done.8.refs_0_ = bf16[64,384]{1,0:T(8,128)(2,1)S(1)} collective-permute-done((bf16[64,384]{1,0:T(8,128)(2,1)S(1)}, bf16[64,384]{1,0:T(8,128)(2,1)S(1)}, u32[]{:S(2)}, u32[]{:S(2)}) %collective-permute-start.8) | collective-permute-done | bytes 49184 | tf_op jit(solution)/shard_map/ppermute | solution.py:202
  28.7 2.1 %collective-permute-done.11.refs_2_ = bf16[64,384]{1,0:T(8,128)(2,1)S(1)} collective-permute-done((bf16[64,384]{1,0:T(8,128)(2,1)S(1)}, bf16[64,384]{1,0:T(8,128)(2,1)S(1)}, u32[]{:S(2)}, u32[]{:S(2)}) %collective-permute-start.11) | collective-permute-done | bytes 49184 | tf_op jit(solution)/shard_map/ppermute | solution.py:202
  30.7 0.5 %collective-permute-done.12.refs_3_ = bf16[64,384]{1,0:T(8,128)(2,1)S(1)} collective-permute-done((bf16[64,384]{1,0:T(8,128)(2,1)S(1)}, bf16[64,384]{1,0:T(8,128)(2,1)S(1)}, u32[]{:S(2)}, u32[]{:S(2)}) %collective-permute-start.12) | collective-permute-done | bytes 49184 | tf_op jit(solution)/shard_map/ppermute | solution.py:202
  31.2 0.7 %unpack.1 = bf16[1,64,1536]{2,1,0:T(8,128)(2,1)} custom-call(bf16[64,384]{1,0:T(8,128)(2,1)S(1)} %get-tuple-element.25.refs_2_.refs_0_, bf16[64,384]{1,0:T(8,128)(2,1)S(1)} %hold.14.refs_1_, bf16[64,384]{1,0:T(8,128)(2,1)S(1)} %collective-permute-done.11.refs_2_, bf16[64,384]{1,0:T(8,128)(2,1)S(1)} %collective-permute-done.12.refs_3_), custom_call_target="tpu_custom_call" | custom-call | bytes 393216 | tf_op jit(solution)/shard_map/unpack/pallas_call | solution.py:251
  (9 shorter events, 0.0 us)
Async XLA Ops:
  1.2 10.1 %collective-permute-start = (bf16[64,768]{1,0:T(8,128)(2,1)S(1)}, bf16[64,768]{1,0:T(8,128)(2,1)S(1)}, u32[]{:S(2)}, u32[]{:S(2)}) collective-permute-start(bf16[64,768]{1,0:T(8,128)(2,1)S(1)} %get-tuple-element.19), channel_id=1, source_target_pairs={{0,4},{4,0},{8,12},{12,8},{1,5},{5,1},{9,13},{13,9},{2,6},{6,2},{1... | collective-permute-start | bytes 294920 | tf_op jit(solution)/shard_map/ppermute | solution.py:202
  4.3 8.2 %collective-permute-start.1 = (bf16[64,768]{1,0:T(8,128)(2,1)S(1)}, bf16[64,768]{1,0:T(8,128)(2,1)S(1)}, u32[]{:S(2)}, u32[]{:S(2)}) collective-permute-start(bf16[64,768]{1,0:T(8,128)(2,1)S(1)} %get-tuple-element.21), channel_id=1, source_target_pairs={{0,12},{4,8},{8,4},{12,0},{1,13},{5,9},{9,5},{13,1},{2,14},{6,10},... | collective-permute-start | bytes 294920 | tf_op jit(solution)/shard_map/ppermute | solution.py:202
  6.7 10.5 %collective-permute-start.2 = (bf16[64,768]{1,0:T(8,128)(2,1)S(1)}, bf16[64,768]{1,0:T(8,128)(2,1)S(1)}, u32[]{:S(2)}, u32[]{:S(2)}) collective-permute-start(bf16[64,768]{1,0:T(8,128)(2,1)S(1)} %get-tuple-element.22), channel_id=1, source_target_pairs={{0,8},{4,12},{8,0},{12,4},{1,9},{5,13},{9,1},{13,5},{2,10},{6,14},... | collective-permute-start | bytes 294920 | tf_op jit(solution)/shard_map/ppermute | solution.py:202
  6.9 12.5 %collective-permute-start.7 = (bf16[64,384]{1,0:T(8,128)(2,1)S(1)}, bf16[64,384]{1,0:T(8,128)(2,1)S(1)}, u32[]{:S(2)}, u32[]{:S(2)}) collective-permute-start(bf16[64,384]{1,0:T(8,128)(2,1)S(1)} %get-tuple-element.24), channel_id=1, source_target_pairs={{0,12},{4,8},{8,4},{12,0},{1,13},{5,9},{9,5},{13,1},{2,14},{6,10},... | collective-permute-start | bytes 147464 | tf_op jit(solution)/shard_map/ppermute | solution.py:202
  9.8 9.0 %collective-permute-start.3 = (bf16[64,768]{1,0:T(8,128)(2,1)S(1)}, bf16[64,768]{1,0:T(8,128)(2,1)S(1)}, u32[]{:S(2)}, u32[]{:S(2)}) collective-permute-start(bf16[64,768]{1,0:T(8,128)(2,1)S(1)} %get-tuple-element.20.refs_1_), channel_id=1, source_target_pairs={{0,2},{2,0},{1,3},{3,1},{4,6},{6,4},{5,7},{7,5},{8,10},{10,8},{9,1... | collective-permute-start | bytes 294920 | tf_op jit(solution)/shard_map/ppermute | solution.py:205
  11.3 10.7 %collective-permute-start.5 = (bf16[64,768]{1,0:T(8,128)(2,1)S(1)}, bf16[64,768]{1,0:T(8,128)(2,1)S(1)}, u32[]{:S(2)}, u32[]{:S(2)}) collective-permute-start(bf16[64,768]{1,0:T(8,128)(2,1)S(1)} %hold.9.refs_0_), channel_id=1, source_target_pairs={{0,2},{2,0},{1,3},{3,1},{4,6},{6,4},{5,7},{7,5},{8,10},{10,8},{9,1... | collective-permute-start | bytes 294920 | tf_op jit(solution)/shard_map/ppermute | solution.py:205
  12.5 9.5 %collective-permute-start.4 = (bf16[64,768]{1,0:T(8,128)(2,1)S(1)}, bf16[64,768]{1,0:T(8,128)(2,1)S(1)}, u32[]{:S(2)}, u32[]{:S(2)}) collective-permute-start(bf16[64,768]{1,0:T(8,128)(2,1)S(1)} %hold.10.refs_2_), channel_id=1, source_target_pairs={{0,2},{2,0},{1,3},{3,1},{4,6},{6,4},{5,7},{7,5},{8,10},{10,8},{9,1... | collective-permute-start | bytes 294920 | tf_op jit(solution)/shard_map/ppermute | solution.py:205
  17.3 4.7 %collective-permute-start.6 = (bf16[64,768]{1,0:T(8,128)(2,1)S(1)}, bf16[64,768]{1,0:T(8,128)(2,1)S(1)}, u32[]{:S(2)}, u32[]{:S(2)}) collective-permute-start(bf16[64,768]{1,0:T(8,128)(2,1)S(1)} %hold.11.refs_3_.refs_1_), channel_id=1, source_target_pairs={{0,2},{2,0},{1,3},{3,1},{4,6},{6,4},{5,7},{7,5},{8,10},{10,8},{9,1... | collective-permute-start | bytes 294920 | tf_op jit(solution)/shard_map/ppermute | solution.py:205
  18.8 6.4 %collective-permute-start.9 = (bf16[64,384]{1,0:T(8,128)(2,1)S(1)}, bf16[64,384]{1,0:T(8,128)(2,1)S(1)}, u32[]{:S(2)}, u32[]{:S(2)}) collective-permute-start(bf16[64,384]{1,0:T(8,128)(2,1)S(1)} %hold.15), channel_id=1, source_target_pairs={{0,8},{4,12},{8,0},{12,4},{1,9},{5,13},{9,1},{13,5},{2,10},{6,14},... | collective-permute-start | bytes 147464 | tf_op jit(solution)/shard_map/ppermute | solution.py:202
  19.4 5.8 %collective-permute-start.10 = (bf16[64,384]{1,0:T(8,128)(2,1)S(1)}, bf16[64,384]{1,0:T(8,128)(2,1)S(1)}, u32[]{:S(2)}, u32[]{:S(2)}) collective-permute-start(bf16[64,384]{1,0:T(8,128)(2,1)S(1)} %hold.16), channel_id=1, source_target_pairs={{0,4},{4,0},{8,12},{12,8},{1,5},{5,1},{9,13},{13,9},{2,6},{6,2},{1... | collective-permute-start | bytes 147464 | tf_op jit(solution)/shard_map/ppermute | solution.py:202
  22.5 6.1 %collective-permute-start.8 = (bf16[64,384]{1,0:T(8,128)(2,1)S(1)}, bf16[64,384]{1,0:T(8,128)(2,1)S(1)}, u32[]{:S(2)}, u32[]{:S(2)}) collective-permute-start(bf16[64,384]{1,0:T(8,128)(2,1)S(1)} %get-tuple-element.26), channel_id=1, source_target_pairs={{0,12},{4,8},{8,4},{12,0},{1,13},{5,9},{9,5},{13,1},{2,14},{6,10},... | collective-permute-start | bytes 147464 | tf_op jit(solution)/shard_map/ppermute | solution.py:202
  25.7 5.1 %collective-permute-start.11 = (bf16[64,384]{1,0:T(8,128)(2,1)S(1)}, bf16[64,384]{1,0:T(8,128)(2,1)S(1)}, u32[]{:S(2)}, u32[]{:S(2)}) collective-permute-start(bf16[64,384]{1,0:T(8,128)(2,1)S(1)} %get-tuple-element.31), channel_id=1, source_target_pairs={{0,8},{4,12},{8,0},{12,4},{1,9},{5,13},{9,1},{13,5},{2,10},{6,14},... | collective-permute-start | bytes 147464 | tf_op jit(solution)/shard_map/ppermute | solution.py:202
  26.8 4.4 %collective-permute-start.12 = (bf16[64,384]{1,0:T(8,128)(2,1)S(1)}, bf16[64,384]{1,0:T(8,128)(2,1)S(1)}, u32[]{:S(2)}, u32[]{:S(2)}) collective-permute-start(bf16[64,384]{1,0:T(8,128)(2,1)S(1)} %get-tuple-element.32), channel_id=1, source_target_pairs={{0,4},{4,0},{8,12},{12,8},{1,5},{5,1},{9,13},{13,9},{2,6},{6,2},{1... | collective-permute-start | bytes 147464 | tf_op jit(solution)/shard_map/ppermute | solution.py:202

commit v16 on v15

--- a/solution.py
+++ b/solution.py
@@ -13,7 +13,7 @@
 EFFORT_OWN = 10**9
 EFFORT_QUERIES = 2 * 10**8
 EFFORT_NEAR = 0
-EFFORT_FAR = (10**9, 5 * 10**8)
+EFFORT_FAR = (5 * 10**8, 5 * 10**8)
 ANY = pl.BlockSpec(memory_space=pl.ANY)
 HBM = pl.BlockSpec(memory_space=pltpu.HBM)
 VMEM = pl.BlockSpec(memory_space=pltpu.VMEM)
@@ -208,7 +208,7 @@
     own_kv, own_q = sent[0, kv], sent[0, q]
     far_kv = [to_block(sent[s, kv], s) for s in far]
     far_kv = [hold([array], (), effort)[0] for array, effort in zip(far_kv, EFFORT_FAR)]
-    near_kv = hold([to_block(sent[1, kv], 1)], (), EFFORT_NEAR)[0]
+    near_kv = hold([to_block(sent[1, kv], 1)], far_kv[:1], EFFORT_NEAR)[0]
 
     own_kv_x, first_x, near_x, second_x = (
         [to_column(group, t) for t in range(1, columns_of)]

time: 32.1 us -> 30.6 us (0.953)
  waiting for transfers between devices: 7.63 us -> 5.62 us
  starting transfers between devices: 21.3 us -> 21.8 us
    ppermute x9, waiting for transfers between devices: 7.62 us -> 5.27 us  [to_block(): return lax.ppermute(array, 'blk', [(i, i ^ s) for i in range(blocks)])]
    ppermute x4, waiting for transfers between devices: 0.01 us -> 0.35 us  [to_column(): lax.ppermute(array, 'uly', [(i, (i + t) % columns_of) for i in range(colu...]
  transfers between devices with their start and end apart: 13 -> 13, of which waited for: 5 -> 4; matrix products, arithmetic and copies ran while one was open for 0% -> 0% of each run, Pallas kernels for 3% -> 3%
where the time goes in v16:
time: 30.6 us; the launch traced here: 30.4 us
  starting transfers between devices  21.8 us (71%)
  waiting for transfers between devices  5.62 us (18%)
  Pallas kernels  2.93 us (10%)
    ppermute x9, starting transfers between devices, to_block(): return lax.ppermute(array, 'blk', [(i, i ^ s) for i in range(blocks)])  16.6 us
    ppermute x9, waiting for transfers between devices, to_block(): return lax.ppermute(array, 'blk', [(i, i ^ s) for i in range(blocks)])  5.27 us
    ppermute x4, starting transfers between devices, to_column(): lax.ppermute(array, 'uly', [(i, (i + t) % columns_of) for i in range(colu...  5.15 us
    pallas_call x1, Pallas kernels, local_blocks(): pl.pallas_call(functools.partial(pack_kernel, messages, part), out_shape=...  1.17 us
    pallas_call x2, Pallas kernels, attend(): pl.pallas_call(functools.partial(attend_kernel, len(holders), keys, query...  1.06 us
    pallas_call x1, Pallas kernels, local_blocks(): pl.pallas_call(functools.partial(unpack_kernel, order, part), out_shape=j...  0.7 us
  transfers between devices with their start and end apart: 13, of which 4 were waited for; matrix products, arithmetic and copies ran while one was open for 0% of the time, Pallas kernels for 3%

profile of v16, /device:TPU:0, one launch (start us, length us, event | category | flops | bytes accessed | tf_op | source)
XLA Modules:
  0.0 30.4 jit_solution(16709642401373807756)
XLA Ops:
  0.0 1.2 %pack.1 = (bf16[64,768]{1,0:T(8,128)(2,1)S(1)}, bf16[64,768]{1,0:T(8,128)(2,1)S(1)}, bf16[64,768]{1,0:T(8,128)(2,1)S(1)}, bf16[64,768]{1,0:T(8,128)(2,1)S(1)}, b...) custom-call(bf16[1,64,1536]{2,1,0:T(8,128)(2,1)} %q_ref.1, ...), custom_call_target="tpu_custom_call" | custom-call | bytes 1179648 | tf_op jit(solution)/shard_map/pack/pallas_call | solution.py:185
  1.2 5.1 %collective-permute-start.1 = (bf16[64,768]{1,0:T(8,128)(2,1)S(1)}, bf16[64,768]{1,0:T(8,128)(2,1)S(1)}, u32[]{:S(2)}, u32[]{:S(2)}) collective-permute-start(bf16[64,768]{1,0:T(8,128)(2,1)S(1)} %get-tuple-element.20), channel_id=1, source_target_pairs={{0,12},{4,8},{8,4},{12,0},{1,13},{5,9},{9,5},{13,1},{2,14},{6,10},... | collective-permute-start | bytes 294920 | tf_op jit(solution)/shard_map/ppermute | solution.py:202
  6.3 0.0 collective-permute-start
  6.3 0.6 %collective-permute-start.2 = (bf16[64,768]{1,0:T(8,128)(2,1)S(1)}, bf16[64,768]{1,0:T(8,128)(2,1)S(1)}, u32[]{:S(2)}, u32[]{:S(2)}) collective-permute-start(bf16[64,768]{1,0:T(8,128)(2,1)S(1)} %get-tuple-element.22), channel_id=1, source_target_pairs={{0,8},{4,12},{8,0},{12,4},{1,9},{5,13},{9,1},{13,5},{2,10},{6,14},... | collective-permute-start | bytes 294920 | tf_op jit(solution)/shard_map/ppermute | solution.py:202
  6.9 1.6 %collective-permute-start.3 = (bf16[64,768]{1,0:T(8,128)(2,1)S(1)}, bf16[64,768]{1,0:T(8,128)(2,1)S(1)}, u32[]{:S(2)}, u32[]{:S(2)}) collective-permute-start(bf16[64,768]{1,0:T(8,128)(2,1)S(1)} %get-tuple-element.21.refs_1_), channel_id=1, source_target_pairs={{0,2},{2,0},{1,3},{3,1},{4,6},{6,4},{5,7},{7,5},{8,10},{10,8},{9,1... | collective-permute-start | bytes 294920 | tf_op jit(solution)/shard_map/ppermute | solution.py:205
  8.6 3.6 %collective-permute-start.7 = (bf16[64,384]{1,0:T(8,128)(2,1)S(1)}, bf16[64,384]{1,0:T(8,128)(2,1)S(1)}, u32[]{:S(2)}, u32[]{:S(2)}) collective-permute-start(bf16[64,384]{1,0:T(8,128)(2,1)S(1)} %get-tuple-element.24), channel_id=1, source_target_pairs={{0,12},{4,8},{8,4},{12,0},{1,13},{5,9},{9,5},{13,1},{2,14},{6,10},... | collective-permute-start | bytes 147464 | tf_op jit(solution)/shard_map/ppermute | solution.py:202
  12.2 0.0 collective-permute-done.1.refs_0_
  12.2 0.5 %collective-permute-start.4 = (bf16[64,768]{1,0:T(8,128)(2,1)S(1)}, bf16[64,768]{1,0:T(8,128)(2,1)S(1)}, u32[]{:S(2)}, u32[]{:S(2)}) collective-permute-start(bf16[64,768]{1,0:T(8,128)(2,1)S(1)} %hold.9.refs_1_.refs_2_), channel_id=1, source_target_pairs={{0,2},{2,0},{1,3},{3,1},{4,6},{6,4},{5,7},{7,5},{8,10},{10,8},{9,1... | collective-permute-start | bytes 294920 | tf_op jit(solution)/shard_map/ppermute | solution.py:205
  12.7 0.0 collective-permute-done.refs_0_
  12.7 1.5 %collective-permute-start.5 = (bf16[64,768]{1,0:T(8,128)(2,1)S(1)}, bf16[64,768]{1,0:T(8,128)(2,1)S(1)}, u32[]{:S(2)}, u32[]{:S(2)}) collective-permute-start(bf16[64,768]{1,0:T(8,128)(2,1)S(1)} %hold.10.refs_0_), channel_id=1, source_target_pairs={{0,2},{2,0},{1,3},{3,1},{4,6},{6,4},{5,7},{7,5},{8,10},{10,8},{9,1... | collective-permute-start | bytes 294920 | tf_op jit(solution)/shard_map/ppermute | solution.py:205
  14.2 1.9 %collective-permute-done.2.refs_0_ = bf16[64,768]{1,0:T(8,128)(2,1)S(1)} collective-permute-done((bf16[64,768]{1,0:T(8,128)(2,1)S(1)}, bf16[64,768]{1,0:T(8,128)(2,1)S(1)}, u32[]{:S(2)}, u32[]{:S(2)}) %collective-permute-start.2) | collective-permute-done | bytes 98336 | tf_op jit(solution)/shard_map/ppermute | solution.py:202
  16.1 1.5 %collective-permute-start.6 = (bf16[64,768]{1,0:T(8,128)(2,1)S(1)}, bf16[64,768]{1,0:T(8,128)(2,1)S(1)}, u32[]{:S(2)}, u32[]{:S(2)}) collective-permute-start(bf16[64,768]{1,0:T(8,128)(2,1)S(1)} %hold.11.refs_3_.refs_1_), channel_id=1, source_target_pairs={{0,2},{2,0},{1,3},{3,1},{4,6},{6,4},{5,7},{7,5},{8,10},{10,8},{9,1... | collective-permute-start | bytes 294920 | tf_op jit(solution)/shard_map/ppermute | solution.py:205
  17.6 0.0 collective-permute-done.3.refs_0_
  17.6 0.4 %collective-permute-start.9 = (bf16[64,384]{1,0:T(8,128)(2,1)S(1)}, bf16[64,384]{1,0:T(8,128)(2,1)S(1)}, u32[]{:S(2)}, u32[]{:S(2)}) collective-permute-start(bf16[64,384]{1,0:T(8,128)(2,1)S(1)} %hold.15), channel_id=1, source_target_pairs={{0,8},{4,12},{8,0},{12,4},{1,9},{5,13},{9,1},{13,5},{2,10},{6,14},... | collective-permute-start | bytes 147464 | tf_op jit(solution)/shard_map/ppermute | solution.py:202
  18.0 0.0 collective-permute-done.7.refs_0_
  18.0 2.4 %collective-permute-start.10 = (bf16[64,384]{1,0:T(8,128)(2,1)S(1)}, bf16[64,384]{1,0:T(8,128)(2,1)S(1)}, u32[]{:S(2)}, u32[]{:S(2)}) collective-permute-start(bf16[64,384]{1,0:T(8,128)(2,1)S(1)} %hold.16), channel_id=1, source_target_pairs={{0,4},{4,0},{8,12},{12,8},{1,5},{5,1},{9,13},{13,9},{2,6},{6,2},{1... | collective-permute-start | bytes 147464 | tf_op jit(solution)/shard_map/ppermute | solution.py:202
  20.4 0.0 collective-permute-done.5.refs_3_.refs_6_
  20.4 0.0 collective-permute-done.4.refs_2_.refs_5_
  20.4 0.3 %collective-permute-done.6.refs_7_ = bf16[64,768]{1,0:T(8,128)(2,1)S(1)} collective-permute-done((bf16[64,768]{1,0:T(8,128)(2,1)S(1)}, bf16[64,768]{1,0:T(8,128)(2,1)S(1)}, u32[]{:S(2)}, u32[]{:S(2)}) %collective-permute-start.6) | collective-permute-done | bytes 98336 | tf_op jit(solution)/shard_map/ppermute | solution.py:205
  20.8 0.5 %attend.2 = (bf16[64,384]{1,0:T(8,128)(2,1)S(1)}, bf16[64,384]{1,0:T(8,128)(2,1)S(1)}) custom-call(bf16[64,768]{1,0:T(8,128)(2,1)S(1)} %hold.10.refs_0_, bf16[64,768]{1,0:T(8,128)(2,1)S(1)} %get-tuple-element.21.refs_1_, bf16[64,768]{1,0:T(8,128)(2,1)S(1)} %hold.9.refs_1_.refs_2_, bf16[64,768]{1,0:T(8,128)(2,1)S(1)} %hold.11.refs_3_.refs_1_, ...), custom_call_target="tpu_custom_call" | custom-call | flops 100663296 | bytes 983040 | tf_op jit(solution)/shard_map/attend/pallas_call | solution.py:228
  21.3 2.3 %collective-permute-start.8 = (bf16[64,384]{1,0:T(8,128)(2,1)S(1)}, bf16[64,384]{1,0:T(8,128)(2,1)S(1)}, u32[]{:S(2)}, u32[]{:S(2)}) collective-permute-start(bf16[64,384]{1,0:T(8,128)(2,1)S(1)} %get-tuple-element.26), channel_id=1, source_target_pairs={{0,12},{4,8},{8,4},{12,0},{1,13},{5,9},{9,5},{13,1},{2,14},{6,10},... | collective-permute-start | bytes 147464 | tf_op jit(solution)/shard_map/ppermute | solution.py:202
  23.6 0.0 collective-permute-done.9.refs_0_
  23.6 0.0 collective-permute-done.10.refs_1_
  23.6 0.5 %attend.3 = (bf16[64,384]{1,0:T(8,128)(2,1)S(1)}, bf16[64,384]{1,0:T(8,128)(2,1)S(1)}) custom-call(bf16[64,768]{1,0:T(8,128)(2,1)S(1)} %hold.10.refs_0_, bf16[64,768]{1,0:T(8,128)(2,1)S(1)} %get-tuple-element.21.refs_1_, bf16[64,768]{1,0:T(8,128)(2,1)S(1)} %hold.9.refs_1_.refs_2_, bf16[64,768]{1,0:T(8,128)(2,1)S(1)} %hold.11.refs_3_.refs_1_, ...), custom_call_target="tpu_custom_call" | custom-call | flops 100663296 | bytes 983040 | tf_op jit(solution)/shard_map/attend/pallas_call | solution.py:228
  24.1 1.2 %collective-permute-start.11 = (bf16[64,384]{1,0:T(8,128)(2,1)S(1)}, bf16[64,384]{1,0:T(8,128)(2,1)S(1)}, u32[]{:S(2)}, u32[]{:S(2)}) collective-permute-start(bf16[64,384]{1,0:T(8,128)(2,1)S(1)} %get-tuple-element.31), channel_id=1, source_target_pairs={{0,8},{4,12},{8,0},{12,4},{1,9},{5,13},{9,1},{13,5},{2,10},{6,14},... | collective-permute-start | bytes 147464 | tf_op jit(solution)/shard_map/ppermute | solution.py:202
  25.2 1.1 %collective-permute-start.12 = (bf16[64,384]{1,0:T(8,128)(2,1)S(1)}, bf16[64,384]{1,0:T(8,128)(2,1)S(1)}, u32[]{:S(2)}, u32[]{:S(2)}) collective-permute-start(bf16[64,384]{1,0:T(8,128)(2,1)S(1)} %get-tuple-element.32), channel_id=1, source_target_pairs={{0,4},{4,0},{8,12},{12,8},{1,5},{5,1},{9,13},{13,9},{2,6},{6,2},{1... | collective-permute-start | bytes 147464 | tf_op jit(solution)/shard_map/ppermute | solution.py:202
  26.3 1.3 %collective-permute-done.8.refs_0_ = bf16[64,384]{1,0:T(8,128)(2,1)S(1)} collective-permute-done((bf16[64,384]{1,0:T(8,128)(2,1)S(1)}, bf16[64,384]{1,0:T(8,128)(2,1)S(1)}, u32[]{:S(2)}, u32[]{:S(2)}) %collective-permute-start.8) | collective-permute-done | bytes 49184 | tf_op jit(solution)/shard_map/ppermute | solution.py:202
  27.7 2.0 %collective-permute-done.11.refs_2_ = bf16[64,384]{1,0:T(8,128)(2,1)S(1)} collective-permute-done((bf16[64,384]{1,0:T(8,128)(2,1)S(1)}, bf16[64,384]{1,0:T(8,128)(2,1)S(1)}, u32[]{:S(2)}, u32[]{:S(2)}) %collective-permute-start.11) | collective-permute-done | bytes 49184 | tf_op jit(solution)/shard_map/ppermute | solution.py:202
  29.7 0.0 collective-permute-done.12.refs_3_
  29.7 0.7 %unpack.1 = bf16[1,64,1536]{2,1,0:T(8,128)(2,1)} custom-call(bf16[64,384]{1,0:T(8,128)(2,1)S(1)} %get-tuple-element.25.refs_2_.refs_0_, bf16[64,384]{1,0:T(8,128)(2,1)S(1)} %hold.14.refs_1_, bf16[64,384]{1,0:T(8,128)(2,1)S(1)} %collective-permute-done.11.refs_2_, bf16[64,384]{1,0:T(8,128)(2,1)S(1)} %collective-permute-done.12.refs_3_), custom_call_target="tpu_custom_call" | custom-call | bytes 393216 | tf_op jit(solution)/shard_map/unpack/pallas_call | solution.py:251
  (9 shorter events, 0.0 us)
Async XLA Ops:
  1.2 11.0 %collective-permute-start.1 = (bf16[64,768]{1,0:T(8,128)(2,1)S(1)}, bf16[64,768]{1,0:T(8,128)(2,1)S(1)}, u32[]{:S(2)}, u32[]{:S(2)}) collective-permute-start(bf16[64,768]{1,0:T(8,128)(2,1)S(1)} %get-tuple-element.20), channel_id=1, source_target_pairs={{0,12},{4,8},{8,4},{12,0},{1,13},{5,9},{9,5},{13,1},{2,14},{6,10},... | collective-permute-start | bytes 294920 | tf_op jit(solution)/shard_map/ppermute | solution.py:202
  6.3 6.4 %collective-permute-start = (bf16[64,768]{1,0:T(8,128)(2,1)S(1)}, bf16[64,768]{1,0:T(8,128)(2,1)S(1)}, u32[]{:S(2)}, u32[]{:S(2)}) collective-permute-start(bf16[64,768]{1,0:T(8,128)(2,1)S(1)} %get-tuple-element.19), channel_id=1, source_target_pairs={{0,4},{4,0},{8,12},{12,8},{1,5},{5,1},{9,13},{13,9},{2,6},{6,2},{1... | collective-permute-start | bytes 294920 | tf_op jit(solution)/shard_map/ppermute | solution.py:202
  6.3 9.8 %collective-permute-start.2 = (bf16[64,768]{1,0:T(8,128)(2,1)S(1)}, bf16[64,768]{1,0:T(8,128)(2,1)S(1)}, u32[]{:S(2)}, u32[]{:S(2)}) collective-permute-start(bf16[64,768]{1,0:T(8,128)(2,1)S(1)} %get-tuple-element.22), channel_id=1, source_target_pairs={{0,8},{4,12},{8,0},{12,4},{1,9},{5,13},{9,1},{13,5},{2,10},{6,14},... | collective-permute-start | bytes 294920 | tf_op jit(solution)/shard_map/ppermute | solution.py:202
  6.9 10.7 %collective-permute-start.3 = (bf16[64,768]{1,0:T(8,128)(2,1)S(1)}, bf16[64,768]{1,0:T(8,128)(2,1)S(1)}, u32[]{:S(2)}, u32[]{:S(2)}) collective-permute-start(bf16[64,768]{1,0:T(8,128)(2,1)S(1)} %get-tuple-element.21.refs_1_), channel_id=1, source_target_pairs={{0,2},{2,0},{1,3},{3,1},{4,6},{6,4},{5,7},{7,5},{8,10},{10,8},{9,1... | collective-permute-start | bytes 294920 | tf_op jit(solution)/shard_map/ppermute | solution.py:205
  8.6 9.4 %collective-permute-start.7 = (bf16[64,384]{1,0:T(8,128)(2,1)S(1)}, bf16[64,384]{1,0:T(8,128)(2,1)S(1)}, u32[]{:S(2)}, u32[]{:S(2)}) collective-permute-start(bf16[64,384]{1,0:T(8,128)(2,1)S(1)} %get-tuple-element.24), channel_id=1, source_target_pairs={{0,12},{4,8},{8,4},{12,0},{1,13},{5,9},{9,5},{13,1},{2,14},{6,10},... | collective-permute-start | bytes 147464 | tf_op jit(solution)/shard_map/ppermute | solution.py:202
  12.2 8.2 %collective-permute-start.4 = (bf16[64,768]{1,0:T(8,128)(2,1)S(1)}, bf16[64,768]{1,0:T(8,128)(2,1)S(1)}, u32[]{:S(2)}, u32[]{:S(2)}) collective-permute-start(bf16[64,768]{1,0:T(8,128)(2,1)S(1)} %hold.9.refs_1_.refs_2_), channel_id=1, source_target_pairs={{0,2},{2,0},{1,3},{3,1},{4,6},{6,4},{5,7},{7,5},{8,10},{10,8},{9,1... | collective-permute-start | bytes 294920 | tf_op jit(solution)/shard_map/ppermute | solution.py:205
  12.7 7.7 %collective-permute-start.5 = (bf16[64,768]{1,0:T(8,128)(2,1)S(1)}, bf16[64,768]{1,0:T(8,128)(2,1)S(1)}, u32[]{:S(2)}, u32[]{:S(2)}) collective-permute-start(bf16[64,768]{1,0:T(8,128)(2,1)S(1)} %hold.10.refs_0_), channel_id=1, source_target_pairs={{0,2},{2,0},{1,3},{3,1},{4,6},{6,4},{5,7},{7,5},{8,10},{10,8},{9,1... | collective-permute-start | bytes 294920 | tf_op jit(solution)/shard_map/ppermute | solution.py:205
  16.1 4.6 %collective-permute-start.6 = (bf16[64,768]{1,0:T(8,128)(2,1)S(1)}, bf16[64,768]{1,0:T(8,128)(2,1)S(1)}, u32[]{:S(2)}, u32[]{:S(2)}) collective-permute-start(bf16[64,768]{1,0:T(8,128)(2,1)S(1)} %hold.11.refs_3_.refs_1_), channel_id=1, source_target_pairs={{0,2},{2,0},{1,3},{3,1},{4,6},{6,4},{5,7},{7,5},{8,10},{10,8},{9,1... | collective-permute-start | bytes 294920 | tf_op jit(solution)/shard_map/ppermute | solution.py:205
  17.6 5.9 %collective-permute-start.9 = (bf16[64,384]{1,0:T(8,128)(2,1)S(1)}, bf16[64,384]{1,0:T(8,128)(2,1)S(1)}, u32[]{:S(2)}, u32[]{:S(2)}) collective-permute-start(bf16[64,384]{1,0:T(8,128)(2,1)S(1)} %hold.15), channel_id=1, source_target_pairs={{0,8},{4,12},{8,0},{12,4},{1,9},{5,13},{9,1},{13,5},{2,10},{6,14},... | collective-permute-start | bytes 147464 | tf_op jit(solution)/shard_map/ppermute | solution.py:202
  18.0 5.5 %collective-permute-start.10 = (bf16[64,384]{1,0:T(8,128)(2,1)S(1)}, bf16[64,384]{1,0:T(8,128)(2,1)S(1)}, u32[]{:S(2)}, u32[]{:S(2)}) collective-permute-start(bf16[64,384]{1,0:T(8,128)(2,1)S(1)} %hold.16), channel_id=1, source_target_pairs={{0,4},{4,0},{8,12},{12,8},{1,5},{5,1},{9,13},{13,9},{2,6},{6,2},{1... | collective-permute-start | bytes 147464 | tf_op jit(solution)/shard_map/ppermute | solution.py:202
  21.3 6.4 %collective-permute-start.8 = (bf16[64,384]{1,0:T(8,128)(2,1)S(1)}, bf16[64,384]{1,0:T(8,128)(2,1)S(1)}, u32[]{:S(2)}, u32[]{:S(2)}) collective-permute-start(bf16[64,384]{1,0:T(8,128)(2,1)S(1)} %get-tuple-element.26), channel_id=1, source_target_pairs={{0,12},{4,8},{8,4},{12,0},{1,13},{5,9},{9,5},{13,1},{2,14},{6,10},... | collective-permute-start | bytes 147464 | tf_op jit(solution)/shard_map/ppermute | solution.py:202
  24.1 5.6 %collective-permute-start.11 = (bf16[64,384]{1,0:T(8,128)(2,1)S(1)}, bf16[64,384]{1,0:T(8,128)(2,1)S(1)}, u32[]{:S(2)}, u32[]{:S(2)}) collective-permute-start(bf16[64,384]{1,0:T(8,128)(2,1)S(1)} %get-tuple-element.31), channel_id=1, source_target_pairs={{0,8},{4,12},{8,0},{12,4},{1,9},{5,13},{9,1},{13,5},{2,10},{6,14},... | collective-permute-start | bytes 147464 | tf_op jit(solution)/shard_map/ppermute | solution.py:202
  25.2 4.4 %collective-permute-start.12 = (bf16[64,384]{1,0:T(8,128)(2,1)S(1)}, bf16[64,384]{1,0:T(8,128)(2,1)S(1)}, u32[]{:S(2)}, u32[]{:S(2)}) collective-permute-start(bf16[64,384]{1,0:T(8,128)(2,1)S(1)} %get-tuple-element.32), channel_id=1, source_target_pairs={{0,4},{4,0},{8,12},{12,8},{1,5},{5,1},{9,13},{13,9},{2,6},{6,2},{1... | collective-permute-start | bytes 147464 | tf_op jit(solution)/shard_map/ppermute | solution.py:202

commit v17 on v14

--- a/solution.py
+++ b/solution.py
@@ -10,6 +10,7 @@
 
 HD = 128
 EFFORT = 0
+EFFORT_BACK = 10**9
 EFFORT_OWN = 10**9
 EFFORT_QUERIES = 2 * 10**8
 EFFORT_NEAR = 0
@@ -230,7 +231,7 @@
     far_kv = [to_block(sent[s, kv], s) for s in far]
     near_kvq = to_block(sent[1, kv + q], 1)
     far_kv = [hold([array], (), effort)[0] for array, effort in zip(far_kv, EFFORT_FAR)]
-    near_kv = join([near_kvq], [0], 2 * part, EFFORT_NEAR)
+    near_kv = join([near_kvq], [0], 2 * part, EFFORT_NEAR, far_kv[:1])
     far_q = [to_block(sent[far[0], q], far[0])]
     far_q += [to_block(hold([sent[s, q]], [array])[0], s) for s, array in zip(far[1:], far_kv[1:])]
     own_kv_x, first_x, near_x, second_x = (
@@ -265,10 +266,9 @@
     mixed = dict(zip([0, 1] + far[:-1], attend([near_q] + far_q[:-1], [(0, 0), (0, 1), (1, None)])))
     last_q = hold([far_q[-1]], [mixed[0]])
     mixed[far[-1]] = attend(last_q, [(0, None)])[0]
-    mixed[1] = hold([mixed[1]], [mixed[far[-1]]])[0]
     back = {s: to_block(mixed[s], s) for s in far + [1]}
-    early = far[:-1]
-    back.update(zip(early, hold([back[s] for s in early], effort=EFFORT)))
+    back[1] = hold([back[1]], effort=EFFORT_BACK)[0]
+    back[1], back[far[0]] = hold([back[1], back[far[0]]], effort=EFFORT_BACK)
     back[0] = mixed[0]
     order = [0] + far + [1]
     back = [back[s] for s in order]

time: 30 us -> 30.9 us (1.030)
  waiting for transfers between devices: 6.12 us -> 7.92 us
  starting transfers between devices: 20.6 us -> 19.7 us
    ppermute x8, waiting for transfers between devices: 4.31 us -> 6.11 us  [to_block(): return lax.ppermute(array, 'blk', [(i, i ^ s) for i in range(blocks)])]
    ppermute x8, starting transfers between devices: 15.6 us -> 14.6 us  [to_block(): return lax.ppermute(array, 'blk', [(i, i ^ s) for i in range(blocks)])]
where the time goes in v17:
time: 30.9 us; the launch traced here: 30.7 us
  starting transfers between devices  19.7 us (64%)
  waiting for transfers between devices  7.92 us (26%)
  Pallas kernels  3.02 us (10%)
    ppermute x8, starting transfers between devices, to_block(): return lax.ppermute(array, 'blk', [(i, i ^ s) for i in range(blocks)])  14.6 us
    ppermute x8, waiting for transfers between devices, to_block(): return lax.ppermute(array, 'blk', [(i, i ^ s) for i in range(blocks)])  6.11 us
    ppermute x4, starting transfers between devices, to_column(): lax.ppermute(array, 'uly', [(i, (i + t) % columns_of) for i in range(colu...  5.06 us
    ppermute x4, waiting for transfers between devices, to_column(): lax.ppermute(array, 'uly', [(i, (i + t) % columns_of) for i in range(colu...  1.81 us
    pallas_call x1, Pallas kernels, local_blocks(): pl.pallas_call(functools.partial(pack_kernel, messages, part), out_shape=...  1.17 us
    pallas_call x2, Pallas kernels, attend(): pl.pallas_call(functools.partial(attend_kernel, len(holders), keys, query...  1.13 us
    pallas_call x1, Pallas kernels, local_blocks(): pl.pallas_call(functools.partial(unpack_kernel, order, part), out_shape=j...  0.7 us
  transfers between devices with their start and end apart: 12, of which 6 were waited for; matrix products, arithmetic and copies ran while one was open for 0% of the time, Pallas kernels for 4%

profile of v17, /device:TPU:0, one launch (start us, length us, event | category | flops | bytes accessed | tf_op | source)
XLA Modules:
  0.0 30.7 jit_solution(9864600493064627174)
XLA Ops:
  0.0 1.2 %pack.1 = (bf16[64,768]{1,0:T(8,128)(2,1)S(1)}, bf16[64,768]{1,0:T(8,128)(2,1)S(1)}, bf16[64,1152]{1,0:T(8,128)(2,1)S(1)}, bf16[64,384]{1,0:T(8,128)(2,1)S(1)}, ...) custom-call(bf16[1,64,1536]{2,1,0:T(8,128)(2,1)} %q_ref.1, ...), custom_call_target="tpu_custom_call" | custom-call | bytes 1179648 | tf_op jit(solution)/shard_map/pack/pallas_call | solution.py:207
  1.2 5.1 %collective-permute-start.1 = (bf16[64,768]{1,0:T(8,128)(2,1)S(1)}, bf16[64,768]{1,0:T(8,128)(2,1)S(1)}, u32[]{:S(2)}, u32[]{:S(2)}) collective-permute-start(bf16[64,768]{1,0:T(8,128)(2,1)S(1)} %get-tuple-element.19), channel_id=1, source_target_pairs={{0,12},{4,8},{8,4},{12,0},{1,13},{5,9},{9,5},{13,1},{2,14},{6,10},... | collective-permute-start | bytes 294920 | tf_op jit(solution)/shard_map/ppermute | solution.py:224
  6.3 0.0 collective-permute-start
  6.3 0.6 %collective-permute-start.2 = (bf16[64,768]{1,0:T(8,128)(2,1)S(1)}, bf16[64,768]{1,0:T(8,128)(2,1)S(1)}, u32[]{:S(2)}, u32[]{:S(2)}) collective-permute-start(bf16[64,768]{1,0:T(8,128)(2,1)S(1)} %get-tuple-element.20), channel_id=1, source_target_pairs={{0,8},{4,12},{8,0},{12,4},{1,9},{5,13},{9,1},{13,5},{2,10},{6,14},... | collective-permute-start | bytes 294920 | tf_op jit(solution)/shard_map/ppermute | solution.py:224
  6.9 3.7 %collective-permute-start.7 = (bf16[64,384]{1,0:T(8,128)(2,1)S(1)}, bf16[64,384]{1,0:T(8,128)(2,1)S(1)}, u32[]{:S(2)}, u32[]{:S(2)}) collective-permute-start(bf16[64,384]{1,0:T(8,128)(2,1)S(1)} %get-tuple-element.22), channel_id=1, source_target_pairs={{0,12},{4,8},{8,4},{12,0},{1,13},{5,9},{9,5},{13,1},{2,14},{6,10},... | collective-permute-start | bytes 147464 | tf_op jit(solution)/shard_map/ppermute | solution.py:224
  10.7 1.5 %collective-permute-start.3 = (bf16[64,768]{1,0:T(8,128)(2,1)S(1)}, bf16[64,768]{1,0:T(8,128)(2,1)S(1)}, u32[]{:S(2)}, u32[]{:S(2)}) collective-permute-start(bf16[64,768]{1,0:T(8,128)(2,1)S(1)} %get-tuple-element.18.refs_1_), channel_id=1, source_target_pairs={{0,2},{2,0},{1,3},{3,1},{4,6},{6,4},{5,7},{7,5},{8,10},{10,8},{9,1... | collective-permute-start | bytes 294920 | tf_op jit(solution)/shard_map/ppermute | solution.py:227
  12.2 0.0 collective-permute-done.1.refs_0_
  12.2 0.5 %collective-permute-start.4 = (bf16[64,768]{1,0:T(8,128)(2,1)S(1)}, bf16[64,768]{1,0:T(8,128)(2,1)S(1)}, u32[]{:S(2)}, u32[]{:S(2)}) collective-permute-start(bf16[64,768]{1,0:T(8,128)(2,1)S(1)} %hold.9.refs_1_.refs_2_), channel_id=1, source_target_pairs={{0,2},{2,0},{1,3},{3,1},{4,6},{6,4},{5,7},{7,5},{8,10},{10,8},{9,1... | collective-permute-start | bytes 294920 | tf_op jit(solution)/shard_map/ppermute | solution.py:227
  12.7 1.9 %collective-permute-done.refs_0_.refs_1_ = bf16[64,1152]{1,0:T(8,128)(2,1)S(1)} collective-permute-done((bf16[64,1152]{1,0:T(8,128)(2,1)S(1)}, bf16[64,1152]{1,0:T(8,128)(2,1)S(1)}, u32[]{:S(2)}, u32[]{:S(2)}) %collective-permute-start) | collective-permute-done | bytes 147488 | tf_op jit(solution)/shard_map/ppermute | solution.py:224
  14.6 1.8 %collective-permute-start.5 = (bf16[64,768]{1,0:T(8,128)(2,1)S(1)}, bf16[64,768]{1,0:T(8,128)(2,1)S(1)}, u32[]{:S(2)}, u32[]{:S(2)}) collective-permute-start(bf16[64,768]{1,0:T(8,128)(2,1)S(1)} %bitcast.1), channel_id=1, source_target_pairs={{0,2},{2,0},{1,3},{3,1},{4,6},{6,4},{5,7},{7,5},{8,10},{10,8},{9,1... | collective-permute-start | bytes 294920 | tf_op jit(solution)/shard_map/ppermute | solution.py:227
  16.4 0.0 collective-permute-done.2.refs_0_
  16.4 1.2 %collective-permute-start.6 = (bf16[64,768]{1,0:T(8,128)(2,1)S(1)}, bf16[64,768]{1,0:T(8,128)(2,1)S(1)}, u32[]{:S(2)}, u32[]{:S(2)}) collective-permute-start(bf16[64,768]{1,0:T(8,128)(2,1)S(1)} %hold.10.refs_3_.refs_1_), channel_id=1, source_target_pairs={{0,2},{2,0},{1,3},{3,1},{4,6},{6,4},{5,7},{7,5},{8,10},{10,8},{9,1... | collective-permute-start | bytes 294920 | tf_op jit(solution)/shard_map/ppermute | solution.py:227
  17.6 0.0 collective-permute-done.3.refs_0_
  17.6 1.5 %collective-permute-start.10 = (bf16[64,384]{1,0:T(8,128)(2,1)S(1)}, bf16[64,384]{1,0:T(8,128)(2,1)S(1)}, u32[]{:S(2)}, u32[]{:S(2)}) collective-permute-start(bf16[64,384]{1,0:T(8,128)(2,1)S(1)} %hold.16), channel_id=1, source_target_pairs={{0,8},{4,12},{8,0},{12,4},{1,9},{5,13},{9,1},{13,5},{2,10},{6,14},... | collective-permute-start | bytes 147464 | tf_op jit(solution)/shard_map/ppermute | solution.py:224
  19.2 0.0 collective-permute-done.7.refs_0_
  19.2 0.0 collective-permute-done.4.refs_2_.refs_5_
  19.2 0.8 %collective-permute-done.5.refs_3_.refs_6_ = bf16[64,768]{1,0:T(8,128)(2,1)S(1)} collective-permute-done((bf16[64,768]{1,0:T(8,128)(2,1)S(1)}, bf16[64,768]{1,0:T(8,128)(2,1)S(1)}, u32[]{:S(2)}, u32[]{:S(2)}) %collective-permute-start.5) | collective-permute-done | bytes 98336 | tf_op jit(solution)/shard_map/ppermute | solution.py:227
  20.0 1.1 %collective-permute-done.6.refs_7_ = bf16[64,768]{1,0:T(8,128)(2,1)S(1)} collective-permute-done((bf16[64,768]{1,0:T(8,128)(2,1)S(1)}, bf16[64,768]{1,0:T(8,128)(2,1)S(1)}, u32[]{:S(2)}, u32[]{:S(2)}) %collective-permute-start.6) | collective-permute-done | bytes 98336 | tf_op jit(solution)/shard_map/ppermute | solution.py:227
  21.0 0.6 %attend.2 = (bf16[64,384]{1,0:T(8,128)(2,1)S(1)}, bf16[64,384]{1,0:T(8,128)(2,1)S(1)}, bf16[64,384]{1,0:T(8,128)(2,1)S(1)}) custom-call(bf16[64,1152]{1,0:T(8,128)(2,1)S(1)} %collective-permute-done.refs_0_.refs_1_, bf16[64,768]{1,0:T(8,128)(2,1)S(1)} %get-tuple-element.18.refs_1_, bf16[64,768]{1,0:T(8,128)(2,1)S(1)} %hold.9.refs_1_.refs_2_, ...), custom_call_target="tpu_custom_call" | custom-call | flops 150994944 | bytes 1081344 | tf_op jit(solution)/shard_map/attend/pallas_call | solution.py:252
  21.6 0.4 %collective-permute-start.8 = (bf16[64,384]{1,0:T(8,128)(2,1)S(1)}, bf16[64,384]{1,0:T(8,128)(2,1)S(1)}, u32[]{:S(2)}, u32[]{:S(2)}) collective-permute-start(bf16[64,384]{1,0:T(8,128)(2,1)S(1)} %get-tuple-element.24), channel_id=1, source_target_pairs={{0,4},{4,0},{8,12},{12,8},{1,5},{5,1},{9,13},{13,9},{2,6},{6,2},{1... | collective-permute-start | bytes 147464 | tf_op jit(solution)/shard_map/ppermute | solution.py:224
  22.0 2.4 %collective-permute-start.9 = (bf16[64,384]{1,0:T(8,128)(2,1)S(1)}, bf16[64,384]{1,0:T(8,128)(2,1)S(1)}, u32[]{:S(2)}, u32[]{:S(2)}) collective-permute-start(bf16[64,384]{1,0:T(8,128)(2,1)S(1)} %get-tuple-element.25), channel_id=1, source_target_pairs={{0,12},{4,8},{8,4},{12,0},{1,13},{5,9},{9,5},{13,1},{2,14},{6,10},... | collective-permute-start | bytes 147464 | tf_op jit(solution)/shard_map/ppermute | solution.py:224
  24.4 0.0 collective-permute-done.10.refs_0_
  24.5 0.5 %attend.3 = bf16[64,384]{1,0:T(8,128)(2,1)S(1)} custom-call(bf16[64,1152]{1,0:T(8,128)(2,1)S(1)} %collective-permute-done.refs_0_.refs_1_, bf16[64,768]{1,0:T(8,128)(2,1)S(1)} %get-tuple-element.18.refs_1_, bf16[64,768]{1,0:T(8,128)(2,1)S(1)} %hold.9.refs_1_.refs_2_, bf16[64,768]{1,0:T(8,128)(2,1)S(1)} %hold.10.refs_3_.refs_1_, ...), custom_call_target="tpu_custom_call" | custom-call | flops 50331648 | bytes 884736 | tf_op jit(solution)/shard_map/attend/pallas_call | solution.py:252
  24.9 0.8 %collective-permute-start.11 = (bf16[64,384]{1,0:T(8,128)(2,1)S(1)}, bf16[64,384]{1,0:T(8,128)(2,1)S(1)}, u32[]{:S(2)}, u32[]{:S(2)}) collective-permute-start(bf16[64,384]{1,0:T(8,128)(2,1)S(1)} %attend.3), channel_id=1, source_target_pairs={{0,8},{4,12},{8,0},{12,4},{1,9},{5,13},{9,1},{13,5},{2,10},{6,14},... | collective-permute-start | bytes 147464 | tf_op jit(solution)/shard_map/ppermute | solution.py:224
  25.8 0.3 %collective-permute-done.8.refs_0_ = bf16[64,384]{1,0:T(8,128)(2,1)S(1)} collective-permute-done((bf16[64,384]{1,0:T(8,128)(2,1)S(1)}, bf16[64,384]{1,0:T(8,128)(2,1)S(1)}, u32[]{:S(2)}, u32[]{:S(2)}) %collective-permute-start.8) | collective-permute-done | bytes 49184 | tf_op jit(solution)/shard_map/ppermute | solution.py:224
  26.1 1.8 %collective-permute-done.9.refs_1_ = bf16[64,384]{1,0:T(8,128)(2,1)S(1)} collective-permute-done((bf16[64,384]{1,0:T(8,128)(2,1)S(1)}, bf16[64,384]{1,0:T(8,128)(2,1)S(1)}, u32[]{:S(2)}, u32[]{:S(2)}) %collective-permute-start.9) | collective-permute-done | bytes 49184 | tf_op jit(solution)/shard_map/ppermute | solution.py:224
  27.9 2.1 %collective-permute-done.11.refs_2_ = bf16[64,384]{1,0:T(8,128)(2,1)S(1)} collective-permute-done((bf16[64,384]{1,0:T(8,128)(2,1)S(1)}, bf16[64,384]{1,0:T(8,128)(2,1)S(1)}, u32[]{:S(2)}, u32[]{:S(2)}) %collective-permute-start.11) | collective-permute-done | bytes 49184 | tf_op jit(solution)/shard_map/ppermute | solution.py:224
  30.0 0.7 %unpack.1 = bf16[1,64,1536]{2,1,0:T(8,128)(2,1)} custom-call(bf16[64,384]{1,0:T(8,128)(2,1)S(1)} %get-tuple-element.23.refs_1_.refs_0_, bf16[64,384]{1,0:T(8,128)(2,1)S(1)} %get-tuple-element.26.refs_1_, bf16[64,384]{1,0:T(8,128)(2,1)S(1)} %collective-permute-done.11.refs_2_, bf16[64,384]{1,0:T(8,128)(2,1)S(1)} %get-tuple-element.28.refs_3_), custom_call_target="tpu_custom_call" | custom-call | bytes 393216 | tf_op jit(solution)/shard_map/unpack/pallas_call | solution.py:275
  (11 shorter events, 0.0 us)
Async XLA Ops:
  1.2 11.0 %collective-permute-start.1 = (bf16[64,768]{1,0:T(8,128)(2,1)S(1)}, bf16[64,768]{1,0:T(8,128)(2,1)S(1)}, u32[]{:S(2)}, u32[]{:S(2)}) collective-permute-start(bf16[64,768]{1,0:T(8,128)(2,1)S(1)} %get-tuple-element.19), channel_id=1, source_target_pairs={{0,12},{4,8},{8,4},{12,0},{1,13},{5,9},{9,5},{13,1},{2,14},{6,10},... | collective-permute-start | bytes 294920 | tf_op jit(solution)/shard_map/ppermute | solution.py:224
  6.3 8.3 %collective-permute-start = (bf16[64,1152]{1,0:T(8,128)(2,1)S(1)}, bf16[64,1152]{1,0:T(8,128)(2,1)S(1)}, u32[]{:S(2)}, u32[]{:S(2)}) collective-permute-start(bf16[64,1152]{1,0:T(8,128)(2,1)S(1)} %get-tuple-element.17), channel_id=1, source_target_pairs={{0,4},{4,0},{8,12},{12,8},{1,5},{5,1},{9,13},{13,9},{2,6},{6,2},{1... | collective-permute-start | bytes 442376 | tf_op jit(solution)/shard_map/ppermute | solution.py:224
  6.3 10.1 %collective-permute-start.2 = (bf16[64,768]{1,0:T(8,128)(2,1)S(1)}, bf16[64,768]{1,0:T(8,128)(2,1)S(1)}, u32[]{:S(2)}, u32[]{:S(2)}) collective-permute-start(bf16[64,768]{1,0:T(8,128)(2,1)S(1)} %get-tuple-element.20), channel_id=1, source_target_pairs={{0,8},{4,12},{8,0},{12,4},{1,9},{5,13},{9,1},{13,5},{2,10},{6,14},... | collective-permute-start | bytes 294920 | tf_op jit(solution)/shard_map/ppermute | solution.py:224
  6.9 12.2 %collective-permute-start.7 = (bf16[64,384]{1,0:T(8,128)(2,1)S(1)}, bf16[64,384]{1,0:T(8,128)(2,1)S(1)}, u32[]{:S(2)}, u32[]{:S(2)}) collective-permute-start(bf16[64,384]{1,0:T(8,128)(2,1)S(1)} %get-tuple-element.22), channel_id=1, source_target_pairs={{0,12},{4,8},{8,4},{12,0},{1,13},{5,9},{9,5},{13,1},{2,14},{6,10},... | collective-permute-start | bytes 147464 | tf_op jit(solution)/shard_map/ppermute | solution.py:224
  10.7 6.9 %collective-permute-start.3 = (bf16[64,768]{1,0:T(8,128)(2,1)S(1)}, bf16[64,768]{1,0:T(8,128)(2,1)S(1)}, u32[]{:S(2)}, u32[]{:S(2)}) collective-permute-start(bf16[64,768]{1,0:T(8,128)(2,1)S(1)} %get-tuple-element.18.refs_1_), channel_id=1, source_target_pairs={{0,2},{2,0},{1,3},{3,1},{4,6},{6,4},{5,7},{7,5},{8,10},{10,8},{9,1... | collective-permute-start | bytes 294920 | tf_op jit(solution)/shard_map/ppermute | solution.py:227
  12.2 7.0 %collective-permute-start.4 = (bf16[64,768]{1,0:T(8,128)(2,1)S(1)}, bf16[64,768]{1,0:T(8,128)(2,1)S(1)}, u32[]{:S(2)}, u32[]{:S(2)}) collective-permute-start(bf16[64,768]{1,0:T(8,128)(2,1)S(1)} %hold.9.refs_1_.refs_2_), channel_id=1, source_target_pairs={{0,2},{2,0},{1,3},{3,1},{4,6},{6,4},{5,7},{7,5},{8,10},{10,8},{9,1... | collective-permute-start | bytes 294920 | tf_op jit(solution)/shard_map/ppermute | solution.py:227
  14.6 5.4 %collective-permute-start.5 = (bf16[64,768]{1,0:T(8,128)(2,1)S(1)}, bf16[64,768]{1,0:T(8,128)(2,1)S(1)}, u32[]{:S(2)}, u32[]{:S(2)}) collective-permute-start(bf16[64,768]{1,0:T(8,128)(2,1)S(1)} %bitcast.1), channel_id=1, source_target_pairs={{0,2},{2,0},{1,3},{3,1},{4,6},{6,4},{5,7},{7,5},{8,10},{10,8},{9,1... | collective-permute-start | bytes 294920 | tf_op jit(solution)/shard_map/ppermute | solution.py:227
  16.4 4.6 %collective-permute-start.6 = (bf16[64,768]{1,0:T(8,128)(2,1)S(1)}, bf16[64,768]{1,0:T(8,128)(2,1)S(1)}, u32[]{:S(2)}, u32[]{:S(2)}) collective-permute-start(bf16[64,768]{1,0:T(8,128)(2,1)S(1)} %hold.10.refs_3_.refs_1_), channel_id=1, source_target_pairs={{0,2},{2,0},{1,3},{3,1},{4,6},{6,4},{5,7},{7,5},{8,10},{10,8},{9,1... | collective-permute-start | bytes 294920 | tf_op jit(solution)/shard_map/ppermute | solution.py:227
  17.6 6.8 %collective-permute-start.10 = (bf16[64,384]{1,0:T(8,128)(2,1)S(1)}, bf16[64,384]{1,0:T(8,128)(2,1)S(1)}, u32[]{:S(2)}, u32[]{:S(2)}) collective-permute-start(bf16[64,384]{1,0:T(8,128)(2,1)S(1)} %hold.16), channel_id=1, source_target_pairs={{0,8},{4,12},{8,0},{12,4},{1,9},{5,13},{9,1},{13,5},{2,10},{6,14},... | collective-permute-start | bytes 147464 | tf_op jit(solution)/shard_map/ppermute | solution.py:224
  21.6 4.5 %collective-permute-start.8 = (bf16[64,384]{1,0:T(8,128)(2,1)S(1)}, bf16[64,384]{1,0:T(8,128)(2,1)S(1)}, u32[]{:S(2)}, u32[]{:S(2)}) collective-permute-start(bf16[64,384]{1,0:T(8,128)(2,1)S(1)} %get-tuple-element.24), channel_id=1, source_target_pairs={{0,4},{4,0},{8,12},{12,8},{1,5},{5,1},{9,13},{13,9},{2,6},{6,2},{1... | collective-permute-start | bytes 147464 | tf_op jit(solution)/shard_map/ppermute | solution.py:224
  22.0 5.9 %collective-permute-start.9 = (bf16[64,384]{1,0:T(8,128)(2,1)S(1)}, bf16[64,384]{1,0:T(8,128)(2,1)S(1)}, u32[]{:S(2)}, u32[]{:S(2)}) collective-permute-start(bf16[64,384]{1,0:T(8,128)(2,1)S(1)} %get-tuple-element.25), channel_id=1, source_target_pairs={{0,12},{4,8},{8,4},{12,0},{1,13},{5,9},{9,5},{13,1},{2,14},{6,10},... | collective-permute-start | bytes 147464 | tf_op jit(solution)/shard_map/ppermute | solution.py:224
  24.9 5.1 %collective-permute-start.11 = (bf16[64,384]{1,0:T(8,128)(2,1)S(1)}, bf16[64,384]{1,0:T(8,128)(2,1)S(1)}, u32[]{:S(2)}, u32[]{:S(2)}) collective-permute-start(bf16[64,384]{1,0:T(8,128)(2,1)S(1)} %attend.3), channel_id=1, source_target_pairs={{0,8},{4,12},{8,0},{12,4},{1,9},{5,13},{9,1},{13,5},{2,10},{6,14},... | collective-permute-start | bytes 147464 | tf_op jit(solution)/shard_map/ppermute | solution.py:224

commit v18 on v14

--- a/solution.py
+++ b/solution.py
@@ -227,7 +227,7 @@
 
     sent = {message: array for message, array in zip(messages, packed)}
     own_kv, own_q = packed[-2:]
-    far_kv = [to_block(sent[s, kv], s) for s in far]
+    far_kv = [to_block(sent[s, kv], s) for s in far[::-1]]
     near_kvq = to_block(sent[1, kv + q], 1)
     far_kv = [hold([array], (), effort)[0] for array, effort in zip(far_kv, EFFORT_FAR)]
     near_kv = join([near_kvq], [0], 2 * part, EFFORT_NEAR)

time: 30 us -> 30.6 us (1.020)
  starting transfers between devices: 20.6 us -> 22.2 us
  waiting for transfers between devices: 6.12 us -> 5.03 us
    ppermute x8, starting transfers between devices: 15.6 us -> 17.2 us  [to_block(): return lax.ppermute(array, 'blk', [(i, i ^ s) for i in range(blocks)])]
    ppermute x4, waiting for transfers between devices: 1.81 us -> 0.8 us  [to_column(): lax.ppermute(array, 'uly', [(i, (i + t) % columns_of) for i in range(colu...]
  transfers between devices with their start and end apart: 12 -> 12, of which waited for: 6 -> 5; matrix products, arithmetic and copies ran while one was open for 0% -> 0% of each run, Pallas kernels for 4% -> 4%
where the time goes in v18:
time: 30.6 us; the launch traced here: 30.4 us
  starting transfers between devices  22.2 us (73%)
  waiting for transfers between devices  5.03 us (16%)
  Pallas kernels  3.02 us (10%)
    ppermute x8, starting transfers between devices, to_block(): return lax.ppermute(array, 'blk', [(i, i ^ s) for i in range(blocks)])  17.2 us
    ppermute x4, starting transfers between devices, to_column(): lax.ppermute(array, 'uly', [(i, (i + t) % columns_of) for i in range(colu...  5.03 us
    ppermute x8, waiting for transfers between devices, to_block(): return lax.ppermute(array, 'blk', [(i, i ^ s) for i in range(blocks)])  4.23 us
    pallas_call x1, Pallas kernels, local_blocks(): pl.pallas_call(functools.partial(pack_kernel, messages, part), out_shape=...  1.17 us
    pallas_call x2, Pallas kernels, attend(): pl.pallas_call(functools.partial(attend_kernel, len(holders), keys, query...  1.13 us
    ppermute x4, waiting for transfers between devices, to_column(): lax.ppermute(array, 'uly', [(i, (i + t) % columns_of) for i in range(colu...  0.8 us
    pallas_call x1, Pallas kernels, local_blocks(): pl.pallas_call(functools.partial(unpack_kernel, order, part), out_shape=j...  0.7 us
  transfers between devices with their start and end apart: 12, of which 5 were waited for; matrix products, arithmetic and copies ran while one was open for 0% of the time, Pallas kernels for 4%

profile of v18, /device:TPU:0, one launch (start us, length us, event | category | flops | bytes accessed | tf_op | source)
XLA Modules:
  0.0 30.4 jit_solution(4254562417024161987)
XLA Ops:
  0.0 1.2 %pack.1 = (bf16[64,768]{1,0:T(8,128)(2,1)S(1)}, bf16[64,768]{1,0:T(8,128)(2,1)S(1)}, bf16[64,1152]{1,0:T(8,128)(2,1)S(1)}, bf16[64,384]{1,0:T(8,128)(2,1)S(1)}, ...) custom-call(bf16[1,64,1536]{2,1,0:T(8,128)(2,1)} %q_ref.1, ...), custom_call_target="tpu_custom_call" | custom-call | bytes 1179648 | tf_op jit(solution)/shard_map/pack/pallas_call | solution.py:206
  1.2 4.1 %collective-permute-start.1 = (bf16[64,768]{1,0:T(8,128)(2,1)S(1)}, bf16[64,768]{1,0:T(8,128)(2,1)S(1)}, u32[]{:S(2)}, u32[]{:S(2)}) collective-permute-start(bf16[64,768]{1,0:T(8,128)(2,1)S(1)} %get-tuple-element.17), channel_id=1, source_target_pairs={{0,8},{4,12},{8,0},{12,4},{1,9},{5,13},{9,1},{13,5},{2,10},{6,14},... | collective-permute-start | bytes 294920 | tf_op jit(solution)/shard_map/ppermute | solution.py:223
  5.3 1.6 %collective-permute-start = (bf16[64,1152]{1,0:T(8,128)(2,1)S(1)}, bf16[64,1152]{1,0:T(8,128)(2,1)S(1)}, u32[]{:S(2)}, u32[]{:S(2)}) collective-permute-start(bf16[64,1152]{1,0:T(8,128)(2,1)S(1)} %get-tuple-element.15), channel_id=1, source_target_pairs={{0,4},{4,0},{8,12},{12,8},{1,5},{5,1},{9,13},{13,9},{2,6},{6,2},{1... | collective-permute-start | bytes 442376 | tf_op jit(solution)/shard_map/ppermute | solution.py:223
  6.9 0.0 collective-permute-start.2
  6.9 3.8 %collective-permute-start.7 = (bf16[64,384]{1,0:T(8,128)(2,1)S(1)}, bf16[64,384]{1,0:T(8,128)(2,1)S(1)}, u32[]{:S(2)}, u32[]{:S(2)}) collective-permute-start(bf16[64,384]{1,0:T(8,128)(2,1)S(1)} %get-tuple-element.20), channel_id=1, source_target_pairs={{0,12},{4,8},{8,4},{12,0},{1,13},{5,9},{9,5},{13,1},{2,14},{6,10},... | collective-permute-start | bytes 147464 | tf_op jit(solution)/shard_map/ppermute | solution.py:223
  10.7 1.5 %collective-permute-start.3 = (bf16[64,768]{1,0:T(8,128)(2,1)S(1)}, bf16[64,768]{1,0:T(8,128)(2,1)S(1)}, u32[]{:S(2)}, u32[]{:S(2)}) collective-permute-start(bf16[64,768]{1,0:T(8,128)(2,1)S(1)} %get-tuple-element.16.refs_1_), channel_id=1, source_target_pairs={{0,2},{2,0},{1,3},{3,1},{4,6},{6,4},{5,7},{7,5},{8,10},{10,8},{9,1... | collective-permute-start | bytes 294920 | tf_op jit(solution)/shard_map/ppermute | solution.py:226
  12.2 0.0 collective-permute-done.1.refs_0_
  12.2 0.5 %collective-permute-start.4 = (bf16[64,768]{1,0:T(8,128)(2,1)S(1)}, bf16[64,768]{1,0:T(8,128)(2,1)S(1)}, u32[]{:S(2)}, u32[]{:S(2)}) collective-permute-start(bf16[64,768]{1,0:T(8,128)(2,1)S(1)} %hold.9.refs_2_), channel_id=1, source_target_pairs={{0,2},{2,0},{1,3},{3,1},{4,6},{6,4},{5,7},{7,5},{8,10},{10,8},{9,1... | collective-permute-start | bytes 294920 | tf_op jit(solution)/shard_map/ppermute | solution.py:226
  12.7 0.0 collective-permute-done.refs_0_.refs_1_
  12.7 1.6 %collective-permute-start.5 = (bf16[64,768]{1,0:T(8,128)(2,1)S(1)}, bf16[64,768]{1,0:T(8,128)(2,1)S(1)}, u32[]{:S(2)}, u32[]{:S(2)}) collective-permute-start(bf16[64,768]{1,0:T(8,128)(2,1)S(1)} %bitcast.1), channel_id=1, source_target_pairs={{0,2},{2,0},{1,3},{3,1},{4,6},{6,4},{5,7},{7,5},{8,10},{10,8},{9,1... | collective-permute-start | bytes 294920 | tf_op jit(solution)/shard_map/ppermute | solution.py:226
  14.3 0.8 %collective-permute-done.2.refs_0_ = bf16[64,768]{1,0:T(8,128)(2,1)S(1)} collective-permute-done((bf16[64,768]{1,0:T(8,128)(2,1)S(1)}, bf16[64,768]{1,0:T(8,128)(2,1)S(1)}, u32[]{:S(2)}, u32[]{:S(2)}) %collective-permute-start.2) | collective-permute-done | bytes 98336 | tf_op jit(solution)/shard_map/ppermute | solution.py:223
  15.1 1.4 %collective-permute-start.6 = (bf16[64,768]{1,0:T(8,128)(2,1)S(1)}, bf16[64,768]{1,0:T(8,128)(2,1)S(1)}, u32[]{:S(2)}, u32[]{:S(2)}) collective-permute-start(bf16[64,768]{1,0:T(8,128)(2,1)S(1)} %hold.10.refs_3_.refs_1_), channel_id=1, source_target_pairs={{0,2},{2,0},{1,3},{3,1},{4,6},{6,4},{5,7},{7,5},{8,10},{10,8},{9,1... | collective-permute-start | bytes 294920 | tf_op jit(solution)/shard_map/ppermute | solution.py:226
  16.5 0.0 collective-permute-done.3.refs_0_
  16.5 3.2 %collective-permute-start.9 = (bf16[64,384]{1,0:T(8,128)(2,1)S(1)}, bf16[64,384]{1,0:T(8,128)(2,1)S(1)}, u32[]{:S(2)}, u32[]{:S(2)}) collective-permute-start(bf16[64,384]{1,0:T(8,128)(2,1)S(1)} %hold.15), channel_id=1, source_target_pairs={{0,8},{4,12},{8,0},{12,4},{1,9},{5,13},{9,1},{13,5},{2,10},{6,14},... | collective-permute-start | bytes 147464 | tf_op jit(solution)/shard_map/ppermute | solution.py:223
  19.7 0.0 collective-permute-done.7.refs_0_
  19.7 0.0 collective-permute-done.4.refs_2_.refs_5_
  19.8 0.0 collective-permute-done.5.refs_3_.refs_6_
  19.8 0.8 %collective-permute-done.6.refs_7_ = bf16[64,768]{1,0:T(8,128)(2,1)S(1)} collective-permute-done((bf16[64,768]{1,0:T(8,128)(2,1)S(1)}, bf16[64,768]{1,0:T(8,128)(2,1)S(1)}, u32[]{:S(2)}, u32[]{:S(2)}) %collective-permute-start.6) | collective-permute-done | bytes 98336 | tf_op jit(solution)/shard_map/ppermute | solution.py:226
  20.6 0.6 %attend.2 = (bf16[64,384]{1,0:T(8,128)(2,1)S(1)}, bf16[64,384]{1,0:T(8,128)(2,1)S(1)}, bf16[64,384]{1,0:T(8,128)(2,1)S(1)}) custom-call(bf16[64,1152]{1,0:T(8,128)(2,1)S(1)} %collective-permute-done.refs_0_.refs_1_, bf16[64,768]{1,0:T(8,128)(2,1)S(1)} %get-tuple-element.16.refs_1_, bf16[64,768]{1,0:T(8,128)(2,1)S(1)} %hold.9.refs_2_, ...), custom_call_target="tpu_custom_call" | custom-call | flops 150994944 | bytes 1081344 | tf_op jit(solution)/shard_map/attend/pallas_call | solution.py:251
  21.2 2.2 %collective-permute-start.8 = (bf16[64,384]{1,0:T(8,128)(2,1)S(1)}, bf16[64,384]{1,0:T(8,128)(2,1)S(1)}, u32[]{:S(2)}, u32[]{:S(2)}) collective-permute-start(bf16[64,384]{1,0:T(8,128)(2,1)S(1)} %get-tuple-element.22), channel_id=1, source_target_pairs={{0,12},{4,8},{8,4},{12,0},{1,13},{5,9},{9,5},{13,1},{2,14},{6,10},... | collective-permute-start | bytes 147464 | tf_op jit(solution)/shard_map/ppermute | solution.py:223
  23.4 0.0 collective-permute-done.9.refs_0_
  23.4 0.5 %attend.3.refs_1_ = bf16[64,384]{1,0:T(8,128)(2,1)S(1)} custom-call(bf16[64,1152]{1,0:T(8,128)(2,1)S(1)} %collective-permute-done.refs_0_.refs_1_, bf16[64,768]{1,0:T(8,128)(2,1)S(1)} %get-tuple-element.16.refs_1_, bf16[64,768]{1,0:T(8,128)(2,1)S(1)} %hold.9.refs_2_, bf16[64,768]{1,0:T(8,128)(2,1)S(1)} %hold.10.refs_3_.refs_1_, ...), custom_call_target="tpu_custom_call" | custom-call | flops 50331648 | bytes 884736 | tf_op jit(solution)/shard_map/attend/pallas_call | solution.py:251
  23.9 0.8 %collective-permute-start.11 = (bf16[64,384]{1,0:T(8,128)(2,1)S(1)}, bf16[64,384]{1,0:T(8,128)(2,1)S(1)}, u32[]{:S(2)}, u32[]{:S(2)}) collective-permute-start(bf16[64,384]{1,0:T(8,128)(2,1)S(1)} %hold.17), channel_id=1, source_target_pairs={{0,4},{4,0},{8,12},{12,8},{1,5},{5,1},{9,13},{13,9},{2,6},{6,2},{1... | collective-permute-start | bytes 147464 | tf_op jit(solution)/shard_map/ppermute | solution.py:223
  24.7 1.6 %collective-permute-start.10 = (bf16[64,384]{1,0:T(8,128)(2,1)S(1)}, bf16[64,384]{1,0:T(8,128)(2,1)S(1)}, u32[]{:S(2)}, u32[]{:S(2)}) collective-permute-start(bf16[64,384]{1,0:T(8,128)(2,1)S(1)} %attend.3.refs_1_), channel_id=1, source_target_pairs={{0,8},{4,12},{8,0},{12,4},{1,9},{5,13},{9,1},{13,5},{2,10},{6,14},... | collective-permute-start | bytes 147464 | tf_op jit(solution)/shard_map/ppermute | solution.py:223
  26.2 1.0 %collective-permute-done.8.refs_0_ = bf16[64,384]{1,0:T(8,128)(2,1)S(1)} collective-permute-done((bf16[64,384]{1,0:T(8,128)(2,1)S(1)}, bf16[64,384]{1,0:T(8,128)(2,1)S(1)}, u32[]{:S(2)}, u32[]{:S(2)}) %collective-permute-start.8) | collective-permute-done | bytes 49184 | tf_op jit(solution)/shard_map/ppermute | solution.py:223
  27.3 0.9 %collective-permute-done.11.refs_3_ = bf16[64,384]{1,0:T(8,128)(2,1)S(1)} collective-permute-done((bf16[64,384]{1,0:T(8,128)(2,1)S(1)}, bf16[64,384]{1,0:T(8,128)(2,1)S(1)}, u32[]{:S(2)}, u32[]{:S(2)}) %collective-permute-start.11) | collective-permute-done | bytes 49184 | tf_op jit(solution)/shard_map/ppermute | solution.py:223
  28.1 1.5 %collective-permute-done.10.refs_2_ = bf16[64,384]{1,0:T(8,128)(2,1)S(1)} collective-permute-done((bf16[64,384]{1,0:T(8,128)(2,1)S(1)}, bf16[64,384]{1,0:T(8,128)(2,1)S(1)}, u32[]{:S(2)}, u32[]{:S(2)}) %collective-permute-start.10) | collective-permute-done | bytes 49184 | tf_op jit(solution)/shard_map/ppermute | solution.py:223
  29.7 0.7 %unpack.1 = bf16[1,64,1536]{2,1,0:T(8,128)(2,1)} custom-call(bf16[64,384]{1,0:T(8,128)(2,1)S(1)} %get-tuple-element.21.refs_1_.refs_0_, bf16[64,384]{1,0:T(8,128)(2,1)S(1)} %hold.14.refs_1_, bf16[64,384]{1,0:T(8,128)(2,1)S(1)} %collective-permute-done.10.refs_2_, bf16[64,384]{1,0:T(8,128)(2,1)S(1)} %collective-permute-done.11.refs_3_), custom_call_target="tpu_custom_call" | custom-call | bytes 393216 | tf_op jit(solution)/shard_map/unpack/pallas_call | solution.py:275
  (11 shorter events, 0.0 us)
Async XLA Ops:
  1.2 11.0 %collective-permute-start.1 = (bf16[64,768]{1,0:T(8,128)(2,1)S(1)}, bf16[64,768]{1,0:T(8,128)(2,1)S(1)}, u32[]{:S(2)}, u32[]{:S(2)}) collective-permute-start(bf16[64,768]{1,0:T(8,128)(2,1)S(1)} %get-tuple-element.17), channel_id=1, source_target_pairs={{0,8},{4,12},{8,0},{12,4},{1,9},{5,13},{9,1},{13,5},{2,10},{6,14},... | collective-permute-start | bytes 294920 | tf_op jit(solution)/shard_map/ppermute | solution.py:223
  5.3 7.4 %collective-permute-start = (bf16[64,1152]{1,0:T(8,128)(2,1)S(1)}, bf16[64,1152]{1,0:T(8,128)(2,1)S(1)}, u32[]{:S(2)}, u32[]{:S(2)}) collective-permute-start(bf16[64,1152]{1,0:T(8,128)(2,1)S(1)} %get-tuple-element.15), channel_id=1, source_target_pairs={{0,4},{4,0},{8,12},{12,8},{1,5},{5,1},{9,13},{13,9},{2,6},{6,2},{1... | collective-permute-start | bytes 442376 | tf_op jit(solution)/shard_map/ppermute | solution.py:223
  6.9 8.2 %collective-permute-start.2 = (bf16[64,768]{1,0:T(8,128)(2,1)S(1)}, bf16[64,768]{1,0:T(8,128)(2,1)S(1)}, u32[]{:S(2)}, u32[]{:S(2)}) collective-permute-start(bf16[64,768]{1,0:T(8,128)(2,1)S(1)} %get-tuple-element.18), channel_id=1, source_target_pairs={{0,12},{4,8},{8,4},{12,0},{1,13},{5,9},{9,5},{13,1},{2,14},{6,10},... | collective-permute-start | bytes 294920 | tf_op jit(solution)/shard_map/ppermute | solution.py:223
  6.9 12.9 %collective-permute-start.7 = (bf16[64,384]{1,0:T(8,128)(2,1)S(1)}, bf16[64,384]{1,0:T(8,128)(2,1)S(1)}, u32[]{:S(2)}, u32[]{:S(2)}) collective-permute-start(bf16[64,384]{1,0:T(8,128)(2,1)S(1)} %get-tuple-element.20), channel_id=1, source_target_pairs={{0,12},{4,8},{8,4},{12,0},{1,13},{5,9},{9,5},{13,1},{2,14},{6,10},... | collective-permute-start | bytes 147464 | tf_op jit(solution)/shard_map/ppermute | solution.py:223
  10.7 5.8 %collective-permute-start.3 = (bf16[64,768]{1,0:T(8,128)(2,1)S(1)}, bf16[64,768]{1,0:T(8,128)(2,1)S(1)}, u32[]{:S(2)}, u32[]{:S(2)}) collective-permute-start(bf16[64,768]{1,0:T(8,128)(2,1)S(1)} %get-tuple-element.16.refs_1_), channel_id=1, source_target_pairs={{0,2},{2,0},{1,3},{3,1},{4,6},{6,4},{5,7},{7,5},{8,10},{10,8},{9,1... | collective-permute-start | bytes 294920 | tf_op jit(solution)/shard_map/ppermute | solution.py:226
  12.2 7.6 %collective-permute-start.4 = (bf16[64,768]{1,0:T(8,128)(2,1)S(1)}, bf16[64,768]{1,0:T(8,128)(2,1)S(1)}, u32[]{:S(2)}, u32[]{:S(2)}) collective-permute-start(bf16[64,768]{1,0:T(8,128)(2,1)S(1)} %hold.9.refs_2_), channel_id=1, source_target_pairs={{0,2},{2,0},{1,3},{3,1},{4,6},{6,4},{5,7},{7,5},{8,10},{10,8},{9,1... | collective-permute-start | bytes 294920 | tf_op jit(solution)/shard_map/ppermute | solution.py:226
  12.7 7.0 %collective-permute-start.5 = (bf16[64,768]{1,0:T(8,128)(2,1)S(1)}, bf16[64,768]{1,0:T(8,128)(2,1)S(1)}, u32[]{:S(2)}, u32[]{:S(2)}) collective-permute-start(bf16[64,768]{1,0:T(8,128)(2,1)S(1)} %bitcast.1), channel_id=1, source_target_pairs={{0,2},{2,0},{1,3},{3,1},{4,6},{6,4},{5,7},{7,5},{8,10},{10,8},{9,1... | collective-permute-start | bytes 294920 | tf_op jit(solution)/shard_map/ppermute | solution.py:226
  15.1 5.5 %collective-permute-start.6 = (bf16[64,768]{1,0:T(8,128)(2,1)S(1)}, bf16[64,768]{1,0:T(8,128)(2,1)S(1)}, u32[]{:S(2)}, u32[]{:S(2)}) collective-permute-start(bf16[64,768]{1,0:T(8,128)(2,1)S(1)} %hold.10.refs_3_.refs_1_), channel_id=1, source_target_pairs={{0,2},{2,0},{1,3},{3,1},{4,6},{6,4},{5,7},{7,5},{8,10},{10,8},{9,1... | collective-permute-start | bytes 294920 | tf_op jit(solution)/shard_map/ppermute | solution.py:226
  16.5 6.9 %collective-permute-start.9 = (bf16[64,384]{1,0:T(8,128)(2,1)S(1)}, bf16[64,384]{1,0:T(8,128)(2,1)S(1)}, u32[]{:S(2)}, u32[]{:S(2)}) collective-permute-start(bf16[64,384]{1,0:T(8,128)(2,1)S(1)} %hold.15), channel_id=1, source_target_pairs={{0,8},{4,12},{8,0},{12,4},{1,9},{5,13},{9,1},{13,5},{2,10},{6,14},... | collective-permute-start | bytes 147464 | tf_op jit(solution)/shard_map/ppermute | solution.py:223
  21.2 6.1 %collective-permute-start.8 = (bf16[64,384]{1,0:T(8,128)(2,1)S(1)}, bf16[64,384]{1,0:T(8,128)(2,1)S(1)}, u32[]{:S(2)}, u32[]{:S(2)}) collective-permute-start(bf16[64,384]{1,0:T(8,128)(2,1)S(1)} %get-tuple-element.22), channel_id=1, source_target_pairs={{0,12},{4,8},{8,4},{12,0},{1,13},{5,9},{9,5},{13,1},{2,14},{6,10},... | collective-permute-start | bytes 147464 | tf_op jit(solution)/shard_map/ppermute | solution.py:223
  23.9 4.2 %collective-permute-start.11 = (bf16[64,384]{1,0:T(8,128)(2,1)S(1)}, bf16[64,384]{1,0:T(8,128)(2,1)S(1)}, u32[]{:S(2)}, u32[]{:S(2)}) collective-permute-start(bf16[64,384]{1,0:T(8,128)(2,1)S(1)} %hold.17), channel_id=1, source_target_pairs={{0,4},{4,0},{8,12},{12,8},{1,5},{5,1},{9,13},{13,9},{2,6},{6,2},{1... | collective-permute-start | bytes 147464 | tf_op jit(solution)/shard_map/ppermute | solution.py:223
  24.7 5.0 %collective-permute-start.10 = (bf16[64,384]{1,0:T(8,128)(2,1)S(1)}, bf16[64,384]{1,0:T(8,128)(2,1)S(1)}, u32[]{:S(2)}, u32[]{:S(2)}) collective-permute-start(bf16[64,384]{1,0:T(8,128)(2,1)S(1)} %attend.3.refs_1_), channel_id=1, source_target_pairs={{0,8},{4,12},{8,0},{12,4},{1,9},{5,13},{9,1},{13,5},{2,10},{6,14},... | collective-permute-start | bytes 147464 | tf_op jit(solution)/shard_map/ppermute | solution.py:223

commit v19 on v15

--- a/solution.py
+++ b/solution.py
@@ -208,16 +208,16 @@
     own_kv, own_q = sent[0, kv], sent[0, q]
     far_kv = [to_block(sent[s, kv], s) for s in far]
     far_kv = [hold([array], (), effort)[0] for array, effort in zip(far_kv, EFFORT_FAR)]
-    near_kv = hold([to_block(sent[1, kv], 1)], (), EFFORT_NEAR)[0]
+    near_q = to_block(sent[1, q], 1)
+    near_kv = hold([to_block(sent[1, kv], 1)], [far_kv[0], near_q], EFFORT_NEAR)[0]
 
     own_kv_x, first_x, near_x, second_x = (
         [to_column(group, t) for t in range(1, columns_of)]
         for group in (own_kv, far_kv[0], near_kv, far_kv[1])
     )
     own_kv_x = hold(own_kv_x, effort=EFFORT_OWN)
-    first_q = to_block(sent[far[0], q], far[0])
-    first_q = hold([first_q], [*own_kv_x, *first_x, *near_x], EFFORT_QUERIES)[0]
-    second_q, near_q = (to_block(hold([sent[s, q]], far_kv[1:])[0], s) for s in (far[1], 1))
+    early_q = hold([to_block(sent[far[0], q], far[0]), near_q], [*own_kv_x, *first_x, *near_x], EFFORT_QUERIES)
+    second_q = to_block(hold([sent[far[1], q]], far_kv[1:])[0], far[1])
 
     holders = [near_kv, own_kv, *far_kv, *own_kv_x, *first_x, *near_x, *second_x]
     keys = [(at, None) for at in range(len(holders))]
@@ -239,9 +239,10 @@
             name="attend",
         )(*holders, *query_arrays)
 
-    mixed = dict(zip((0, far[0]), attend([own_q, first_q], [(0, None), (1, None)])))
-    last_q = hold([second_q, near_q], [mixed[0]])
-    mixed.update(zip((far[1], 1), attend(last_q, [(0, None), (1, None)])))
+    places = [(at, None) for at in range(3)]
+    mixed = dict(zip((0, far[0], 1), attend([own_q, *early_q], places)))
+    mixed[far[1]] = attend(hold([second_q], [mixed[0]]), places[:1])[0]
+    mixed[1] = hold([mixed[1]], [mixed[far[1]]])[0]
     back = {s: to_block(mixed[s], s) for s in far + [1]}
     early = far[:-1]
     back.update(zip(early, hold([back[s] for s in early], effort=EFFORT_BACK)))

time: 32.1 us -> 32.4 us (level)
  waiting for transfers between devices: 7.63 us -> 8.85 us
  starting transfers between devices: 21.3 us -> 20.3 us
    ppermute x4, waiting for transfers between devices: 0.01 us -> 3.19 us  [to_column(): lax.ppermute(array, 'uly', [(i, (i + t) % columns_of) for i in range(colu...]
    ppermute x9, waiting for transfers between devices: 7.62 us -> 5.66 us  [to_block(): return lax.ppermute(array, 'blk', [(i, i ^ s) for i in range(blocks)])]
    ppermute x9, starting transfers between devices: 16.3 us -> 15 us  [to_block(): return lax.ppermute(array, 'blk', [(i, i ^ s) for i in range(blocks)])]
  transfers between devices with their start and end apart: 13 -> 13, of which waited for: 5 -> 5; matrix products, arithmetic and copies ran while one was open for 0% -> 0% of each run, Pallas kernels for 3% -> 4%
where the time goes in v19:
time: 32.4 us; the launch traced here: 32.2 us
  starting transfers between devices  20.3 us (63%)
  waiting for transfers between devices  8.85 us (27%)
  Pallas kernels  3 us (9%)
    ppermute x9, starting transfers between devices, to_block(): return lax.ppermute(array, 'blk', [(i, i ^ s) for i in range(blocks)])  15 us
    ppermute x9, waiting for transfers between devices, to_block(): return lax.ppermute(array, 'blk', [(i, i ^ s) for i in range(blocks)])  5.66 us
    ppermute x4, starting transfers between devices, to_column(): lax.ppermute(array, 'uly', [(i, (i + t) % columns_of) for i in range(colu...  5.3 us
    ppermute x4, waiting for transfers between devices, to_column(): lax.ppermute(array, 'uly', [(i, (i + t) % columns_of) for i in range(colu...  3.19 us
    pallas_call x1, Pallas kernels, local_blocks(): pl.pallas_call(functools.partial(pack_kernel, messages, part), out_shape=...  1.17 us
    pallas_call x2, Pallas kernels, attend(): pl.pallas_call(functools.partial(attend_kernel, len(holders), keys, query...  1.13 us
    pallas_call x1, Pallas kernels, local_blocks(): pl.pallas_call(functools.partial(unpack_kernel, order, part), out_shape=j...  0.7 us
  transfers between devices with their start and end apart: 13, of which 5 were waited for; matrix products, arithmetic and copies ran while one was open for 0% of the time, Pallas kernels for 4%

profile of v19, /device:TPU:0, one launch (start us, length us, event | category | flops | bytes accessed | tf_op | source)
XLA Modules:
  0.0 32.2 jit_solution(14842198134804009438)
XLA Ops:
  0.0 1.2 %pack.1 = (bf16[64,768]{1,0:T(8,128)(2,1)S(1)}, bf16[64,768]{1,0:T(8,128)(2,1)S(1)}, bf16[64,768]{1,0:T(8,128)(2,1)S(1)}, bf16[64,768]{1,0:T(8,128)(2,1)S(1)}, b...) custom-call(bf16[1,64,1536]{2,1,0:T(8,128)(2,1)} %q_ref.1, ...), custom_call_target="tpu_custom_call" | custom-call | bytes 1179648 | tf_op jit(solution)/shard_map/pack/pallas_call | solution.py:185
  1.2 5.1 %collective-permute-start.1 = (bf16[64,768]{1,0:T(8,128)(2,1)S(1)}, bf16[64,768]{1,0:T(8,128)(2,1)S(1)}, u32[]{:S(2)}, u32[]{:S(2)}) collective-permute-start(bf16[64,768]{1,0:T(8,128)(2,1)S(1)} %get-tuple-element.19), channel_id=1, source_target_pairs={{0,12},{4,8},{8,4},{12,0},{1,13},{5,9},{9,5},{13,1},{2,14},{6,10},... | collective-permute-start | bytes 294920 | tf_op jit(solution)/shard_map/ppermute | solution.py:202
  6.3 0.0 collective-permute-start
  6.3 0.6 %collective-permute-start.3 = (bf16[64,768]{1,0:T(8,128)(2,1)S(1)}, bf16[64,768]{1,0:T(8,128)(2,1)S(1)}, u32[]{:S(2)}, u32[]{:S(2)}) collective-permute-start(bf16[64,768]{1,0:T(8,128)(2,1)S(1)} %get-tuple-element.22), channel_id=1, source_target_pairs={{0,8},{4,12},{8,0},{12,4},{1,9},{5,13},{9,1},{13,5},{2,10},{6,14},... | collective-permute-start | bytes 294920 | tf_op jit(solution)/shard_map/ppermute | solution.py:202
  6.9 1.4 %collective-permute-start.2 = (bf16[64,384]{1,0:T(8,128)(2,1)S(1)}, bf16[64,384]{1,0:T(8,128)(2,1)S(1)}, u32[]{:S(2)}, u32[]{:S(2)}) collective-permute-start(bf16[64,384]{1,0:T(8,128)(2,1)S(1)} %get-tuple-element.20), channel_id=1, source_target_pairs={{0,4},{4,0},{8,12},{12,8},{1,5},{5,1},{9,13},{13,9},{2,6},{6,2},{1... | collective-permute-start | bytes 147464 | tf_op jit(solution)/shard_map/ppermute | solution.py:202
  8.3 2.4 %collective-permute-start.8 = (bf16[64,384]{1,0:T(8,128)(2,1)S(1)}, bf16[64,384]{1,0:T(8,128)(2,1)S(1)}, u32[]{:S(2)}, u32[]{:S(2)}) collective-permute-start(bf16[64,384]{1,0:T(8,128)(2,1)S(1)} %get-tuple-element.24), channel_id=1, source_target_pairs={{0,12},{4,8},{8,4},{12,0},{1,13},{5,9},{9,5},{13,1},{2,14},{6,10},... | collective-permute-start | bytes 147464 | tf_op jit(solution)/shard_map/ppermute | solution.py:202
  10.7 0.0 collective-permute-done.1.refs_0_
  10.7 1.5 %collective-permute-start.4 = (bf16[64,768]{1,0:T(8,128)(2,1)S(1)}, bf16[64,768]{1,0:T(8,128)(2,1)S(1)}, u32[]{:S(2)}, u32[]{:S(2)}) collective-permute-start(bf16[64,768]{1,0:T(8,128)(2,1)S(1)} %get-tuple-element.21.refs_1_), channel_id=1, source_target_pairs={{0,2},{2,0},{1,3},{3,1},{4,6},{6,4},{5,7},{7,5},{8,10},{10,8},{9,1... | collective-permute-start | bytes 294920 | tf_op jit(solution)/shard_map/ppermute | solution.py:205
  12.2 2.0 %collective-permute-done.2.refs_2_.refs_1_ = bf16[64,384]{1,0:T(8,128)(2,1)S(1)} collective-permute-done((bf16[64,384]{1,0:T(8,128)(2,1)S(1)}, bf16[64,384]{1,0:T(8,128)(2,1)S(1)}, u32[]{:S(2)}, u32[]{:S(2)}) %collective-permute-start.2) | collective-permute-done | bytes 49184 | tf_op jit(solution)/shard_map/ppermute | solution.py:202
  14.2 1.8 %collective-permute-start.5 = (bf16[64,768]{1,0:T(8,128)(2,1)S(1)}, bf16[64,768]{1,0:T(8,128)(2,1)S(1)}, u32[]{:S(2)}, u32[]{:S(2)}) collective-permute-start(bf16[64,768]{1,0:T(8,128)(2,1)S(1)} %hold.9.refs_1_.refs_2_), channel_id=1, source_target_pairs={{0,2},{2,0},{1,3},{3,1},{4,6},{6,4},{5,7},{7,5},{8,10},{10,8},{9,1... | collective-permute-start | bytes 294920 | tf_op jit(solution)/shard_map/ppermute | solution.py:205
  16.0 0.0 collective-permute-done.refs_0_
  16.0 0.3 collective-permute-start.6
  16.3 0.0 collective-permute-done.3.refs_0_
  16.3 1.8 %collective-permute-start.7 = (bf16[64,768]{1,0:T(8,128)(2,1)S(1)}, bf16[64,768]{1,0:T(8,128)(2,1)S(1)}, u32[]{:S(2)}, u32[]{:S(2)}) collective-permute-start(bf16[64,768]{1,0:T(8,128)(2,1)S(1)} %hold.11.refs_3_.refs_1_), channel_id=1, source_target_pairs={{0,2},{2,0},{1,3},{3,1},{4,6},{6,4},{5,7},{7,5},{8,10},{10,8},{9,1... | collective-permute-start | bytes 294920 | tf_op jit(solution)/shard_map/ppermute | solution.py:205
  18.0 0.0 collective-permute-done.4.refs_0_
  18.0 1.0 %collective-permute-start.10 = (bf16[64,384]{1,0:T(8,128)(2,1)S(1)}, bf16[64,384]{1,0:T(8,128)(2,1)S(1)}, u32[]{:S(2)}, u32[]{:S(2)}) collective-permute-start(bf16[64,384]{1,0:T(8,128)(2,1)S(1)} %hold.15), channel_id=1, source_target_pairs={{0,8},{4,12},{8,0},{12,4},{1,9},{5,13},{9,1},{13,5},{2,10},{6,14},... | collective-permute-start | bytes 147464 | tf_op jit(solution)/shard_map/ppermute | solution.py:202
  19.0 0.0 collective-permute-done.8.refs_0_
  19.0 2.1 %collective-permute-done.6.refs_4_.refs_6_ = bf16[64,768]{1,0:T(8,128)(2,1)S(1)} collective-permute-done((bf16[64,768]{1,0:T(8,128)(2,1)S(1)}, bf16[64,768]{1,0:T(8,128)(2,1)S(1)}, u32[]{:S(2)}, u32[]{:S(2)}) %collective-permute-start.6) | collective-permute-done | bytes 98336 | tf_op jit(solution)/shard_map/ppermute | solution.py:205
  21.2 0.0 collective-permute-done.5.refs_3_.refs_5_
  21.2 1.0 %collective-permute-done.7.refs_7_ = bf16[64,768]{1,0:T(8,128)(2,1)S(1)} collective-permute-done((bf16[64,768]{1,0:T(8,128)(2,1)S(1)}, bf16[64,768]{1,0:T(8,128)(2,1)S(1)}, u32[]{:S(2)}, u32[]{:S(2)}) %collective-permute-start.7) | collective-permute-done | bytes 98336 | tf_op jit(solution)/shard_map/ppermute | solution.py:205
  22.2 0.6 %attend.2 = (bf16[64,384]{1,0:T(8,128)(2,1)S(1)}, bf16[64,384]{1,0:T(8,128)(2,1)S(1)}, bf16[64,384]{1,0:T(8,128)(2,1)S(1)}) custom-call(bf16[64,768]{1,0:T(8,128)(2,1)S(1)} %hold.10.refs_0_, bf16[64,768]{1,0:T(8,128)(2,1)S(1)} %get-tuple-element.21.refs_1_, bf16[64,768]{1,0:T(8,128)(2,1)S(1)} %hold.9.refs_1_.refs_2_, ...), custom_call_target="tpu_custom_call" | custom-call | flops 150994944 | bytes 1081344 | tf_op jit(solution)/shard_map/attend/pallas_call | solution.py:228
  22.9 2.8 %collective-permute-start.9 = (bf16[64,384]{1,0:T(8,128)(2,1)S(1)}, bf16[64,384]{1,0:T(8,128)(2,1)S(1)}, u32[]{:S(2)}, u32[]{:S(2)}) collective-permute-start(bf16[64,384]{1,0:T(8,128)(2,1)S(1)} %get-tuple-element.28), channel_id=1, source_target_pairs={{0,12},{4,8},{8,4},{12,0},{1,13},{5,9},{9,5},{13,1},{2,14},{6,10},... | collective-permute-start | bytes 147464 | tf_op jit(solution)/shard_map/ppermute | solution.py:202
  25.7 0.0 collective-permute-done.10.refs_0_
  25.7 0.5 %attend.3.refs_1_ = bf16[64,384]{1,0:T(8,128)(2,1)S(1)} custom-call(bf16[64,768]{1,0:T(8,128)(2,1)S(1)} %hold.10.refs_0_, bf16[64,768]{1,0:T(8,128)(2,1)S(1)} %get-tuple-element.21.refs_1_, bf16[64,768]{1,0:T(8,128)(2,1)S(1)} %hold.9.refs_1_.refs_2_, bf16[64,768]{1,0:T(8,128)(2,1)S(1)} %hold.11.refs_3_.refs_1_, bf16[64,768]{1,0:T(8,128)(2,1)S(1)} %hold.12.refs_2_.refs_4_, ...), custom_call_target="tpu_custom_call" | custom-call | flops 50331648 | bytes 884736 | tf_op jit(solution)/shard_map/attend/pallas_call | solution.py:228
  26.2 0.7 %collective-permute-start.11 = (bf16[64,384]{1,0:T(8,128)(2,1)S(1)}, bf16[64,384]{1,0:T(8,128)(2,1)S(1)}, u32[]{:S(2)}, u32[]{:S(2)}) collective-permute-start(bf16[64,384]{1,0:T(8,128)(2,1)S(1)} %attend.3.refs_1_), channel_id=1, source_target_pairs={{0,8},{4,12},{8,0},{12,4},{1,9},{5,13},{9,1},{13,5},{2,10},{6,14},... | collective-permute-start | bytes 147464 | tf_op jit(solution)/shard_map/ppermute | solution.py:202
  26.9 1.0 %collective-permute-start.12 = (bf16[64,384]{1,0:T(8,128)(2,1)S(1)}, bf16[64,384]{1,0:T(8,128)(2,1)S(1)}, u32[]{:S(2)}, u32[]{:S(2)}) collective-permute-start(bf16[64,384]{1,0:T(8,128)(2,1)S(1)} %hold.17), channel_id=1, source_target_pairs={{0,4},{4,0},{8,12},{12,8},{1,5},{5,1},{9,13},{13,9},{2,6},{6,2},{1... | collective-permute-start | bytes 147464 | tf_op jit(solution)/shard_map/ppermute | solution.py:202
  27.9 1.1 %collective-permute-done.9.refs_0_ = bf16[64,384]{1,0:T(8,128)(2,1)S(1)} collective-permute-done((bf16[64,384]{1,0:T(8,128)(2,1)S(1)}, bf16[64,384]{1,0:T(8,128)(2,1)S(1)}, u32[]{:S(2)}, u32[]{:S(2)}) %collective-permute-start.9) | collective-permute-done | bytes 49184 | tf_op jit(solution)/shard_map/ppermute | solution.py:202
  28.9 2.6 %collective-permute-done.12.refs_3_ = bf16[64,384]{1,0:T(8,128)(2,1)S(1)} collective-permute-done((bf16[64,384]{1,0:T(8,128)(2,1)S(1)}, bf16[64,384]{1,0:T(8,128)(2,1)S(1)}, u32[]{:S(2)}, u32[]{:S(2)}) %collective-permute-start.12) | collective-permute-done | bytes 49184 | tf_op jit(solution)/shard_map/ppermute | solution.py:202
  31.5 0.0 collective-permute-done.11.refs_2_
  31.5 0.7 %unpack.1 = bf16[1,64,1536]{2,1,0:T(8,128)(2,1)} custom-call(bf16[64,384]{1,0:T(8,128)(2,1)S(1)} %get-tuple-element.27.refs_1_.refs_0_, bf16[64,384]{1,0:T(8,128)(2,1)S(1)} %hold.14.refs_1_, bf16[64,384]{1,0:T(8,128)(2,1)S(1)} %collective-permute-done.11.refs_2_, bf16[64,384]{1,0:T(8,128)(2,1)S(1)} %collective-permute-done.12.refs_3_), custom_call_target="tpu_custom_call" | custom-call | bytes 393216 | tf_op jit(solution)/shard_map/unpack/pallas_call | solution.py:252
  (9 shorter events, 0.0 us)
Async XLA Ops:
  1.2 9.5 %collective-permute-start.1 = (bf16[64,768]{1,0:T(8,128)(2,1)S(1)}, bf16[64,768]{1,0:T(8,128)(2,1)S(1)}, u32[]{:S(2)}, u32[]{:S(2)}) collective-permute-start(bf16[64,768]{1,0:T(8,128)(2,1)S(1)} %get-tuple-element.19), channel_id=1, source_target_pairs={{0,12},{4,8},{8,4},{12,0},{1,13},{5,9},{9,5},{13,1},{2,14},{6,10},... | collective-permute-start | bytes 294920 | tf_op jit(solution)/shard_map/ppermute | solution.py:202
  6.3 9.7 %collective-permute-start = (bf16[64,768]{1,0:T(8,128)(2,1)S(1)}, bf16[64,768]{1,0:T(8,128)(2,1)S(1)}, u32[]{:S(2)}, u32[]{:S(2)}) collective-permute-start(bf16[64,768]{1,0:T(8,128)(2,1)S(1)} %get-tuple-element.18), channel_id=1, source_target_pairs={{0,4},{4,0},{8,12},{12,8},{1,5},{5,1},{9,13},{13,9},{2,6},{6,2},{1... | collective-permute-start | bytes 294920 | tf_op jit(solution)/shard_map/ppermute | solution.py:202
  6.3 10.0 %collective-permute-start.3 = (bf16[64,768]{1,0:T(8,128)(2,1)S(1)}, bf16[64,768]{1,0:T(8,128)(2,1)S(1)}, u32[]{:S(2)}, u32[]{:S(2)}) collective-permute-start(bf16[64,768]{1,0:T(8,128)(2,1)S(1)} %get-tuple-element.22), channel_id=1, source_target_pairs={{0,8},{4,12},{8,0},{12,4},{1,9},{5,13},{9,1},{13,5},{2,10},{6,14},... | collective-permute-start | bytes 294920 | tf_op jit(solution)/shard_map/ppermute | solution.py:202
  6.9 7.3 %collective-permute-start.2 = (bf16[64,384]{1,0:T(8,128)(2,1)S(1)}, bf16[64,384]{1,0:T(8,128)(2,1)S(1)}, u32[]{:S(2)}, u32[]{:S(2)}) collective-permute-start(bf16[64,384]{1,0:T(8,128)(2,1)S(1)} %get-tuple-element.20), channel_id=1, source_target_pairs={{0,4},{4,0},{8,12},{12,8},{1,5},{5,1},{9,13},{13,9},{2,6},{6,2},{1... | collective-permute-start | bytes 147464 | tf_op jit(solution)/shard_map/ppermute | solution.py:202
  8.3 10.7 %collective-permute-start.8 = (bf16[64,384]{1,0:T(8,128)(2,1)S(1)}, bf16[64,384]{1,0:T(8,128)(2,1)S(1)}, u32[]{:S(2)}, u32[]{:S(2)}) collective-permute-start(bf16[64,384]{1,0:T(8,128)(2,1)S(1)} %get-tuple-element.24), channel_id=1, source_target_pairs={{0,12},{4,8},{8,4},{12,0},{1,13},{5,9},{9,5},{13,1},{2,14},{6,10},... | collective-permute-start | bytes 147464 | tf_op jit(solution)/shard_map/ppermute | solution.py:202
  10.7 7.3 %collective-permute-start.4 = (bf16[64,768]{1,0:T(8,128)(2,1)S(1)}, bf16[64,768]{1,0:T(8,128)(2,1)S(1)}, u32[]{:S(2)}, u32[]{:S(2)}) collective-permute-start(bf16[64,768]{1,0:T(8,128)(2,1)S(1)} %get-tuple-element.21.refs_1_), channel_id=1, source_target_pairs={{0,2},{2,0},{1,3},{3,1},{4,6},{6,4},{5,7},{7,5},{8,10},{10,8},{9,1... | collective-permute-start | bytes 294920 | tf_op jit(solution)/shard_map/ppermute | solution.py:205
  14.2 7.0 %collective-permute-start.5 = (bf16[64,768]{1,0:T(8,128)(2,1)S(1)}, bf16[64,768]{1,0:T(8,128)(2,1)S(1)}, u32[]{:S(2)}, u32[]{:S(2)}) collective-permute-start(bf16[64,768]{1,0:T(8,128)(2,1)S(1)} %hold.9.refs_1_.refs_2_), channel_id=1, source_target_pairs={{0,2},{2,0},{1,3},{3,1},{4,6},{6,4},{5,7},{7,5},{8,10},{10,8},{9,1... | collective-permute-start | bytes 294920 | tf_op jit(solution)/shard_map/ppermute | solution.py:205
  16.0 5.2 %collective-permute-start.6 = (bf16[64,768]{1,0:T(8,128)(2,1)S(1)}, bf16[64,768]{1,0:T(8,128)(2,1)S(1)}, u32[]{:S(2)}, u32[]{:S(2)}) collective-permute-start(bf16[64,768]{1,0:T(8,128)(2,1)S(1)} %hold.10.refs_0_), channel_id=1, source_target_pairs={{0,2},{2,0},{1,3},{3,1},{4,6},{6,4},{5,7},{7,5},{8,10},{10,8},{9,1... | collective-permute-start | bytes 294920 | tf_op jit(solution)/shard_map/ppermute | solution.py:205
  16.3 6.0 %collective-permute-start.7 = (bf16[64,768]{1,0:T(8,128)(2,1)S(1)}, bf16[64,768]{1,0:T(8,128)(2,1)S(1)}, u32[]{:S(2)}, u32[]{:S(2)}) collective-permute-start(bf16[64,768]{1,0:T(8,128)(2,1)S(1)} %hold.11.refs_3_.refs_1_), channel_id=1, source_target_pairs={{0,2},{2,0},{1,3},{3,1},{4,6},{6,4},{5,7},{7,5},{8,10},{10,8},{9,1... | collective-permute-start | bytes 294920 | tf_op jit(solution)/shard_map/ppermute | solution.py:205
  18.0 7.7 %collective-permute-start.10 = (bf16[64,384]{1,0:T(8,128)(2,1)S(1)}, bf16[64,384]{1,0:T(8,128)(2,1)S(1)}, u32[]{:S(2)}, u32[]{:S(2)}) collective-permute-start(bf16[64,384]{1,0:T(8,128)(2,1)S(1)} %hold.15), channel_id=1, source_target_pairs={{0,8},{4,12},{8,0},{12,4},{1,9},{5,13},{9,1},{13,5},{2,10},{6,14},... | collective-permute-start | bytes 147464 | tf_op jit(solution)/shard_map/ppermute | solution.py:202
  22.9 6.1 %collective-permute-start.9 = (bf16[64,384]{1,0:T(8,128)(2,1)S(1)}, bf16[64,384]{1,0:T(8,128)(2,1)S(1)}, u32[]{:S(2)}, u32[]{:S(2)}) collective-permute-start(bf16[64,384]{1,0:T(8,128)(2,1)S(1)} %get-tuple-element.28), channel_id=1, source_target_pairs={{0,12},{4,8},{8,4},{12,0},{1,13},{5,9},{9,5},{13,1},{2,14},{6,10},... | collective-permute-start | bytes 147464 | tf_op jit(solution)/shard_map/ppermute | solution.py:202
  26.2 5.3 %collective-permute-start.11 = (bf16[64,384]{1,0:T(8,128)(2,1)S(1)}, bf16[64,384]{1,0:T(8,128)(2,1)S(1)}, u32[]{:S(2)}, u32[]{:S(2)}) collective-permute-start(bf16[64,384]{1,0:T(8,128)(2,1)S(1)} %attend.3.refs_1_), channel_id=1, source_target_pairs={{0,8},{4,12},{8,0},{12,4},{1,9},{5,13},{9,1},{13,5},{2,10},{6,14},... | collective-permute-start | bytes 147464 | tf_op jit(solution)/shard_map/ppermute | solution.py:202
  26.9 4.6 %collective-permute-start.12 = (bf16[64,384]{1,0:T(8,128)(2,1)S(1)}, bf16[64,384]{1,0:T(8,128)(2,1)S(1)}, u32[]{:S(2)}, u32[]{:S(2)}) collective-permute-start(bf16[64,384]{1,0:T(8,128)(2,1)S(1)} %hold.17), channel_id=1, source_target_pairs={{0,4},{4,0},{8,12},{12,8},{1,5},{5,1},{9,13},{13,9},{2,6},{6,2},{1... | collective-permute-start | bytes 147464 | tf_op jit(solution)/shard_map/ppermute | solution.py:202

commit v20 on v13

--- a/solution.py
+++ b/solution.py
@@ -265,7 +265,7 @@
     mixed[1] = hold([mixed[1]], [mixed[far[-1]]])[0]
     back = {s: to_block(mixed[s], s) for s in far + [1]}
     early = far[:-1]
-    back.update(zip(early, hold([back[s] for s in early], effort=EFFORT)))
+    back.update(zip(early, hold([back[s] for s in early])))
     back[0] = mixed[0]
     order = [0] + far + [1]
     back = [back[s] for s in order]

time: 30.5 us -> 30 us (0.984)
  waiting for transfers between devices: 6.15 us -> 5.66 us
    ppermute x8, waiting for transfers between devices: 4.29 us -> 3.79 us  [to_block(): return lax.ppermute(array, 'blk', [(i, i ^ s) for i in range(blocks)])]
  transfers between devices with their start and end apart: 12 -> 12, of which waited for: 5 -> 6; matrix products, arithmetic and copies ran while one was open for 0% -> 0% of each run, Pallas kernels for 4% -> 4%
where the time goes in v20:
time: 30 us; the launch traced here: 29.8 us
  starting transfers between devices  21.1 us (70%)
  waiting for transfers between devices  5.66 us (19%)
  Pallas kernels  3.03 us (10%)
    ppermute x8, starting transfers between devices, to_block(): return lax.ppermute(array, 'blk', [(i, i ^ s) for i in range(blocks)])  15.7 us
    ppermute x4, starting transfers between devices, to_column(): lax.ppermute(array, 'uly', [(i, (i + t) % columns_of) for i in range(colu...  5.41 us
    ppermute x8, waiting for transfers between devices, to_block(): return lax.ppermute(array, 'blk', [(i, i ^ s) for i in range(blocks)])  3.79 us
    ppermute x4, waiting for transfers between devices, to_column(): lax.ppermute(array, 'uly', [(i, (i + t) % columns_of) for i in range(colu...  1.87 us
    pallas_call x1, Pallas kernels, local_blocks(): pl.pallas_call(functools.partial(pack_kernel, messages, part), out_shape=...  1.17 us
    pallas_call x2, Pallas kernels, attend(): pl.pallas_call(functools.partial(attend_kernel, len(holders), keys, query...  1.13 us
    pallas_call x1, Pallas kernels, local_blocks(): pl.pallas_call(functools.partial(unpack_kernel, order, part), out_shape=j...  0.7 us
  transfers between devices with their start and end apart: 12, of which 6 were waited for; matrix products, arithmetic and copies ran while one was open for 0% of the time, Pallas kernels for 4%

profile of v20, /device:TPU:0, one launch (start us, length us, event | category | flops | bytes accessed | tf_op | source)
XLA Modules:
  0.0 29.8 jit_solution(7470409626603563639)
XLA Ops:
  0.0 1.2 %pack.1 = (bf16[64,768]{1,0:T(8,128)(2,1)S(1)}, bf16[64,768]{1,0:T(8,128)(2,1)S(1)}, bf16[64,1152]{1,0:T(8,128)(2,1)S(1)}, bf16[64,384]{1,0:T(8,128)(2,1)S(1)}, ...) custom-call(bf16[1,64,1536]{2,1,0:T(8,128)(2,1)} %q_ref.1, ...), custom_call_target="tpu_custom_call" | custom-call | bytes 1179648 | tf_op jit(solution)/shard_map/pack/pallas_call | solution.py:205
  1.2 5.1 %collective-permute-start.1 = (bf16[64,768]{1,0:T(8,128)(2,1)S(1)}, bf16[64,768]{1,0:T(8,128)(2,1)S(1)}, u32[]{:S(2)}, u32[]{:S(2)}) collective-permute-start(bf16[64,768]{1,0:T(8,128)(2,1)S(1)} %get-tuple-element.17), channel_id=1, source_target_pairs={{0,12},{4,8},{8,4},{12,0},{1,13},{5,9},{9,5},{13,1},{2,14},{6,10},... | collective-permute-start | bytes 294920 | tf_op jit(solution)/shard_map/ppermute | solution.py:222
  6.3 0.0 collective-permute-start
  6.3 0.6 %collective-permute-start.2 = (bf16[64,768]{1,0:T(8,128)(2,1)S(1)}, bf16[64,768]{1,0:T(8,128)(2,1)S(1)}, u32[]{:S(2)}, u32[]{:S(2)}) collective-permute-start(bf16[64,768]{1,0:T(8,128)(2,1)S(1)} %get-tuple-element.18), channel_id=1, source_target_pairs={{0,8},{4,12},{8,0},{12,4},{1,9},{5,13},{9,1},{13,5},{2,10},{6,14},... | collective-permute-start | bytes 294920 | tf_op jit(solution)/shard_map/ppermute | solution.py:222
  6.9 1.6 %collective-permute-start.3 = (bf16[64,768]{1,0:T(8,128)(2,1)S(1)}, bf16[64,768]{1,0:T(8,128)(2,1)S(1)}, u32[]{:S(2)}, u32[]{:S(2)}) collective-permute-start(bf16[64,768]{1,0:T(8,128)(2,1)S(1)} %get-tuple-element.16.refs_1_), channel_id=1, source_target_pairs={{0,2},{2,0},{1,3},{3,1},{4,6},{6,4},{5,7},{7,5},{8,10},{10,8},{9,1... | collective-permute-start | bytes 294920 | tf_op jit(solution)/shard_map/ppermute | solution.py:225
  8.6 1.4 %collective-permute-done.1.refs_0_ = bf16[64,768]{1,0:T(8,128)(2,1)S(1)} collective-permute-done((bf16[64,768]{1,0:T(8,128)(2,1)S(1)}, bf16[64,768]{1,0:T(8,128)(2,1)S(1)}, u32[]{:S(2)}, u32[]{:S(2)}) %collective-permute-start.1) | collective-permute-done | bytes 98336 | tf_op jit(solution)/shard_map/ppermute | solution.py:222
  10.0 1.7 %collective-permute-start.4 = (bf16[64,768]{1,0:T(8,128)(2,1)S(1)}, bf16[64,768]{1,0:T(8,128)(2,1)S(1)}, u32[]{:S(2)}, u32[]{:S(2)}) collective-permute-start(bf16[64,768]{1,0:T(8,128)(2,1)S(1)} %hold.8.refs_1_.refs_2_), channel_id=1, source_target_pairs={{0,2},{2,0},{1,3},{3,1},{4,6},{6,4},{5,7},{7,5},{8,10},{10,8},{9,1... | collective-permute-start | bytes 294920 | tf_op jit(solution)/shard_map/ppermute | solution.py:225
  11.7 3.7 %collective-permute-start.7 = (bf16[64,384]{1,0:T(8,128)(2,1)S(1)}, bf16[64,384]{1,0:T(8,128)(2,1)S(1)}, u32[]{:S(2)}, u32[]{:S(2)}) collective-permute-start(bf16[64,384]{1,0:T(8,128)(2,1)S(1)} %hold.11), channel_id=1, source_target_pairs={{0,12},{4,8},{8,4},{12,0},{1,13},{5,9},{9,5},{13,1},{2,14},{6,10},... | collective-permute-start | bytes 147464 | tf_op jit(solution)/shard_map/ppermute | solution.py:222
  15.3 0.0 collective-permute-done.refs_0_.refs_1_
  15.3 1.0 %collective-permute-start.5 = (bf16[64,768]{1,0:T(8,128)(2,1)S(1)}, bf16[64,768]{1,0:T(8,128)(2,1)S(1)}, u32[]{:S(2)}, u32[]{:S(2)}) collective-permute-start(bf16[64,768]{1,0:T(8,128)(2,1)S(1)} %bitcast.1), channel_id=1, source_target_pairs={{0,2},{2,0},{1,3},{3,1},{4,6},{6,4},{5,7},{7,5},{8,10},{10,8},{9,1... | collective-permute-start | bytes 294920 | tf_op jit(solution)/shard_map/ppermute | solution.py:225
  16.4 0.0 collective-permute-done.2.refs_0_
  16.4 1.1 %collective-permute-start.6 = (bf16[64,768]{1,0:T(8,128)(2,1)S(1)}, bf16[64,768]{1,0:T(8,128)(2,1)S(1)}, u32[]{:S(2)}, u32[]{:S(2)}) collective-permute-start(bf16[64,768]{1,0:T(8,128)(2,1)S(1)} %hold.9.refs_3_.refs_1_), channel_id=1, source_target_pairs={{0,2},{2,0},{1,3},{3,1},{4,6},{6,4},{5,7},{7,5},{8,10},{10,8},{9,1... | collective-permute-start | bytes 294920 | tf_op jit(solution)/shard_map/ppermute | solution.py:225
  17.4 0.0 collective-permute-done.3.refs_0_
  17.4 1.7 %collective-permute-start.9 = (bf16[64,384]{1,0:T(8,128)(2,1)S(1)}, bf16[64,384]{1,0:T(8,128)(2,1)S(1)}, u32[]{:S(2)}, u32[]{:S(2)}) collective-permute-start(bf16[64,384]{1,0:T(8,128)(2,1)S(1)} %hold.13), channel_id=1, source_target_pairs={{0,8},{4,12},{8,0},{12,4},{1,9},{5,13},{9,1},{13,5},{2,10},{6,14},... | collective-permute-start | bytes 147464 | tf_op jit(solution)/shard_map/ppermute | solution.py:222
  19.2 0.0 collective-permute-done.7.refs_0_
  19.2 0.0 collective-permute-done.4.refs_2_.refs_5_
  19.2 0.8 %collective-permute-done.5.refs_3_.refs_6_ = bf16[64,768]{1,0:T(8,128)(2,1)S(1)} collective-permute-done((bf16[64,768]{1,0:T(8,128)(2,1)S(1)}, bf16[64,768]{1,0:T(8,128)(2,1)S(1)}, u32[]{:S(2)}, u32[]{:S(2)}) %collective-permute-start.5) | collective-permute-done | bytes 98336 | tf_op jit(solution)/shard_map/ppermute | solution.py:225
  20.0 1.0 %collective-permute-done.6.refs_7_ = bf16[64,768]{1,0:T(8,128)(2,1)S(1)} collective-permute-done((bf16[64,768]{1,0:T(8,128)(2,1)S(1)}, bf16[64,768]{1,0:T(8,128)(2,1)S(1)}, u32[]{:S(2)}, u32[]{:S(2)}) %collective-permute-start.6) | collective-permute-done | bytes 98336 | tf_op jit(solution)/shard_map/ppermute | solution.py:225
  21.1 0.6 %attend.2 = (bf16[64,384]{1,0:T(8,128)(2,1)S(1)}, bf16[64,384]{1,0:T(8,128)(2,1)S(1)}, bf16[64,384]{1,0:T(8,128)(2,1)S(1)}) custom-call(bf16[64,1152]{1,0:T(8,128)(2,1)S(1)} %collective-permute-done.refs_0_.refs_1_, bf16[64,768]{1,0:T(8,128)(2,1)S(1)} %get-tuple-element.16.refs_1_, bf16[64,768]{1,0:T(8,128)(2,1)S(1)} %hold.8.refs_1_.refs_2_, ...), custom_call_target="tpu_custom_call" | custom-call | flops 150994944 | bytes 1081344 | tf_op jit(solution)/shard_map/attend/pallas_call | solution.py:248
  21.7 1.4 %collective-permute-start.8 = (bf16[64,384]{1,0:T(8,128)(2,1)S(1)}, bf16[64,384]{1,0:T(8,128)(2,1)S(1)}, u32[]{:S(2)}, u32[]{:S(2)}) collective-permute-start(bf16[64,384]{1,0:T(8,128)(2,1)S(1)} %get-tuple-element.22), channel_id=1, source_target_pairs={{0,12},{4,8},{8,4},{12,0},{1,13},{5,9},{9,5},{13,1},{2,14},{6,10},... | collective-permute-start | bytes 147464 | tf_op jit(solution)/shard_map/ppermute | solution.py:222
  23.1 0.0 collective-permute-done.9.refs_0_
  23.1 0.5 %attend.3.refs_1_ = bf16[64,384]{1,0:T(8,128)(2,1)S(1)} custom-call(bf16[64,1152]{1,0:T(8,128)(2,1)S(1)} %collective-permute-done.refs_0_.refs_1_, bf16[64,768]{1,0:T(8,128)(2,1)S(1)} %get-tuple-element.16.refs_1_, bf16[64,768]{1,0:T(8,128)(2,1)S(1)} %hold.8.refs_1_.refs_2_, bf16[64,768]{1,0:T(8,128)(2,1)S(1)} %hold.9.refs_3_.refs_1_, ...), custom_call_target="tpu_custom_call" | custom-call | flops 50331648 | bytes 884736 | tf_op jit(solution)/shard_map/attend/pallas_call | solution.py:248
  23.6 0.6 %collective-permute-start.11 = (bf16[64,384]{1,0:T(8,128)(2,1)S(1)}, bf16[64,384]{1,0:T(8,128)(2,1)S(1)}, u32[]{:S(2)}, u32[]{:S(2)}) collective-permute-start(bf16[64,384]{1,0:T(8,128)(2,1)S(1)} %hold.15), channel_id=1, source_target_pairs={{0,4},{4,0},{8,12},{12,8},{1,5},{5,1},{9,13},{13,9},{2,6},{6,2},{1... | collective-permute-start | bytes 147464 | tf_op jit(solution)/shard_map/ppermute | solution.py:222
  24.1 2.6 %collective-permute-start.10 = (bf16[64,384]{1,0:T(8,128)(2,1)S(1)}, bf16[64,384]{1,0:T(8,128)(2,1)S(1)}, u32[]{:S(2)}, u32[]{:S(2)}) collective-permute-start(bf16[64,384]{1,0:T(8,128)(2,1)S(1)} %attend.3.refs_1_), channel_id=1, source_target_pairs={{0,8},{4,12},{8,0},{12,4},{1,9},{5,13},{9,1},{13,5},{2,10},{6,14},... | collective-permute-start | bytes 147464 | tf_op jit(solution)/shard_map/ppermute | solution.py:222
  26.7 1.0 %collective-permute-done.8.refs_0_ = bf16[64,384]{1,0:T(8,128)(2,1)S(1)} collective-permute-done((bf16[64,384]{1,0:T(8,128)(2,1)S(1)}, bf16[64,384]{1,0:T(8,128)(2,1)S(1)}, u32[]{:S(2)}, u32[]{:S(2)}) %collective-permute-start.8) | collective-permute-done | bytes 49184 | tf_op jit(solution)/shard_map/ppermute | solution.py:222
  27.7 0.5 %collective-permute-done.11.refs_3_ = bf16[64,384]{1,0:T(8,128)(2,1)S(1)} collective-permute-done((bf16[64,384]{1,0:T(8,128)(2,1)S(1)}, bf16[64,384]{1,0:T(8,128)(2,1)S(1)}, u32[]{:S(2)}, u32[]{:S(2)}) %collective-permute-start.11) | collective-permute-done | bytes 49184 | tf_op jit(solution)/shard_map/ppermute | solution.py:222
  28.2 0.9 %collective-permute-done.10.refs_2_ = bf16[64,384]{1,0:T(8,128)(2,1)S(1)} collective-permute-done((bf16[64,384]{1,0:T(8,128)(2,1)S(1)}, bf16[64,384]{1,0:T(8,128)(2,1)S(1)}, u32[]{:S(2)}, u32[]{:S(2)}) %collective-permute-start.10) | collective-permute-done | bytes 49184 | tf_op jit(solution)/shard_map/ppermute | solution.py:222
  29.1 0.7 %unpack.1 = bf16[1,64,1536]{2,1,0:T(8,128)(2,1)} custom-call(bf16[64,384]{1,0:T(8,128)(2,1)S(1)} %get-tuple-element.21.refs_1_.refs_0_, bf16[64,384]{1,0:T(8,128)(2,1)S(1)} %hold.12.refs_1_, bf16[64,384]{1,0:T(8,128)(2,1)S(1)} %collective-permute-done.10.refs_2_, bf16[64,384]{1,0:T(8,128)(2,1)S(1)} %collective-permute-done.11.refs_3_), custom_call_target="tpu_custom_call" | custom-call | bytes 393216 | tf_op jit(solution)/shard_map/unpack/pallas_call | solution.py:272
  (11 shorter events, 0.0 us)
Async XLA Ops:
  1.2 8.8 %collective-permute-start.1 = (bf16[64,768]{1,0:T(8,128)(2,1)S(1)}, bf16[64,768]{1,0:T(8,128)(2,1)S(1)}, u32[]{:S(2)}, u32[]{:S(2)}) collective-permute-start(bf16[64,768]{1,0:T(8,128)(2,1)S(1)} %get-tuple-element.17), channel_id=1, source_target_pairs={{0,12},{4,8},{8,4},{12,0},{1,13},{5,9},{9,5},{13,1},{2,14},{6,10},... | collective-permute-start | bytes 294920 | tf_op jit(solution)/shard_map/ppermute | solution.py:222
  6.3 9.0 %collective-permute-start = (bf16[64,1152]{1,0:T(8,128)(2,1)S(1)}, bf16[64,1152]{1,0:T(8,128)(2,1)S(1)}, u32[]{:S(2)}, u32[]{:S(2)}) collective-permute-start(bf16[64,1152]{1,0:T(8,128)(2,1)S(1)} %get-tuple-element.15), channel_id=1, source_target_pairs={{0,4},{4,0},{8,12},{12,8},{1,5},{5,1},{9,13},{13,9},{2,6},{6,2},{1... | collective-permute-start | bytes 442376 | tf_op jit(solution)/shard_map/ppermute | solution.py:222
  6.3 10.1 %collective-permute-start.2 = (bf16[64,768]{1,0:T(8,128)(2,1)S(1)}, bf16[64,768]{1,0:T(8,128)(2,1)S(1)}, u32[]{:S(2)}, u32[]{:S(2)}) collective-permute-start(bf16[64,768]{1,0:T(8,128)(2,1)S(1)} %get-tuple-element.18), channel_id=1, source_target_pairs={{0,8},{4,12},{8,0},{12,4},{1,9},{5,13},{9,1},{13,5},{2,10},{6,14},... | collective-permute-start | bytes 294920 | tf_op jit(solution)/shard_map/ppermute | solution.py:222
  6.9 10.5 %collective-permute-start.3 = (bf16[64,768]{1,0:T(8,128)(2,1)S(1)}, bf16[64,768]{1,0:T(8,128)(2,1)S(1)}, u32[]{:S(2)}, u32[]{:S(2)}) collective-permute-start(bf16[64,768]{1,0:T(8,128)(2,1)S(1)} %get-tuple-element.16.refs_1_), channel_id=1, source_target_pairs={{0,2},{2,0},{1,3},{3,1},{4,6},{6,4},{5,7},{7,5},{8,10},{10,8},{9,1... | collective-permute-start | bytes 294920 | tf_op jit(solution)/shard_map/ppermute | solution.py:225
  10.0 9.2 %collective-permute-start.4 = (bf16[64,768]{1,0:T(8,128)(2,1)S(1)}, bf16[64,768]{1,0:T(8,128)(2,1)S(1)}, u32[]{:S(2)}, u32[]{:S(2)}) collective-permute-start(bf16[64,768]{1,0:T(8,128)(2,1)S(1)} %hold.8.refs_1_.refs_2_), channel_id=1, source_target_pairs={{0,2},{2,0},{1,3},{3,1},{4,6},{6,4},{5,7},{7,5},{8,10},{10,8},{9,1... | collective-permute-start | bytes 294920 | tf_op jit(solution)/shard_map/ppermute | solution.py:225
  11.7 7.5 %collective-permute-start.7 = (bf16[64,384]{1,0:T(8,128)(2,1)S(1)}, bf16[64,384]{1,0:T(8,128)(2,1)S(1)}, u32[]{:S(2)}, u32[]{:S(2)}) collective-permute-start(bf16[64,384]{1,0:T(8,128)(2,1)S(1)} %hold.11), channel_id=1, source_target_pairs={{0,12},{4,8},{8,4},{12,0},{1,13},{5,9},{9,5},{13,1},{2,14},{6,10},... | collective-permute-start | bytes 147464 | tf_op jit(solution)/shard_map/ppermute | solution.py:222
  15.3 4.7 %collective-permute-start.5 = (bf16[64,768]{1,0:T(8,128)(2,1)S(1)}, bf16[64,768]{1,0:T(8,128)(2,1)S(1)}, u32[]{:S(2)}, u32[]{:S(2)}) collective-permute-start(bf16[64,768]{1,0:T(8,128)(2,1)S(1)} %bitcast.1), channel_id=1, source_target_pairs={{0,2},{2,0},{1,3},{3,1},{4,6},{6,4},{5,7},{7,5},{8,10},{10,8},{9,1... | collective-permute-start | bytes 294920 | tf_op jit(solution)/shard_map/ppermute | solution.py:225
  16.4 4.7 %collective-permute-start.6 = (bf16[64,768]{1,0:T(8,128)(2,1)S(1)}, bf16[64,768]{1,0:T(8,128)(2,1)S(1)}, u32[]{:S(2)}, u32[]{:S(2)}) collective-permute-start(bf16[64,768]{1,0:T(8,128)(2,1)S(1)} %hold.9.refs_3_.refs_1_), channel_id=1, source_target_pairs={{0,2},{2,0},{1,3},{3,1},{4,6},{6,4},{5,7},{7,5},{8,10},{10,8},{9,1... | collective-permute-start | bytes 294920 | tf_op jit(solution)/shard_map/ppermute | solution.py:225
  17.4 5.6 %collective-permute-start.9 = (bf16[64,384]{1,0:T(8,128)(2,1)S(1)}, bf16[64,384]{1,0:T(8,128)(2,1)S(1)}, u32[]{:S(2)}, u32[]{:S(2)}) collective-permute-start(bf16[64,384]{1,0:T(8,128)(2,1)S(1)} %hold.13), channel_id=1, source_target_pairs={{0,8},{4,12},{8,0},{12,4},{1,9},{5,13},{9,1},{13,5},{2,10},{6,14},... | collective-permute-start | bytes 147464 | tf_op jit(solution)/shard_map/ppermute | solution.py:222
  21.7 6.0 %collective-permute-start.8 = (bf16[64,384]{1,0:T(8,128)(2,1)S(1)}, bf16[64,384]{1,0:T(8,128)(2,1)S(1)}, u32[]{:S(2)}, u32[]{:S(2)}) collective-permute-start(bf16[64,384]{1,0:T(8,128)(2,1)S(1)} %get-tuple-element.22), channel_id=1, source_target_pairs={{0,12},{4,8},{8,4},{12,0},{1,13},{5,9},{9,5},{13,1},{2,14},{6,10},... | collective-permute-start | bytes 147464 | tf_op jit(solution)/shard_map/ppermute | solution.py:222
  23.6 4.6 %collective-permute-start.11 = (bf16[64,384]{1,0:T(8,128)(2,1)S(1)}, bf16[64,384]{1,0:T(8,128)(2,1)S(1)}, u32[]{:S(2)}, u32[]{:S(2)}) collective-permute-start(bf16[64,384]{1,0:T(8,128)(2,1)S(1)} %hold.15), channel_id=1, source_target_pairs={{0,4},{4,0},{8,12},{12,8},{1,5},{5,1},{9,13},{13,9},{2,6},{6,2},{1... | collective-permute-start | bytes 147464 | tf_op jit(solution)/shard_map/ppermute | solution.py:222
  24.1 5.0 %collective-permute-start.10 = (bf16[64,384]{1,0:T(8,128)(2,1)S(1)}, bf16[64,384]{1,0:T(8,128)(2,1)S(1)}, u32[]{:S(2)}, u32[]{:S(2)}) collective-permute-start(bf16[64,384]{1,0:T(8,128)(2,1)S(1)} %attend.3.refs_1_), channel_id=1, source_target_pairs={{0,8},{4,12},{8,0},{12,4},{1,9},{5,13},{9,1},{13,5},{2,10},{6,14},... | collective-permute-start | bytes 147464 | tf_op jit(solution)/shard_map/ppermute | solution.py:222

commit v21 on v14

--- a/solution.py
+++ b/solution.py
@@ -203,21 +203,27 @@
 
     kv, q = (("k", 0, part), ("v", 0, part)), (("q", 0, part),)
     messages = [(s, kv) for s in far] + [(1, kv + q)] + [(s, q) for s in far] + [(0, kv), (0, q)]
-    packed = pl.pallas_call(
-        functools.partial(pack_kernel, messages, part),
-        out_shape=[
-            jax.ShapeDtypeStruct((tokens, sum(piece[2] for piece in pieces)), kind)
-            for s, pieces in messages
-        ],
-        in_specs=[HBM] * 3,
-        out_specs=[VMEM] * len(messages),
-        scratch_shapes=[pltpu.SemaphoreType.DMA((sum(len(m[1]) for m in messages),))],
-        compiler_params=SMALL,
-        cost_estimate=pl.CostEstimate(
-            flops=0, bytes_accessed=6 * tokens * width * 2, transcendentals=0
-        ),
-        name="pack",
-    )(*[pltpu.with_memory_space_constraint(x, pltpu.HBM) for x in (query_rows, key_rows, value_rows)])
+    inputs = [pltpu.with_memory_space_constraint(x, pltpu.HBM) for x in (query_rows, key_rows, value_rows)]
+
+    def pack(cut):
+        copies = sum(len(names) for s, names in cut)
+        size = 2 * tokens * part * copies
+        return pl.pallas_call(
+            functools.partial(pack_kernel, cut, part),
+            out_shape=[
+                jax.ShapeDtypeStruct((tokens, sum(piece[2] for piece in names)), kind)
+                for s, names in cut
+            ],
+            in_specs=[HBM] * 3,
+            out_specs=[VMEM] * len(cut),
+            scratch_shapes=[pltpu.SemaphoreType.DMA((copies,))],
+            compiler_params=SMALL,
+            cost_estimate=pl.CostEstimate(flops=0, bytes_accessed=2 * size, transcendentals=0),
+            name="pack",
+        )(*inputs)
+
+    first = len(far) + 1
+    packed = [*pack(messages[:first]), *pack(messages[first:])]
 
     def to_block(array, s):
         return lax.ppermute(array, "blk", [(i, i ^ s) for i in range(blocks)])

time: 30 us -> 30.1 us (level)
  waiting for transfers between devices: 6.12 us -> 5.32 us
  Pallas kernels: 3.02 us -> 3.79 us
    ppermute x8, waiting for transfers between devices: 4.31 us -> 2.93 us  [to_block(): return lax.ppermute(array, 'blk', [(i, i ^ s) for i in range(blocks)])]
    pallas_call x1 -> x2, Pallas kernels: 1.17 us -> 1.94 us  [pack(): pl.pallas_call(functools.partial(pack_kernel, cut, part), out_shape=[jax....]
    ppermute x4, waiting for transfers between devices: 1.81 us -> 2.39 us  [to_column(): lax.ppermute(array, 'uly', [(i, (i + t) % columns_of) for i in range(colu...]
  transfers between devices with their start and end apart: 12 -> 12, of which waited for: 6 -> 6; matrix products, arithmetic and copies ran while one was open for 0% -> 0% of each run, Pallas kernels for 4% -> 7%
where the time goes in v21:
time: 30.1 us; the launch traced here: 29.9 us
  starting transfers between devices  20.7 us (69%)
  waiting for transfers between devices  5.32 us (18%)
  Pallas kernels  3.79 us (13%)
    ppermute x8, starting transfers between devices, to_block(): return lax.ppermute(array, 'blk', [(i, i ^ s) for i in range(blocks)])  15.6 us
    ppermute x4, starting transfers between devices, to_column(): lax.ppermute(array, 'uly', [(i, (i + t) % columns_of) for i in range(colu...  5.06 us
    ppermute x8, waiting for transfers between devices, to_block(): return lax.ppermute(array, 'blk', [(i, i ^ s) for i in range(blocks)])  2.93 us
    ppermute x4, waiting for transfers between devices, to_column(): lax.ppermute(array, 'uly', [(i, (i + t) % columns_of) for i in range(colu...  2.39 us
    pallas_call x2, Pallas kernels, pack(): pl.pallas_call(functools.partial(pack_kernel, cut, part), out_shape=[jax....  1.94 us
    pallas_call x2, Pallas kernels, attend(): pl.pallas_call(functools.partial(attend_kernel, len(holders), keys, query...  1.13 us
    pallas_call x1, Pallas kernels, local_blocks(): pl.pallas_call(functools.partial(unpack_kernel, order, part), out_shape=j...  0.7 us
  transfers between devices with their start and end apart: 12, of which 6 were waited for; matrix products, arithmetic and copies ran while one was open for 0% of the time, Pallas kernels for 7%

profile of v21, /device:TPU:0, one launch (start us, length us, event | category | flops | bytes accessed | tf_op | source)
XLA Modules:
  0.0 29.9 jit_solution(13211333270532602632)
XLA Ops:
  0.0 1.0 %pack.2 = (bf16[64,768]{1,0:T(8,128)(2,1)S(1)}, bf16[64,768]{1,0:T(8,128)(2,1)S(1)}, bf16[64,1152]{1,0:T(8,128)(2,1)S(1)}) custom-call(bf16[1,64,1536]{2,1,0:T(8,128)(2,1)} %q_ref.3, bf16[1,64,1536]{2,1,0:T(8,128)(2,1)} %k_ref.3, bf16[1,64,1536]{2,1,0:T(8,128)(2,1)} %v_ref.3), custom_call_target="tpu_custom_call" | custom-call | bytes 688128 | tf_op jit(solution)/shard_map/pack/pallas_call | solution.py:211
  1.0 5.1 %collective-permute-start.1 = (bf16[64,768]{1,0:T(8,128)(2,1)S(1)}, bf16[64,768]{1,0:T(8,128)(2,1)S(1)}, u32[]{:S(2)}, u32[]{:S(2)}) collective-permute-start(bf16[64,768]{1,0:T(8,128)(2,1)S(1)} %get-tuple-element.17), channel_id=1, source_target_pairs={{0,12},{4,8},{8,4},{12,0},{1,13},{5,9},{9,5},{13,1},{2,14},{6,10},... | collective-permute-start | bytes 294920 | tf_op jit(solution)/shard_map/ppermute | solution.py:229
  6.1 0.0 collective-permute-start
  6.1 0.6 %collective-permute-start.2 = (bf16[64,768]{1,0:T(8,128)(2,1)S(1)}, bf16[64,768]{1,0:T(8,128)(2,1)S(1)}, u32[]{:S(2)}, u32[]{:S(2)}) collective-permute-start(bf16[64,768]{1,0:T(8,128)(2,1)S(1)} %get-tuple-element.18), channel_id=1, source_target_pairs={{0,8},{4,12},{8,0},{12,4},{1,9},{5,13},{9,1},{13,5},{2,10},{6,14},... | collective-permute-start | bytes 294920 | tf_op jit(solution)/shard_map/ppermute | solution.py:229
  6.8 0.9 %pack.3 = (bf16[64,384]{1,0:T(8,128)(2,1)S(1)}, bf16[64,384]{1,0:T(8,128)(2,1)S(1)}, bf16[64,768]{1,0:T(8,128)(2,1)S(1)}, bf16[64,384]{1,0:T(8,128)(2,1)S(1)}) custom-call(bf16[1,64,1536]{2,1,0:T(8,128)(2,1)} %q_ref.3, bf16[1,64,1536]{2,1,0:T(8,128)(2,1)} %k_ref.3, bf16[1,64,1536]{2,1,0:T(8,128)(2,1)} %v_ref.3), custom_call_target="tpu_custom_call" | custom-call | bytes 491520 | tf_op jit(solution)/shard_map/pack/pallas_call | solution.py:211
  7.7 3.8 %collective-permute-start.7 = (bf16[64,384]{1,0:T(8,128)(2,1)S(1)}, bf16[64,384]{1,0:T(8,128)(2,1)S(1)}, u32[]{:S(2)}, u32[]{:S(2)}) collective-permute-start(bf16[64,384]{1,0:T(8,128)(2,1)S(1)} %get-tuple-element.20), channel_id=1, source_target_pairs={{0,12},{4,8},{8,4},{12,0},{1,13},{5,9},{9,5},{13,1},{2,14},{6,10},... | collective-permute-start | bytes 147464 | tf_op jit(solution)/shard_map/ppermute | solution.py:229
  11.5 1.5 %collective-permute-start.3 = (bf16[64,768]{1,0:T(8,128)(2,1)S(1)}, bf16[64,768]{1,0:T(8,128)(2,1)S(1)}, u32[]{:S(2)}, u32[]{:S(2)}) collective-permute-start(bf16[64,768]{1,0:T(8,128)(2,1)S(1)} %get-tuple-element.16.refs_1_), channel_id=1, source_target_pairs={{0,2},{2,0},{1,3},{3,1},{4,6},{6,4},{5,7},{7,5},{8,10},{10,8},{9,1... | collective-permute-start | bytes 294920 | tf_op jit(solution)/shard_map/ppermute | solution.py:232
  13.0 0.0 collective-permute-done.1.refs_0_
  13.0 0.5 %collective-permute-start.4 = (bf16[64,768]{1,0:T(8,128)(2,1)S(1)}, bf16[64,768]{1,0:T(8,128)(2,1)S(1)}, u32[]{:S(2)}, u32[]{:S(2)}) collective-permute-start(bf16[64,768]{1,0:T(8,128)(2,1)S(1)} %hold.9.refs_2_), channel_id=1, source_target_pairs={{0,2},{2,0},{1,3},{3,1},{4,6},{6,4},{5,7},{7,5},{8,10},{10,8},{9,1... | collective-permute-start | bytes 294920 | tf_op jit(solution)/shard_map/ppermute | solution.py:232
  13.6 0.9 %collective-permute-done.refs_0_.refs_1_ = bf16[64,1152]{1,0:T(8,128)(2,1)S(1)} collective-permute-done((bf16[64,1152]{1,0:T(8,128)(2,1)S(1)}, bf16[64,1152]{1,0:T(8,128)(2,1)S(1)}, u32[]{:S(2)}, u32[]{:S(2)}) %collective-permute-start) | collective-permute-done | bytes 147488 | tf_op jit(solution)/shard_map/ppermute | solution.py:229
  14.4 1.8 %collective-permute-start.5 = (bf16[64,768]{1,0:T(8,128)(2,1)S(1)}, bf16[64,768]{1,0:T(8,128)(2,1)S(1)}, u32[]{:S(2)}, u32[]{:S(2)}) collective-permute-start(bf16[64,768]{1,0:T(8,128)(2,1)S(1)} %bitcast.1), channel_id=1, source_target_pairs={{0,2},{2,0},{1,3},{3,1},{4,6},{6,4},{5,7},{7,5},{8,10},{10,8},{9,1... | collective-permute-start | bytes 294920 | tf_op jit(solution)/shard_map/ppermute | solution.py:232
  16.2 0.0 collective-permute-done.2.refs_0_
  16.2 1.2 %collective-permute-start.6 = (bf16[64,768]{1,0:T(8,128)(2,1)S(1)}, bf16[64,768]{1,0:T(8,128)(2,1)S(1)}, u32[]{:S(2)}, u32[]{:S(2)}) collective-permute-start(bf16[64,768]{1,0:T(8,128)(2,1)S(1)} %hold.10.refs_3_.refs_1_), channel_id=1, source_target_pairs={{0,2},{2,0},{1,3},{3,1},{4,6},{6,4},{5,7},{7,5},{8,10},{10,8},{9,1... | collective-permute-start | bytes 294920 | tf_op jit(solution)/shard_map/ppermute | solution.py:232
  17.5 0.0 collective-permute-done.3.refs_0_
  17.5 1.5 %collective-permute-start.9 = (bf16[64,384]{1,0:T(8,128)(2,1)S(1)}, bf16[64,384]{1,0:T(8,128)(2,1)S(1)}, u32[]{:S(2)}, u32[]{:S(2)}) collective-permute-start(bf16[64,384]{1,0:T(8,128)(2,1)S(1)} %hold.15), channel_id=1, source_target_pairs={{0,8},{4,12},{8,0},{12,4},{1,9},{5,13},{9,1},{13,5},{2,10},{6,14},... | collective-permute-start | bytes 147464 | tf_op jit(solution)/shard_map/ppermute | solution.py:229
  19.0 0.0 collective-permute-done.7.refs_0_
  19.0 0.0 collective-permute-done.4.refs_2_.refs_5_
  19.0 1.3 %collective-permute-done.5.refs_3_.refs_6_ = bf16[64,768]{1,0:T(8,128)(2,1)S(1)} collective-permute-done((bf16[64,768]{1,0:T(8,128)(2,1)S(1)}, bf16[64,768]{1,0:T(8,128)(2,1)S(1)}, u32[]{:S(2)}, u32[]{:S(2)}) %collective-permute-start.5) | collective-permute-done | bytes 98336 | tf_op jit(solution)/shard_map/ppermute | solution.py:232
  20.4 1.1 %collective-permute-done.6.refs_7_ = bf16[64,768]{1,0:T(8,128)(2,1)S(1)} collective-permute-done((bf16[64,768]{1,0:T(8,128)(2,1)S(1)}, bf16[64,768]{1,0:T(8,128)(2,1)S(1)}, u32[]{:S(2)}, u32[]{:S(2)}) %collective-permute-start.6) | collective-permute-done | bytes 98336 | tf_op jit(solution)/shard_map/ppermute | solution.py:232
  21.4 0.6 %attend.2 = (bf16[64,384]{1,0:T(8,128)(2,1)S(1)}, bf16[64,384]{1,0:T(8,128)(2,1)S(1)}, bf16[64,384]{1,0:T(8,128)(2,1)S(1)}) custom-call(bf16[64,1152]{1,0:T(8,128)(2,1)S(1)} %collective-permute-done.refs_0_.refs_1_, bf16[64,768]{1,0:T(8,128)(2,1)S(1)} %get-tuple-element.16.refs_1_, bf16[64,768]{1,0:T(8,128)(2,1)S(1)} %hold.9.refs_2_, ...), custom_call_target="tpu_custom_call" | custom-call | flops 150994944 | bytes 1081344 | tf_op jit(solution)/shard_map/attend/pallas_call | solution.py:257
  22.1 0.8 %collective-permute-start.8 = (bf16[64,384]{1,0:T(8,128)(2,1)S(1)}, bf16[64,384]{1,0:T(8,128)(2,1)S(1)}, u32[]{:S(2)}, u32[]{:S(2)}) collective-permute-start(bf16[64,384]{1,0:T(8,128)(2,1)S(1)} %get-tuple-element.22), channel_id=1, source_target_pairs={{0,12},{4,8},{8,4},{12,0},{1,13},{5,9},{9,5},{13,1},{2,14},{6,10},... | collective-permute-start | bytes 147464 | tf_op jit(solution)/shard_map/ppermute | solution.py:229
  22.9 0.0 collective-permute-done.9.refs_0_
  22.9 0.5 %attend.3.refs_1_ = bf16[64,384]{1,0:T(8,128)(2,1)S(1)} custom-call(bf16[64,1152]{1,0:T(8,128)(2,1)S(1)} %collective-permute-done.refs_0_.refs_1_, bf16[64,768]{1,0:T(8,128)(2,1)S(1)} %get-tuple-element.16.refs_1_, bf16[64,768]{1,0:T(8,128)(2,1)S(1)} %hold.9.refs_2_, bf16[64,768]{1,0:T(8,128)(2,1)S(1)} %hold.10.refs_3_.refs_1_, ...), custom_call_target="tpu_custom_call" | custom-call | flops 50331648 | bytes 884736 | tf_op jit(solution)/shard_map/attend/pallas_call | solution.py:257
  23.4 0.5 %collective-permute-start.11 = (bf16[64,384]{1,0:T(8,128)(2,1)S(1)}, bf16[64,384]{1,0:T(8,128)(2,1)S(1)}, u32[]{:S(2)}, u32[]{:S(2)}) collective-permute-start(bf16[64,384]{1,0:T(8,128)(2,1)S(1)} %hold.17), channel_id=1, source_target_pairs={{0,4},{4,0},{8,12},{12,8},{1,5},{5,1},{9,13},{13,9},{2,6},{6,2},{1... | collective-permute-start | bytes 147464 | tf_op jit(solution)/shard_map/ppermute | solution.py:229
  24.0 3.1 %collective-permute-start.10 = (bf16[64,384]{1,0:T(8,128)(2,1)S(1)}, bf16[64,384]{1,0:T(8,128)(2,1)S(1)}, u32[]{:S(2)}, u32[]{:S(2)}) collective-permute-start(bf16[64,384]{1,0:T(8,128)(2,1)S(1)} %attend.3.refs_1_), channel_id=1, source_target_pairs={{0,8},{4,12},{8,0},{12,4},{1,9},{5,13},{9,1},{13,5},{2,10},{6,14},... | collective-permute-start | bytes 147464 | tf_op jit(solution)/shard_map/ppermute | solution.py:229
  27.1 1.0 %collective-permute-done.8.refs_0_ = bf16[64,384]{1,0:T(8,128)(2,1)S(1)} collective-permute-done((bf16[64,384]{1,0:T(8,128)(2,1)S(1)}, bf16[64,384]{1,0:T(8,128)(2,1)S(1)}, u32[]{:S(2)}, u32[]{:S(2)}) %collective-permute-start.8) | collective-permute-done | bytes 49184 | tf_op jit(solution)/shard_map/ppermute | solution.py:229
  28.1 0.1 collective-permute-done.11.refs_3_
  28.2 1.0 %collective-permute-done.10.refs_2_ = bf16[64,384]{1,0:T(8,128)(2,1)S(1)} collective-permute-done((bf16[64,384]{1,0:T(8,128)(2,1)S(1)}, bf16[64,384]{1,0:T(8,128)(2,1)S(1)}, u32[]{:S(2)}, u32[]{:S(2)}) %collective-permute-start.10) | collective-permute-done | bytes 49184 | tf_op jit(solution)/shard_map/ppermute | solution.py:229
  29.2 0.7 %unpack.1 = bf16[1,64,1536]{2,1,0:T(8,128)(2,1)} custom-call(bf16[64,384]{1,0:T(8,128)(2,1)S(1)} %get-tuple-element.21.refs_1_.refs_0_, bf16[64,384]{1,0:T(8,128)(2,1)S(1)} %hold.14.refs_1_, bf16[64,384]{1,0:T(8,128)(2,1)S(1)} %collective-permute-done.10.refs_2_, bf16[64,384]{1,0:T(8,128)(2,1)S(1)} %collective-permute-done.11.refs_3_), custom_call_target="tpu_custom_call" | custom-call | bytes 393216 | tf_op jit(solution)/shard_map/unpack/pallas_call | solution.py:281
  (11 shorter events, 0.0 us)
Async XLA Ops:
  1.0 12.0 %collective-permute-start.1 = (bf16[64,768]{1,0:T(8,128)(2,1)S(1)}, bf16[64,768]{1,0:T(8,128)(2,1)S(1)}, u32[]{:S(2)}, u32[]{:S(2)}) collective-permute-start(bf16[64,768]{1,0:T(8,128)(2,1)S(1)} %get-tuple-element.17), channel_id=1, source_target_pairs={{0,12},{4,8},{8,4},{12,0},{1,13},{5,9},{9,5},{13,1},{2,14},{6,10},... | collective-permute-start | bytes 294920 | tf_op jit(solution)/shard_map/ppermute | solution.py:229
  6.1 8.3 %collective-permute-start = (bf16[64,1152]{1,0:T(8,128)(2,1)S(1)}, bf16[64,1152]{1,0:T(8,128)(2,1)S(1)}, u32[]{:S(2)}, u32[]{:S(2)}) collective-permute-start(bf16[64,1152]{1,0:T(8,128)(2,1)S(1)} %get-tuple-element.15), channel_id=1, source_target_pairs={{0,4},{4,0},{8,12},{12,8},{1,5},{5,1},{9,13},{13,9},{2,6},{6,2},{1... | collective-permute-start | bytes 442376 | tf_op jit(solution)/shard_map/ppermute | solution.py:229
  6.1 10.1 %collective-permute-start.2 = (bf16[64,768]{1,0:T(8,128)(2,1)S(1)}, bf16[64,768]{1,0:T(8,128)(2,1)S(1)}, u32[]{:S(2)}, u32[]{:S(2)}) collective-permute-start(bf16[64,768]{1,0:T(8,128)(2,1)S(1)} %get-tuple-element.18), channel_id=1, source_target_pairs={{0,8},{4,12},{8,0},{12,4},{1,9},{5,13},{9,1},{13,5},{2,10},{6,14},... | collective-permute-start | bytes 294920 | tf_op jit(solution)/shard_map/ppermute | solution.py:229
  7.7 11.3 %collective-permute-start.7 = (bf16[64,384]{1,0:T(8,128)(2,1)S(1)}, bf16[64,384]{1,0:T(8,128)(2,1)S(1)}, u32[]{:S(2)}, u32[]{:S(2)}) collective-permute-start(bf16[64,384]{1,0:T(8,128)(2,1)S(1)} %get-tuple-element.20), channel_id=1, source_target_pairs={{0,12},{4,8},{8,4},{12,0},{1,13},{5,9},{9,5},{13,1},{2,14},{6,10},... | collective-permute-start | bytes 147464 | tf_op jit(solution)/shard_map/ppermute | solution.py:229
  11.5 5.9 %collective-permute-start.3 = (bf16[64,768]{1,0:T(8,128)(2,1)S(1)}, bf16[64,768]{1,0:T(8,128)(2,1)S(1)}, u32[]{:S(2)}, u32[]{:S(2)}) collective-permute-start(bf16[64,768]{1,0:T(8,128)(2,1)S(1)} %get-tuple-element.16.refs_1_), channel_id=1, source_target_pairs={{0,2},{2,0},{1,3},{3,1},{4,6},{6,4},{5,7},{7,5},{8,10},{10,8},{9,1... | collective-permute-start | bytes 294920 | tf_op jit(solution)/shard_map/ppermute | solution.py:232
  13.0 6.0 %collective-permute-start.4 = (bf16[64,768]{1,0:T(8,128)(2,1)S(1)}, bf16[64,768]{1,0:T(8,128)(2,1)S(1)}, u32[]{:S(2)}, u32[]{:S(2)}) collective-permute-start(bf16[64,768]{1,0:T(8,128)(2,1)S(1)} %hold.9.refs_2_), channel_id=1, source_target_pairs={{0,2},{2,0},{1,3},{3,1},{4,6},{6,4},{5,7},{7,5},{8,10},{10,8},{9,1... | collective-permute-start | bytes 294920 | tf_op jit(solution)/shard_map/ppermute | solution.py:232
  14.4 5.9 %collective-permute-start.5 = (bf16[64,768]{1,0:T(8,128)(2,1)S(1)}, bf16[64,768]{1,0:T(8,128)(2,1)S(1)}, u32[]{:S(2)}, u32[]{:S(2)}) collective-permute-start(bf16[64,768]{1,0:T(8,128)(2,1)S(1)} %bitcast.1), channel_id=1, source_target_pairs={{0,2},{2,0},{1,3},{3,1},{4,6},{6,4},{5,7},{7,5},{8,10},{10,8},{9,1... | collective-permute-start | bytes 294920 | tf_op jit(solution)/shard_map/ppermute | solution.py:232
  16.2 5.2 %collective-permute-start.6 = (bf16[64,768]{1,0:T(8,128)(2,1)S(1)}, bf16[64,768]{1,0:T(8,128)(2,1)S(1)}, u32[]{:S(2)}, u32[]{:S(2)}) collective-permute-start(bf16[64,768]{1,0:T(8,128)(2,1)S(1)} %hold.10.refs_3_.refs_1_), channel_id=1, source_target_pairs={{0,2},{2,0},{1,3},{3,1},{4,6},{6,4},{5,7},{7,5},{8,10},{10,8},{9,1... | collective-permute-start | bytes 294920 | tf_op jit(solution)/shard_map/ppermute | solution.py:232
  17.5 5.4 %collective-permute-start.9 = (bf16[64,384]{1,0:T(8,128)(2,1)S(1)}, bf16[64,384]{1,0:T(8,128)(2,1)S(1)}, u32[]{:S(2)}, u32[]{:S(2)}) collective-permute-start(bf16[64,384]{1,0:T(8,128)(2,1)S(1)} %hold.15), channel_id=1, source_target_pairs={{0,8},{4,12},{8,0},{12,4},{1,9},{5,13},{9,1},{13,5},{2,10},{6,14},... | collective-permute-start | bytes 147464 | tf_op jit(solution)/shard_map/ppermute | solution.py:229
  22.1 6.0 %collective-permute-start.8 = (bf16[64,384]{1,0:T(8,128)(2,1)S(1)}, bf16[64,384]{1,0:T(8,128)(2,1)S(1)}, u32[]{:S(2)}, u32[]{:S(2)}) collective-permute-start(bf16[64,384]{1,0:T(8,128)(2,1)S(1)} %get-tuple-element.22), channel_id=1, source_target_pairs={{0,12},{4,8},{8,4},{12,0},{1,13},{5,9},{9,5},{13,1},{2,14},{6,10},... | collective-permute-start | bytes 147464 | tf_op jit(solution)/shard_map/ppermute | solution.py:229
  23.4 4.8 %collective-permute-start.11 = (bf16[64,384]{1,0:T(8,128)(2,1)S(1)}, bf16[64,384]{1,0:T(8,128)(2,1)S(1)}, u32[]{:S(2)}, u32[]{:S(2)}) collective-permute-start(bf16[64,384]{1,0:T(8,128)(2,1)S(1)} %hold.17), channel_id=1, source_target_pairs={{0,4},{4,0},{8,12},{12,8},{1,5},{5,1},{9,13},{13,9},{2,6},{6,2},{1... | collective-permute-start | bytes 147464 | tf_op jit(solution)/shard_map/ppermute | solution.py:229
  24.0 5.2 %collective-permute-start.10 = (bf16[64,384]{1,0:T(8,128)(2,1)S(1)}, bf16[64,384]{1,0:T(8,128)(2,1)S(1)}, u32[]{:S(2)}, u32[]{:S(2)}) collective-permute-start(bf16[64,384]{1,0:T(8,128)(2,1)S(1)} %attend.3.refs_1_), channel_id=1, source_target_pairs={{0,8},{4,12},{8,0},{12,4},{1,9},{5,13},{9,1},{13,5},{2,10},{6,14},... | collective-permute-start | bytes 147464 | tf_op jit(solution)/shard_map/ppermute | solution.py:229

commit v22 on v21

--- a/solution.py
+++ b/solution.py
@@ -9,11 +9,10 @@
 from jax.sharding import PartitionSpec as P
 
 HD = 128
-EFFORT = 0
-EFFORT_OWN = 10**9
-EFFORT_QUERIES = 2 * 10**8
+EFFORT = 10**9
+EFFORT_OWN = 3 * 10**8
 EFFORT_NEAR = 0
-EFFORT_FAR = (10**9, 5 * 10**8)
+EFFORT_FAR = (10**9, 2 * 10**9)
 ANY = pl.BlockSpec(memory_space=pl.ANY)
 HBM = pl.BlockSpec(memory_space=pltpu.HBM)
 VMEM = pl.BlockSpec(memory_space=pltpu.VMEM)
@@ -202,7 +201,7 @@
     far = list(range(blocks - 1, 1, -1))
 
     kv, q = (("k", 0, part), ("v", 0, part)), (("q", 0, part),)
-    messages = [(s, kv) for s in far] + [(1, kv + q)] + [(s, q) for s in far] + [(0, kv), (0, q)]
+    messages = [(s, kv) for s in far] + [(1, kv + q), (0, kv)] + [(s, q) for s in far + [0]]
     inputs = [pltpu.with_memory_space_constraint(x, pltpu.HBM) for x in (query_rows, key_rows, value_rows)]
 
     def pack(cut):
@@ -222,7 +221,7 @@
             name="pack",
         )(*inputs)
 
-    first = len(far) + 1
+    first = len(far) + 2
     packed = [*pack(messages[:first]), *pack(messages[first:])]
 
     def to_block(array, s):
@@ -232,21 +231,19 @@
         return lax.ppermute(array, "uly", [(i, (i + t) % columns_of) for i in range(columns_of)])
 
     sent = {message: array for message, array in zip(messages, packed)}
-    own_kv, own_q = packed[-2:]
+    own_kv, own_q = sent[0, kv], sent[0, q]
     far_kv = [to_block(sent[s, kv], s) for s in far]
     near_kvq = to_block(sent[1, kv + q], 1)
     far_kv = [hold([array], (), effort)[0] for array, effort in zip(far_kv, EFFORT_FAR)]
     near_kv = join([near_kvq], [0], 2 * part, EFFORT_NEAR)
-    far_q = [to_block(sent[far[0], q], far[0])]
-    far_q += [to_block(hold([sent[s, q]], [array])[0], s) for s, array in zip(far[1:], far_kv[1:])]
+    far_q = [to_block(hold([sent[s, q]], [array])[0], s) for s, array in zip(far, far_kv)]
     own_kv_x, first_x, near_x, second_x = (
         [to_column(group, t) for t in range(1, columns_of)]
         for group in (own_kv, far_kv[0], near_kv[0], far_kv[1])
     )
     own_kv_x = hold(own_kv_x, effort=EFFORT_OWN)
     near_q = join([own_q, near_kvq], [0, 2 * part], part)
-    far_q[:1] = hold(far_q[:1], [*own_kv_x, *first_x, *near_x], EFFORT)
-    far_q[:1] = hold(far_q[:1], (), EFFORT_QUERIES)
+    far_q[0] = join(far_q[:1], [0], part, EFFORT, [*own_kv_x, *first_x, *near_x])
 
     holders = [near_kvq, own_kv, *far_kv, *own_kv_x, *first_x, *near_x, *second_x]
     keys = [(at, None) for at in range(len(holders))]
@@ -268,13 +265,13 @@
             name="attend",
         )(*holders, *query_arrays)
 
-    mixed = dict(zip([0, 1] + far[:-1], attend([near_q] + far_q[:-1], [(0, 0), (0, 1), (1, None)])))
+    mixed = dict(zip([0, 1] + far[:-1], attend([near_q] + far_q[:-1], [(0, 0), (0, 1), (1, 0)])))
     last_q = hold([far_q[-1]], [mixed[0]])
     mixed[far[-1]] = attend(last_q, [(0, None)])[0]
     mixed[1] = hold([mixed[1]], [mixed[far[-1]]])[0]
     back = {s: to_block(mixed[s], s) for s in far + [1]}
     early = far[:-1]
-    back.update(zip(early, hold([back[s] for s in early], effort=EFFORT)))
+    back.update(zip(early, hold([back[s] for s in early])))
     back[0] = mixed[0]
     order = [0] + far + [1]
     back = [back[s] for s in order]

time: 30.1 us -> 30 us (level)
  waiting for transfers between devices: 5.32 us -> 4.78 us
  starting transfers between devices: 20.7 us -> 21.1 us
    ppermute x4, waiting for transfers between devices: 2.39 us -> 1.86 us  [to_column(): lax.ppermute(array, 'uly', [(i, (i + t) % columns_of) for i in range(colu...]
    ppermute x4, starting transfers between devices: 5.06 us -> 5.41 us  [to_column(): lax.ppermute(array, 'uly', [(i, (i + t) % columns_of) for i in range(colu...]
where the time goes in v22:
time: 30 us; the launch traced here: 29.7 us
  starting transfers between devices  21.1 us (70%)
  waiting for transfers between devices  4.78 us (16%)
  Pallas kernels  3.8 us (13%)
    ppermute x8, starting transfers between devices, to_block(): return lax.ppermute(array, 'blk', [(i, i ^ s) for i in range(blocks)])  15.7 us
    ppermute x4, starting transfers between devices, to_column(): lax.ppermute(array, 'uly', [(i, (i + t) % columns_of) for i in range(colu...  5.41 us
    ppermute x8, waiting for transfers between devices, to_block(): return lax.ppermute(array, 'blk', [(i, i ^ s) for i in range(blocks)])  2.92 us
    pallas_call x2, Pallas kernels, pack(): pl.pallas_call(functools.partial(pack_kernel, cut, part), out_shape=[jax....  1.94 us
    ppermute x4, waiting for transfers between devices, to_column(): lax.ppermute(array, 'uly', [(i, (i + t) % columns_of) for i in range(colu...  1.86 us
    pallas_call x2, Pallas kernels, attend(): pl.pallas_call(functools.partial(attend_kernel, len(holders), keys, query...  1.13 us
    pallas_call x1, Pallas kernels, local_blocks(): pl.pallas_call(functools.partial(unpack_kernel, order, part), out_shape=j...  0.7 us
  transfers between devices with their start and end apart: 12, of which 6 were waited for; matrix products, arithmetic and copies ran while one was open for 0% of the time, Pallas kernels for 7%

profile of v22, /device:TPU:0, one launch (start us, length us, event | category | flops | bytes accessed | tf_op | source)
XLA Modules:
  0.0 29.7 jit_solution(5650780704312948587)
XLA Ops:
  0.0 1.1 %pack.2 = (bf16[64,768]{1,0:T(8,128)(2,1)S(1)}, bf16[64,768]{1,0:T(8,128)(2,1)S(1)}, bf16[64,1152]{1,0:T(8,128)(2,1)S(1)}, bf16[64,768]{1,0:T(8,128)(2,1)S(1)}) custom-call(bf16[1,64,1536]{2,1,0:T(8,128)(2,1)} %q_ref.3, bf16[1,64,1536]{2,1,0:T(8,128)(2,1)} %k_ref.3, bf16[1,64,1536]{2,1,0:T(8,128)(2,1)} %v_ref.3), custom_call_target="tpu_custom_call" | custom-call | bytes 884736 | tf_op jit(solution)/shard_map/pack/pallas_call | solution.py:210
  1.1 5.1 %collective-permute-start.1 = (bf16[64,768]{1,0:T(8,128)(2,1)S(1)}, bf16[64,768]{1,0:T(8,128)(2,1)S(1)}, u32[]{:S(2)}, u32[]{:S(2)}) collective-permute-start(bf16[64,768]{1,0:T(8,128)(2,1)S(1)} %get-tuple-element.17), channel_id=1, source_target_pairs={{0,12},{4,8},{8,4},{12,0},{1,13},{5,9},{9,5},{13,1},{2,14},{6,10},... | collective-permute-start | bytes 294920 | tf_op jit(solution)/shard_map/ppermute | solution.py:228
  6.2 0.0 collective-permute-start
  6.2 0.6 %collective-permute-start.2 = (bf16[64,768]{1,0:T(8,128)(2,1)S(1)}, bf16[64,768]{1,0:T(8,128)(2,1)S(1)}, u32[]{:S(2)}, u32[]{:S(2)}) collective-permute-start(bf16[64,768]{1,0:T(8,128)(2,1)S(1)} %get-tuple-element.18), channel_id=1, source_target_pairs={{0,8},{4,12},{8,0},{12,4},{1,9},{5,13},{9,1},{13,5},{2,10},{6,14},... | collective-permute-start | bytes 294920 | tf_op jit(solution)/shard_map/ppermute | solution.py:228
  6.8 1.6 %collective-permute-start.3 = (bf16[64,768]{1,0:T(8,128)(2,1)S(1)}, bf16[64,768]{1,0:T(8,128)(2,1)S(1)}, u32[]{:S(2)}, u32[]{:S(2)}) collective-permute-start(bf16[64,768]{1,0:T(8,128)(2,1)S(1)} %get-tuple-element.16.refs_1_), channel_id=1, source_target_pairs={{0,2},{2,0},{1,3},{3,1},{4,6},{6,4},{5,7},{7,5},{8,10},{10,8},{9,1... | collective-permute-start | bytes 294920 | tf_op jit(solution)/shard_map/ppermute | solution.py:231
  8.5 0.9 %pack.3 = (bf16[64,384]{1,0:T(8,128)(2,1)S(1)}, bf16[64,384]{1,0:T(8,128)(2,1)S(1)}, bf16[64,384]{1,0:T(8,128)(2,1)S(1)}) custom-call(bf16[1,64,1536]{2,1,0:T(8,128)(2,1)} %q_ref.3, bf16[1,64,1536]{2,1,0:T(8,128)(2,1)} %k_ref.3, bf16[1,64,1536]{2,1,0:T(8,128)(2,1)} %v_ref.3), custom_call_target="tpu_custom_call" | custom-call | bytes 294912 | tf_op jit(solution)/shard_map/pack/pallas_call | solution.py:210
  9.3 0.5 %collective-permute-done.1.refs_0_ = bf16[64,768]{1,0:T(8,128)(2,1)S(1)} collective-permute-done((bf16[64,768]{1,0:T(8,128)(2,1)S(1)}, bf16[64,768]{1,0:T(8,128)(2,1)S(1)}, u32[]{:S(2)}, u32[]{:S(2)}) %collective-permute-start.1) | collective-permute-done | bytes 98336 | tf_op jit(solution)/shard_map/ppermute | solution.py:228
  9.9 1.7 %collective-permute-start.4 = (bf16[64,768]{1,0:T(8,128)(2,1)S(1)}, bf16[64,768]{1,0:T(8,128)(2,1)S(1)}, u32[]{:S(2)}, u32[]{:S(2)}) collective-permute-start(bf16[64,768]{1,0:T(8,128)(2,1)S(1)} %hold.8.refs_1_.refs_2_), channel_id=1, source_target_pairs={{0,2},{2,0},{1,3},{3,1},{4,6},{6,4},{5,7},{7,5},{8,10},{10,8},{9,1... | collective-permute-start | bytes 294920 | tf_op jit(solution)/shard_map/ppermute | solution.py:231
  11.6 3.7 %collective-permute-start.7 = (bf16[64,384]{1,0:T(8,128)(2,1)S(1)}, bf16[64,384]{1,0:T(8,128)(2,1)S(1)}, u32[]{:S(2)}, u32[]{:S(2)}) collective-permute-start(bf16[64,384]{1,0:T(8,128)(2,1)S(1)} %hold.11), channel_id=1, source_target_pairs={{0,12},{4,8},{8,4},{12,0},{1,13},{5,9},{9,5},{13,1},{2,14},{6,10},... | collective-permute-start | bytes 147464 | tf_op jit(solution)/shard_map/ppermute | solution.py:228
  15.2 0.0 collective-permute-done.refs_0_.refs_1_
  15.2 1.0 %collective-permute-start.5 = (bf16[64,768]{1,0:T(8,128)(2,1)S(1)}, bf16[64,768]{1,0:T(8,128)(2,1)S(1)}, u32[]{:S(2)}, u32[]{:S(2)}) collective-permute-start(bf16[64,768]{1,0:T(8,128)(2,1)S(1)} %bitcast.1), channel_id=1, source_target_pairs={{0,2},{2,0},{1,3},{3,1},{4,6},{6,4},{5,7},{7,5},{8,10},{10,8},{9,1... | collective-permute-start | bytes 294920 | tf_op jit(solution)/shard_map/ppermute | solution.py:231
  16.3 0.0 collective-permute-done.2.refs_0_
  16.3 1.1 %collective-permute-start.6 = (bf16[64,768]{1,0:T(8,128)(2,1)S(1)}, bf16[64,768]{1,0:T(8,128)(2,1)S(1)}, u32[]{:S(2)}, u32[]{:S(2)}) collective-permute-start(bf16[64,768]{1,0:T(8,128)(2,1)S(1)} %hold.9.refs_3_.refs_1_), channel_id=1, source_target_pairs={{0,2},{2,0},{1,3},{3,1},{4,6},{6,4},{5,7},{7,5},{8,10},{10,8},{9,1... | collective-permute-start | bytes 294920 | tf_op jit(solution)/shard_map/ppermute | solution.py:231
  17.3 0.0 collective-permute-done.3.refs_0_
  17.3 1.7 %collective-permute-start.9 = (bf16[64,384]{1,0:T(8,128)(2,1)S(1)}, bf16[64,384]{1,0:T(8,128)(2,1)S(1)}, u32[]{:S(2)}, u32[]{:S(2)}) collective-permute-start(bf16[64,384]{1,0:T(8,128)(2,1)S(1)} %hold.13), channel_id=1, source_target_pairs={{0,8},{4,12},{8,0},{12,4},{1,9},{5,13},{9,1},{13,5},{2,10},{6,14},... | collective-permute-start | bytes 147464 | tf_op jit(solution)/shard_map/ppermute | solution.py:228
  19.1 0.0 collective-permute-done.7.refs_0_
  19.1 0.0 collective-permute-done.4.refs_2_.refs_5_
  19.1 0.8 %collective-permute-done.5.refs_3_.refs_6_ = bf16[64,768]{1,0:T(8,128)(2,1)S(1)} collective-permute-done((bf16[64,768]{1,0:T(8,128)(2,1)S(1)}, bf16[64,768]{1,0:T(8,128)(2,1)S(1)}, u32[]{:S(2)}, u32[]{:S(2)}) %collective-permute-start.5) | collective-permute-done | bytes 98336 | tf_op jit(solution)/shard_map/ppermute | solution.py:231
  19.9 1.0 %collective-permute-done.6.refs_7_ = bf16[64,768]{1,0:T(8,128)(2,1)S(1)} collective-permute-done((bf16[64,768]{1,0:T(8,128)(2,1)S(1)}, bf16[64,768]{1,0:T(8,128)(2,1)S(1)}, u32[]{:S(2)}, u32[]{:S(2)}) %collective-permute-start.6) | collective-permute-done | bytes 98336 | tf_op jit(solution)/shard_map/ppermute | solution.py:231
  21.0 0.6 %attend.2 = (bf16[64,384]{1,0:T(8,128)(2,1)S(1)}, bf16[64,384]{1,0:T(8,128)(2,1)S(1)}, bf16[64,384]{1,0:T(8,128)(2,1)S(1)}) custom-call(bf16[64,1152]{1,0:T(8,128)(2,1)S(1)} %collective-permute-done.refs_0_.refs_1_, bf16[64,768]{1,0:T(8,128)(2,1)S(1)} %get-tuple-element.16.refs_1_, bf16[64,768]{1,0:T(8,128)(2,1)S(1)} %hold.8.refs_1_.refs_2_, ...), custom_call_target="tpu_custom_call" | custom-call | flops 150994944 | bytes 1081344 | tf_op jit(solution)/shard_map/attend/pallas_call | solution.py:254
  21.6 1.4 %collective-permute-start.8 = (bf16[64,384]{1,0:T(8,128)(2,1)S(1)}, bf16[64,384]{1,0:T(8,128)(2,1)S(1)}, u32[]{:S(2)}, u32[]{:S(2)}) collective-permute-start(bf16[64,384]{1,0:T(8,128)(2,1)S(1)} %get-tuple-element.22), channel_id=1, source_target_pairs={{0,12},{4,8},{8,4},{12,0},{1,13},{5,9},{9,5},{13,1},{2,14},{6,10},... | collective-permute-start | bytes 147464 | tf_op jit(solution)/shard_map/ppermute | solution.py:228
  23.0 0.0 collective-permute-done.9.refs_0_
  23.0 0.5 %attend.3.refs_1_ = bf16[64,384]{1,0:T(8,128)(2,1)S(1)} custom-call(bf16[64,1152]{1,0:T(8,128)(2,1)S(1)} %collective-permute-done.refs_0_.refs_1_, bf16[64,768]{1,0:T(8,128)(2,1)S(1)} %get-tuple-element.16.refs_1_, bf16[64,768]{1,0:T(8,128)(2,1)S(1)} %hold.8.refs_1_.refs_2_, bf16[64,768]{1,0:T(8,128)(2,1)S(1)} %hold.9.refs_3_.refs_1_, ...), custom_call_target="tpu_custom_call" | custom-call | flops 50331648 | bytes 884736 | tf_op jit(solution)/shard_map/attend/pallas_call | solution.py:254
  23.5 0.6 %collective-permute-start.11 = (bf16[64,384]{1,0:T(8,128)(2,1)S(1)}, bf16[64,384]{1,0:T(8,128)(2,1)S(1)}, u32[]{:S(2)}, u32[]{:S(2)}) collective-permute-start(bf16[64,384]{1,0:T(8,128)(2,1)S(1)} %hold.15), channel_id=1, source_target_pairs={{0,4},{4,0},{8,12},{12,8},{1,5},{5,1},{9,13},{13,9},{2,6},{6,2},{1... | collective-permute-start | bytes 147464 | tf_op jit(solution)/shard_map/ppermute | solution.py:228
  24.0 2.6 %collective-permute-start.10 = (bf16[64,384]{1,0:T(8,128)(2,1)S(1)}, bf16[64,384]{1,0:T(8,128)(2,1)S(1)}, u32[]{:S(2)}, u32[]{:S(2)}) collective-permute-start(bf16[64,384]{1,0:T(8,128)(2,1)S(1)} %attend.3.refs_1_), channel_id=1, source_target_pairs={{0,8},{4,12},{8,0},{12,4},{1,9},{5,13},{9,1},{13,5},{2,10},{6,14},... | collective-permute-start | bytes 147464 | tf_op jit(solution)/shard_map/ppermute | solution.py:228
  26.6 1.0 %collective-permute-done.8.refs_0_ = bf16[64,384]{1,0:T(8,128)(2,1)S(1)} collective-permute-done((bf16[64,384]{1,0:T(8,128)(2,1)S(1)}, bf16[64,384]{1,0:T(8,128)(2,1)S(1)}, u32[]{:S(2)}, u32[]{:S(2)}) %collective-permute-start.8) | collective-permute-done | bytes 49184 | tf_op jit(solution)/shard_map/ppermute | solution.py:228
  27.6 0.5 %collective-permute-done.11.refs_3_ = bf16[64,384]{1,0:T(8,128)(2,1)S(1)} collective-permute-done((bf16[64,384]{1,0:T(8,128)(2,1)S(1)}, bf16[64,384]{1,0:T(8,128)(2,1)S(1)}, u32[]{:S(2)}, u32[]{:S(2)}) %collective-permute-start.11) | collective-permute-done | bytes 49184 | tf_op jit(solution)/shard_map/ppermute | solution.py:228
  28.1 0.9 %collective-permute-done.10.refs_2_ = bf16[64,384]{1,0:T(8,128)(2,1)S(1)} collective-permute-done((bf16[64,384]{1,0:T(8,128)(2,1)S(1)}, bf16[64,384]{1,0:T(8,128)(2,1)S(1)}, u32[]{:S(2)}, u32[]{:S(2)}) %collective-permute-start.10) | collective-permute-done | bytes 49184 | tf_op jit(solution)/shard_map/ppermute | solution.py:228
  29.0 0.7 %unpack.1 = bf16[1,64,1536]{2,1,0:T(8,128)(2,1)} custom-call(bf16[64,384]{1,0:T(8,128)(2,1)S(1)} %get-tuple-element.21.refs_1_.refs_0_, bf16[64,384]{1,0:T(8,128)(2,1)S(1)} %hold.12.refs_1_, bf16[64,384]{1,0:T(8,128)(2,1)S(1)} %collective-permute-done.10.refs_2_, bf16[64,384]{1,0:T(8,128)(2,1)S(1)} %collective-permute-done.11.refs_3_), custom_call_target="tpu_custom_call" | custom-call | bytes 393216 | tf_op jit(solution)/shard_map/unpack/pallas_call | solution.py:278
  (11 shorter events, 0.0 us)
Async XLA Ops:
  1.1 8.8 %collective-permute-start.1 = (bf16[64,768]{1,0:T(8,128)(2,1)S(1)}, bf16[64,768]{1,0:T(8,128)(2,1)S(1)}, u32[]{:S(2)}, u32[]{:S(2)}) collective-permute-start(bf16[64,768]{1,0:T(8,128)(2,1)S(1)} %get-tuple-element.17), channel_id=1, source_target_pairs={{0,12},{4,8},{8,4},{12,0},{1,13},{5,9},{9,5},{13,1},{2,14},{6,10},... | collective-permute-start | bytes 294920 | tf_op jit(solution)/shard_map/ppermute | solution.py:228
  6.2 9.0 %collective-permute-start = (bf16[64,1152]{1,0:T(8,128)(2,1)S(1)}, bf16[64,1152]{1,0:T(8,128)(2,1)S(1)}, u32[]{:S(2)}, u32[]{:S(2)}) collective-permute-start(bf16[64,1152]{1,0:T(8,128)(2,1)S(1)} %get-tuple-element.15), channel_id=1, source_target_pairs={{0,4},{4,0},{8,12},{12,8},{1,5},{5,1},{9,13},{13,9},{2,6},{6,2},{1... | collective-permute-start | bytes 442376 | tf_op jit(solution)/shard_map/ppermute | solution.py:228
  6.2 10.1 %collective-permute-start.2 = (bf16[64,768]{1,0:T(8,128)(2,1)S(1)}, bf16[64,768]{1,0:T(8,128)(2,1)S(1)}, u32[]{:S(2)}, u32[]{:S(2)}) collective-permute-start(bf16[64,768]{1,0:T(8,128)(2,1)S(1)} %get-tuple-element.18), channel_id=1, source_target_pairs={{0,8},{4,12},{8,0},{12,4},{1,9},{5,13},{9,1},{13,5},{2,10},{6,14},... | collective-permute-start | bytes 294920 | tf_op jit(solution)/shard_map/ppermute | solution.py:228
  6.8 10.5 %collective-permute-start.3 = (bf16[64,768]{1,0:T(8,128)(2,1)S(1)}, bf16[64,768]{1,0:T(8,128)(2,1)S(1)}, u32[]{:S(2)}, u32[]{:S(2)}) collective-permute-start(bf16[64,768]{1,0:T(8,128)(2,1)S(1)} %get-tuple-element.16.refs_1_), channel_id=1, source_target_pairs={{0,2},{2,0},{1,3},{3,1},{4,6},{6,4},{5,7},{7,5},{8,10},{10,8},{9,1... | collective-permute-start | bytes 294920 | tf_op jit(solution)/shard_map/ppermute | solution.py:231
  9.9 9.2 %collective-permute-start.4 = (bf16[64,768]{1,0:T(8,128)(2,1)S(1)}, bf16[64,768]{1,0:T(8,128)(2,1)S(1)}, u32[]{:S(2)}, u32[]{:S(2)}) collective-permute-start(bf16[64,768]{1,0:T(8,128)(2,1)S(1)} %hold.8.refs_1_.refs_2_), channel_id=1, source_target_pairs={{0,2},{2,0},{1,3},{3,1},{4,6},{6,4},{5,7},{7,5},{8,10},{10,8},{9,1... | collective-permute-start | bytes 294920 | tf_op jit(solution)/shard_map/ppermute | solution.py:231
  11.6 7.5 %collective-permute-start.7 = (bf16[64,384]{1,0:T(8,128)(2,1)S(1)}, bf16[64,384]{1,0:T(8,128)(2,1)S(1)}, u32[]{:S(2)}, u32[]{:S(2)}) collective-permute-start(bf16[64,384]{1,0:T(8,128)(2,1)S(1)} %hold.11), channel_id=1, source_target_pairs={{0,12},{4,8},{8,4},{12,0},{1,13},{5,9},{9,5},{13,1},{2,14},{6,10},... | collective-permute-start | bytes 147464 | tf_op jit(solution)/shard_map/ppermute | solution.py:228
  15.2 4.7 %collective-permute-start.5 = (bf16[64,768]{1,0:T(8,128)(2,1)S(1)}, bf16[64,768]{1,0:T(8,128)(2,1)S(1)}, u32[]{:S(2)}, u32[]{:S(2)}) collective-permute-start(bf16[64,768]{1,0:T(8,128)(2,1)S(1)} %bitcast.1), channel_id=1, source_target_pairs={{0,2},{2,0},{1,3},{3,1},{4,6},{6,4},{5,7},{7,5},{8,10},{10,8},{9,1... | collective-permute-start | bytes 294920 | tf_op jit(solution)/shard_map/ppermute | solution.py:231
  16.3 4.7 %collective-permute-start.6 = (bf16[64,768]{1,0:T(8,128)(2,1)S(1)}, bf16[64,768]{1,0:T(8,128)(2,1)S(1)}, u32[]{:S(2)}, u32[]{:S(2)}) collective-permute-start(bf16[64,768]{1,0:T(8,128)(2,1)S(1)} %hold.9.refs_3_.refs_1_), channel_id=1, source_target_pairs={{0,2},{2,0},{1,3},{3,1},{4,6},{6,4},{5,7},{7,5},{8,10},{10,8},{9,1... | collective-permute-start | bytes 294920 | tf_op jit(solution)/shard_map/ppermute | solution.py:231
  17.3 5.6 %collective-permute-start.9 = (bf16[64,384]{1,0:T(8,128)(2,1)S(1)}, bf16[64,384]{1,0:T(8,128)(2,1)S(1)}, u32[]{:S(2)}, u32[]{:S(2)}) collective-permute-start(bf16[64,384]{1,0:T(8,128)(2,1)S(1)} %hold.13), channel_id=1, source_target_pairs={{0,8},{4,12},{8,0},{12,4},{1,9},{5,13},{9,1},{13,5},{2,10},{6,14},... | collective-permute-start | bytes 147464 | tf_op jit(solution)/shard_map/ppermute | solution.py:228
  21.6 6.0 %collective-permute-start.8 = (bf16[64,384]{1,0:T(8,128)(2,1)S(1)}, bf16[64,384]{1,0:T(8,128)(2,1)S(1)}, u32[]{:S(2)}, u32[]{:S(2)}) collective-permute-start(bf16[64,384]{1,0:T(8,128)(2,1)S(1)} %get-tuple-element.22), channel_id=1, source_target_pairs={{0,12},{4,8},{8,4},{12,0},{1,13},{5,9},{9,5},{13,1},{2,14},{6,10},... | collective-permute-start | bytes 147464 | tf_op jit(solution)/shard_map/ppermute | solution.py:228
  23.5 4.6 %collective-permute-start.11 = (bf16[64,384]{1,0:T(8,128)(2,1)S(1)}, bf16[64,384]{1,0:T(8,128)(2,1)S(1)}, u32[]{:S(2)}, u32[]{:S(2)}) collective-permute-start(bf16[64,384]{1,0:T(8,128)(2,1)S(1)} %hold.15), channel_id=1, source_target_pairs={{0,4},{4,0},{8,12},{12,8},{1,5},{5,1},{9,13},{13,9},{2,6},{6,2},{1... | collective-permute-start | bytes 147464 | tf_op jit(solution)/shard_map/ppermute | solution.py:228
  24.0 5.0 %collective-permute-start.10 = (bf16[64,384]{1,0:T(8,128)(2,1)S(1)}, bf16[64,384]{1,0:T(8,128)(2,1)S(1)}, u32[]{:S(2)}, u32[]{:S(2)}) collective-permute-start(bf16[64,384]{1,0:T(8,128)(2,1)S(1)} %attend.3.refs_1_), channel_id=1, source_target_pairs={{0,8},{4,12},{8,0},{12,4},{1,9},{5,13},{9,1},{13,5},{2,10},{6,14},... | collective-permute-start | bytes 147464 | tf_op jit(solution)/shard_map/ppermute | solution.py:228

commit v23 on v21

--- a/solution.py
+++ b/solution.py
@@ -13,7 +13,7 @@
 EFFORT_OWN = 10**9
 EFFORT_QUERIES = 2 * 10**8
 EFFORT_NEAR = 0
-EFFORT_FAR = (10**9, 5 * 10**8)
+EFFORT_FAR = (53 * 10**7, 5 * 10**8)
 ANY = pl.BlockSpec(memory_space=pl.ANY)
 HBM = pl.BlockSpec(memory_space=pltpu.HBM)
 VMEM = pl.BlockSpec(memory_space=pltpu.VMEM)
@@ -202,7 +202,7 @@
     far = list(range(blocks - 1, 1, -1))
 
     kv, q = (("k", 0, part), ("v", 0, part)), (("q", 0, part),)
-    messages = [(s, kv) for s in far] + [(1, kv + q)] + [(s, q) for s in far] + [(0, kv), (0, q)]
+    messages = [(s, kv) for s in far] + [(1, kv + q), (0, kv)] + [(s, q) for s in far + [0]]
     inputs = [pltpu.with_memory_space_constraint(x, pltpu.HBM) for x in (query_rows, key_rows, value_rows)]
 
     def pack(cut):
@@ -222,7 +222,7 @@
             name="pack",
         )(*inputs)
 
-    first = len(far) + 1
+    first = len(far) + 2
     packed = [*pack(messages[:first]), *pack(messages[first:])]
 
     def to_block(array, s):
@@ -232,11 +232,11 @@
         return lax.ppermute(array, "uly", [(i, (i + t) % columns_of) for i in range(columns_of)])
 
     sent = {message: array for message, array in zip(messages, packed)}
-    own_kv, own_q = packed[-2:]
+    own_kv, own_q = sent[0, kv], sent[0, q]
     far_kv = [to_block(sent[s, kv], s) for s in far]
     near_kvq = to_block(sent[1, kv + q], 1)
     far_kv = [hold([array], (), effort)[0] for array, effort in zip(far_kv, EFFORT_FAR)]
-    near_kv = join([near_kvq], [0], 2 * part, EFFORT_NEAR)
+    near_kv = join([near_kvq], [0], 2 * part, EFFORT_NEAR, far_kv[:1])
     far_q = [to_block(sent[far[0], q], far[0])]
     far_q += [to_block(hold([sent[s, q]], [array])[0], s) for s, array in zip(far[1:], far_kv[1:])]
     own_kv_x, first_x, near_x, second_x = (

time: 30.1 us -> 30.1 us (level)
  no operation moved by 1% of the time
where the time goes in v23:
time: 30.1 us; the launch traced here: 29.8 us
  starting transfers between devices  20.7 us (69%)
  waiting for transfers between devices  5.31 us (18%)
  Pallas kernels  3.79 us (13%)
    ppermute x8, starting transfers between devices, to_block(): return lax.ppermute(array, 'blk', [(i, i ^ s) for i in range(blocks)])  15.5 us
    ppermute x4, starting transfers between devices, to_column(): lax.ppermute(array, 'uly', [(i, (i + t) % columns_of) for i in range(colu...  5.2 us
    ppermute x8, waiting for transfers between devices, to_block(): return lax.ppermute(array, 'blk', [(i, i ^ s) for i in range(blocks)])  2.99 us
    ppermute x4, waiting for transfers between devices, to_column(): lax.ppermute(array, 'uly', [(i, (i + t) % columns_of) for i in range(colu...  2.32 us
    pallas_call x2, Pallas kernels, pack(): pl.pallas_call(functools.partial(pack_kernel, cut, part), out_shape=[jax....  1.94 us
    pallas_call x2, Pallas kernels, attend(): pl.pallas_call(functools.partial(attend_kernel, len(holders), keys, query...  1.13 us
    pallas_call x1, Pallas kernels, local_blocks(): pl.pallas_call(functools.partial(unpack_kernel, order, part), out_shape=j...  0.7 us
  transfers between devices with their start and end apart: 12, of which 6 were waited for; matrix products, arithmetic and copies ran while one was open for 0% of the time, Pallas kernels for 7%

profile of v23, /device:TPU:0, one launch (start us, length us, event | category | flops | bytes accessed | tf_op | source)
XLA Modules:
  0.0 29.8 jit_solution(17566566782237009277)
XLA Ops:
  0.0 1.1 %pack.2 = (bf16[64,768]{1,0:T(8,128)(2,1)S(1)}, bf16[64,768]{1,0:T(8,128)(2,1)S(1)}, bf16[64,1152]{1,0:T(8,128)(2,1)S(1)}, bf16[64,768]{1,0:T(8,128)(2,1)S(1)}) custom-call(bf16[1,64,1536]{2,1,0:T(8,128)(2,1)} %q_ref.3, bf16[1,64,1536]{2,1,0:T(8,128)(2,1)} %k_ref.3, bf16[1,64,1536]{2,1,0:T(8,128)(2,1)} %v_ref.3), custom_call_target="tpu_custom_call" | custom-call | bytes 884736 | tf_op jit(solution)/shard_map/pack/pallas_call | solution.py:211
  1.1 5.1 %collective-permute-start.1 = (bf16[64,768]{1,0:T(8,128)(2,1)S(1)}, bf16[64,768]{1,0:T(8,128)(2,1)S(1)}, u32[]{:S(2)}, u32[]{:S(2)}) collective-permute-start(bf16[64,768]{1,0:T(8,128)(2,1)S(1)} %get-tuple-element.17), channel_id=1, source_target_pairs={{0,12},{4,8},{8,4},{12,0},{1,13},{5,9},{9,5},{13,1},{2,14},{6,10},... | collective-permute-start | bytes 294920 | tf_op jit(solution)/shard_map/ppermute | solution.py:229
  6.2 0.0 collective-permute-start
  6.2 0.6 %collective-permute-start.2 = (bf16[64,768]{1,0:T(8,128)(2,1)S(1)}, bf16[64,768]{1,0:T(8,128)(2,1)S(1)}, u32[]{:S(2)}, u32[]{:S(2)}) collective-permute-start(bf16[64,768]{1,0:T(8,128)(2,1)S(1)} %get-tuple-element.18), channel_id=1, source_target_pairs={{0,8},{4,12},{8,0},{12,4},{1,9},{5,13},{9,1},{13,5},{2,10},{6,14},... | collective-permute-start | bytes 294920 | tf_op jit(solution)/shard_map/ppermute | solution.py:229
  6.8 1.6 %collective-permute-start.3 = (bf16[64,768]{1,0:T(8,128)(2,1)S(1)}, bf16[64,768]{1,0:T(8,128)(2,1)S(1)}, u32[]{:S(2)}, u32[]{:S(2)}) collective-permute-start(bf16[64,768]{1,0:T(8,128)(2,1)S(1)} %get-tuple-element.16.refs_1_), channel_id=1, source_target_pairs={{0,2},{2,0},{1,3},{3,1},{4,6},{6,4},{5,7},{7,5},{8,10},{10,8},{9,1... | collective-permute-start | bytes 294920 | tf_op jit(solution)/shard_map/ppermute | solution.py:232
  8.5 0.9 %pack.3 = (bf16[64,384]{1,0:T(8,128)(2,1)S(1)}, bf16[64,384]{1,0:T(8,128)(2,1)S(1)}, bf16[64,384]{1,0:T(8,128)(2,1)S(1)}) custom-call(bf16[1,64,1536]{2,1,0:T(8,128)(2,1)} %q_ref.3, bf16[1,64,1536]{2,1,0:T(8,128)(2,1)} %k_ref.3, bf16[1,64,1536]{2,1,0:T(8,128)(2,1)} %v_ref.3), custom_call_target="tpu_custom_call" | custom-call | bytes 294912 | tf_op jit(solution)/shard_map/pack/pallas_call | solution.py:211
  9.3 3.7 %collective-permute-start.7 = (bf16[64,384]{1,0:T(8,128)(2,1)S(1)}, bf16[64,384]{1,0:T(8,128)(2,1)S(1)}, u32[]{:S(2)}, u32[]{:S(2)}) collective-permute-start(bf16[64,384]{1,0:T(8,128)(2,1)S(1)} %get-tuple-element.20), channel_id=1, source_target_pairs={{0,12},{4,8},{8,4},{12,0},{1,13},{5,9},{9,5},{13,1},{2,14},{6,10},... | collective-permute-start | bytes 147464 | tf_op jit(solution)/shard_map/ppermute | solution.py:229
  13.0 0.0 collective-permute-done.1.refs_0_
  13.0 0.5 %collective-permute-start.4 = (bf16[64,768]{1,0:T(8,128)(2,1)S(1)}, bf16[64,768]{1,0:T(8,128)(2,1)S(1)}, u32[]{:S(2)}, u32[]{:S(2)}) collective-permute-start(bf16[64,768]{1,0:T(8,128)(2,1)S(1)} %hold.9.refs_1_.refs_2_), channel_id=1, source_target_pairs={{0,2},{2,0},{1,3},{3,1},{4,6},{6,4},{5,7},{7,5},{8,10},{10,8},{9,1... | collective-permute-start | bytes 294920 | tf_op jit(solution)/shard_map/ppermute | solution.py:232
  13.6 0.9 %collective-permute-done.refs_0_.refs_1_ = bf16[64,1152]{1,0:T(8,128)(2,1)S(1)} collective-permute-done((bf16[64,1152]{1,0:T(8,128)(2,1)S(1)}, bf16[64,1152]{1,0:T(8,128)(2,1)S(1)}, u32[]{:S(2)}, u32[]{:S(2)}) %collective-permute-start) | collective-permute-done | bytes 147488 | tf_op jit(solution)/shard_map/ppermute | solution.py:229
  14.5 1.8 %collective-permute-start.5 = (bf16[64,768]{1,0:T(8,128)(2,1)S(1)}, bf16[64,768]{1,0:T(8,128)(2,1)S(1)}, u32[]{:S(2)}, u32[]{:S(2)}) collective-permute-start(bf16[64,768]{1,0:T(8,128)(2,1)S(1)} %bitcast.1), channel_id=1, source_target_pairs={{0,2},{2,0},{1,3},{3,1},{4,6},{6,4},{5,7},{7,5},{8,10},{10,8},{9,1... | collective-permute-start | bytes 294920 | tf_op jit(solution)/shard_map/ppermute | solution.py:232
  16.3 0.0 collective-permute-done.2.refs_0_
  16.3 1.2 %collective-permute-start.6 = (bf16[64,768]{1,0:T(8,128)(2,1)S(1)}, bf16[64,768]{1,0:T(8,128)(2,1)S(1)}, u32[]{:S(2)}, u32[]{:S(2)}) collective-permute-start(bf16[64,768]{1,0:T(8,128)(2,1)S(1)} %hold.10.refs_3_.refs_1_), channel_id=1, source_target_pairs={{0,2},{2,0},{1,3},{3,1},{4,6},{6,4},{5,7},{7,5},{8,10},{10,8},{9,1... | collective-permute-start | bytes 294920 | tf_op jit(solution)/shard_map/ppermute | solution.py:232
  17.5 0.0 collective-permute-done.3.refs_0_
  17.5 1.5 %collective-permute-start.9 = (bf16[64,384]{1,0:T(8,128)(2,1)S(1)}, bf16[64,384]{1,0:T(8,128)(2,1)S(1)}, u32[]{:S(2)}, u32[]{:S(2)}) collective-permute-start(bf16[64,384]{1,0:T(8,128)(2,1)S(1)} %hold.15), channel_id=1, source_target_pairs={{0,8},{4,12},{8,0},{12,4},{1,9},{5,13},{9,1},{13,5},{2,10},{6,14},... | collective-permute-start | bytes 147464 | tf_op jit(solution)/shard_map/ppermute | solution.py:229
  19.1 0.0 collective-permute-done.7.refs_0_
  19.1 0.0 collective-permute-done.4.refs_2_.refs_5_
  19.1 1.3 %collective-permute-done.5.refs_3_.refs_6_ = bf16[64,768]{1,0:T(8,128)(2,1)S(1)} collective-permute-done((bf16[64,768]{1,0:T(8,128)(2,1)S(1)}, bf16[64,768]{1,0:T(8,128)(2,1)S(1)}, u32[]{:S(2)}, u32[]{:S(2)}) %collective-permute-start.5) | collective-permute-done | bytes 98336 | tf_op jit(solution)/shard_map/ppermute | solution.py:232
  20.4 1.1 %collective-permute-done.6.refs_7_ = bf16[64,768]{1,0:T(8,128)(2,1)S(1)} collective-permute-done((bf16[64,768]{1,0:T(8,128)(2,1)S(1)}, bf16[64,768]{1,0:T(8,128)(2,1)S(1)}, u32[]{:S(2)}, u32[]{:S(2)}) %collective-permute-start.6) | collective-permute-done | bytes 98336 | tf_op jit(solution)/shard_map/ppermute | solution.py:232
  21.4 0.6 %attend.2 = (bf16[64,384]{1,0:T(8,128)(2,1)S(1)}, bf16[64,384]{1,0:T(8,128)(2,1)S(1)}, bf16[64,384]{1,0:T(8,128)(2,1)S(1)}) custom-call(bf16[64,1152]{1,0:T(8,128)(2,1)S(1)} %collective-permute-done.refs_0_.refs_1_, bf16[64,768]{1,0:T(8,128)(2,1)S(1)} %get-tuple-element.16.refs_1_, bf16[64,768]{1,0:T(8,128)(2,1)S(1)} %hold.9.refs_1_.refs_2_, ...), custom_call_target="tpu_custom_call" | custom-call | flops 150994944 | bytes 1081344 | tf_op jit(solution)/shard_map/attend/pallas_call | solution.py:257
  22.0 0.9 %collective-permute-start.8 = (bf16[64,384]{1,0:T(8,128)(2,1)S(1)}, bf16[64,384]{1,0:T(8,128)(2,1)S(1)}, u32[]{:S(2)}, u32[]{:S(2)}) collective-permute-start(bf16[64,384]{1,0:T(8,128)(2,1)S(1)} %get-tuple-element.22), channel_id=1, source_target_pairs={{0,12},{4,8},{8,4},{12,0},{1,13},{5,9},{9,5},{13,1},{2,14},{6,10},... | collective-permute-start | bytes 147464 | tf_op jit(solution)/shard_map/ppermute | solution.py:229
  23.0 0.0 collective-permute-done.9.refs_0_
  23.0 0.5 %attend.3.refs_1_ = bf16[64,384]{1,0:T(8,128)(2,1)S(1)} custom-call(bf16[64,1152]{1,0:T(8,128)(2,1)S(1)} %collective-permute-done.refs_0_.refs_1_, bf16[64,768]{1,0:T(8,128)(2,1)S(1)} %get-tuple-element.16.refs_1_, bf16[64,768]{1,0:T(8,128)(2,1)S(1)} %hold.9.refs_1_.refs_2_, bf16[64,768]{1,0:T(8,128)(2,1)S(1)} %hold.10.refs_3_.refs_1_, ...), custom_call_target="tpu_custom_call" | custom-call | flops 50331648 | bytes 884736 | tf_op jit(solution)/shard_map/attend/pallas_call | solution.py:257
  23.5 0.5 %collective-permute-start.11 = (bf16[64,384]{1,0:T(8,128)(2,1)S(1)}, bf16[64,384]{1,0:T(8,128)(2,1)S(1)}, u32[]{:S(2)}, u32[]{:S(2)}) collective-permute-start(bf16[64,384]{1,0:T(8,128)(2,1)S(1)} %hold.17), channel_id=1, source_target_pairs={{0,4},{4,0},{8,12},{12,8},{1,5},{5,1},{9,13},{13,9},{2,6},{6,2},{1... | collective-permute-start | bytes 147464 | tf_op jit(solution)/shard_map/ppermute | solution.py:229
  24.0 3.1 %collective-permute-start.10 = (bf16[64,384]{1,0:T(8,128)(2,1)S(1)}, bf16[64,384]{1,0:T(8,128)(2,1)S(1)}, u32[]{:S(2)}, u32[]{:S(2)}) collective-permute-start(bf16[64,384]{1,0:T(8,128)(2,1)S(1)} %attend.3.refs_1_), channel_id=1, source_target_pairs={{0,8},{4,12},{8,0},{12,4},{1,9},{5,13},{9,1},{13,5},{2,10},{6,14},... | collective-permute-start | bytes 147464 | tf_op jit(solution)/shard_map/ppermute | solution.py:229
  27.1 1.0 %collective-permute-done.8.refs_0_ = bf16[64,384]{1,0:T(8,128)(2,1)S(1)} collective-permute-done((bf16[64,384]{1,0:T(8,128)(2,1)S(1)}, bf16[64,384]{1,0:T(8,128)(2,1)S(1)}, u32[]{:S(2)}, u32[]{:S(2)}) %collective-permute-start.8) | collective-permute-done | bytes 49184 | tf_op jit(solution)/shard_map/ppermute | solution.py:229
  28.1 0.1 collective-permute-done.11.refs_3_
  28.2 1.0 %collective-permute-done.10.refs_2_ = bf16[64,384]{1,0:T(8,128)(2,1)S(1)} collective-permute-done((bf16[64,384]{1,0:T(8,128)(2,1)S(1)}, bf16[64,384]{1,0:T(8,128)(2,1)S(1)}, u32[]{:S(2)}, u32[]{:S(2)}) %collective-permute-start.10) | collective-permute-done | bytes 49184 | tf_op jit(solution)/shard_map/ppermute | solution.py:229
  29.1 0.7 %unpack.1 = bf16[1,64,1536]{2,1,0:T(8,128)(2,1)} custom-call(bf16[64,384]{1,0:T(8,128)(2,1)S(1)} %get-tuple-element.21.refs_1_.refs_0_, bf16[64,384]{1,0:T(8,128)(2,1)S(1)} %hold.14.refs_1_, bf16[64,384]{1,0:T(8,128)(2,1)S(1)} %collective-permute-done.10.refs_2_, bf16[64,384]{1,0:T(8,128)(2,1)S(1)} %collective-permute-done.11.refs_3_), custom_call_target="tpu_custom_call" | custom-call | bytes 393216 | tf_op jit(solution)/shard_map/unpack/pallas_call | solution.py:281
  (11 shorter events, 0.0 us)
Async XLA Ops:
  1.1 11.9 %collective-permute-start.1 = (bf16[64,768]{1,0:T(8,128)(2,1)S(1)}, bf16[64,768]{1,0:T(8,128)(2,1)S(1)}, u32[]{:S(2)}, u32[]{:S(2)}) collective-permute-start(bf16[64,768]{1,0:T(8,128)(2,1)S(1)} %get-tuple-element.17), channel_id=1, source_target_pairs={{0,12},{4,8},{8,4},{12,0},{1,13},{5,9},{9,5},{13,1},{2,14},{6,10},... | collective-permute-start | bytes 294920 | tf_op jit(solution)/shard_map/ppermute | solution.py:229
  6.2 8.3 %collective-permute-start = (bf16[64,1152]{1,0:T(8,128)(2,1)S(1)}, bf16[64,1152]{1,0:T(8,128)(2,1)S(1)}, u32[]{:S(2)}, u32[]{:S(2)}) collective-permute-start(bf16[64,1152]{1,0:T(8,128)(2,1)S(1)} %get-tuple-element.15), channel_id=1, source_target_pairs={{0,4},{4,0},{8,12},{12,8},{1,5},{5,1},{9,13},{13,9},{2,6},{6,2},{1... | collective-permute-start | bytes 442376 | tf_op jit(solution)/shard_map/ppermute | solution.py:229
  6.2 10.1 %collective-permute-start.2 = (bf16[64,768]{1,0:T(8,128)(2,1)S(1)}, bf16[64,768]{1,0:T(8,128)(2,1)S(1)}, u32[]{:S(2)}, u32[]{:S(2)}) collective-permute-start(bf16[64,768]{1,0:T(8,128)(2,1)S(1)} %get-tuple-element.18), channel_id=1, source_target_pairs={{0,8},{4,12},{8,0},{12,4},{1,9},{5,13},{9,1},{13,5},{2,10},{6,14},... | collective-permute-start | bytes 294920 | tf_op jit(solution)/shard_map/ppermute | solution.py:229
  6.8 10.7 %collective-permute-start.3 = (bf16[64,768]{1,0:T(8,128)(2,1)S(1)}, bf16[64,768]{1,0:T(8,128)(2,1)S(1)}, u32[]{:S(2)}, u32[]{:S(2)}) collective-permute-start(bf16[64,768]{1,0:T(8,128)(2,1)S(1)} %get-tuple-element.16.refs_1_), channel_id=1, source_target_pairs={{0,2},{2,0},{1,3},{3,1},{4,6},{6,4},{5,7},{7,5},{8,10},{10,8},{9,1... | collective-permute-start | bytes 294920 | tf_op jit(solution)/shard_map/ppermute | solution.py:232
  9.3 9.7 %collective-permute-start.7 = (bf16[64,384]{1,0:T(8,128)(2,1)S(1)}, bf16[64,384]{1,0:T(8,128)(2,1)S(1)}, u32[]{:S(2)}, u32[]{:S(2)}) collective-permute-start(bf16[64,384]{1,0:T(8,128)(2,1)S(1)} %get-tuple-element.20), channel_id=1, source_target_pairs={{0,12},{4,8},{8,4},{12,0},{1,13},{5,9},{9,5},{13,1},{2,14},{6,10},... | collective-permute-start | bytes 147464 | tf_op jit(solution)/shard_map/ppermute | solution.py:229
  13.0 6.1 %collective-permute-start.4 = (bf16[64,768]{1,0:T(8,128)(2,1)S(1)}, bf16[64,768]{1,0:T(8,128)(2,1)S(1)}, u32[]{:S(2)}, u32[]{:S(2)}) collective-permute-start(bf16[64,768]{1,0:T(8,128)(2,1)S(1)} %hold.9.refs_1_.refs_2_), channel_id=1, source_target_pairs={{0,2},{2,0},{1,3},{3,1},{4,6},{6,4},{5,7},{7,5},{8,10},{10,8},{9,1... | collective-permute-start | bytes 294920 | tf_op jit(solution)/shard_map/ppermute | solution.py:232
  14.5 5.9 %collective-permute-start.5 = (bf16[64,768]{1,0:T(8,128)(2,1)S(1)}, bf16[64,768]{1,0:T(8,128)(2,1)S(1)}, u32[]{:S(2)}, u32[]{:S(2)}) collective-permute-start(bf16[64,768]{1,0:T(8,128)(2,1)S(1)} %bitcast.1), channel_id=1, source_target_pairs={{0,2},{2,0},{1,3},{3,1},{4,6},{6,4},{5,7},{7,5},{8,10},{10,8},{9,1... | collective-permute-start | bytes 294920 | tf_op jit(solution)/shard_map/ppermute | solution.py:232
  16.3 5.1 %collective-permute-start.6 = (bf16[64,768]{1,0:T(8,128)(2,1)S(1)}, bf16[64,768]{1,0:T(8,128)(2,1)S(1)}, u32[]{:S(2)}, u32[]{:S(2)}) collective-permute-start(bf16[64,768]{1,0:T(8,128)(2,1)S(1)} %hold.10.refs_3_.refs_1_), channel_id=1, source_target_pairs={{0,2},{2,0},{1,3},{3,1},{4,6},{6,4},{5,7},{7,5},{8,10},{10,8},{9,1... | collective-permute-start | bytes 294920 | tf_op jit(solution)/shard_map/ppermute | solution.py:232
  17.5 5.4 %collective-permute-start.9 = (bf16[64,384]{1,0:T(8,128)(2,1)S(1)}, bf16[64,384]{1,0:T(8,128)(2,1)S(1)}, u32[]{:S(2)}, u32[]{:S(2)}) collective-permute-start(bf16[64,384]{1,0:T(8,128)(2,1)S(1)} %hold.15), channel_id=1, source_target_pairs={{0,8},{4,12},{8,0},{12,4},{1,9},{5,13},{9,1},{13,5},{2,10},{6,14},... | collective-permute-start | bytes 147464 | tf_op jit(solution)/shard_map/ppermute | solution.py:229
  22.0 6.0 %collective-permute-start.8 = (bf16[64,384]{1,0:T(8,128)(2,1)S(1)}, bf16[64,384]{1,0:T(8,128)(2,1)S(1)}, u32[]{:S(2)}, u32[]{:S(2)}) collective-permute-start(bf16[64,384]{1,0:T(8,128)(2,1)S(1)} %get-tuple-element.22), channel_id=1, source_target_pairs={{0,12},{4,8},{8,4},{12,0},{1,13},{5,9},{9,5},{13,1},{2,14},{6,10},... | collective-permute-start | bytes 147464 | tf_op jit(solution)/shard_map/ppermute | solution.py:229
  23.5 4.7 %collective-permute-start.11 = (bf16[64,384]{1,0:T(8,128)(2,1)S(1)}, bf16[64,384]{1,0:T(8,128)(2,1)S(1)}, u32[]{:S(2)}, u32[]{:S(2)}) collective-permute-start(bf16[64,384]{1,0:T(8,128)(2,1)S(1)} %hold.17), channel_id=1, source_target_pairs={{0,4},{4,0},{8,12},{12,8},{1,5},{5,1},{9,13},{13,9},{2,6},{6,2},{1... | collective-permute-start | bytes 147464 | tf_op jit(solution)/shard_map/ppermute | solution.py:229
  24.0 5.1 %collective-permute-start.10 = (bf16[64,384]{1,0:T(8,128)(2,1)S(1)}, bf16[64,384]{1,0:T(8,128)(2,1)S(1)}, u32[]{:S(2)}, u32[]{:S(2)}) collective-permute-start(bf16[64,384]{1,0:T(8,128)(2,1)S(1)} %attend.3.refs_1_), channel_id=1, source_target_pairs={{0,8},{4,12},{8,0},{12,4},{1,9},{5,13},{9,1},{13,5},{2,10},{6,14},... | collective-permute-start | bytes 147464 | tf_op jit(solution)/shard_map/ppermute | solution.py:229

commit v24 on v23

--- a/solution.py
+++ b/solution.py
@@ -202,7 +202,7 @@
     far = list(range(blocks - 1, 1, -1))
 
     kv, q = (("k", 0, part), ("v", 0, part)), (("q", 0, part),)
-    messages = [(s, kv) for s in far] + [(1, kv + q), (0, kv)] + [(s, q) for s in far + [0]]
+    messages = [(far[0], kv), (1, kv + q), (0, kv), (far[1], kv)] + [(s, q) for s in far + [0]]
     inputs = [pltpu.with_memory_space_constraint(x, pltpu.HBM) for x in (query_rows, key_rows, value_rows)]
 
     def pack(cut):
@@ -222,7 +222,7 @@
             name="pack",
         )(*inputs)
 
-    first = len(far) + 2
+    first = 3
     packed = [*pack(messages[:first]), *pack(messages[first:])]
 
     def to_block(array, s):

time: 30.1 us -> 29.9 us (level)
    ppermute x4, waiting for transfers between devices: 2.32 us -> 1.85 us  [to_column(): lax.ppermute(array, 'uly', [(i, (i + t) % columns_of) for i in range(colu...]
    ppermute x8, waiting for transfers between devices: 2.99 us -> 3.3 us  [to_block(): return lax.ppermute(array, 'blk', [(i, i ^ s) for i in range(blocks)])]
  transfers between devices with their start and end apart: 12 -> 12, of which waited for: 6 -> 7; matrix products, arithmetic and copies ran while one was open for 0% -> 0% of each run, Pallas kernels for 7% -> 7%
where the time goes in v24:
time: 29.9 us; the launch traced here: 29.7 us
  starting transfers between devices  20.6 us (69%)
  waiting for transfers between devices  5.16 us (17%)
  Pallas kernels  3.79 us (13%)
    ppermute x8, starting transfers between devices, to_block(): return lax.ppermute(array, 'blk', [(i, i ^ s) for i in range(blocks)])  15.4 us
    ppermute x4, starting transfers between devices, to_column(): lax.ppermute(array, 'uly', [(i, (i + t) % columns_of) for i in range(colu...  5.23 us
    ppermute x8, waiting for transfers between devices, to_block(): return lax.ppermute(array, 'blk', [(i, i ^ s) for i in range(blocks)])  3.3 us
    pallas_call x2, Pallas kernels, pack(): pl.pallas_call(functools.partial(pack_kernel, cut, part), out_shape=[jax....  1.94 us
    ppermute x4, waiting for transfers between devices, to_column(): lax.ppermute(array, 'uly', [(i, (i + t) % columns_of) for i in range(colu...  1.85 us
    pallas_call x2, Pallas kernels, attend(): pl.pallas_call(functools.partial(attend_kernel, len(holders), keys, query...  1.13 us
    pallas_call x1, Pallas kernels, local_blocks(): pl.pallas_call(functools.partial(unpack_kernel, order, part), out_shape=j...  0.7 us
  transfers between devices with their start and end apart: 12, of which 7 were waited for; matrix products, arithmetic and copies ran while one was open for 0% of the time, Pallas kernels for 7%

profile of v24, /device:TPU:0, one launch (start us, length us, event | category | flops | bytes accessed | tf_op | source)
XLA Modules:
  0.0 29.7 jit_solution(17005587444954903664)
XLA Ops:
  0.0 1.0 %pack.2 = (bf16[64,768]{1,0:T(8,128)(2,1)S(1)}, bf16[64,1152]{1,0:T(8,128)(2,1)S(1)}, bf16[64,768]{1,0:T(8,128)(2,1)S(1)}) custom-call(bf16[1,64,1536]{2,1,0:T(8,128)(2,1)} %q_ref.3, bf16[1,64,1536]{2,1,0:T(8,128)(2,1)} %k_ref.3, bf16[1,64,1536]{2,1,0:T(8,128)(2,1)} %v_ref.3), custom_call_target="tpu_custom_call" | custom-call | bytes 688128 | tf_op jit(solution)/shard_map/pack/pallas_call | solution.py:211
  1.0 5.1 %collective-permute-start.1 = (bf16[64,768]{1,0:T(8,128)(2,1)S(1)}, bf16[64,768]{1,0:T(8,128)(2,1)S(1)}, u32[]{:S(2)}, u32[]{:S(2)}) collective-permute-start(bf16[64,768]{1,0:T(8,128)(2,1)S(1)} %get-tuple-element.17), channel_id=1, source_target_pairs={{0,12},{4,8},{8,4},{12,0},{1,13},{5,9},{9,5},{13,1},{2,14},{6,10},... | collective-permute-start | bytes 294920 | tf_op jit(solution)/shard_map/ppermute | solution.py:229
  6.1 0.0 collective-permute-start
  6.1 0.9 %pack.3 = (bf16[64,768]{1,0:T(8,128)(2,1)S(1)}, bf16[64,384]{1,0:T(8,128)(2,1)S(1)}, bf16[64,384]{1,0:T(8,128)(2,1)S(1)}, bf16[64,384]{1,0:T(8,128)(2,1)S(1)}) custom-call(bf16[1,64,1536]{2,1,0:T(8,128)(2,1)} %q_ref.3, bf16[1,64,1536]{2,1,0:T(8,128)(2,1)} %k_ref.3, bf16[1,64,1536]{2,1,0:T(8,128)(2,1)} %v_ref.3), custom_call_target="tpu_custom_call" | custom-call | bytes 491520 | tf_op jit(solution)/shard_map/pack/pallas_call | solution.py:211
  7.1 0.7 %collective-permute-start.2 = (bf16[64,768]{1,0:T(8,128)(2,1)S(1)}, bf16[64,768]{1,0:T(8,128)(2,1)S(1)}, u32[]{:S(2)}, u32[]{:S(2)}) collective-permute-start(bf16[64,768]{1,0:T(8,128)(2,1)S(1)} %get-tuple-element.18), channel_id=1, source_target_pairs={{0,8},{4,12},{8,0},{12,4},{1,9},{5,13},{9,1},{13,5},{2,10},{6,14},... | collective-permute-start | bytes 294920 | tf_op jit(solution)/shard_map/ppermute | solution.py:229
  7.8 1.6 %collective-permute-start.3 = (bf16[64,768]{1,0:T(8,128)(2,1)S(1)}, bf16[64,768]{1,0:T(8,128)(2,1)S(1)}, u32[]{:S(2)}, u32[]{:S(2)}) collective-permute-start(bf16[64,768]{1,0:T(8,128)(2,1)S(1)} %get-tuple-element.16.refs_1_), channel_id=1, source_target_pairs={{0,2},{2,0},{1,3},{3,1},{4,6},{6,4},{5,7},{7,5},{8,10},{10,8},{9,1... | collective-permute-start | bytes 294920 | tf_op jit(solution)/shard_map/ppermute | solution.py:232
  9.4 3.6 %collective-permute-start.7 = (bf16[64,384]{1,0:T(8,128)(2,1)S(1)}, bf16[64,384]{1,0:T(8,128)(2,1)S(1)}, u32[]{:S(2)}, u32[]{:S(2)}) collective-permute-start(bf16[64,384]{1,0:T(8,128)(2,1)S(1)} %get-tuple-element.20), channel_id=1, source_target_pairs={{0,12},{4,8},{8,4},{12,0},{1,13},{5,9},{9,5},{13,1},{2,14},{6,10},... | collective-permute-start | bytes 147464 | tf_op jit(solution)/shard_map/ppermute | solution.py:229
  13.0 0.0 collective-permute-done.1.refs_0_
  13.0 0.5 %collective-permute-start.4 = (bf16[64,768]{1,0:T(8,128)(2,1)S(1)}, bf16[64,768]{1,0:T(8,128)(2,1)S(1)}, u32[]{:S(2)}, u32[]{:S(2)}) collective-permute-start(bf16[64,768]{1,0:T(8,128)(2,1)S(1)} %hold.9.refs_1_.refs_2_), channel_id=1, source_target_pairs={{0,2},{2,0},{1,3},{3,1},{4,6},{6,4},{5,7},{7,5},{8,10},{10,8},{9,1... | collective-permute-start | bytes 294920 | tf_op jit(solution)/shard_map/ppermute | solution.py:232
  13.6 0.4 %collective-permute-done.refs_0_.refs_1_ = bf16[64,1152]{1,0:T(8,128)(2,1)S(1)} collective-permute-done((bf16[64,1152]{1,0:T(8,128)(2,1)S(1)}, bf16[64,1152]{1,0:T(8,128)(2,1)S(1)}, u32[]{:S(2)}, u32[]{:S(2)}) %collective-permute-start) | collective-permute-done | bytes 147488 | tf_op jit(solution)/shard_map/ppermute | solution.py:229
  14.0 1.8 %collective-permute-start.5 = (bf16[64,768]{1,0:T(8,128)(2,1)S(1)}, bf16[64,768]{1,0:T(8,128)(2,1)S(1)}, u32[]{:S(2)}, u32[]{:S(2)}) collective-permute-start(bf16[64,768]{1,0:T(8,128)(2,1)S(1)} %bitcast.1), channel_id=1, source_target_pairs={{0,2},{2,0},{1,3},{3,1},{4,6},{6,4},{5,7},{7,5},{8,10},{10,8},{9,1... | collective-permute-start | bytes 294920 | tf_op jit(solution)/shard_map/ppermute | solution.py:232
  15.8 0.5 %collective-permute-done.2.refs_0_ = bf16[64,768]{1,0:T(8,128)(2,1)S(1)} collective-permute-done((bf16[64,768]{1,0:T(8,128)(2,1)S(1)}, bf16[64,768]{1,0:T(8,128)(2,1)S(1)}, u32[]{:S(2)}, u32[]{:S(2)}) %collective-permute-start.2) | collective-permute-done | bytes 98336 | tf_op jit(solution)/shard_map/ppermute | solution.py:229
  16.3 1.3 %collective-permute-start.6 = (bf16[64,768]{1,0:T(8,128)(2,1)S(1)}, bf16[64,768]{1,0:T(8,128)(2,1)S(1)}, u32[]{:S(2)}, u32[]{:S(2)}) collective-permute-start(bf16[64,768]{1,0:T(8,128)(2,1)S(1)} %hold.10.refs_3_.refs_1_), channel_id=1, source_target_pairs={{0,2},{2,0},{1,3},{3,1},{4,6},{6,4},{5,7},{7,5},{8,10},{10,8},{9,1... | collective-permute-start | bytes 294920 | tf_op jit(solution)/shard_map/ppermute | solution.py:232
  17.5 0.0 collective-permute-done.3.refs_0_
  17.5 1.5 %collective-permute-start.9 = (bf16[64,384]{1,0:T(8,128)(2,1)S(1)}, bf16[64,384]{1,0:T(8,128)(2,1)S(1)}, u32[]{:S(2)}, u32[]{:S(2)}) collective-permute-start(bf16[64,384]{1,0:T(8,128)(2,1)S(1)} %hold.15), channel_id=1, source_target_pairs={{0,8},{4,12},{8,0},{12,4},{1,9},{5,13},{9,1},{13,5},{2,10},{6,14},... | collective-permute-start | bytes 147464 | tf_op jit(solution)/shard_map/ppermute | solution.py:229
  19.0 0.0 collective-permute-done.7.refs_0_
  19.0 0.0 collective-permute-done.4.refs_2_.refs_5_
  19.0 0.8 %collective-permute-done.5.refs_3_.refs_6_ = bf16[64,768]{1,0:T(8,128)(2,1)S(1)} collective-permute-done((bf16[64,768]{1,0:T(8,128)(2,1)S(1)}, bf16[64,768]{1,0:T(8,128)(2,1)S(1)}, u32[]{:S(2)}, u32[]{:S(2)}) %collective-permute-start.5) | collective-permute-done | bytes 98336 | tf_op jit(solution)/shard_map/ppermute | solution.py:232
  19.8 1.1 %collective-permute-done.6.refs_7_ = bf16[64,768]{1,0:T(8,128)(2,1)S(1)} collective-permute-done((bf16[64,768]{1,0:T(8,128)(2,1)S(1)}, bf16[64,768]{1,0:T(8,128)(2,1)S(1)}, u32[]{:S(2)}, u32[]{:S(2)}) %collective-permute-start.6) | collective-permute-done | bytes 98336 | tf_op jit(solution)/shard_map/ppermute | solution.py:232
  20.9 0.6 %attend.2 = (bf16[64,384]{1,0:T(8,128)(2,1)S(1)}, bf16[64,384]{1,0:T(8,128)(2,1)S(1)}, bf16[64,384]{1,0:T(8,128)(2,1)S(1)}) custom-call(bf16[64,1152]{1,0:T(8,128)(2,1)S(1)} %collective-permute-done.refs_0_.refs_1_, bf16[64,768]{1,0:T(8,128)(2,1)S(1)} %get-tuple-element.16.refs_1_, bf16[64,768]{1,0:T(8,128)(2,1)S(1)} %hold.9.refs_1_.refs_2_, ...), custom_call_target="tpu_custom_call" | custom-call | flops 150994944 | bytes 1081344 | tf_op jit(solution)/shard_map/attend/pallas_call | solution.py:257
  21.5 1.2 %collective-permute-start.8 = (bf16[64,384]{1,0:T(8,128)(2,1)S(1)}, bf16[64,384]{1,0:T(8,128)(2,1)S(1)}, u32[]{:S(2)}, u32[]{:S(2)}) collective-permute-start(bf16[64,384]{1,0:T(8,128)(2,1)S(1)} %get-tuple-element.22), channel_id=1, source_target_pairs={{0,12},{4,8},{8,4},{12,0},{1,13},{5,9},{9,5},{13,1},{2,14},{6,10},... | collective-permute-start | bytes 147464 | tf_op jit(solution)/shard_map/ppermute | solution.py:229
  22.8 0.0 collective-permute-done.9.refs_0_
  22.8 0.5 %attend.3.refs_1_ = bf16[64,384]{1,0:T(8,128)(2,1)S(1)} custom-call(bf16[64,1152]{1,0:T(8,128)(2,1)S(1)} %collective-permute-done.refs_0_.refs_1_, bf16[64,768]{1,0:T(8,128)(2,1)S(1)} %get-tuple-element.16.refs_1_, bf16[64,768]{1,0:T(8,128)(2,1)S(1)} %hold.9.refs_1_.refs_2_, bf16[64,768]{1,0:T(8,128)(2,1)S(1)} %hold.10.refs_3_.refs_1_, ...), custom_call_target="tpu_custom_call" | custom-call | flops 50331648 | bytes 884736 | tf_op jit(solution)/shard_map/attend/pallas_call | solution.py:257
  23.3 0.7 %collective-permute-start.11 = (bf16[64,384]{1,0:T(8,128)(2,1)S(1)}, bf16[64,384]{1,0:T(8,128)(2,1)S(1)}, u32[]{:S(2)}, u32[]{:S(2)}) collective-permute-start(bf16[64,384]{1,0:T(8,128)(2,1)S(1)} %hold.17), channel_id=1, source_target_pairs={{0,4},{4,0},{8,12},{12,8},{1,5},{5,1},{9,13},{13,9},{2,6},{6,2},{1... | collective-permute-start | bytes 147464 | tf_op jit(solution)/shard_map/ppermute | solution.py:229
  24.0 2.6 %collective-permute-start.10 = (bf16[64,384]{1,0:T(8,128)(2,1)S(1)}, bf16[64,384]{1,0:T(8,128)(2,1)S(1)}, u32[]{:S(2)}, u32[]{:S(2)}) collective-permute-start(bf16[64,384]{1,0:T(8,128)(2,1)S(1)} %attend.3.refs_1_), channel_id=1, source_target_pairs={{0,8},{4,12},{8,0},{12,4},{1,9},{5,13},{9,1},{13,5},{2,10},{6,14},... | collective-permute-start | bytes 147464 | tf_op jit(solution)/shard_map/ppermute | solution.py:229
  26.5 1.0 %collective-permute-done.8.refs_0_ = bf16[64,384]{1,0:T(8,128)(2,1)S(1)} collective-permute-done((bf16[64,384]{1,0:T(8,128)(2,1)S(1)}, bf16[64,384]{1,0:T(8,128)(2,1)S(1)}, u32[]{:S(2)}, u32[]{:S(2)}) %collective-permute-start.8) | collective-permute-done | bytes 49184 | tf_op jit(solution)/shard_map/ppermute | solution.py:229
  27.6 0.4 %collective-permute-done.11.refs_3_ = bf16[64,384]{1,0:T(8,128)(2,1)S(1)} collective-permute-done((bf16[64,384]{1,0:T(8,128)(2,1)S(1)}, bf16[64,384]{1,0:T(8,128)(2,1)S(1)}, u32[]{:S(2)}, u32[]{:S(2)}) %collective-permute-start.11) | collective-permute-done | bytes 49184 | tf_op jit(solution)/shard_map/ppermute | solution.py:229
  27.9 1.0 %collective-permute-done.10.refs_2_ = bf16[64,384]{1,0:T(8,128)(2,1)S(1)} collective-permute-done((bf16[64,384]{1,0:T(8,128)(2,1)S(1)}, bf16[64,384]{1,0:T(8,128)(2,1)S(1)}, u32[]{:S(2)}, u32[]{:S(2)}) %collective-permute-start.10) | collective-permute-done | bytes 49184 | tf_op jit(solution)/shard_map/ppermute | solution.py:229
  29.0 0.7 %unpack.1 = bf16[1,64,1536]{2,1,0:T(8,128)(2,1)} custom-call(bf16[64,384]{1,0:T(8,128)(2,1)S(1)} %get-tuple-element.21.refs_1_.refs_0_, bf16[64,384]{1,0:T(8,128)(2,1)S(1)} %hold.14.refs_1_, bf16[64,384]{1,0:T(8,128)(2,1)S(1)} %collective-permute-done.10.refs_2_, bf16[64,384]{1,0:T(8,128)(2,1)S(1)} %collective-permute-done.11.refs_3_), custom_call_target="tpu_custom_call" | custom-call | bytes 393216 | tf_op jit(solution)/shard_map/unpack/pallas_call | solution.py:281
  (11 shorter events, 0.0 us)
Async XLA Ops:
  1.0 12.0 %collective-permute-start.1 = (bf16[64,768]{1,0:T(8,128)(2,1)S(1)}, bf16[64,768]{1,0:T(8,128)(2,1)S(1)}, u32[]{:S(2)}, u32[]{:S(2)}) collective-permute-start(bf16[64,768]{1,0:T(8,128)(2,1)S(1)} %get-tuple-element.17), channel_id=1, source_target_pairs={{0,12},{4,8},{8,4},{12,0},{1,13},{5,9},{9,5},{13,1},{2,14},{6,10},... | collective-permute-start | bytes 294920 | tf_op jit(solution)/shard_map/ppermute | solution.py:229
  6.1 7.8 %collective-permute-start = (bf16[64,1152]{1,0:T(8,128)(2,1)S(1)}, bf16[64,1152]{1,0:T(8,128)(2,1)S(1)}, u32[]{:S(2)}, u32[]{:S(2)}) collective-permute-start(bf16[64,1152]{1,0:T(8,128)(2,1)S(1)} %get-tuple-element.15), channel_id=1, source_target_pairs={{0,4},{4,0},{8,12},{12,8},{1,5},{5,1},{9,13},{13,9},{2,6},{6,2},{1... | collective-permute-start | bytes 442376 | tf_op jit(solution)/shard_map/ppermute | solution.py:229
  7.1 9.2 %collective-permute-start.2 = (bf16[64,768]{1,0:T(8,128)(2,1)S(1)}, bf16[64,768]{1,0:T(8,128)(2,1)S(1)}, u32[]{:S(2)}, u32[]{:S(2)}) collective-permute-start(bf16[64,768]{1,0:T(8,128)(2,1)S(1)} %get-tuple-element.18), channel_id=1, source_target_pairs={{0,8},{4,12},{8,0},{12,4},{1,9},{5,13},{9,1},{13,5},{2,10},{6,14},... | collective-permute-start | bytes 294920 | tf_op jit(solution)/shard_map/ppermute | solution.py:229
  7.8 9.7 %collective-permute-start.3 = (bf16[64,768]{1,0:T(8,128)(2,1)S(1)}, bf16[64,768]{1,0:T(8,128)(2,1)S(1)}, u32[]{:S(2)}, u32[]{:S(2)}) collective-permute-start(bf16[64,768]{1,0:T(8,128)(2,1)S(1)} %get-tuple-element.16.refs_1_), channel_id=1, source_target_pairs={{0,2},{2,0},{1,3},{3,1},{4,6},{6,4},{5,7},{7,5},{8,10},{10,8},{9,1... | collective-permute-start | bytes 294920 | tf_op jit(solution)/shard_map/ppermute | solution.py:232
  9.4 9.6 %collective-permute-start.7 = (bf16[64,384]{1,0:T(8,128)(2,1)S(1)}, bf16[64,384]{1,0:T(8,128)(2,1)S(1)}, u32[]{:S(2)}, u32[]{:S(2)}) collective-permute-start(bf16[64,384]{1,0:T(8,128)(2,1)S(1)} %get-tuple-element.20), channel_id=1, source_target_pairs={{0,12},{4,8},{8,4},{12,0},{1,13},{5,9},{9,5},{13,1},{2,14},{6,10},... | collective-permute-start | bytes 147464 | tf_op jit(solution)/shard_map/ppermute | solution.py:229
  13.0 6.0 %collective-permute-start.4 = (bf16[64,768]{1,0:T(8,128)(2,1)S(1)}, bf16[64,768]{1,0:T(8,128)(2,1)S(1)}, u32[]{:S(2)}, u32[]{:S(2)}) collective-permute-start(bf16[64,768]{1,0:T(8,128)(2,1)S(1)} %hold.9.refs_1_.refs_2_), channel_id=1, source_target_pairs={{0,2},{2,0},{1,3},{3,1},{4,6},{6,4},{5,7},{7,5},{8,10},{10,8},{9,1... | collective-permute-start | bytes 294920 | tf_op jit(solution)/shard_map/ppermute | solution.py:232
  14.0 5.9 %collective-permute-start.5 = (bf16[64,768]{1,0:T(8,128)(2,1)S(1)}, bf16[64,768]{1,0:T(8,128)(2,1)S(1)}, u32[]{:S(2)}, u32[]{:S(2)}) collective-permute-start(bf16[64,768]{1,0:T(8,128)(2,1)S(1)} %bitcast.1), channel_id=1, source_target_pairs={{0,2},{2,0},{1,3},{3,1},{4,6},{6,4},{5,7},{7,5},{8,10},{10,8},{9,1... | collective-permute-start | bytes 294920 | tf_op jit(solution)/shard_map/ppermute | solution.py:232
  16.3 4.6 %collective-permute-start.6 = (bf16[64,768]{1,0:T(8,128)(2,1)S(1)}, bf16[64,768]{1,0:T(8,128)(2,1)S(1)}, u32[]{:S(2)}, u32[]{:S(2)}) collective-permute-start(bf16[64,768]{1,0:T(8,128)(2,1)S(1)} %hold.10.refs_3_.refs_1_), channel_id=1, source_target_pairs={{0,2},{2,0},{1,3},{3,1},{4,6},{6,4},{5,7},{7,5},{8,10},{10,8},{9,1... | collective-permute-start | bytes 294920 | tf_op jit(solution)/shard_map/ppermute | solution.py:232
  17.5 5.2 %collective-permute-start.9 = (bf16[64,384]{1,0:T(8,128)(2,1)S(1)}, bf16[64,384]{1,0:T(8,128)(2,1)S(1)}, u32[]{:S(2)}, u32[]{:S(2)}) collective-permute-start(bf16[64,384]{1,0:T(8,128)(2,1)S(1)} %hold.15), channel_id=1, source_target_pairs={{0,8},{4,12},{8,0},{12,4},{1,9},{5,13},{9,1},{13,5},{2,10},{6,14},... | collective-permute-start | bytes 147464 | tf_op jit(solution)/shard_map/ppermute | solution.py:229
  21.5 6.1 %collective-permute-start.8 = (bf16[64,384]{1,0:T(8,128)(2,1)S(1)}, bf16[64,384]{1,0:T(8,128)(2,1)S(1)}, u32[]{:S(2)}, u32[]{:S(2)}) collective-permute-start(bf16[64,384]{1,0:T(8,128)(2,1)S(1)} %get-tuple-element.22), channel_id=1, source_target_pairs={{0,12},{4,8},{8,4},{12,0},{1,13},{5,9},{9,5},{13,1},{2,14},{6,10},... | collective-permute-start | bytes 147464 | tf_op jit(solution)/shard_map/ppermute | solution.py:229
  23.3 4.7 %collective-permute-start.11 = (bf16[64,384]{1,0:T(8,128)(2,1)S(1)}, bf16[64,384]{1,0:T(8,128)(2,1)S(1)}, u32[]{:S(2)}, u32[]{:S(2)}) collective-permute-start(bf16[64,384]{1,0:T(8,128)(2,1)S(1)} %hold.17), channel_id=1, source_target_pairs={{0,4},{4,0},{8,12},{12,8},{1,5},{5,1},{9,13},{13,9},{2,6},{6,2},{1... | collective-permute-start | bytes 147464 | tf_op jit(solution)/shard_map/ppermute | solution.py:229
  24.0 5.0 %collective-permute-start.10 = (bf16[64,384]{1,0:T(8,128)(2,1)S(1)}, bf16[64,384]{1,0:T(8,128)(2,1)S(1)}, u32[]{:S(2)}, u32[]{:S(2)}) collective-permute-start(bf16[64,384]{1,0:T(8,128)(2,1)S(1)} %attend.3.refs_1_), channel_id=1, source_target_pairs={{0,8},{4,12},{8,0},{12,4},{1,9},{5,13},{9,1},{13,5},{2,10},{6,14},... | collective-permute-start | bytes 147464 | tf_op jit(solution)/shard_map/ppermute | solution.py:229

commit v25 on v24

--- a/solution.py
+++ b/solution.py
@@ -202,7 +202,7 @@
     far = list(range(blocks - 1, 1, -1))
 
     kv, q = (("k", 0, part), ("v", 0, part)), (("q", 0, part),)
-    messages = [(far[0], kv), (1, kv + q), (0, kv), (far[1], kv)] + [(s, q) for s in far + [0]]
+    messages = [(far[0], kv), (1, kv + q), (far[1], kv), (0, kv)] + [(s, q) for s in far + [0]]
     inputs = [pltpu.with_memory_space_constraint(x, pltpu.HBM) for x in (query_rows, key_rows, value_rows)]
 
     def pack(cut):
@@ -222,7 +222,7 @@
             name="pack",
         )(*inputs)
 
-    first = 3
+    first = 2
     packed = [*pack(messages[:first]), *pack(messages[first:])]
 
     def to_block(array, s):

time: 29.9 us -> 29.8 us (level)
  no operation moved by 1% of the time
where the time goes in v25:
time: 29.8 us; the launch traced here: 29.6 us
  starting transfers between devices  20.5 us (69%)
  waiting for transfers between devices  5.22 us (18%)
  Pallas kernels  3.79 us (13%)
    ppermute x8, starting transfers between devices, to_block(): return lax.ppermute(array, 'blk', [(i, i ^ s) for i in range(blocks)])  15.3 us
    ppermute x4, starting transfers between devices, to_column(): lax.ppermute(array, 'uly', [(i, (i + t) % columns_of) for i in range(colu...  5.16 us
    ppermute x8, waiting for transfers between devices, to_block(): return lax.ppermute(array, 'blk', [(i, i ^ s) for i in range(blocks)])  3.31 us
    pallas_call x2, Pallas kernels, pack(): pl.pallas_call(functools.partial(pack_kernel, cut, part), out_shape=[jax....  1.94 us
    ppermute x4, waiting for transfers between devices, to_column(): lax.ppermute(array, 'uly', [(i, (i + t) % columns_of) for i in range(colu...  1.91 us
    pallas_call x2, Pallas kernels, attend(): pl.pallas_call(functools.partial(attend_kernel, len(holders), keys, query...  1.13 us
    pallas_call x1, Pallas kernels, local_blocks(): pl.pallas_call(functools.partial(unpack_kernel, order, part), out_shape=j...  0.7 us
  transfers between devices with their start and end apart: 12, of which 7 were waited for; matrix products, arithmetic and copies ran while one was open for 0% of the time, Pallas kernels for 7%

profile of v25, /device:TPU:0, one launch (start us, length us, event | category | flops | bytes accessed | tf_op | source)
XLA Modules:
  0.0 29.6 jit_solution(10535840369071807574)
XLA Ops:
  0.0 0.9 %pack.2 = (bf16[64,768]{1,0:T(8,128)(2,1)S(1)}, bf16[64,1152]{1,0:T(8,128)(2,1)S(1)}) custom-call(bf16[1,64,1536]{2,1,0:T(8,128)(2,1)} %q_ref.3, bf16[1,64,1536]{2,1,0:T(8,128)(2,1)} %k_ref.3, bf16[1,64,1536]{2,1,0:T(8,128)(2,1)} %v_ref.3), custom_call_target="tpu_custom_call" | custom-call | bytes 491520 | tf_op jit(solution)/shard_map/pack/pallas_call | solution.py:211
  0.9 5.1 %collective-permute-start.1 = (bf16[64,768]{1,0:T(8,128)(2,1)S(1)}, bf16[64,768]{1,0:T(8,128)(2,1)S(1)}, u32[]{:S(2)}, u32[]{:S(2)}) collective-permute-start(bf16[64,768]{1,0:T(8,128)(2,1)S(1)} %get-tuple-element.17), channel_id=1, source_target_pairs={{0,12},{4,8},{8,4},{12,0},{1,13},{5,9},{9,5},{13,1},{2,14},{6,10},... | collective-permute-start | bytes 294920 | tf_op jit(solution)/shard_map/ppermute | solution.py:229
  6.1 0.0 collective-permute-start
  6.1 1.0 %pack.3 = (bf16[64,768]{1,0:T(8,128)(2,1)S(1)}, bf16[64,768]{1,0:T(8,128)(2,1)S(1)}, bf16[64,384]{1,0:T(8,128)(2,1)S(1)}, bf16[64,384]{1,0:T(8,128)(2,1)S(1)}, bf16[64,384]{1,0:T(8,128)(2,1)S(1)}) custom-call(bf16[1,64,1536]{2,1,0:T(8,128)(2,1)} %q_ref.3, bf16[1,64,1536]{2,1,0:T(8,128)(2,1)} %k_ref.3, bf16[1,64,1536]{2,1,0:T(8,128)(2,1)} %v_ref.3), custom_call_target="tpu_custom_call" | custom-call | bytes 688128 | tf_op jit(solution)/shard_map/pack/pallas_call | solution.py:211
  7.1 0.7 %collective-permute-start.2 = (bf16[64,768]{1,0:T(8,128)(2,1)S(1)}, bf16[64,768]{1,0:T(8,128)(2,1)S(1)}, u32[]{:S(2)}, u32[]{:S(2)}) collective-permute-start(bf16[64,768]{1,0:T(8,128)(2,1)S(1)} %get-tuple-element.18), channel_id=1, source_target_pairs={{0,8},{4,12},{8,0},{12,4},{1,9},{5,13},{9,1},{13,5},{2,10},{6,14},... | collective-permute-start | bytes 294920 | tf_op jit(solution)/shard_map/ppermute | solution.py:229
  7.8 1.6 %collective-permute-start.3 = (bf16[64,768]{1,0:T(8,128)(2,1)S(1)}, bf16[64,768]{1,0:T(8,128)(2,1)S(1)}, u32[]{:S(2)}, u32[]{:S(2)}) collective-permute-start(bf16[64,768]{1,0:T(8,128)(2,1)S(1)} %get-tuple-element.16.refs_1_), channel_id=1, source_target_pairs={{0,2},{2,0},{1,3},{3,1},{4,6},{6,4},{5,7},{7,5},{8,10},{10,8},{9,1... | collective-permute-start | bytes 294920 | tf_op jit(solution)/shard_map/ppermute | solution.py:232
  9.4 3.6 %collective-permute-start.7 = (bf16[64,384]{1,0:T(8,128)(2,1)S(1)}, bf16[64,384]{1,0:T(8,128)(2,1)S(1)}, u32[]{:S(2)}, u32[]{:S(2)}) collective-permute-start(bf16[64,384]{1,0:T(8,128)(2,1)S(1)} %get-tuple-element.20), channel_id=1, source_target_pairs={{0,12},{4,8},{8,4},{12,0},{1,13},{5,9},{9,5},{13,1},{2,14},{6,10},... | collective-permute-start | bytes 147464 | tf_op jit(solution)/shard_map/ppermute | solution.py:229
  13.0 0.0 collective-permute-done.1.refs_0_
  13.0 0.5 %collective-permute-start.4 = (bf16[64,768]{1,0:T(8,128)(2,1)S(1)}, bf16[64,768]{1,0:T(8,128)(2,1)S(1)}, u32[]{:S(2)}, u32[]{:S(2)}) collective-permute-start(bf16[64,768]{1,0:T(8,128)(2,1)S(1)} %hold.9.refs_1_.refs_2_), channel_id=1, source_target_pairs={{0,2},{2,0},{1,3},{3,1},{4,6},{6,4},{5,7},{7,5},{8,10},{10,8},{9,1... | collective-permute-start | bytes 294920 | tf_op jit(solution)/shard_map/ppermute | solution.py:232
  13.6 0.3 %collective-permute-done.refs_0_.refs_1_ = bf16[64,1152]{1,0:T(8,128)(2,1)S(1)} collective-permute-done((bf16[64,1152]{1,0:T(8,128)(2,1)S(1)}, bf16[64,1152]{1,0:T(8,128)(2,1)S(1)}, u32[]{:S(2)}, u32[]{:S(2)}) %collective-permute-start) | collective-permute-done | bytes 147488 | tf_op jit(solution)/shard_map/ppermute | solution.py:229
  13.9 1.7 %collective-permute-start.5 = (bf16[64,768]{1,0:T(8,128)(2,1)S(1)}, bf16[64,768]{1,0:T(8,128)(2,1)S(1)}, u32[]{:S(2)}, u32[]{:S(2)}) collective-permute-start(bf16[64,768]{1,0:T(8,128)(2,1)S(1)} %bitcast.1), channel_id=1, source_target_pairs={{0,2},{2,0},{1,3},{3,1},{4,6},{6,4},{5,7},{7,5},{8,10},{10,8},{9,1... | collective-permute-start | bytes 294920 | tf_op jit(solution)/shard_map/ppermute | solution.py:232
  15.6 0.6 %collective-permute-done.2.refs_0_ = bf16[64,768]{1,0:T(8,128)(2,1)S(1)} collective-permute-done((bf16[64,768]{1,0:T(8,128)(2,1)S(1)}, bf16[64,768]{1,0:T(8,128)(2,1)S(1)}, u32[]{:S(2)}, u32[]{:S(2)}) %collective-permute-start.2) | collective-permute-done | bytes 98336 | tf_op jit(solution)/shard_map/ppermute | solution.py:229
  16.3 1.3 %collective-permute-start.6 = (bf16[64,768]{1,0:T(8,128)(2,1)S(1)}, bf16[64,768]{1,0:T(8,128)(2,1)S(1)}, u32[]{:S(2)}, u32[]{:S(2)}) collective-permute-start(bf16[64,768]{1,0:T(8,128)(2,1)S(1)} %hold.10.refs_3_.refs_1_), channel_id=1, source_target_pairs={{0,2},{2,0},{1,3},{3,1},{4,6},{6,4},{5,7},{7,5},{8,10},{10,8},{9,1... | collective-permute-start | bytes 294920 | tf_op jit(solution)/shard_map/ppermute | solution.py:232
  17.5 0.0 collective-permute-done.3.refs_0_
  17.5 1.4 %collective-permute-start.9 = (bf16[64,384]{1,0:T(8,128)(2,1)S(1)}, bf16[64,384]{1,0:T(8,128)(2,1)S(1)}, u32[]{:S(2)}, u32[]{:S(2)}) collective-permute-start(bf16[64,384]{1,0:T(8,128)(2,1)S(1)} %hold.15), channel_id=1, source_target_pairs={{0,8},{4,12},{8,0},{12,4},{1,9},{5,13},{9,1},{13,5},{2,10},{6,14},... | collective-permute-start | bytes 147464 | tf_op jit(solution)/shard_map/ppermute | solution.py:229
  18.9 0.0 collective-permute-done.7.refs_0_
  19.0 0.0 collective-permute-done.4.refs_2_.refs_5_
  19.0 0.8 %collective-permute-done.5.refs_3_.refs_6_ = bf16[64,768]{1,0:T(8,128)(2,1)S(1)} collective-permute-done((bf16[64,768]{1,0:T(8,128)(2,1)S(1)}, bf16[64,768]{1,0:T(8,128)(2,1)S(1)}, u32[]{:S(2)}, u32[]{:S(2)}) %collective-permute-start.5) | collective-permute-done | bytes 98336 | tf_op jit(solution)/shard_map/ppermute | solution.py:232
  19.8 1.1 %collective-permute-done.6.refs_7_ = bf16[64,768]{1,0:T(8,128)(2,1)S(1)} collective-permute-done((bf16[64,768]{1,0:T(8,128)(2,1)S(1)}, bf16[64,768]{1,0:T(8,128)(2,1)S(1)}, u32[]{:S(2)}, u32[]{:S(2)}) %collective-permute-start.6) | collective-permute-done | bytes 98336 | tf_op jit(solution)/shard_map/ppermute | solution.py:232
  20.9 0.6 %attend.2 = (bf16[64,384]{1,0:T(8,128)(2,1)S(1)}, bf16[64,384]{1,0:T(8,128)(2,1)S(1)}, bf16[64,384]{1,0:T(8,128)(2,1)S(1)}) custom-call(bf16[64,1152]{1,0:T(8,128)(2,1)S(1)} %collective-permute-done.refs_0_.refs_1_, bf16[64,768]{1,0:T(8,128)(2,1)S(1)} %get-tuple-element.16.refs_1_, bf16[64,768]{1,0:T(8,128)(2,1)S(1)} %hold.9.refs_1_.refs_2_, ...), custom_call_target="tpu_custom_call" | custom-call | flops 150994944 | bytes 1081344 | tf_op jit(solution)/shard_map/attend/pallas_call | solution.py:257
  21.5 1.2 %collective-permute-start.8 = (bf16[64,384]{1,0:T(8,128)(2,1)S(1)}, bf16[64,384]{1,0:T(8,128)(2,1)S(1)}, u32[]{:S(2)}, u32[]{:S(2)}) collective-permute-start(bf16[64,384]{1,0:T(8,128)(2,1)S(1)} %get-tuple-element.22), channel_id=1, source_target_pairs={{0,12},{4,8},{8,4},{12,0},{1,13},{5,9},{9,5},{13,1},{2,14},{6,10},... | collective-permute-start | bytes 147464 | tf_op jit(solution)/shard_map/ppermute | solution.py:229
  22.7 0.0 collective-permute-done.9.refs_0_
  22.7 0.5 %attend.3.refs_1_ = bf16[64,384]{1,0:T(8,128)(2,1)S(1)} custom-call(bf16[64,1152]{1,0:T(8,128)(2,1)S(1)} %collective-permute-done.refs_0_.refs_1_, bf16[64,768]{1,0:T(8,128)(2,1)S(1)} %get-tuple-element.16.refs_1_, bf16[64,768]{1,0:T(8,128)(2,1)S(1)} %hold.9.refs_1_.refs_2_, bf16[64,768]{1,0:T(8,128)(2,1)S(1)} %hold.10.refs_3_.refs_1_, ...), custom_call_target="tpu_custom_call" | custom-call | flops 50331648 | bytes 884736 | tf_op jit(solution)/shard_map/attend/pallas_call | solution.py:257
  23.2 0.7 %collective-permute-start.11 = (bf16[64,384]{1,0:T(8,128)(2,1)S(1)}, bf16[64,384]{1,0:T(8,128)(2,1)S(1)}, u32[]{:S(2)}, u32[]{:S(2)}) collective-permute-start(bf16[64,384]{1,0:T(8,128)(2,1)S(1)} %hold.17), channel_id=1, source_target_pairs={{0,4},{4,0},{8,12},{12,8},{1,5},{5,1},{9,13},{13,9},{2,6},{6,2},{1... | collective-permute-start | bytes 147464 | tf_op jit(solution)/shard_map/ppermute | solution.py:229
  23.9 2.6 %collective-permute-start.10 = (bf16[64,384]{1,0:T(8,128)(2,1)S(1)}, bf16[64,384]{1,0:T(8,128)(2,1)S(1)}, u32[]{:S(2)}, u32[]{:S(2)}) collective-permute-start(bf16[64,384]{1,0:T(8,128)(2,1)S(1)} %attend.3.refs_1_), channel_id=1, source_target_pairs={{0,8},{4,12},{8,0},{12,4},{1,9},{5,13},{9,1},{13,5},{2,10},{6,14},... | collective-permute-start | bytes 147464 | tf_op jit(solution)/shard_map/ppermute | solution.py:229
  26.5 1.0 %collective-permute-done.8.refs_0_ = bf16[64,384]{1,0:T(8,128)(2,1)S(1)} collective-permute-done((bf16[64,384]{1,0:T(8,128)(2,1)S(1)}, bf16[64,384]{1,0:T(8,128)(2,1)S(1)}, u32[]{:S(2)}, u32[]{:S(2)}) %collective-permute-start.8) | collective-permute-done | bytes 49184 | tf_op jit(solution)/shard_map/ppermute | solution.py:229
  27.6 0.3 collective-permute-done.11.refs_3_
  27.9 1.0 %collective-permute-done.10.refs_2_ = bf16[64,384]{1,0:T(8,128)(2,1)S(1)} collective-permute-done((bf16[64,384]{1,0:T(8,128)(2,1)S(1)}, bf16[64,384]{1,0:T(8,128)(2,1)S(1)}, u32[]{:S(2)}, u32[]{:S(2)}) %collective-permute-start.10) | collective-permute-done | bytes 49184 | tf_op jit(solution)/shard_map/ppermute | solution.py:229
  28.9 0.7 %unpack.1 = bf16[1,64,1536]{2,1,0:T(8,128)(2,1)} custom-call(bf16[64,384]{1,0:T(8,128)(2,1)S(1)} %get-tuple-element.21.refs_1_.refs_0_, bf16[64,384]{1,0:T(8,128)(2,1)S(1)} %hold.14.refs_1_, bf16[64,384]{1,0:T(8,128)(2,1)S(1)} %collective-permute-done.10.refs_2_, bf16[64,384]{1,0:T(8,128)(2,1)S(1)} %collective-permute-done.11.refs_3_), custom_call_target="tpu_custom_call" | custom-call | bytes 393216 | tf_op jit(solution)/shard_map/unpack/pallas_call | solution.py:281
  (11 shorter events, 0.0 us)
Async XLA Ops:
  0.9 12.1 %collective-permute-start.1 = (bf16[64,768]{1,0:T(8,128)(2,1)S(1)}, bf16[64,768]{1,0:T(8,128)(2,1)S(1)}, u32[]{:S(2)}, u32[]{:S(2)}) collective-permute-start(bf16[64,768]{1,0:T(8,128)(2,1)S(1)} %get-tuple-element.17), channel_id=1, source_target_pairs={{0,12},{4,8},{8,4},{12,0},{1,13},{5,9},{9,5},{13,1},{2,14},{6,10},... | collective-permute-start | bytes 294920 | tf_op jit(solution)/shard_map/ppermute | solution.py:229
  6.1 7.8 %collective-permute-start = (bf16[64,1152]{1,0:T(8,128)(2,1)S(1)}, bf16[64,1152]{1,0:T(8,128)(2,1)S(1)}, u32[]{:S(2)}, u32[]{:S(2)}) collective-permute-start(bf16[64,1152]{1,0:T(8,128)(2,1)S(1)} %get-tuple-element.15), channel_id=1, source_target_pairs={{0,4},{4,0},{8,12},{12,8},{1,5},{5,1},{9,13},{13,9},{2,6},{6,2},{1... | collective-permute-start | bytes 442376 | tf_op jit(solution)/shard_map/ppermute | solution.py:229
  7.1 9.2 %collective-permute-start.2 = (bf16[64,768]{1,0:T(8,128)(2,1)S(1)}, bf16[64,768]{1,0:T(8,128)(2,1)S(1)}, u32[]{:S(2)}, u32[]{:S(2)}) collective-permute-start(bf16[64,768]{1,0:T(8,128)(2,1)S(1)} %get-tuple-element.18), channel_id=1, source_target_pairs={{0,8},{4,12},{8,0},{12,4},{1,9},{5,13},{9,1},{13,5},{2,10},{6,14},... | collective-permute-start | bytes 294920 | tf_op jit(solution)/shard_map/ppermute | solution.py:229
  7.8 9.7 %collective-permute-start.3 = (bf16[64,768]{1,0:T(8,128)(2,1)S(1)}, bf16[64,768]{1,0:T(8,128)(2,1)S(1)}, u32[]{:S(2)}, u32[]{:S(2)}) collective-permute-start(bf16[64,768]{1,0:T(8,128)(2,1)S(1)} %get-tuple-element.16.refs_1_), channel_id=1, source_target_pairs={{0,2},{2,0},{1,3},{3,1},{4,6},{6,4},{5,7},{7,5},{8,10},{10,8},{9,1... | collective-permute-start | bytes 294920 | tf_op jit(solution)/shard_map/ppermute | solution.py:232
  9.4 9.5 %collective-permute-start.7 = (bf16[64,384]{1,0:T(8,128)(2,1)S(1)}, bf16[64,384]{1,0:T(8,128)(2,1)S(1)}, u32[]{:S(2)}, u32[]{:S(2)}) collective-permute-start(bf16[64,384]{1,0:T(8,128)(2,1)S(1)} %get-tuple-element.20), channel_id=1, source_target_pairs={{0,12},{4,8},{8,4},{12,0},{1,13},{5,9},{9,5},{13,1},{2,14},{6,10},... | collective-permute-start | bytes 147464 | tf_op jit(solution)/shard_map/ppermute | solution.py:229
  13.0 5.9 %collective-permute-start.4 = (bf16[64,768]{1,0:T(8,128)(2,1)S(1)}, bf16[64,768]{1,0:T(8,128)(2,1)S(1)}, u32[]{:S(2)}, u32[]{:S(2)}) collective-permute-start(bf16[64,768]{1,0:T(8,128)(2,1)S(1)} %hold.9.refs_1_.refs_2_), channel_id=1, source_target_pairs={{0,2},{2,0},{1,3},{3,1},{4,6},{6,4},{5,7},{7,5},{8,10},{10,8},{9,1... | collective-permute-start | bytes 294920 | tf_op jit(solution)/shard_map/ppermute | solution.py:232
  13.9 5.9 %collective-permute-start.5 = (bf16[64,768]{1,0:T(8,128)(2,1)S(1)}, bf16[64,768]{1,0:T(8,128)(2,1)S(1)}, u32[]{:S(2)}, u32[]{:S(2)}) collective-permute-start(bf16[64,768]{1,0:T(8,128)(2,1)S(1)} %bitcast.1), channel_id=1, source_target_pairs={{0,2},{2,0},{1,3},{3,1},{4,6},{6,4},{5,7},{7,5},{8,10},{10,8},{9,1... | collective-permute-start | bytes 294920 | tf_op jit(solution)/shard_map/ppermute | solution.py:232
  16.3 4.6 %collective-permute-start.6 = (bf16[64,768]{1,0:T(8,128)(2,1)S(1)}, bf16[64,768]{1,0:T(8,128)(2,1)S(1)}, u32[]{:S(2)}, u32[]{:S(2)}) collective-permute-start(bf16[64,768]{1,0:T(8,128)(2,1)S(1)} %hold.10.refs_3_.refs_1_), channel_id=1, source_target_pairs={{0,2},{2,0},{1,3},{3,1},{4,6},{6,4},{5,7},{7,5},{8,10},{10,8},{9,1... | collective-permute-start | bytes 294920 | tf_op jit(solution)/shard_map/ppermute | solution.py:232
  17.5 5.1 %collective-permute-start.9 = (bf16[64,384]{1,0:T(8,128)(2,1)S(1)}, bf16[64,384]{1,0:T(8,128)(2,1)S(1)}, u32[]{:S(2)}, u32[]{:S(2)}) collective-permute-start(bf16[64,384]{1,0:T(8,128)(2,1)S(1)} %hold.15), channel_id=1, source_target_pairs={{0,8},{4,12},{8,0},{12,4},{1,9},{5,13},{9,1},{13,5},{2,10},{6,14},... | collective-permute-start | bytes 147464 | tf_op jit(solution)/shard_map/ppermute | solution.py:229
  21.5 6.1 %collective-permute-start.8 = (bf16[64,384]{1,0:T(8,128)(2,1)S(1)}, bf16[64,384]{1,0:T(8,128)(2,1)S(1)}, u32[]{:S(2)}, u32[]{:S(2)}) collective-permute-start(bf16[64,384]{1,0:T(8,128)(2,1)S(1)} %get-tuple-element.22), channel_id=1, source_target_pairs={{0,12},{4,8},{8,4},{12,0},{1,13},{5,9},{9,5},{13,1},{2,14},{6,10},... | collective-permute-start | bytes 147464 | tf_op jit(solution)/shard_map/ppermute | solution.py:229
  23.2 4.7 %collective-permute-start.11 = (bf16[64,384]{1,0:T(8,128)(2,1)S(1)}, bf16[64,384]{1,0:T(8,128)(2,1)S(1)}, u32[]{:S(2)}, u32[]{:S(2)}) collective-permute-start(bf16[64,384]{1,0:T(8,128)(2,1)S(1)} %hold.17), channel_id=1, source_target_pairs={{0,4},{4,0},{8,12},{12,8},{1,5},{5,1},{9,13},{13,9},{2,6},{6,2},{1... | collective-permute-start | bytes 147464 | tf_op jit(solution)/shard_map/ppermute | solution.py:229
  23.9 5.0 %collective-permute-start.10 = (bf16[64,384]{1,0:T(8,128)(2,1)S(1)}, bf16[64,384]{1,0:T(8,128)(2,1)S(1)}, u32[]{:S(2)}, u32[]{:S(2)}) collective-permute-start(bf16[64,384]{1,0:T(8,128)(2,1)S(1)} %attend.3.refs_1_), channel_id=1, source_target_pairs={{0,8},{4,12},{8,0},{12,4},{1,9},{5,13},{9,1},{13,5},{2,10},{6,14},... | collective-permute-start | bytes 147464 | tf_op jit(solution)/shard_map/ppermute | solution.py:229

commit v26 on v25

--- a/solution.py
+++ b/solution.py
@@ -271,7 +271,6 @@
     mixed = dict(zip([0, 1] + far[:-1], attend([near_q] + far_q[:-1], [(0, 0), (0, 1), (1, None)])))
     last_q = hold([far_q[-1]], [mixed[0]])
     mixed[far[-1]] = attend(last_q, [(0, None)])[0]
-    mixed[1] = hold([mixed[1]], [mixed[far[-1]]])[0]
     back = {s: to_block(mixed[s], s) for s in far + [1]}
     early = far[:-1]
     back.update(zip(early, hold([back[s] for s in early], effort=EFFORT)))

time: 29.8 us -> 29.8 us (level)
  transfers between devices with their start and end apart: 12 -> 12, of which waited for: 7 -> 6; matrix products, arithmetic and copies ran while one was open for 0% -> 0% of each run, Pallas kernels for 7% -> 7%
where the time goes in v26:
time: 29.8 us; the launch traced here: 29.6 us
  starting transfers between devices  20.5 us (69%)
  waiting for transfers between devices  5.21 us (17%)
  Pallas kernels  3.79 us (13%)
    ppermute x8, starting transfers between devices, to_block(): return lax.ppermute(array, 'blk', [(i, i ^ s) for i in range(blocks)])  15.3 us
    ppermute x4, starting transfers between devices, to_column(): lax.ppermute(array, 'uly', [(i, (i + t) % columns_of) for i in range(colu...  5.16 us
    ppermute x8, waiting for transfers between devices, to_block(): return lax.ppermute(array, 'blk', [(i, i ^ s) for i in range(blocks)])  3.3 us
    pallas_call x2, Pallas kernels, pack(): pl.pallas_call(functools.partial(pack_kernel, cut, part), out_shape=[jax....  1.94 us
    ppermute x4, waiting for transfers between devices, to_column(): lax.ppermute(array, 'uly', [(i, (i + t) % columns_of) for i in range(colu...  1.91 us
    pallas_call x2, Pallas kernels, attend(): pl.pallas_call(functools.partial(attend_kernel, len(holders), keys, query...  1.13 us
    pallas_call x1, Pallas kernels, local_blocks(): pl.pallas_call(functools.partial(unpack_kernel, order, part), out_shape=j...  0.7 us
  transfers between devices with their start and end apart: 12, of which 6 were waited for; matrix products, arithmetic and copies ran while one was open for 0% of the time, Pallas kernels for 7%

profile of v26, /device:TPU:0, one launch (start us, length us, event | category | flops | bytes accessed | tf_op | source)
XLA Modules:
  0.0 29.6 jit_solution(13438292991397483511)
XLA Ops:
  0.0 0.9 %pack.2 = (bf16[64,768]{1,0:T(8,128)(2,1)S(1)}, bf16[64,1152]{1,0:T(8,128)(2,1)S(1)}) custom-call(bf16[1,64,1536]{2,1,0:T(8,128)(2,1)} %q_ref.3, bf16[1,64,1536]{2,1,0:T(8,128)(2,1)} %k_ref.3, bf16[1,64,1536]{2,1,0:T(8,128)(2,1)} %v_ref.3), custom_call_target="tpu_custom_call" | custom-call | bytes 491520 | tf_op jit(solution)/shard_map/pack/pallas_call | solution.py:211
  0.9 5.1 %collective-permute-start.1 = (bf16[64,768]{1,0:T(8,128)(2,1)S(1)}, bf16[64,768]{1,0:T(8,128)(2,1)S(1)}, u32[]{:S(2)}, u32[]{:S(2)}) collective-permute-start(bf16[64,768]{1,0:T(8,128)(2,1)S(1)} %get-tuple-element.17), channel_id=1, source_target_pairs={{0,12},{4,8},{8,4},{12,0},{1,13},{5,9},{9,5},{13,1},{2,14},{6,10},... | collective-permute-start | bytes 294920 | tf_op jit(solution)/shard_map/ppermute | solution.py:229
  6.1 0.0 collective-permute-start
  6.1 1.0 %pack.3 = (bf16[64,768]{1,0:T(8,128)(2,1)S(1)}, bf16[64,768]{1,0:T(8,128)(2,1)S(1)}, bf16[64,384]{1,0:T(8,128)(2,1)S(1)}, bf16[64,384]{1,0:T(8,128)(2,1)S(1)}, bf16[64,384]{1,0:T(8,128)(2,1)S(1)}) custom-call(bf16[1,64,1536]{2,1,0:T(8,128)(2,1)} %q_ref.3, bf16[1,64,1536]{2,1,0:T(8,128)(2,1)} %k_ref.3, bf16[1,64,1536]{2,1,0:T(8,128)(2,1)} %v_ref.3), custom_call_target="tpu_custom_call" | custom-call | bytes 688128 | tf_op jit(solution)/shard_map/pack/pallas_call | solution.py:211
  7.1 0.7 %collective-permute-start.2 = (bf16[64,768]{1,0:T(8,128)(2,1)S(1)}, bf16[64,768]{1,0:T(8,128)(2,1)S(1)}, u32[]{:S(2)}, u32[]{:S(2)}) collective-permute-start(bf16[64,768]{1,0:T(8,128)(2,1)S(1)} %get-tuple-element.18), channel_id=1, source_target_pairs={{0,8},{4,12},{8,0},{12,4},{1,9},{5,13},{9,1},{13,5},{2,10},{6,14},... | collective-permute-start | bytes 294920 | tf_op jit(solution)/shard_map/ppermute | solution.py:229
  7.8 1.6 %collective-permute-start.3 = (bf16[64,768]{1,0:T(8,128)(2,1)S(1)}, bf16[64,768]{1,0:T(8,128)(2,1)S(1)}, u32[]{:S(2)}, u32[]{:S(2)}) collective-permute-start(bf16[64,768]{1,0:T(8,128)(2,1)S(1)} %get-tuple-element.16.refs_1_), channel_id=1, source_target_pairs={{0,2},{2,0},{1,3},{3,1},{4,6},{6,4},{5,7},{7,5},{8,10},{10,8},{9,1... | collective-permute-start | bytes 294920 | tf_op jit(solution)/shard_map/ppermute | solution.py:232
  9.4 3.6 %collective-permute-start.7 = (bf16[64,384]{1,0:T(8,128)(2,1)S(1)}, bf16[64,384]{1,0:T(8,128)(2,1)S(1)}, u32[]{:S(2)}, u32[]{:S(2)}) collective-permute-start(bf16[64,384]{1,0:T(8,128)(2,1)S(1)} %get-tuple-element.20), channel_id=1, source_target_pairs={{0,12},{4,8},{8,4},{12,0},{1,13},{5,9},{9,5},{13,1},{2,14},{6,10},... | collective-permute-start | bytes 147464 | tf_op jit(solution)/shard_map/ppermute | solution.py:229
  13.0 0.0 collective-permute-done.1.refs_0_
  13.0 0.5 %collective-permute-start.4 = (bf16[64,768]{1,0:T(8,128)(2,1)S(1)}, bf16[64,768]{1,0:T(8,128)(2,1)S(1)}, u32[]{:S(2)}, u32[]{:S(2)}) collective-permute-start(bf16[64,768]{1,0:T(8,128)(2,1)S(1)} %hold.8.refs_1_.refs_2_), channel_id=1, source_target_pairs={{0,2},{2,0},{1,3},{3,1},{4,6},{6,4},{5,7},{7,5},{8,10},{10,8},{9,1... | collective-permute-start | bytes 294920 | tf_op jit(solution)/shard_map/ppermute | solution.py:232
  13.6 0.3 %collective-permute-done.refs_0_.refs_1_ = bf16[64,1152]{1,0:T(8,128)(2,1)S(1)} collective-permute-done((bf16[64,1152]{1,0:T(8,128)(2,1)S(1)}, bf16[64,1152]{1,0:T(8,128)(2,1)S(1)}, u32[]{:S(2)}, u32[]{:S(2)}) %collective-permute-start) | collective-permute-done | bytes 147488 | tf_op jit(solution)/shard_map/ppermute | solution.py:229
  13.9 1.7 %collective-permute-start.5 = (bf16[64,768]{1,0:T(8,128)(2,1)S(1)}, bf16[64,768]{1,0:T(8,128)(2,1)S(1)}, u32[]{:S(2)}, u32[]{:S(2)}) collective-permute-start(bf16[64,768]{1,0:T(8,128)(2,1)S(1)} %bitcast.1), channel_id=1, source_target_pairs={{0,2},{2,0},{1,3},{3,1},{4,6},{6,4},{5,7},{7,5},{8,10},{10,8},{9,1... | collective-permute-start | bytes 294920 | tf_op jit(solution)/shard_map/ppermute | solution.py:232
  15.6 0.6 %collective-permute-done.2.refs_0_ = bf16[64,768]{1,0:T(8,128)(2,1)S(1)} collective-permute-done((bf16[64,768]{1,0:T(8,128)(2,1)S(1)}, bf16[64,768]{1,0:T(8,128)(2,1)S(1)}, u32[]{:S(2)}, u32[]{:S(2)}) %collective-permute-start.2) | collective-permute-done | bytes 98336 | tf_op jit(solution)/shard_map/ppermute | solution.py:229
  16.3 1.3 %collective-permute-start.6 = (bf16[64,768]{1,0:T(8,128)(2,1)S(1)}, bf16[64,768]{1,0:T(8,128)(2,1)S(1)}, u32[]{:S(2)}, u32[]{:S(2)}) collective-permute-start(bf16[64,768]{1,0:T(8,128)(2,1)S(1)} %hold.9.refs_3_.refs_1_), channel_id=1, source_target_pairs={{0,2},{2,0},{1,3},{3,1},{4,6},{6,4},{5,7},{7,5},{8,10},{10,8},{9,1... | collective-permute-start | bytes 294920 | tf_op jit(solution)/shard_map/ppermute | solution.py:232
  17.5 0.0 collective-permute-done.3.refs_0_
  17.5 1.4 %collective-permute-start.9 = (bf16[64,384]{1,0:T(8,128)(2,1)S(1)}, bf16[64,384]{1,0:T(8,128)(2,1)S(1)}, u32[]{:S(2)}, u32[]{:S(2)}) collective-permute-start(bf16[64,384]{1,0:T(8,128)(2,1)S(1)} %hold.14), channel_id=1, source_target_pairs={{0,8},{4,12},{8,0},{12,4},{1,9},{5,13},{9,1},{13,5},{2,10},{6,14},... | collective-permute-start | bytes 147464 | tf_op jit(solution)/shard_map/ppermute | solution.py:229
  18.9 0.0 collective-permute-done.7.refs_0_
  19.0 0.0 collective-permute-done.4.refs_2_.refs_5_
  19.0 0.8 %collective-permute-done.5.refs_3_.refs_6_ = bf16[64,768]{1,0:T(8,128)(2,1)S(1)} collective-permute-done((bf16[64,768]{1,0:T(8,128)(2,1)S(1)}, bf16[64,768]{1,0:T(8,128)(2,1)S(1)}, u32[]{:S(2)}, u32[]{:S(2)}) %collective-permute-start.5) | collective-permute-done | bytes 98336 | tf_op jit(solution)/shard_map/ppermute | solution.py:232
  19.8 1.1 %collective-permute-done.6.refs_7_ = bf16[64,768]{1,0:T(8,128)(2,1)S(1)} collective-permute-done((bf16[64,768]{1,0:T(8,128)(2,1)S(1)}, bf16[64,768]{1,0:T(8,128)(2,1)S(1)}, u32[]{:S(2)}, u32[]{:S(2)}) %collective-permute-start.6) | collective-permute-done | bytes 98336 | tf_op jit(solution)/shard_map/ppermute | solution.py:232
  20.9 0.6 %attend.2 = (bf16[64,384]{1,0:T(8,128)(2,1)S(1)}, bf16[64,384]{1,0:T(8,128)(2,1)S(1)}, bf16[64,384]{1,0:T(8,128)(2,1)S(1)}) custom-call(bf16[64,1152]{1,0:T(8,128)(2,1)S(1)} %collective-permute-done.refs_0_.refs_1_, bf16[64,768]{1,0:T(8,128)(2,1)S(1)} %get-tuple-element.16.refs_1_, bf16[64,768]{1,0:T(8,128)(2,1)S(1)} %hold.8.refs_1_.refs_2_, ...), custom_call_target="tpu_custom_call" | custom-call | flops 150994944 | bytes 1081344 | tf_op jit(solution)/shard_map/attend/pallas_call | solution.py:257
  21.5 1.2 %collective-permute-start.8 = (bf16[64,384]{1,0:T(8,128)(2,1)S(1)}, bf16[64,384]{1,0:T(8,128)(2,1)S(1)}, u32[]{:S(2)}, u32[]{:S(2)}) collective-permute-start(bf16[64,384]{1,0:T(8,128)(2,1)S(1)} %get-tuple-element.22), channel_id=1, source_target_pairs={{0,12},{4,8},{8,4},{12,0},{1,13},{5,9},{9,5},{13,1},{2,14},{6,10},... | collective-permute-start | bytes 147464 | tf_op jit(solution)/shard_map/ppermute | solution.py:229
  22.7 0.7 %collective-permute-start.11 = (bf16[64,384]{1,0:T(8,128)(2,1)S(1)}, bf16[64,384]{1,0:T(8,128)(2,1)S(1)}, u32[]{:S(2)}, u32[]{:S(2)}) collective-permute-start(bf16[64,384]{1,0:T(8,128)(2,1)S(1)} %get-tuple-element.24), channel_id=1, source_target_pairs={{0,4},{4,0},{8,12},{12,8},{1,5},{5,1},{9,13},{13,9},{2,6},{6,2},{1... | collective-permute-start | bytes 147464 | tf_op jit(solution)/shard_map/ppermute | solution.py:229
  23.3 0.0 collective-permute-done.9.refs_0_
  23.3 0.5 %attend.3 = bf16[64,384]{1,0:T(8,128)(2,1)S(1)} custom-call(bf16[64,1152]{1,0:T(8,128)(2,1)S(1)} %collective-permute-done.refs_0_.refs_1_, bf16[64,768]{1,0:T(8,128)(2,1)S(1)} %get-tuple-element.16.refs_1_, bf16[64,768]{1,0:T(8,128)(2,1)S(1)} %hold.8.refs_1_.refs_2_, bf16[64,768]{1,0:T(8,128)(2,1)S(1)} %hold.9.refs_3_.refs_1_, ...), custom_call_target="tpu_custom_call" | custom-call | flops 50331648 | bytes 884736 | tf_op jit(solution)/shard_map/attend/pallas_call | solution.py:257
  23.8 2.7 %collective-permute-start.10 = (bf16[64,384]{1,0:T(8,128)(2,1)S(1)}, bf16[64,384]{1,0:T(8,128)(2,1)S(1)}, u32[]{:S(2)}, u32[]{:S(2)}) collective-permute-start(bf16[64,384]{1,0:T(8,128)(2,1)S(1)} %attend.3), channel_id=1, source_target_pairs={{0,8},{4,12},{8,0},{12,4},{1,9},{5,13},{9,1},{13,5},{2,10},{6,14},... | collective-permute-start | bytes 147464 | tf_op jit(solution)/shard_map/ppermute | solution.py:229
  26.5 0.9 %collective-permute-done.8.refs_0_ = bf16[64,384]{1,0:T(8,128)(2,1)S(1)} collective-permute-done((bf16[64,384]{1,0:T(8,128)(2,1)S(1)}, bf16[64,384]{1,0:T(8,128)(2,1)S(1)}, u32[]{:S(2)}, u32[]{:S(2)}) %collective-permute-start.8) | collective-permute-done | bytes 49184 | tf_op jit(solution)/shard_map/ppermute | solution.py:229
  27.5 0.0 collective-permute-done.11.refs_3_
  27.5 1.4 %collective-permute-done.10.refs_2_ = bf16[64,384]{1,0:T(8,128)(2,1)S(1)} collective-permute-done((bf16[64,384]{1,0:T(8,128)(2,1)S(1)}, bf16[64,384]{1,0:T(8,128)(2,1)S(1)}, u32[]{:S(2)}, u32[]{:S(2)}) %collective-permute-start.10) | collective-permute-done | bytes 49184 | tf_op jit(solution)/shard_map/ppermute | solution.py:229
  28.9 0.7 %unpack.1 = bf16[1,64,1536]{2,1,0:T(8,128)(2,1)} custom-call(bf16[64,384]{1,0:T(8,128)(2,1)S(1)} %get-tuple-element.21.refs_1_.refs_0_, bf16[64,384]{1,0:T(8,128)(2,1)S(1)} %hold.13.refs_1_, bf16[64,384]{1,0:T(8,128)(2,1)S(1)} %collective-permute-done.10.refs_2_, bf16[64,384]{1,0:T(8,128)(2,1)S(1)} %collective-permute-done.11.refs_3_), custom_call_target="tpu_custom_call" | custom-call | bytes 393216 | tf_op jit(solution)/shard_map/unpack/pallas_call | solution.py:280
  (10 shorter events, 0.0 us)
Async XLA Ops:
  0.9 12.1 %collective-permute-start.1 = (bf16[64,768]{1,0:T(8,128)(2,1)S(1)}, bf16[64,768]{1,0:T(8,128)(2,1)S(1)}, u32[]{:S(2)}, u32[]{:S(2)}) collective-permute-start(bf16[64,768]{1,0:T(8,128)(2,1)S(1)} %get-tuple-element.17), channel_id=1, source_target_pairs={{0,12},{4,8},{8,4},{12,0},{1,13},{5,9},{9,5},{13,1},{2,14},{6,10},... | collective-permute-start | bytes 294920 | tf_op jit(solution)/shard_map/ppermute | solution.py:229
  6.1 7.8 %collective-permute-start = (bf16[64,1152]{1,0:T(8,128)(2,1)S(1)}, bf16[64,1152]{1,0:T(8,128)(2,1)S(1)}, u32[]{:S(2)}, u32[]{:S(2)}) collective-permute-start(bf16[64,1152]{1,0:T(8,128)(2,1)S(1)} %get-tuple-element.15), channel_id=1, source_target_pairs={{0,4},{4,0},{8,12},{12,8},{1,5},{5,1},{9,13},{13,9},{2,6},{6,2},{1... | collective-permute-start | bytes 442376 | tf_op jit(solution)/shard_map/ppermute | solution.py:229
  7.1 9.2 %collective-permute-start.2 = (bf16[64,768]{1,0:T(8,128)(2,1)S(1)}, bf16[64,768]{1,0:T(8,128)(2,1)S(1)}, u32[]{:S(2)}, u32[]{:S(2)}) collective-permute-start(bf16[64,768]{1,0:T(8,128)(2,1)S(1)} %get-tuple-element.18), channel_id=1, source_target_pairs={{0,8},{4,12},{8,0},{12,4},{1,9},{5,13},{9,1},{13,5},{2,10},{6,14},... | collective-permute-start | bytes 294920 | tf_op jit(solution)/shard_map/ppermute | solution.py:229
  7.8 9.7 %collective-permute-start.3 = (bf16[64,768]{1,0:T(8,128)(2,1)S(1)}, bf16[64,768]{1,0:T(8,128)(2,1)S(1)}, u32[]{:S(2)}, u32[]{:S(2)}) collective-permute-start(bf16[64,768]{1,0:T(8,128)(2,1)S(1)} %get-tuple-element.16.refs_1_), channel_id=1, source_target_pairs={{0,2},{2,0},{1,3},{3,1},{4,6},{6,4},{5,7},{7,5},{8,10},{10,8},{9,1... | collective-permute-start | bytes 294920 | tf_op jit(solution)/shard_map/ppermute | solution.py:232
  9.4 9.5 %collective-permute-start.7 = (bf16[64,384]{1,0:T(8,128)(2,1)S(1)}, bf16[64,384]{1,0:T(8,128)(2,1)S(1)}, u32[]{:S(2)}, u32[]{:S(2)}) collective-permute-start(bf16[64,384]{1,0:T(8,128)(2,1)S(1)} %get-tuple-element.20), channel_id=1, source_target_pairs={{0,12},{4,8},{8,4},{12,0},{1,13},{5,9},{9,5},{13,1},{2,14},{6,10},... | collective-permute-start | bytes 147464 | tf_op jit(solution)/shard_map/ppermute | solution.py:229
  13.0 5.9 %collective-permute-start.4 = (bf16[64,768]{1,0:T(8,128)(2,1)S(1)}, bf16[64,768]{1,0:T(8,128)(2,1)S(1)}, u32[]{:S(2)}, u32[]{:S(2)}) collective-permute-start(bf16[64,768]{1,0:T(8,128)(2,1)S(1)} %hold.8.refs_1_.refs_2_), channel_id=1, source_target_pairs={{0,2},{2,0},{1,3},{3,1},{4,6},{6,4},{5,7},{7,5},{8,10},{10,8},{9,1... | collective-permute-start | bytes 294920 | tf_op jit(solution)/shard_map/ppermute | solution.py:232
  13.9 5.9 %collective-permute-start.5 = (bf16[64,768]{1,0:T(8,128)(2,1)S(1)}, bf16[64,768]{1,0:T(8,128)(2,1)S(1)}, u32[]{:S(2)}, u32[]{:S(2)}) collective-permute-start(bf16[64,768]{1,0:T(8,128)(2,1)S(1)} %bitcast.1), channel_id=1, source_target_pairs={{0,2},{2,0},{1,3},{3,1},{4,6},{6,4},{5,7},{7,5},{8,10},{10,8},{9,1... | collective-permute-start | bytes 294920 | tf_op jit(solution)/shard_map/ppermute | solution.py:232
  16.3 4.6 %collective-permute-start.6 = (bf16[64,768]{1,0:T(8,128)(2,1)S(1)}, bf16[64,768]{1,0:T(8,128)(2,1)S(1)}, u32[]{:S(2)}, u32[]{:S(2)}) collective-permute-start(bf16[64,768]{1,0:T(8,128)(2,1)S(1)} %hold.9.refs_3_.refs_1_), channel_id=1, source_target_pairs={{0,2},{2,0},{1,3},{3,1},{4,6},{6,4},{5,7},{7,5},{8,10},{10,8},{9,1... | collective-permute-start | bytes 294920 | tf_op jit(solution)/shard_map/ppermute | solution.py:232
  17.5 5.8 %collective-permute-start.9 = (bf16[64,384]{1,0:T(8,128)(2,1)S(1)}, bf16[64,384]{1,0:T(8,128)(2,1)S(1)}, u32[]{:S(2)}, u32[]{:S(2)}) collective-permute-start(bf16[64,384]{1,0:T(8,128)(2,1)S(1)} %hold.14), channel_id=1, source_target_pairs={{0,8},{4,12},{8,0},{12,4},{1,9},{5,13},{9,1},{13,5},{2,10},{6,14},... | collective-permute-start | bytes 147464 | tf_op jit(solution)/shard_map/ppermute | solution.py:229
  21.5 6.0 %collective-permute-start.8 = (bf16[64,384]{1,0:T(8,128)(2,1)S(1)}, bf16[64,384]{1,0:T(8,128)(2,1)S(1)}, u32[]{:S(2)}, u32[]{:S(2)}) collective-permute-start(bf16[64,384]{1,0:T(8,128)(2,1)S(1)} %get-tuple-element.22), channel_id=1, source_target_pairs={{0,12},{4,8},{8,4},{12,0},{1,13},{5,9},{9,5},{13,1},{2,14},{6,10},... | collective-permute-start | bytes 147464 | tf_op jit(solution)/shard_map/ppermute | solution.py:229
  22.7 4.8 %collective-permute-start.11 = (bf16[64,384]{1,0:T(8,128)(2,1)S(1)}, bf16[64,384]{1,0:T(8,128)(2,1)S(1)}, u32[]{:S(2)}, u32[]{:S(2)}) collective-permute-start(bf16[64,384]{1,0:T(8,128)(2,1)S(1)} %get-tuple-element.24), channel_id=1, source_target_pairs={{0,4},{4,0},{8,12},{12,8},{1,5},{5,1},{9,13},{13,9},{2,6},{6,2},{1... | collective-permute-start | bytes 147464 | tf_op jit(solution)/shard_map/ppermute | solution.py:229
  23.8 5.1 %collective-permute-start.10 = (bf16[64,384]{1,0:T(8,128)(2,1)S(1)}, bf16[64,384]{1,0:T(8,128)(2,1)S(1)}, u32[]{:S(2)}, u32[]{:S(2)}) collective-permute-start(bf16[64,384]{1,0:T(8,128)(2,1)S(1)} %attend.3), channel_id=1, source_target_pairs={{0,8},{4,12},{8,0},{12,4},{1,9},{5,13},{9,1},{13,5},{2,10},{6,14},... | collective-permute-start | bytes 147464 | tf_op jit(solution)/shard_map/ppermute | solution.py:229
